TPU v7x, 32 devices: a whole 2x2x4 slice. The times are simulated.
32 devices in a mesh: dp: 4 (over y, core), fsdp: 8 (over z, x).
Axes of the slice: x: 2, y: 2, z: 4, core: 2. Of those that a mesh axis runs over, the one named last changes fastest.
Arguments:
- tokens: bfloat16 [4096, 768], P(('dp', 'fsdp')), may hold values from -6 to 6
- cotangent: bfloat16 [4096, 768], P(('dp', 'fsdp')), may hold values from -6 to 6
- seq_lens: int32 [32, 8], P(('dp', 'fsdp')), may hold values from 0 to 128, as said below
- routes: int32 [4096, 1], P(('dp', 'fsdp')), may hold values from 0 to 7
- norm_gain: bfloat16 [768], P(('dp', 'fsdp')), may hold values from 0.5 to 1.5
- input_proj: bfloat16 [768, 3072], P(('dp', 'fsdp')), may hold values from -0.21875 to 0.21875
- conv_weight: bfloat16 [4, 1536], P(None, ('dp', 'fsdp')), may hold values from -3 to 3
- conv_bias: bfloat16 [1536], P(('dp', 'fsdp')), may hold values from -1.5 to 1.5
- select_proj: bfloat16 [1536, 80], P(('dp', 'fsdp')), may hold values from -0.15625 to 0.15625
- step_proj: bfloat16 [48, 1536], P(None, ('dp', 'fsdp')), may hold values from -0.875 to 0.875
- step_bias: bfloat16 [1536], P(('dp', 'fsdp')), may hold values from -4 to -1
- decay_log: bfloat16 [16, 1536], P(None, ('dp', 'fsdp')), may hold values from 0 to 2.765625
- skip_gain: bfloat16 [1536], P(('dp', 'fsdp')), may hold values from 0.5 to 1.5
- output_proj: bfloat16 [1536, 768], P(('dp', 'fsdp')), may hold values from -0.3125 to 0.3125
- moe_gain: bfloat16 [768], P(('dp', 'fsdp')), may hold values from 0.5 to 1.5
- router_weight: bfloat16 [768, 8], P(('dp', 'fsdp')), may hold values from -0.21875 to 0.21875
- up_weight: bfloat16 [8, 3072, 768], P('fsdp', 'dp'), may hold values from -0.21875 to 0.21875
- down_weight: bfloat16 [8, 3072, 768], P('fsdp', 'dp'), may hold values from -0.21875 to 0.21875
Outputs:
- block_out: bfloat16 [4096, 768], P(('dp', 'fsdp'))
- tokens_grad: float32 [4096, 768], P(('dp', 'fsdp'))
- norm_gain_grad: float32 [768], P(('dp', 'fsdp'))
- input_proj_grad: float32 [768, 3072], P(('dp', 'fsdp'))
- conv_weight_grad: float32 [4, 1536], P(None, ('dp', 'fsdp'))
- conv_bias_grad: float32 [1536], P(('dp', 'fsdp'))
- select_proj_grad: float32 [1536, 80], P(('dp', 'fsdp'))
- step_proj_grad: float32 [48, 1536], P(None, ('dp', 'fsdp'))
- step_bias_grad: float32 [1536], P(('dp', 'fsdp'))
- decay_log_grad: float32 [16, 1536], P(None, ('dp', 'fsdp'))
- skip_gain_grad: float32 [1536], P(('dp', 'fsdp'))
- output_proj_grad: float32 [1536, 768], P(('dp', 'fsdp'))
- moe_gain_grad: float32 [768], P(('dp', 'fsdp'))
- router_weight_grad: float32 [768, 8], P(('dp', 'fsdp'))
- up_weight_grad: float32 [8, 3072, 768], P('fsdp', 'dp')
- down_weight_grad: float32 [8, 3072, 768], P('fsdp', 'dp')
Inputs may be any that keep to these rules, and one draw needn't show every extreme that they name: `seq_lens`: row b lists the lengths of the sequences packed in order from the start of block b; a row sums to at most 128, the rest of the block is padding; in some rows one sequence fills the block.
All inputs are finite; a program needn't handle non-finite values.
Results may differ from a plain program's by a relative error of at most 0.012.
The roundings to bfloat16 on the way count: a program that leaves them out, or rounds other values in their place, can miss the bound.
Values may be sent and summed in bfloat16 or wider, within the bound.
No kernel may reach another device: no remote copies, remote signals or barrier semaphores. Data moves between devices by JAX's collectives and lax.ppermute only.
A program may use at most 256 MiB of HBM per device.

v0:
```python
import jax
import jax.numpy as jnp
from jax import lax
from jax.sharding import PartitionSpec as P

SCAN_BLOCK = 64


EPS = 1e-05


def scale_norm(values, gain_row):
    return values * lax.rsqrt(jnp.mean(values * values, axis=-1, keepdims=True) + EPS) * gain_row


def causal_conv(inner_vals, conv_taps, conv_shift, offset):
    tap_count = conv_taps.shape[0]
    result = conv_shift[None, :] + conv_taps[tap_count - 1][None, :] * inner_vals
    for lag_steps in range(1, tap_count):
        moved = jnp.concatenate(
            [
                jnp.zeros((lag_steps, inner_vals.shape[1]), inner_vals.dtype),
                inner_vals[:-lag_steps],
            ],
            axis=0,
        )
        allowed = (offset >= lag_steps).astype(inner_vals.dtype)[:, None]
        result = result + conv_taps[tap_count - 1 - lag_steps][None, :] * moved * allowed
    return result


def pair_combine(earlier, later):
    return (earlier[0] * later[0], later[0] * earlier[1] + later[1])


def block_scan(carried, pieces, a_neg):
    step_dt, write_in, read_out, drive_x, keep_on = pieces
    decay = jnp.exp(step_dt[:, None, :] * a_neg[None]) * keep_on[:, None, None]
    drive = write_in[:, :, None] * (step_dt * drive_x)[:, None, :]
    total_decay, total_drive = lax.associative_scan(pair_combine, (decay, drive), axis=0)
    states = total_decay * carried[None] + total_drive
    return (states[-1], jnp.sum(states * read_out[:, :, None], axis=1))


def selective_scan(step_dt, write_in, read_out, drive_x, keep_on, a_neg):
    blocks = step_dt.shape[0] // SCAN_BLOCK

    def to_blocks(array):
        return array.reshape((blocks, SCAN_BLOCK) + array.shape[1:])

    stepper = jax.checkpoint(lambda carried, pieces: block_scan(carried, pieces, a_neg))
    zero_state = jnp.zeros(a_neg.shape, step_dt.dtype)
    final_state, block_outs = lax.scan(
        stepper,
        zero_state,
        (
            to_blocks(step_dt),
            to_blocks(write_in),
            to_blocks(read_out),
            to_blocks(drive_x),
            to_blocks(keep_on),
        ),
    )
    return block_outs.reshape(step_dt.shape)


def mixer_tail(drive_x, write_in, read_out, step_pre, gate_half, decay_log, skip_gain, keep_on):
    step_dt = jax.nn.softplus(step_pre)
    a_neg = -jnp.exp(decay_log)
    scanned = selective_scan(step_dt, write_in, read_out, drive_x, keep_on, a_neg)
    return (scanned + skip_gain[None, :] * drive_x) * jax.nn.silu(gate_half)


def routing_tables(lens_row, route_row, experts, capacity, tok_count):
    position = jnp.arange(tok_count, dtype=jnp.int32)
    seq_ends = jnp.cumsum(lens_row, dtype=jnp.int32)
    seq_starts = jnp.sum(
        (position[:, None] >= seq_ends[None, :]).astype(jnp.int32) * lens_row[None, :],
        axis=1,
        dtype=jnp.int32,
    )
    offset = position - seq_starts
    valid_mask = position < seq_ends[-1]
    route_hot = (route_row[:, None] == jnp.arange(experts, dtype=jnp.int32)[None, :]).astype(
        jnp.int32
    )
    live_hot = route_hot * valid_mask.astype(jnp.int32)[:, None]
    before = jnp.cumsum(live_hot, axis=0, dtype=jnp.int32) - live_hot
    rank_in = jnp.sum(before * route_hot, axis=1, dtype=jnp.int32)
    kept_mask = valid_mask & (rank_in < capacity)
    slot_raw = route_row * capacity + rank_in
    target = jnp.where(kept_mask, slot_raw, experts * capacity)
    slot_index = (
        jnp.full((experts * capacity,), tok_count, jnp.int32).at[target].set(position, mode="drop")
    )
    slot_pick = jnp.where(kept_mask, slot_raw, 0)
    return (offset, valid_mask, route_hot, slot_index, slot_pick, kept_mask)


def gelu_tanh(values):
    return jax.nn.gelu(values, approximate=True)


def body(
    tokens,
    cotangent,
    seq_lens,
    routes,
    norm_gain,
    input_proj,
    conv_weight,
    conv_bias,
    select_proj,
    step_proj,
    step_bias,
    decay_log,
    skip_gain,
    output_proj,
    moe_gain,
    router_weight,
    up_weight,
    down_weight,
):
    gathered = (
        lax.all_gather(norm_gain, ("dp", "fsdp"), axis=0, tiled=True),
        lax.all_gather(input_proj, ("dp", "fsdp"), axis=0, tiled=True),
        lax.all_gather(conv_weight, ("dp", "fsdp"), axis=1, tiled=True),
        lax.all_gather(conv_bias, ("dp", "fsdp"), axis=0, tiled=True),
        lax.all_gather(select_proj, ("dp", "fsdp"), axis=0, tiled=True),
        lax.all_gather(step_proj, ("dp", "fsdp"), axis=1, tiled=True),
        lax.all_gather(step_bias, ("dp", "fsdp"), axis=0, tiled=True),
        lax.all_gather(decay_log, ("dp", "fsdp"), axis=1, tiled=True),
        lax.all_gather(skip_gain, ("dp", "fsdp"), axis=0, tiled=True),
        lax.all_gather(output_proj, ("dp", "fsdp"), axis=0, tiled=True),
        lax.all_gather(moe_gain, ("dp", "fsdp"), axis=0, tiled=True),
        lax.all_gather(router_weight, ("dp", "fsdp"), axis=0, tiled=True),
    )
    (
        gain_one,
        proj_in,
        conv_taps,
        conv_shift,
        proj_select,
        proj_step,
        step_shift,
        decay_rates,
        skip_weight,
        proj_out,
        gain_two,
        router,
    ) = gathered
    tok_count = tokens.shape[0]
    model_width = tokens.shape[1]
    inner_width = proj_step.shape[1]
    step_rank = proj_step.shape[0]
    state_count = decay_rates.shape[0]
    experts = router.shape[1]
    capacity = 5 * tok_count // (4 * experts)
    offset, valid_mask, route_hot, slot_index, slot_pick, kept_mask = routing_tables(
        seq_lens[0], routes[:, 0], experts, capacity, tok_count
    )
    keep_on = (offset > 0).astype(jnp.float32)
    valid_f = valid_mask.astype(jnp.float32)
    kept_f = kept_mask.astype(jnp.float32)
    hot_f = route_hot.astype(jnp.float32)
    inputs = tokens.astype(jnp.float32)
    normed, norm_one_back = jax.vjp(scale_norm, inputs, gain_one.astype(jnp.float32))
    normed_low = normed.astype(jnp.bfloat16)
    both_halves = jnp.dot(normed_low, proj_in, preferred_element_type=jnp.float32)
    mixed_in = both_halves[:, :inner_width]
    gate_half = both_halves[:, inner_width:]
    conv_act, conv_back = jax.vjp(
        lambda inner_vals, taps_f, shift_f: jax.nn.silu(
            causal_conv(inner_vals, taps_f, shift_f, offset)
        ),
        mixed_in,
        conv_taps.astype(jnp.float32),
        conv_shift.astype(jnp.float32),
    )
    conv_low = conv_act.astype(jnp.bfloat16)
    selected = jnp.dot(conv_low, proj_select, preferred_element_type=jnp.float32)
    step_low = selected[:, :step_rank].astype(jnp.bfloat16)
    write_in = selected[:, step_rank : step_rank + state_count]
    read_out = selected[:, step_rank + state_count :]
    step_pre = (
        jnp.dot(step_low, proj_step, preferred_element_type=jnp.float32)
        + step_shift.astype(jnp.float32)[None, :]
    )
    gated_out, tail_back = jax.vjp(
        lambda drive_x, write_vals, read_vals, step_vals, gate_vals, decay_vals, skip_vals: mixer_tail(
            drive_x, write_vals, read_vals, step_vals, gate_vals, decay_vals, skip_vals, keep_on
        ),
        conv_low.astype(jnp.float32),
        write_in,
        read_out,
        step_pre,
        gate_half,
        decay_rates.astype(jnp.float32),
        skip_weight.astype(jnp.float32),
    )
    gated_low = gated_out.astype(jnp.bfloat16)
    branch = jnp.dot(gated_low, proj_out, preferred_element_type=jnp.float32)
    hidden = inputs + branch
    moe_pre, norm_two_back = jax.vjp(scale_norm, hidden, gain_two.astype(jnp.float32))
    moe_in = moe_pre.astype(jnp.bfloat16)
    logits = jnp.dot(moe_in, router, preferred_element_type=jnp.float32)
    gate_value = jax.nn.sigmoid(jnp.sum(logits * hot_f, axis=1))
    padded = jnp.concatenate([moe_in, jnp.zeros((1, model_width), jnp.bfloat16)], axis=0)
    outgoing = padded[slot_index].reshape(experts, capacity, model_width)
    arrived = lax.all_to_all(outgoing, "fsdp", split_axis=0, concat_axis=0, tiled=True)
    up_all, down_all = (
        lax.all_gather(up_weight, "dp", axis=1, tiled=True),
        lax.all_gather(down_weight, "dp", axis=1, tiled=True),
    )
    rows_in = arrived.reshape(-1, model_width)
    pre_act = jnp.einsum("cd,fd->cf", rows_in, up_all[0], preferred_element_type=jnp.float32)
    act_low = gelu_tanh(pre_act).astype(jnp.bfloat16)
    returned = (
        jnp.dot(act_low, down_all[0], preferred_element_type=jnp.float32)
        .astype(jnp.bfloat16)
        .reshape(arrived.shape)
    )
    coming = lax.all_to_all(returned, "fsdp", split_axis=0, concat_axis=0, tiled=True)
    picked = coming.reshape(-1, model_width)[slot_pick].astype(jnp.float32) * kept_f[:, None]
    result = valid_f[:, None] * (hidden + gate_value[:, None] * picked)
    grad_out = cotangent.astype(jnp.float32) * valid_f[:, None]
    grad_gate = jnp.sum(grad_out * picked, axis=1)
    grad_chosen = grad_gate * gate_value * (1.0 - gate_value)
    grad_logits = (grad_chosen[:, None] * hot_f).astype(jnp.bfloat16)
    back_rows = grad_out * (gate_value * kept_f)[:, None]
    back_pad = jnp.concatenate([back_rows, jnp.zeros((1, model_width), jnp.float32)], axis=0)
    back_slots = back_pad[slot_index].astype(jnp.bfloat16).reshape(experts, capacity, model_width)
    grad_arrived = lax.all_to_all(back_slots, "fsdp", split_axis=0, concat_axis=0, tiled=True)
    up_again, down_again = (
        lax.all_gather(up_weight, "dp", axis=1, tiled=True),
        lax.all_gather(down_weight, "dp", axis=1, tiled=True),
    )
    grad_rows = grad_arrived.reshape(-1, model_width)
    grad_act = jnp.einsum("cd,fd->cf", grad_rows, down_again[0], preferred_element_type=jnp.float32)
    grad_pre = jax.vjp(gelu_tanh, pre_act)[1](grad_act)[0].astype(jnp.bfloat16)
    down_grad = jnp.einsum("cf,cd->fd", act_low, grad_rows, preferred_element_type=jnp.float32)
    up_grad = jnp.einsum("cf,cd->fd", grad_pre, rows_in, preferred_element_type=jnp.float32)
    grad_in = (
        jnp.dot(grad_pre, up_again[0], preferred_element_type=jnp.float32)
        .astype(jnp.bfloat16)
        .reshape(arrived.shape)
    )
    up_share, down_share = (
        lax.psum_scatter(
            up_grad[None].astype(jnp.bfloat16), "dp", scatter_dimension=1, tiled=True
        ).astype(jnp.float32),
        lax.psum_scatter(
            down_grad[None].astype(jnp.bfloat16), "dp", scatter_dimension=1, tiled=True
        ).astype(jnp.float32),
    )
    grad_back = lax.all_to_all(grad_in, "fsdp", split_axis=0, concat_axis=0, tiled=True)
    grad_sent = grad_back.reshape(-1, model_width)[slot_pick].astype(jnp.float32) * kept_f[:, None]
    proj_in, proj_select, proj_step, proj_out, router = (
        lax.all_gather(input_proj, ("dp", "fsdp"), axis=0, tiled=True),
        lax.all_gather(select_proj, ("dp", "fsdp"), axis=0, tiled=True),
        lax.all_gather(step_proj, ("dp", "fsdp"), axis=1, tiled=True),
        lax.all_gather(output_proj, ("dp", "fsdp"), axis=0, tiled=True),
        lax.all_gather(router_weight, ("dp", "fsdp"), axis=0, tiled=True),
    )
    grad_moe_in = (
        jnp.einsum("te,de->td", grad_logits, router, preferred_element_type=jnp.float32) + grad_sent
    )
    router_grad = jnp.einsum("td,te->de", moe_in, grad_logits, preferred_element_type=jnp.float32)
    grad_hidden_norm, gain_two_grad = norm_two_back(grad_moe_in)
    grad_hidden = grad_out + grad_hidden_norm
    grad_branch = grad_hidden.astype(jnp.bfloat16)
    out_grad = jnp.einsum("te,td->ed", gated_low, grad_branch, preferred_element_type=jnp.float32)
    grad_gated = jnp.einsum("td,ed->te", grad_branch, proj_out, preferred_element_type=jnp.float32)
    grad_drive, grad_write, grad_read, grad_step, grad_gate_half, decay_grad, skip_grad = tail_back(
        grad_gated
    )
    step_bias_grad = jnp.sum(grad_step, axis=0)
    grad_step_low = grad_step.astype(jnp.bfloat16)
    step_grad = jnp.einsum("tr,te->re", step_low, grad_step_low, preferred_element_type=jnp.float32)
    grad_step_in = jnp.einsum(
        "te,re->tr", grad_step_low, proj_step, preferred_element_type=jnp.float32
    )
    grad_select = jnp.concatenate([grad_step_in, grad_write, grad_read], axis=1).astype(
        jnp.bfloat16
    )
    select_grad = jnp.einsum("te,tk->ek", conv_low, grad_select, preferred_element_type=jnp.float32)
    grad_conv = (
        jnp.einsum("tk,ek->te", grad_select, proj_select, preferred_element_type=jnp.float32)
        + grad_drive
    )
    grad_mixed, taps_grad, shift_grad = conv_back(grad_conv)
    grad_both = jnp.concatenate([grad_mixed, grad_gate_half], axis=1).astype(jnp.bfloat16)
    in_grad = jnp.einsum("td,tk->dk", normed_low, grad_both, preferred_element_type=jnp.float32)
    grad_normed = jnp.einsum("tk,dk->td", grad_both, proj_in, preferred_element_type=jnp.float32)
    grad_inputs, gain_one_grad = norm_one_back(grad_normed)
    input_grad = grad_hidden + grad_inputs
    shares = (
        lax.psum_scatter(gain_one_grad, ("dp", "fsdp"), scatter_dimension=0, tiled=True),
        lax.psum_scatter(in_grad, ("dp", "fsdp"), scatter_dimension=0, tiled=True),
        lax.psum_scatter(taps_grad, ("dp", "fsdp"), scatter_dimension=1, tiled=True),
        lax.psum_scatter(shift_grad, ("dp", "fsdp"), scatter_dimension=0, tiled=True),
        lax.psum_scatter(select_grad, ("dp", "fsdp"), scatter_dimension=0, tiled=True),
        lax.psum_scatter(step_grad, ("dp", "fsdp"), scatter_dimension=1, tiled=True),
        lax.psum_scatter(step_bias_grad, ("dp", "fsdp"), scatter_dimension=0, tiled=True),
        lax.psum_scatter(decay_grad, ("dp", "fsdp"), scatter_dimension=1, tiled=True),
        lax.psum_scatter(skip_grad, ("dp", "fsdp"), scatter_dimension=0, tiled=True),
        lax.psum_scatter(out_grad, ("dp", "fsdp"), scatter_dimension=0, tiled=True),
        lax.psum_scatter(gain_two_grad, ("dp", "fsdp"), scatter_dimension=0, tiled=True),
        lax.psum_scatter(router_grad, ("dp", "fsdp"), scatter_dimension=0, tiled=True),
    )
    return (
        result.astype(jnp.bfloat16),
        input_grad,
        shares[0],
        shares[1],
        shares[2],
        shares[3],
        shares[4],
        shares[5],
        shares[6],
        shares[7],
        shares[8],
        shares[9],
        shares[10],
        shares[11],
        up_share,
        down_share,
    )


def solution(mesh):
    in_specs = (
        P(("dp", "fsdp"), None),
        P(("dp", "fsdp"), None),
        P(("dp", "fsdp"), None),
        P(("dp", "fsdp"), None),
        P(("dp", "fsdp")),
        P(("dp", "fsdp"), None),
        P(None, ("dp", "fsdp")),
        P(("dp", "fsdp")),
        P(("dp", "fsdp"), None),
        P(None, ("dp", "fsdp")),
        P(("dp", "fsdp")),
        P(None, ("dp", "fsdp")),
        P(("dp", "fsdp")),
        P(("dp", "fsdp"), None),
        P(("dp", "fsdp")),
        P(("dp", "fsdp"), None),
        P("fsdp", "dp", None),
        P("fsdp", "dp", None),
    )
    out_specs = (
        P(("dp", "fsdp"), None),
        P(("dp", "fsdp"), None),
        P(("dp", "fsdp")),
        P(("dp", "fsdp"), None),
        P(None, ("dp", "fsdp")),
        P(("dp", "fsdp")),
        P(("dp", "fsdp"), None),
        P(None, ("dp", "fsdp")),
        P(("dp", "fsdp")),
        P(None, ("dp", "fsdp")),
        P(("dp", "fsdp")),
        P(("dp", "fsdp"), None),
        P(("dp", "fsdp")),
        P(("dp", "fsdp"), None),
        P("fsdp", "dp", None),
        P("fsdp", "dp", None),
    )
    return jax.shard_map(body, mesh=mesh, in_specs=in_specs, out_specs=out_specs, check_vma=False)
```

profile of v0, /device:TPU:0, one launch (start us, length us, event | category | flops | bytes accessed | tf_op | source)
XLA Modules:
  0.0 3032.9 jit_solution(6795715879163247746)
XLA Ops:
  16.5 42.4 %all-reduce.127 = (bf16[768]{0:T(1024)(128)(2,1)S(1)}, bf16[1536]{0:T(1024)(128)(2,1)S(1)}, bf16[1536]{0:T(1024)(128)(2,1)S(1)}, bf16[1536]{0:T(1024)(128)(2,1)S(1)}, bf16[768]{0:T(1024)(128)(2,1)S(1)}) all-reduce(bf16[768]{0:T(1024)(128)(2,1)S(1)} %dynamic-update-slice.1, ...), channel_id=1, replica_groups=mesh['dp'=4,'fsdp'=8] {'dp','fsdp'}, use_global_device_ids=true, to_apply=%add.116 | all-reduce | flops 6144 | bytes 24576
  60.0 66.3 %all-gather = bf16[32,48,4]{1,2,0:T(4,128)(2,1)S(1)} all-gather(bf16[1,48,4]{1,2,0:T(4,128)(2,1)} %bitcast.229), channel_id=1, replica_groups=mesh['dp'=4,'fsdp'=8] {'dp','fsdp'}, dimensions={0}, use_global_device_ids=true | all-gather | bytes 12672 | tf_op jit(solution)/shard_map/all_gather | solution.py:127
  126.5 66.9 %all_gather.53 = bf16[1536,80]{1,0:T(8,128)(2,1)S(1)} all-gather(bf16[48,80]{1,0:T(8,128)(2,1)S(1)} %copy-done.170), channel_id=1, replica_groups=mesh['dp'=4,'fsdp'=8] {'dp','fsdp'}, dimensions={0}, use_global_device_ids=true | all-gather | bytes 253440 | tf_op jit(solution)/shard_map/all_gather | solution.py:129
  193.5 67.8 %all_gather.54 = bf16[48,1536]{0,1:T(8,128)(2,1)S(1)} all-gather(bf16[48,48]{0,1:T(8,128)(2,1)S(1)} %copy.86), channel_id=1, replica_groups=mesh['dp'=4,'fsdp'=8] {'dp','fsdp'}, dimensions={1}, use_global_device_ids=true | all-gather | bytes 152064 | tf_op jit(solution)/shard_map/all_gather | solution.py:130
  261.9 64.3 %all-gather.1 = bf16[32,48,16]{1,2,0:T(8,128)(2,1)S(1)} all-gather(bf16[1,48,16]{1,2,0:T(8,128)(2,1)S(1)} %bitcast.227), channel_id=1, replica_groups=mesh['dp'=4,'fsdp'=8] {'dp','fsdp'}, dimensions={0}, use_global_device_ids=true | all-gather | bytes 50688 | tf_op jit(solution)/shard_map/all_gather | solution.py:132
  342.9 491.5 %while.39 = (s32[]{:T(128)}, f32[16,1536]{1,0:T(8,128)}, f32[2,64,1536]{2,1,0:T(8,128)}, f32[2,16,1536]{2,1,0:T(8,128)}, f32[2,64,1536]{2,1,0:T(8,128)}, /*index...) while((s32[]{:T(128)}, f32[16,1536]{1,0:T(8,128)}, ...), condition=%wide.region_5.6_spmd, body=%wide.region_3.5_spmd.sunk | while | flops 31899648 | bytes 374777760 | solution.py:53
  466.2 20.0 pad.1528
  520.0 20.0 pad.1526
  711.7 20.0 pad.1528
  765.6 20.0 pad.1526
  844.8 66.2 %all-gather.2 = bf16[32,24,8]{1,2,0:T(8,128)(2,1)S(1)} all-gather(bf16[1,24,8]{1,2,0:T(8,128)(2,1)S(1)} %bitcast.228), channel_id=1, replica_groups=mesh['dp'=4,'fsdp'=8] {'dp','fsdp'}, dimensions={0}, use_global_device_ids=true | all-gather | bytes 12672 | tf_op jit(solution)/shard_map/all_gather | solution.py:136
  990.4 1273.4 %while.40 = (s32[]{:T(128)}, f32[16,1536]{1,0:T(8,128)}, f32[16,1536]{1,0:T(8,128)}, f32[2,64,1536]{2,1,0:T(8,128)}, bf16[2,64,16]{2,1,0:T(8,128)(2,1)}, /*index...) while((s32[]{:T(128)}, f32[16,1536]{1,0:T(8,128)}, ...), condition=%wide.region_20.21_spmd.clone, body=%wide.region_13.20_spmd.clone.sunk | while | flops 98154496 | bytes 1120116864 | solution.py:53
  1303.8 20.1 pad.1638
  1323.8 20.0 pad.1639
  1471.2 20.5 pad.1631
  1504.8 19.6 pad.1633
  1567.0 20.5 pad.1636
  1591.6 20.0 pad.1637
  1936.2 20.1 pad.1638
  1956.2 20.0 pad.1639
  2103.4 20.5 pad.1631
  2199.2 20.5 pad.1636
  2223.8 20.0 pad.1637
  2305.9 39.1 %all-reduce.126 = (f32[768]{0:T(1024)S(1)}, f32[1536]{0:T(1024)S(1)}, f32[1536]{0:T(1024)S(1)}, f32[1536]{0:T(1024)S(1)}, f32[768]{0:T(1024)S(1)}, /*index=5*/f32[768,8]{0,1:T(8,128)S(1)}) all-reduce(f32[768]{0:T(1024)S(1)} %get-tuple-element.574, ...), channel_id=2, replica_groups=mesh['dp'=4,'fsdp'=8] {'dp','fsdp'}, use_global_device_ids=true, to_apply=%region_23.24.clone | all-reduce | flops 12288 | bytes 98304
  2349.5 21.7 reduce-scatter.26.cloned.1.call-done
  2372.6 98.2 %reduce-scatter.30.cloned.1.call-done = f32[48,16]{1,0:T(8,128)} async-done(((f32[1536,16]{1,0:T(8,128)}), f32[48,16]{1,0:T(8,128)}) %reduce-scatter.30.cloned.1.call-update) | async-done | bytes 3088
  2472.1 98.3 %reduce-scatter.28.cloned.1.call-done = f32[48,48]{1,0:T(8,128)} async-done(((f32[1536,48]{1,0:T(8,128)}), f32[48,48]{1,0:T(8,128)}) %reduce-scatter.28.cloned.1.call-update) | async-done | bytes 9232
  2571.9 48.1 %reduce-scatter.24.cloned.1.call-done = bf16[1,768,768]{2,1,0:T(8,128)(2,1)} async-done(((bf16[1,3072,768]{2,1,0:T(8,128)(2,1)}), bf16[1,768,768]{2,1,0:T(8,128)(2,1)}) %reduce-scatter.24.cloned.1.call-update) | async-done | bytes 1179664 | tf_op jit(solution)/shard_map/reduce_scatter | solution.py:252
  2622.8 47.7 %reduce-scatter.22.cloned.1.call-done = bf16[1,768,768]{2,1,0:T(8,128)(2,1)} async-done(((bf16[1,3072,768]{2,1,0:T(8,128)(2,1)}), bf16[1,768,768]{2,1,0:T(8,128)(2,1)}) %reduce-scatter.22.cloned.1.call-update) | async-done | bytes 1179664 | tf_op jit(solution)/shard_map/reduce_scatter | solution.py:249
  2673.4 98.2 %reduce-scatter.18.cloned.1.call-done = f32[48,80]{1,0:T(8,128)} async-done(((f32[1536,80]{1,0:T(8,128)}), f32[48,80]{1,0:T(8,128)}) %reduce-scatter.18.cloned.1.call-update) | async-done | bytes 15376 | tf_op jit(solution)/shard_map/reduce_scatter | solution.py:302
  2771.6 112.1 %reduce-scatter.20.cloned.1.call-done = f32[48,768]{1,0:T(8,128)} async-done(((f32[1536,768]{1,0:T(8,128)}), f32[48,768]{1,0:T(8,128)}) %reduce-scatter.20.cloned.1.call-update) | async-done | bytes 147472 | tf_op jit(solution)/shard_map/reduce_scatter | solution.py:307
  2883.7 142.1 %reduce-scatter.16.cloned.1.call-done = f32[24,3072]{1,0:T(8,128)} async-done(((f32[768,3072]{1,0:T(8,128)}), f32[24,3072]{1,0:T(8,128)}) %reduce-scatter.16.cloned.1.call-update) | async-done | bytes 294928 | tf_op jit(solution)/shard_map/reduce_scatter | solution.py:299
  (1273 shorter events, 1623.1 us)
Async XLA Ops:
  7.2 325.0 %copy-start.105 = (bf16[128,768]{1,0:T(8,128)(2,1)S(1)}, bf16[128,768]{1,0:T(8,128)(2,1)}, u32[]{:S(2)}) copy-start(bf16[128,768]{1,0:T(8,128)(2,1)} %param.22) | copy-start | bytes 589828
  7.2 186.2 %copy-start.171 = (bf16[48,48]{1,0:T(8,128)(2,1)S(1)}, bf16[48,48]{1,0:T(8,128)(2,1)}, u32[]{:S(2)}) copy-start(bf16[48,48]{1,0:T(8,128)(2,1)} %param.31) | copy-start | bytes 13828
  7.2 254.7 %copy-start.184 = (bf16[16,48]{1,0:T(8,128)(2,1)S(1)}, bf16[16,48]{1,0:T(8,128)(2,1)}, u32[]{:S(2)}) copy-start(bf16[16,48]{1,0:T(8,128)(2,1)} %param.33) | copy-start | bytes 4612
  7.2 321.8 %copy-start.166 = (s32[128,1]{0,1:T(1,128)S(1)}, s32[128,1]{0,1:T(1,128)}, u32[]{:S(2)}) copy-start(s32[128,1]{0,1:T(1,128)} %param.25) | copy-start | bytes 1540
  7.2 325.0 %all-gather.8.cloned.1.call-start = ((), (), s32[]{:S(2)}) async-start(), calls=%async_computation.12 | async-start | bytes 4866048 | tf_op jit(solution)/shard_map/all_gather | solution.py:126
  8.0 828.2 %all-gather.10.cloned.1.call-start = ((), (), s32[]{:S(2)}) async-start(), calls=%async_computation.13 | async-start | bytes 2433024 | tf_op jit(solution)/shard_map/all_gather | solution.py:134
  8.7 903.2 %all-gather.12.cloned.1.call-start = ((), (), s32[]{:S(2)}) async-start(), calls=%async_computation.14 | async-start | bytes 5898240 | tf_op jit(solution)/shard_map/all_gather | solution.py:212
  9.5 906.7 %all-gather.14.cloned.1.call-start = ((), (), s32[]{:S(2)}) async-start(), calls=%async_computation.15 | async-start | bytes 5898240 | tf_op jit(solution)/shard_map/all_gather | solution.py:213
  11.6 324.1 %copy-start.179 = (f32[128]{0:T(128)}, f32[128]{0:T(128)S(1)}, u32[]{:S(2)}) copy-start(f32[128]{0:T(128)S(1)} %get-tuple-element.799) | copy-start | bytes 1540
  11.6 324.1 %copy-start.180 = (f32[128]{0:T(128)}, f32[128]{0:T(128)S(1)}, u32[]{:S(2)}) copy-start(f32[128]{0:T(128)S(1)} %get-tuple-element.800) | copy-start | bytes 1540
  11.6 324.1 %copy-start.181 = (f32[128]{0:T(128)}, f32[128]{0:T(128)S(1)}, u32[]{:S(2)}) copy-start(f32[128]{0:T(128)S(1)} %get-tuple-element.801) | copy-start | bytes 1540
  58.9 276.5 %copy-start.142 = (f32[768]{0:T(1024)}, f32[768]{0:T(1024)S(1)}, u32[]{:S(2)}) copy-start(f32[768]{0:T(1024)S(1)} %convert_element_type.157) | copy-start | bytes 9220
  59.9 269.1 %copy-start.187 = (f32[128]{0:T(128)}, f32[128]{0:T(128)S(1)}, u32[]{:S(2)}) copy-start(f32[128]{0:T(128)S(1)} %fusion.61) | copy-start | bytes 1540
  59.9 275.5 %copy-start.173 = (f32[128]{0:T(128)}, f32[128]{0:T(128)S(1)}, u32[]{:S(2)}) copy-start(f32[128]{0:T(128)S(1)} %fusion.87) | copy-start | bytes 1540
  126.5 209.2 %copy-start.150 = (f32[1536]{0:T(1024)}, f32[1536]{0:T(1024)S(1)}, u32[]{:S(2)}) copy-start(f32[1536]{0:T(1024)S(1)} %get-tuple-element.576) | copy-start | bytes 18436
  126.5 209.2 %copy-start.152 = (f32[1536]{0:T(1024)}, f32[1536]{0:T(1024)S(1)}, u32[]{:S(2)}) copy-start(f32[1536]{0:T(1024)S(1)} %get-tuple-element.579) | copy-start | bytes 18436
  126.5 209.2 %copy-start.154 = (f32[1536]{0:T(1024)}, f32[1536]{0:T(1024)S(1)}, u32[]{:S(2)}) copy-start(f32[1536]{0:T(1024)S(1)} %get-tuple-element.577) | copy-start | bytes 18436
  126.5 209.2 %copy-start.156 = (f32[1536]{0:T(1024)}, f32[1536]{0:T(1024)S(1)}, u32[]{:S(2)}) copy-start(f32[1536]{0:T(1024)S(1)} %get-tuple-element.578) | copy-start | bytes 18436
  342.9 491.6 %copy-start.158 = (f32[1536]{0:T(1024)S(1)}, f32[1536]{0:T(1024)}, u32[]{:S(2)}) copy-start(f32[1536]{0:T(1024)} %convert_element_type.167) | copy-start | bytes 18436
  841.3 69.8 %all-to-all-start = ((bf16[8,20,768]{2,1,0:T(8,128)(2,1)}), bf16[8,20,768]{2,1,0:T(8,128)(2,1)S(1)}, u32[]{:S(2)}, u32[]{:S(2)}) async-start(bf16[8,20,768]{2,1,0:T(8,128)(2,1)} %reshape.292), calls=%async_computation | async-start | bytes 589824 | tf_op jit(solution)/shard_map/all_to_all | solution.py:210
  921.2 12.5 all-to-all-start.1
  962.7 12.5 all-to-all-start.3
  966.8 1404.4 %reduce-scatter.26.cloned.1.call-start = ((), (), s32[]{:S(2)}) async-start(), calls=%async_computation.21 | async-start | bytes 811008
  1009.0 208.7 %copy-start.34 = (f32[4,16,1536]{2,1,0:T(8,128)}, f32[4,16,1536]{2,1,0:T(8,128)S(1)}, u32[]{:S(2)}) copy-start(f32[4,16,1536]{2,1,0:T(8,128)S(1)} %get-tuple-element.1153) | copy-start | bytes 1179652 | tf_op jit(solution)/shard_map/transpose(jvp())/while
  1641.2 209.0 %copy-start.34 = (f32[4,16,1536]{2,1,0:T(8,128)}, f32[4,16,1536]{2,1,0:T(8,128)S(1)}, u32[]{:S(2)}) copy-start(f32[4,16,1536]{2,1,0:T(8,128)S(1)} %get-tuple-element.1153) | copy-start | bytes 1179652 | tf_op jit(solution)/shard_map/transpose(jvp())/while
  2277.5 193.2 %reduce-scatter.30.cloned.1.call-start = ((), (), s32[]{:S(2)}) async-start(), calls=%async_computation.23 | async-start | bytes 811008
  2278.9 291.6 %reduce-scatter.28.cloned.1.call-start = ((), (), s32[]{:S(2)}) async-start(), calls=%async_computation.22 | async-start | bytes 811008
  2280.2 339.8 %reduce-scatter.24.cloned.1.call-start = ((), (), s32[]{:S(2)}) async-start(), calls=%async_computation.20 | async-start | bytes 5898240 | tf_op jit(solution)/shard_map/reduce_scatter | solution.py:252
  2284.2 386.3 %reduce-scatter.22.cloned.1.call-start = ((), (), s32[]{:S(2)}) async-start(), calls=%async_computation.19 | async-start | bytes 5898240 | tf_op jit(solution)/shard_map/reduce_scatter | solution.py:249
  2289.1 482.4 %reduce-scatter.18.cloned.1.call-start = ((), (), s32[]{:S(2)}) async-start(), calls=%async_computation.17 | async-start | bytes 811008 | tf_op jit(solution)/shard_map/reduce_scatter | solution.py:302
  2291.3 592.4 %reduce-scatter.20.cloned.1.call-start = ((), (), s32[]{:S(2)}) async-start(), calls=%async_computation.18 | async-start | bytes 4866048 | tf_op jit(solution)/shard_map/reduce_scatter | solution.py:307
  2294.4 731.4 %reduce-scatter.16.cloned.1.call-start = ((), (), s32[]{:S(2)}) async-start(), calls=%async_computation.16 | async-start | bytes 9732096 | tf_op jit(solution)/shard_map/reduce_scatter | solution.py:299
  (316 other events, 3138.2 us)
Sparse Core Ops, SparseCore 0:
  11.1 66.3 all-gather.7
  80.4 56.6 all-gather.9
  138.7 37.0 all-gather.11
  177.2 38.2 all-gather.13
  2277.6 93.4 reduce-scatter.25
  2376.1 94.5 reduce-scatter.29
  2475.8 94.5 reduce-scatter.27
  2573.0 46.9 reduce-scatter.23
  2622.7 47.7 reduce-scatter.21
  2676.0 95.4 reduce-scatter.17
  2777.6 106.0 reduce-scatter.19
  2891.0 134.7 reduce-scatter.15
where the time goes:
time: 3080 us; the launch traced here: 3030 us
  local copies, waits for them, and re-layouts  1320 us (43%)
  waiting for transfers between devices  685 us (22%)
  other arithmetic  511 us (17%)
  blocking collectives  425 us (14%)
  matrix products  56.4 us (2%)
    pad x156, local copies, waits for them, and re-layouts, block_scan(): lax.associative_scan(pair_combine, (decay, drive), axis=0)  1160 us
    unnamed x15, waiting for transfers between devices  221 us
    mul x50, other arithmetic, pair_combine(): return (earlier[0] * later[0], later[0] * earlier[1] + later[1])  159 us
    reduce_scatter x1, waiting for transfers between devices, body(): lax.psum_scatter(in_grad, ('dp', 'fsdp'), scatter_dimension=0, tiled=True)  142 us
    reduce_scatter x1, waiting for transfers between devices, body(): lax.psum_scatter(out_grad, ('dp', 'fsdp'), scatter_dimension=0, tiled=True)  112 us
    reduce_scatter x1, waiting for transfers between devices, body(): lax.psum_scatter(select_grad, ('dp', 'fsdp'), scatter_dimension=0, tiled=...  98.2 us
    add x40, other arithmetic, block_scan(): lax.associative_scan(pair_combine, (decay, drive), axis=0)  93.6 us
    unnamed x2, blocking collectives  81.5 us
  transfers between devices with their start and end apart: 15, of which 10 were waited for; matrix products, arithmetic and copies ran while one was open for 18% of the time, Pallas kernels for 0%

commit v1 on v0

v1 whole, which is shorter than its diff:
```python
import functools

import jax
import jax.numpy as jnp
import numpy as np
from jax import lax
from jax.experimental import pallas as pl
from jax.experimental.pallas import tpu as pltpu
from jax.sharding import Mesh
from jax.sharding import PartitionSpec as P

EPS = 1e-05
F32 = jnp.float32
BF16 = jnp.bfloat16
LANES = 128
LOG2E = 1.4426950408889634
LN2 = 0.6931471805599453
GELU_C = 0.7978845608028654
GELU_K = 0.044715
ALL = ("y", "c", "z", "x")
GROUP = ("y", "z", "x")
ROW_BIAS, ROW_STEP, ROW_SKIP, ROW_DECAY = 4, 5, 6, 8
NN = (((1,), (0,)), ((), ()))
NT = (((1,), (1,)), ((), ()))
TN = (((0,), (0,)), ((), ()))


def mm(left, right, dims=NN):
    return lax.dot_general(left, right, dims, preferred_element_type=F32)


def split_mm(left, right, dims=NN):
    high = left.astype(BF16)
    rest = left - high.astype(F32)
    mid = rest.astype(BF16)
    low = (rest - mid.astype(F32)).astype(BF16)
    return mm(high, right, dims) + (mm(mid, right, dims) + mm(low, right, dims))


def iota(shape, dim):
    return lax.broadcasted_iota(jnp.int32, shape, dim)


def sigmoid(v):
    return 1.0 / (1.0 + jnp.exp(-v))


def softplus(v):
    return jnp.maximum(v, 0.0) + jnp.log1p(jnp.exp(-jnp.abs(v)))


def positions(lens_ref, row, tok):
    pos = iota((tok, 1), 0)
    end = jnp.int32(0)
    start = jnp.zeros((tok, 1), jnp.int32)
    for j in range(lens_ref.shape[1]):
        length = lens_ref[row, j]
        end = end + length
        start = start + jnp.where(pos >= end, length, 0)
    return pos - start, pos < end


def both_offsets(lens_ref, tok):
    return jnp.concatenate([positions(lens_ref, row, tok)[0] for row in range(2)], axis=0)


def fold(parts):
    rows = iota((8, LANES), 0)
    step = 1
    while len(parts) > 1:
        first = (rows & step) == 0
        merged = []
        for k in range(0, len(parts), 2):
            a, b = parts[k], parts[k + 1]
            merged.append(jnp.where(first, a, b) + pltpu.roll(jnp.where(first, b, a), step, 0))
        parts = merged
        step *= 2
    return parts[0]


def call(kernel, outs, args, specs=None, scratch=(), name=None, cost=None, vmem=60):
    whole = pl.BlockSpec(memory_space=pltpu.VMEM)
    windowed = specs is not None and any(s is not None and s.block_shape is not None for s in specs)
    return pl.pallas_call(
        kernel,
        grid=(1,) if windowed else (),
        out_shape=[jax.ShapeDtypeStruct(s, d) for s, d in outs],
        in_specs=[whole] * len(args) if specs is None else [whole if s is None else s for s in specs],
        out_specs=[whole] * len(outs),
        scratch_shapes=list(scratch),
        name=name,
        cost_estimate=cost,
        compiler_params=pltpu.CompilerParams(vmem_limit_bytes=vmem << 20),
    )(*args)


SMEM = pl.BlockSpec(memory_space=pltpu.SMEM)


def perm_matrix(nat_ref):
    width = nat_ref.shape[1]
    return (iota((width, width), 0) == nat_ref[...]).astype(F32).astype(BF16)


def enter_kernel(lens, tok2, nat, g1, u_o, xin_o, xc_o, sel_o, small_o, dnat_o):
    rows, width = tok2.shape
    tok = rows // 2
    inner = xin_o.shape[1]
    at = inner
    perm = perm_matrix(nat)
    dnat = mm(g1[:, at : at + LANES], perm, (((0,), (1,)), ((), ())))
    dnat_o[...] = dnat[: dnat_o.shape[0]]
    vals = tok2[...].astype(F32)
    scale = lax.rsqrt(jnp.mean(vals * vals, axis=1, keepdims=True) + EPS)
    u = (vals * scale * dnat[0:1]).astype(BF16)
    u = mm(u, perm).astype(BF16)
    u_o[...] = u
    xin = mm(u, g1[:, :inner])
    xin_o[...] = xin
    small = jnp.transpose(g1[:, at + 2 * LANES : at + 3 * LANES].astype(F32))
    small_o[...] = small[: small_o.shape[0]]
    offset = both_offsets(lens, tok)
    conv = conv_of(xin, small, offset)
    xc = (conv * sigmoid(conv)).astype(BF16)
    xc_o[...] = xc
    sel_o[...] = mm(xc, g1[:, at + LANES : at + 2 * LANES])


def conv_of(xin, small, offset):
    conv = small[ROW_BIAS : ROW_BIAS + 1] + small[3:4] * xin
    for lag in range(1, 4):
        moved = pltpu.roll(xin, lag, 0)
        conv = conv + jnp.where(offset >= lag, small[3 - lag : 4 - lag] * moved, 0.0)
    return conv


def swap_halves(rows):
    half = rows.shape[0] // 2
    return jnp.concatenate([rows[half:], rows[:half]], axis=0)


def scan_kernel(
    rank, states, lens, sel_a, sel_b, u, xc, g1sel, g2, small,
    gated_o, ys_o, zg_o, step_o, sel_o, keep_o, mine_o, send_o, check_o,
    dm_s, dx_s, wr_s, rd_s, rate_s, h_s,
):
    rows, inner = ys_o.shape
    tok = rows // 2
    sel = sel_a[...] + swap_halves(sel_b[...])
    sel_o[...] = sel
    lane = iota((rows, LANES), 1)
    tail = LANES - rank
    q = jnp.where(lane >= tail, pltpu.roll(sel, tail, 1), 0.0).astype(BF16)
    step_pre = mm(q, g1sel[...], NT) + small[ROW_STEP : ROW_STEP + 1]
    step_o[...] = step_pre
    delta = softplus(step_pre)
    offset = both_offsets(lens, tok)
    xcf = xc[...].astype(F32)
    dm_s[...] = jnp.where(offset > 0, delta, 1e30)
    keep_o[...] = jnp.broadcast_to((offset > 0).astype(F32), keep_o.shape)
    dx_s[...] = delta * xcf
    for b in range(2):
        turned = jnp.transpose(sel[b * tok : (b + 1) * tok])
        wr_s[b] = turned[rank : rank + states]
        rd_s[b] = turned[rank + states : rank + 2 * states]
    rate_s[...] = jnp.exp(small[ROW_DECAY : ROW_DECAY + states]) * (-LOG2E)
    h_s[...] = jnp.zeros_like(h_s)
    half = states // 2

    def chunk(ci, carry):
        t0 = pl.multiple_of(ci * 8, 8)
        for b in range(2):
            at = pl.multiple_of(b * tok + t0, 8)
            wr8 = pltpu.roll(wr_s[b], tok - t0, 1)
            rd8 = pltpu.roll(rd_s[b], tok - t0, 1)
            wcol = [jnp.broadcast_to(wr8[:, j : j + 1], (states, LANES)) for j in range(8)]
            rcol = [jnp.broadcast_to(rd8[:, j : j + 1], (states, LANES)) for j in range(8)]
            for g in range(inner // LANES):
                lanes = slice(g * LANES, (g + 1) * LANES)
                h = h_s[b, :, lanes]
                check_o[ci * 2 + b, :, lanes] = h
                rate = rate_s[:, lanes]
                dm8 = dm_s[pl.ds(at, 8), lanes]
                dx8 = dx_s[pl.ds(at, 8), lanes]
                parts = []
                for j in range(8):
                    d = jnp.broadcast_to(dm8[j : j + 1], (states, LANES))
                    x = jnp.broadcast_to(dx8[j : j + 1], (states, LANES))
                    h = jnp.exp2(d * rate) * h + wcol[j] * x
                    p = rcol[j] * h
                    parts.append(p[:half] + p[half:])
                ys_o[pl.ds(at, 8), lanes] = fold(parts)
                h_s[b, :, lanes] = h
        return carry

    lax.fori_loop(0, tok // 8, chunk, 0)
    zg = mm(u[...], g2[:, :inner])
    zg_o[...] = zg
    gated = (ys_o[...] + small[ROW_SKIP : ROW_SKIP + 1] * xcf) * (zg * sigmoid(zg))
    gated = gated.astype(BF16)
    gated_o[...] = gated
    branch = mm(gated, g2[:, inner:])
    mine_o[...] = branch[:tok]
    send_o[...] = branch[tok:]


def route_tables(lens, routes, experts, capacity, tok):
    _, valid = positions(lens, 0, tok)
    valid_f = valid.astype(F32)
    width = max(LANES, experts)
    hot = (routes[...] == iota((tok, width), 1)).astype(F32)
    live = hot * valid_f
    earlier = (iota((tok, tok), 1) < iota((tok, tok), 0)).astype(F32).astype(BF16)
    before = mm(earlier, live.astype(BF16))
    rank = jnp.sum(before * hot, axis=1, keepdims=True).astype(jnp.int32)
    kept = valid & (rank < capacity)
    return valid_f, hot, rank, kept


def slot_hot(k, routes, rank, kept, capacity, tok):
    inside = kept & (routes[...] == k)
    return (inside & (rank == iota((tok, capacity), 1))).astype(F32).astype(BF16)


def moe_enter_kernel(experts, capacity, lens, tok, cot, routes, mine, got, dnat, disp_o, hidden_o, gate_o):
    rows, width = tok.shape
    hidden = tok[...].astype(F32) + (mine[...] + got[...])
    hidden_o[...] = hidden
    scale = lax.rsqrt(jnp.mean(hidden * hidden, axis=1, keepdims=True) + EPS)
    mv = (hidden * scale * dnat[1:2]).astype(BF16)
    logits = mm(mv, dnat[...].astype(BF16), NT)
    hot = (routes[...] + 2 == iota(logits.shape, 1)).astype(F32)
    gate = sigmoid(jnp.sum(logits * hot, axis=1, keepdims=True))
    gate_o[...] = jnp.broadcast_to(gate, gate_o.shape)
    valid_f, _, rank, kept = route_tables(lens, routes, experts, capacity, rows)
    back = (cot[...].astype(F32) * valid_f * (gate * kept.astype(F32))).astype(BF16)
    both = jnp.concatenate([mv, back], axis=1)
    for k in range(experts):
        disp_o[k] = mm(slot_hot(k, routes, rank, kept, capacity, rows), both, TN).astype(BF16)


def expert_kernel(width, own, peer, up, down, out_own, out_peer, up_g, down_g, rows_s, acc_s):
    half = own.shape[0]
    total = rows_s.shape[0]
    rows_s[:half] = own[...]
    rows_s[half:] = peer[...]
    hidden = up.shape[1]
    part = 256
    for f in range(0, hidden, part):
        x = rows_s[:, :width]
        g = rows_s[:, width:]
        pre = mm(x, up[0, f : f + part], NT)
        g_act = mm(g, down[0, f : f + part], NT)
        sq = pre * pre
        th = jnp.tanh(GELU_C * (pre + GELU_K * sq * pre))
        act = (0.5 * pre * (1.0 + th)).astype(BF16)
        slope = 0.5 * (1.0 + th) + 0.5 * pre * (1.0 - th * th) * (GELU_C * (1.0 + 3.0 * GELU_K * sq))
        g_pre = (g_act * slope).astype(BF16)
        down_g[0, f : f + part] = mm(act, g, TN)
        up_g[0, f : f + part] = mm(g_pre, x, TN)
        e_part = mm(act, down[0, f : f + part])
        i_part = mm(g_pre, up[0, f : f + part])
        if f == 0:
            acc_s[:, :width] = e_part
            acc_s[:, width:] = i_part
        else:
            acc_s[:, :width] += e_part
            acc_s[:, width:] += i_part
    out_own[...] = acc_s[:half]
    out_peer[...] = acc_s[half:].astype(BF16)


def moe_leave_kernel(
    experts, capacity, lens, routes, cot, hidden, gate_in, dnat, back,
    out_o, ghid_o, gbr_o, dgrad_o,
):
    rows, width = hidden.shape
    valid_f, _, rank, kept = route_tables(lens, routes, experts, capacity, rows)
    kept_f = kept.astype(F32)
    gate = gate_in[:, 0:1]
    picked = jnp.zeros((rows, 2 * width), F32)
    for k in range(experts):
        picked = picked + mm(slot_hot(k, routes, rank, kept, capacity, rows), back[k])
    ex_out = picked[:, :width]
    sent = picked[:, width:]
    hid = hidden[...]
    out_o[...] = (valid_f * (hid + gate * ex_out)).astype(BF16)
    gy = cot[...].astype(F32) * valid_f
    g_gate = jnp.sum(gy * ex_out, axis=1, keepdims=True)
    chosen = g_gate * gate * (1.0 - gate)
    small_rows = dnat.shape[0]
    hot = (routes[...] + 2 == iota((rows, small_rows), 1)).astype(F32)
    g_logit = (chosen * hot).astype(BF16)
    g_mv = mm(g_logit, dnat[...].astype(BF16)) + sent
    scale = lax.rsqrt(jnp.mean(hid * hid, axis=1, keepdims=True) + EPS)
    hat = hid * scale
    gain = dnat[1:2]
    mv = (hat * gain).astype(BF16)
    router_g = mm(g_logit, mv, TN)
    gain_g = jnp.sum(g_mv * hat, axis=0, keepdims=True)
    dgrad_o[...] = jnp.where(iota(dgrad_o.shape, 0) == 1, gain_g, router_g)
    gg = g_mv * gain
    mean = jnp.sum(gg * hat, axis=1, keepdims=True) * (1.0 / width)
    ghid = gy + scale * (gg - hat * mean)
    ghid_o[...] = ghid
    gbr_o[...] = ghid.astype(BF16)


def scan_back_kernel(
    rank, states, gbr_a, gbr_b, g2, gated, xc, ys, zg, step_pre, sel, keep, small, g1sel, check,
    gsel_o, gxcs_o, gzg_o, gsr_o, q_o, smallg_o, outg_o,
    dm_s, dx_s, gy_s, gdx_s, gdl_s, wr_s, rd_s, gwr_s, grd_s, rate_s, lam_s, ga_s,
):
    rows, inner = ys.shape
    tok = rows // 2
    half = states // 2
    gbr = jnp.concatenate([gbr_a[...], gbr_b[...]], axis=0)
    outg_o[...] = mm(gated[...], gbr, TN).astype(BF16)
    g_gated = mm(gbr, g2[:, inner:], NT)
    xcf = xc[...].astype(F32)
    skip = small[ROW_SKIP : ROW_SKIP + 1]
    sig = sigmoid(zg[...])
    gy = g_gated * (zg[...] * sig)
    gy_s[...] = gy
    gzg_o[...] = (g_gated * (ys[...] + skip * xcf) * (sig * (1.0 + zg[...] * (1.0 - sig)))).astype(BF16)
    delta = softplus(step_pre[...])
    dm_s[...] = jnp.where(keep[:, 0:1] > 0.0, delta, 1e30)
    dx_s[...] = delta * xcf
    for b in range(2):
        turned = jnp.transpose(sel[b * tok : (b + 1) * tok])
        wr_s[b] = turned[rank : rank + states]
        rd_s[b] = turned[rank + states : rank + 2 * states]
    rate_s[...] = jnp.exp(small[ROW_DECAY : ROW_DECAY + states]) * (-LOG2E)
    lam_s[...] = jnp.zeros_like(lam_s)
    ga_s[...] = jnp.zeros_like(ga_s)
    gwr_s[...] = jnp.zeros_like(gwr_s)
    grd_s[...] = jnp.zeros_like(grd_s)
    shape = (states, LANES)

    def chunk(i, carry):
        ci = tok // 8 - 1 - i
        t0 = pl.multiple_of(ci * 8, 8)
        for b in range(2):
            at = pl.multiple_of(b * tok + t0, 8)
            wr8 = pltpu.roll(wr_s[b], tok - t0, 1)
            rd8 = pltpu.roll(rd_s[b], tok - t0, 1)
            wcol = [jnp.broadcast_to(wr8[:, j : j + 1], shape) for j in range(8)]
            rcol = [jnp.broadcast_to(rd8[:, j : j + 1], shape) for j in range(8)]
            grd = [jnp.zeros(shape, F32)] * 8
            gwr = [jnp.zeros(shape, F32)] * 8
            for g in range(inner // LANES):
                lanes = slice(g * LANES, (g + 1) * LANES)
                h = check[ci * 2 + b, :, lanes]
                rate = rate_s[:, lanes]
                dm8 = dm_s[pl.ds(at, 8), lanes]
                dx8 = dx_s[pl.ds(at, 8), lanes]
                gy8 = gy_s[pl.ds(at, 8), lanes]
                decays, olds = [], []
                for j in range(8):
                    d = jnp.broadcast_to(dm8[j : j + 1], shape)
                    x = jnp.broadcast_to(dx8[j : j + 1], shape)
                    a = jnp.exp2(d * rate)
                    old = a * h
                    h = old + wcol[j] * x
                    grd[j] = grd[j] + h * jnp.broadcast_to(gy8[j : j + 1], shape)
                    decays.append(a)
                    olds.append(old)
                lam_in = lam_s[b, :, lanes]
                ga = ga_s[:, lanes]
                to_dx, to_dl = [None] * 8, [None] * 8
                for j in range(7, -1, -1):
                    lam = rcol[j] * jnp.broadcast_to(gy8[j : j + 1], shape) + lam_in
                    lam_in = decays[j] * lam
                    w = lam * olds[j]
                    ga = ga + w * jnp.broadcast_to(dm8[j : j + 1], shape)
                    p = lam * wcol[j]
                    to_dx[j] = p[:half] + p[half:]
                    p = w * rate
                    to_dl[j] = p[:half] + p[half:]
                    gwr[j] = gwr[j] + lam * jnp.broadcast_to(dx8[j : j + 1], shape)
                lam_s[b, :, lanes] = lam_in
                ga_s[:, lanes] = ga
                gdx_s[pl.ds(at, 8), lanes] = fold(to_dx)
                gdl_s[pl.ds(at, 8), lanes] = fold(to_dl)
            lane = iota(shape, 1)
            all_wr, all_rd = gwr_s[b], grd_s[b]
            for j in range(8):
                here = lane == t0 + j
                all_wr = jnp.where(here, jnp.sum(gwr[j], axis=1, keepdims=True), all_wr)
                all_rd = jnp.where(here, jnp.sum(grd[j], axis=1, keepdims=True), all_rd)
            gwr_s[b] = all_wr
            grd_s[b] = all_rd
        return carry

    lax.fori_loop(0, tok // 8, chunk, 0)
    delta = softplus(step_pre[...])
    gdx = gdx_s[...]
    xcf = xc[...].astype(F32)
    gy = gy_s[...]
    gxcs_o[...] = gy * skip + gdx * delta
    g_step = (gdx * xcf + LN2 * gdl_s[...]) * sigmoid(step_pre[...])
    gsr = g_step.astype(BF16)
    gsr_o[...] = gsr
    lane = iota((rows, LANES), 1)
    tail = LANES - rank
    q_o[...] = jnp.where(lane >= tail, pltpu.roll(sel[...], tail, 1), 0.0).astype(BF16)
    back = jnp.where(lane >= tail, mm(gsr, g1sel[...]), 0.0)
    back = pltpu.roll(back, rank, 1)
    zeros_top = jnp.zeros((rank, tok), F32)
    zeros_end = jnp.zeros((LANES - rank - 2 * states, tok), F32)
    for b in range(2):
        stack = jnp.concatenate([zeros_top, gwr_s[b], grd_s[b], zeros_end], axis=0)
        span = slice(b * tok, (b + 1) * tok)
        gsel_o[span] = back[span] + jnp.transpose(stack)
    smallg_o[0:ROW_STEP] = jnp.zeros((ROW_STEP, inner), F32)
    smallg_o[ROW_STEP : ROW_STEP + 1] = jnp.sum(g_step, axis=0, keepdims=True)
    smallg_o[ROW_SKIP : ROW_SKIP + 1] = jnp.sum(gy * xcf, axis=0, keepdims=True)
    smallg_o[ROW_SKIP + 1 : ROW_DECAY] = jnp.zeros((ROW_DECAY - ROW_SKIP - 1, inner), F32)
    smallg_o[ROW_DECAY : ROW_DECAY + states] = ga_s[...] * rate_s[...] * LN2
    rest = smallg_o.shape[0] - ROW_DECAY - states
    if rest:
        smallg_o[ROW_DECAY + states :] = jnp.zeros((rest, inner), F32)


def leave_kernel(
    lens, nat, gsel_a, gsel_b, gxcs, gzg, gsr, q, smallg, xin, xc, u, small, g1, g2z, tok2, dnat, dgrad,
    mine_o, send_o, gx_o, gz_o, gsmall_o,
):
    rows, inner = xin.shape
    tok = rows // 2
    width = tok2.shape[1]
    perm = perm_matrix(nat)
    g_sel = (gsel_a[...] + swap_halves(gsel_b[...])).astype(BF16)
    selblk = g1[:, inner + LANES : inner + 2 * LANES]
    block = mm(xc[...], g_sel, TN) + mm(gsr[...], q[...], TN)
    gsmall_o[:, LANES : 2 * LANES] = block.astype(BF16)
    g_xc = mm(g_sel, selblk, NT) + gxcs[...]
    offset = both_offsets(lens, tok)
    x = xin[...]
    sm = small[...]
    conv = conv_of(x, sm, offset)
    sig = sigmoid(conv)
    g_conv = g_xc * (sig * (1.0 + conv * (1.0 - sig)))
    g_xin = sm[3:4] * g_conv
    taps = [None, None, None, jnp.sum(g_conv * x, axis=0, keepdims=True)]
    for lag in range(1, 4):
        held = jnp.where(offset >= lag, g_conv, 0.0)
        g_xin = g_xin + sm[3 - lag : 4 - lag] * pltpu.roll(held, rows - lag, 0)
        taps[3 - lag] = jnp.sum(held * pltpu.roll(x, lag, 0), axis=0, keepdims=True)
    g_bias = jnp.sum(g_conv, axis=0, keepdims=True)
    top = jnp.concatenate(taps + [g_bias, jnp.zeros((3, inner), F32)], axis=0)
    full = jnp.concatenate([smallg[0:8] + top, smallg[8:]], axis=0)
    pad = jnp.zeros((LANES - full.shape[0], inner), F32)
    gsmall_o[:, 2 * LANES : 3 * LANES] = jnp.transpose(jnp.concatenate([full, pad], axis=0)).astype(BF16)
    g_xin = g_xin.astype(BF16)
    gx_o[...] = mm(u[...], g_xin, TN).astype(BF16)
    gz_o[...] = mm(u[...], gzg[...], TN).astype(BF16)
    gn = mm(g_xin, g1[:, :inner], NT) + mm(gzg[...], g2z[...], NT)
    gn = split_mm(gn, perm, NT)
    vals = tok2[...].astype(F32)
    scale = lax.rsqrt(jnp.mean(vals * vals, axis=1, keepdims=True) + EPS)
    gain_g = jnp.sum(gn * (vals * scale), axis=0, keepdims=True)
    dg = jnp.where(iota(dgrad.shape, 0) == 0, gain_g, dgrad[...])
    dg = split_mm(dg, perm)
    dpad = jnp.zeros((LANES - dg.shape[0], width), F32)
    gsmall_o[:, :LANES] = jnp.transpose(jnp.concatenate([dg, dpad], axis=0)).astype(BF16)
    mine_o[...] = gn[:tok]
    send_o[...] = gn[tok:]


def final_kernel(tok, mine, got, ghid, dnat, out_o):
    width = tok.shape[1]
    vals = tok[...].astype(F32)
    scale = lax.rsqrt(jnp.mean(vals * vals, axis=1, keepdims=True) + EPS)
    hat = vals * scale
    gg = (mine[...] + got[...]) * dnat[0:1]
    mean = jnp.sum(gg * hat, axis=1, keepdims=True) * (1.0 / width)
    out_o[...] = ghid[...] + scale * (gg - hat * mean)


def swap(values, axis):
    return lax.ppermute(values, axis, [(0, 1), (1, 0)])


def gather_group(piece, count):
    many = jnp.broadcast_to(piece[None], (count,) + piece.shape)
    many = lax.all_to_all(many, GROUP, split_axis=0, concat_axis=0, tiled=True)
    return many.reshape((count * piece.shape[0],) + piece.shape[1:])


def reduce_group(array, count):
    parts = array.reshape((count, array.shape[0] // count) + array.shape[1:])
    parts = lax.all_to_all(parts, GROUP, split_axis=0, concat_axis=0, tiled=True)
    return jnp.sum(parts.astype(F32), axis=0)


def body(
    sizes,
    tokens,
    cotangent,
    seq_lens,
    routes,
    norm_gain,
    input_proj,
    conv_weight,
    conv_bias,
    select_proj,
    step_proj,
    step_bias,
    decay_log,
    skip_gain,
    output_proj,
    moe_gain,
    router_weight,
    up_weight,
    down_weight,
):
    ny, nz, nx = sizes
    nf = nz * nx
    ng = ny * nf
    tok, width = tokens.shape
    rank, er = step_proj.shape
    states = decay_log.shape[0]
    experts = router_weight.shape[1]
    capacity = 5 * tok // (4 * experts)
    dr = norm_gain.shape[0]
    inner = ng * er
    core = lax.axis_index("c")
    rows = 2 * tok
    small_n = -(-(ROW_DECAY + states) // 8) * 8
    dn = -(-(2 + experts) // 8) * 8

    nat = np.arange(width).reshape(ny, 2, nf, dr).transpose(0, 2, 1, 3).reshape(1, width)
    nat = jnp.asarray(nat, jnp.int32)

    tok_peer = swap(tokens, "c")
    lens2 = jnp.concatenate([seq_lens, swap(seq_lens, "c")], axis=0)
    tok2 = jnp.concatenate([tokens, tok_peer], axis=0)

    cols = input_proj.reshape(dr, 2, ny, 2, nf * er)
    mine_w = lax.dynamic_index_in_dim(cols, core, 3, keepdims=False).reshape(dr, 2 * inner)
    other_w = lax.dynamic_index_in_dim(cols, 1 - core, 3, keepdims=False).reshape(dr, 2 * inner)
    dsmall = jnp.concatenate([norm_gain[:, None], moe_gain[:, None], router_weight], axis=1)
    dsmall = jnp.pad(dsmall, ((0, 0), (0, LANES - dsmall.shape[1])))
    got = swap(jnp.concatenate([other_w, dsmall], axis=1), "c")
    mine_a = jnp.concatenate([mine_w, dsmall], axis=1)
    first = jnp.where(core == 0, mine_a, got)
    second = jnp.where(core == 0, got, mine_a)
    pack_a = jnp.concatenate([first, second], axis=0)
    small = jnp.concatenate(
        [
            conv_weight.T,
            conv_bias[:, None],
            step_bias[:, None],
            skip_gain[:, None],
            jnp.zeros((er, 1), BF16),
            decay_log.T,
        ],
        axis=1,
    )
    small = jnp.pad(small, ((0, 0), (0, LANES - small.shape[1])))
    gap = jnp.zeros((er, LANES - rank - select_proj.shape[1]), BF16)
    pack_b = jnp.concatenate([select_proj, gap, step_proj.T, small], axis=1)
    group1 = jnp.concatenate([pack_a[:, :inner], pack_a[:, 2 * inner :], pack_b], axis=1)
    group2 = jnp.concatenate([pack_a[:, inner : 2 * inner], output_proj], axis=1)
    g1 = gather_group(group1, ng)
    g2 = gather_group(group2, ng)

    u, xin, xc, selp, small_t, dnat = call(
        enter_kernel,
        [((rows, width), BF16), ((rows, inner), F32), ((rows, inner), BF16), ((rows, LANES), F32), ((small_n, inner), F32), ((dn, width), F32)],
        [lens2, tok2, nat, g1],
        [SMEM, None, None, None],
        name="enter",
    )
    selq = swap(selp, "c")
    g1sel_spec = pl.BlockSpec((inner, LANES), lambda i: (0, inner // LANES + 1))
    chunks = tok // 8
    gated, ys, zg, step_pre, sel, keep, br_mine, br_send, check = call(
        functools.partial(scan_kernel, rank, states),
        [((rows, inner), BF16), ((rows, inner), F32), ((rows, inner), F32), ((rows, inner), F32), ((rows, LANES), F32), ((rows, LANES), F32), ((tok, width), F32), ((tok, width), F32), ((2 * chunks, states, inner), F32)],
        [lens2, selp, selq, u, xc, g1, g2, small_t],
        [SMEM, None, None, None, None, g1sel_spec, None, None],
        scratch=[pltpu.VMEM((rows, inner), F32), pltpu.VMEM((rows, inner), F32), pltpu.VMEM((2, states, tok), F32), pltpu.VMEM((2, states, tok), F32), pltpu.VMEM((states, inner), F32), pltpu.VMEM((2, states, inner), F32)],
        name="scan",
    )
    br_got = swap(br_send, "c")
    disp, hidden, gate = call(
        functools.partial(moe_enter_kernel, experts, capacity),
        [((experts, capacity, 2 * width), BF16), ((tok, width), F32), ((tok, LANES), F32)],
        [seq_lens, tokens, cotangent, routes, br_mine, br_got, dnat],
        [SMEM] + [None] * 6,
        name="moe_enter",
    )
    line = lax.all_to_all(disp, ("z", "x"), split_axis=0, concat_axis=0, tiled=True)
    line = line.reshape(nf * capacity, 2 * width)
    if ny > 1:
        line = jnp.concatenate([line, swap(line, "y")], axis=0)
    peer = swap(line, "c")
    total = 2 * line.shape[0]
    hid = up_weight.shape[1]
    out_own, out_peer, up_grad, down_grad = call(
        functools.partial(expert_kernel, width),
        [((total // 2, 2 * width), F32), ((total // 2, 2 * width), BF16), ((1, hid, width), F32), ((1, hid, width), F32)],
        [line, peer, up_weight, down_weight],
        scratch=[pltpu.VMEM((total, 2 * width), BF16), pltpu.VMEM((total, 2 * width), F32)],
        name="expert",
    )
    summed = out_own + swap(out_peer, "c").astype(F32)
    if ny > 1:
        cut = nf * capacity
        summed = summed[:cut] + swap(summed[cut:].astype(BF16), "y").astype(F32)
    back = lax.all_to_all(
        summed.astype(BF16).reshape(nf, capacity, 2 * width), ("z", "x"), split_axis=0, concat_axis=0, tiled=True
    )
    result, ghid, gbr, dgrad = call(
        functools.partial(moe_leave_kernel, experts, capacity),
        [((tok, width), BF16), ((tok, width), F32), ((tok, width), BF16), ((dn, width), F32)],
        [seq_lens, routes, cotangent, hidden, gate, dnat, back],
        [SMEM] + [None] * 6,
        name="moe_leave",
    )
    gbr_got = swap(gbr, "c")
    gsel, gxcs, gzg, gsr, q, smallg, outg = call(
        functools.partial(scan_back_kernel, rank, states),
        [((rows, LANES), F32), ((rows, inner), F32), ((rows, inner), BF16), ((rows, inner), BF16), ((rows, LANES), BF16), ((small_n, inner), F32), ((inner, width), BF16)],
        [gbr, gbr_got, g2, gated, xc, ys, zg, step_pre, sel, keep, small_t, g1, check],
        [None] * 11 + [g1sel_spec, None],
        scratch=[pltpu.VMEM((rows, inner), F32)] * 5 + [pltpu.VMEM((2, states, tok), F32)] * 4 + [pltpu.VMEM((states, inner), F32), pltpu.VMEM((2, states, inner), F32), pltpu.VMEM((states, inner), F32)],
        name="scan_back",
    )
    gsel_got = swap(gsel, "c")
    g2z_spec = pl.BlockSpec((inner, inner), lambda i: (0, 0))
    gn_mine, gn_send, gx, gz, gsmall = call(
        leave_kernel,
        [((tok, width), F32), ((tok, width), F32), ((width, inner), BF16), ((width, inner), BF16), ((inner, 3 * LANES), BF16)],
        [lens2, nat, gsel, gsel_got, gxcs, gzg, gsr, q, smallg, xin, xc, u, small_t, g1, g2, tok2, dnat, dgrad],
        [SMEM] + [None] * 13 + [g2z_spec, None, None, None],
        name="leave",
    )
    gn_got = swap(gn_send, "c")
    (input_grad,) = call(
        final_kernel, [((tok, width), F32)], [tokens, gn_mine, gn_got, ghid, dnat], name="final"
    )
    packed = jnp.concatenate([gx, gz, gsmall, outg], axis=1)
    share = reduce_group(packed, ng)
    wide = jnp.concatenate([share[:, : 2 * inner], share[:, 2 * inner : 2 * inner + LANES]], axis=1)
    keep_rows = lax.dynamic_slice_in_dim(wide, core * dr, dr, 0)
    send_rows = lax.dynamic_slice_in_dim(wide, (1 - core) * dr, dr, 0)
    got_rows = swap(send_rows, "c")
    own_cols = keep_rows[:, : 2 * inner].reshape(dr, 2, ny, 1, nf * er)
    got_cols = got_rows[:, : 2 * inner].reshape(dr, 2, ny, 1, nf * er)
    lo = jnp.where(core == 0, own_cols, got_cols)
    hi = jnp.where(core == 0, got_cols, own_cols)
    in_grad = jnp.concatenate([lo, hi], axis=3).reshape(dr, 4 * inner)
    dsum = keep_rows[:, 2 * inner :] + got_rows[:, 2 * inner :]
    at = 2 * inner + LANES
    sel_n = select_proj.shape[1]
    select_grad = share[:, at : at + sel_n]
    step_grad = share[:, at + LANES - rank : at + LANES].T
    ch = share[:, at + LANES : at + 2 * LANES]
    out_grad = share[:, at + 2 * LANES :]
    return (
        result,
        input_grad,
        dsum[:, 0],
        in_grad,
        ch[:, 0:4].T,
        ch[:, ROW_BIAS],
        select_grad,
        step_grad,
        ch[:, ROW_STEP],
        ch[:, ROW_DECAY : ROW_DECAY + states].T,
        ch[:, ROW_SKIP],
        out_grad,
        dsum[:, 1],
        dsum[:, 2 : 2 + experts],
        up_grad,
        down_grad,
    )


def solution(mesh):
    dp, fsdp = mesh.shape["dp"], mesh.shape["fsdp"]
    ny, nx = dp // 2, 2
    nz = fsdp // nx
    fine = Mesh(mesh.devices.reshape(ny, 2, nz, nx), ALL)
    tok = P(ALL, None)
    vec = P(ALL)
    col = P(None, ALL)
    exp = P(("z", "x"), ("y", "c"), None)
    in_specs = (tok, tok, tok, tok, vec, tok, col, vec, tok, col, vec, col, vec, tok, vec, tok, exp, exp)
    out_specs = (tok, tok, vec, tok, col, vec, tok, col, vec, col, vec, tok, vec, tok, exp, exp)
    return jax.shard_map(
        functools.partial(body, (ny, nz, nx)), mesh=fine, in_specs=in_specs, out_specs=out_specs, check_vma=False
    )
```

time: 3080 us -> 374 us (0.12); the launches traced: 3030 us -> 371 us
  local copies, waits for them, and re-layouts: 1320 us -> 23.7 us
  other arithmetic: 511 us -> 9.82 us
  waiting for transfers between devices: 685 us -> 207 us
  blocking collectives: 425 us -> 41 us
  Pallas kernels: 0 us -> 65.6 us
  matrix products: 56.4 us -> 0 us
    pad x156 -> x1, local copies, waits for them, and re-layouts: 1160 us -> 0.01 us  [body(): small = jnp.pad(small, ((0, 0), (0, LANES - small.shape[1])))]
    reduce_scatter x5 -> x0, waiting for transfers between devices: 448 us -> none  [the longest x1 142 us: body(): lax.psum_scatter(in_grad, ('dp', 'fsdp'), scatter_dimension=0, tiled=True)]
    all_gather x5 -> x0, blocking collectives: 332 us -> none  [the longest x1 67.8 us: body(): lax.all_gather(step_proj, ('dp', 'fsdp'), axis=1, tiled=True)]
    unnamed x15 -> x0, waiting for transfers between devices: 221 us -> none
    mul x72 -> x0, other arithmetic: 180 us -> none  [the longest x50 159 us: pair_combine(): return (earlier[0] * later[0], later[0] * earlier[1] + later[1])]
    all_to_all x3, waiting for transfers between devices: 15.4 us -> 172 us  [the longest x1 86.6 us: reduce_group(): lax.all_to_all(parts, GROUP, split_axis=0, concat_axis=0, tiled=True)]
    add x52 -> x2, other arithmetic: 102 us -> 1.79 us  [the longest x1 1.78 us: body(): summed = out_own + swap(out_peer, 'c').astype(F32)]
    unnamed x2 -> x0, blocking collectives: 81.5 us -> none
  transfers between devices with their start and end apart: 15 -> 16, of which waited for: 10 -> 13; matrix products, arithmetic and copies ran while one was open for 18% -> 3% of each run, Pallas kernels for 0% -> 2%
where the time goes in v1:
time: 374 us; the launch traced here: 371 us
  waiting for transfers between devices  207 us (55%)
  Pallas kernels  65.6 us (18%)
  blocking collectives  41 us (11%)
  local copies, waits for them, and re-layouts  23.7 us (6%)
  starting transfers between devices  22.4 us (6%)
  other arithmetic  9.82 us (3%)
    all_to_all x1, waiting for transfers between devices, reduce_group(): lax.all_to_all(parts, GROUP, split_axis=0, concat_axis=0, tiled=True)  86.6 us
    all_to_all x2, waiting for transfers between devices, gather_group(): many = lax.all_to_all(many, GROUP, split_axis=0, concat_axis=0, tiled=True)  85.7 us
    pallas_call x8, Pallas kernels, call(): pl.pallas_call(kernel, grid=(1,) if windowed else (), out_shape=[jax.Shap...  65.6 us
    ppermute x13, waiting for transfers between devices, swap(): return lax.ppermute(values, axis, [(0, 1), (1, 0)])  34.9 us
    all_to_all x1, blocking collectives, body(): lax.all_to_all(disp, ('z', 'x'), split_axis=0, concat_axis=0, tiled=True)  20.8 us
    all_to_all x1, blocking collectives, body(): lax.all_to_all(summed.astype(BF16).reshape(nf, capacity, 2 * width), ('z'...  20.1 us
    all_to_all x2, starting transfers between devices, gather_group(): many = lax.all_to_all(many, GROUP, split_axis=0, concat_axis=0, tiled=True)  12.7 us
    unnamed x41, local copies, waits for them, and re-layouts  10.7 us
  transfers between devices with their start and end apart: 16, of which 13 were waited for; matrix products, arithmetic and copies ran while one was open for 3% of the time, Pallas kernels for 2%

profile of v1, /device:TPU:0, one launch (start us, length us, event | category | flops | bytes accessed | tf_op | source)
XLA Modules:
  0.0 370.7 jit_solution(18187352524260053152)
XLA Ops:
  9.8 1.3 broadcast_in_dim.36
  11.1 7.9 %all-to-all-start = ((bf16[16,48,1152]{2,1,0:T(8,128)(2,1)}), bf16[16,48,1152]{2,1,0:T(8,128)(2,1)S(1)}, u32[]{:S(2)}, u32[]{:S(2)}) async-start(bf16[16,48,1152]{2,1,0:T(8,128)(2,1)} %broadcast_in_dim.36), calls=%async_computation | async-start | bytes 3538944 | tf_op jit(solution)/shard_map/all_to_all | solution.py:487
  19.0 41.4 %all-to-all-done = bf16[16,48,1152]{2,1,0:T(8,128)(2,1)S(1)} async-done(((bf16[16,48,1152]{2,1,0:T(8,128)(2,1)}), bf16[16,48,1152]{2,1,0:T(8,128)(2,1)S(1)}, u32[]{:S(2)}, u32[]{:S(2)}) %all-to-all-start) | async-done | bytes 1769504 | tf_op jit(solution)/shard_map/all_to_all | solution.py:487
  60.4 1.8 broadcast_in_dim.37
  62.3 4.8 %all-to-all-start.1 = ((bf16[16,48,1536]{2,1,0:T(8,128)(2,1)}), bf16[16,48,1536]{2,1,0:T(8,128)(2,1)}, u32[]{:S(2)}, u32[]{:S(2)}) async-start(bf16[16,48,1536]{2,1,0:T(8,128)(2,1)} %broadcast_in_dim.37), calls=%async_computation.1 | async-start | bytes 4718592 | tf_op jit(solution)/shard_map/all_to_all | solution.py:487
  69.6 4.3 %enter.1 = (bf16[256,768]{1,0:T(8,128)(2,1)}, f32[256,768]{1,0:T(8,128)}, bf16[256,768]{1,0:T(8,128)(2,1)}, f32[256,128]{1,0:T(8,128)}, f32[24,768]{1,0:T(8,128)}, /*index=5*/f32[16,768]{1,0:T(8,128)}) custom-call(s32[2,8]{1,0:T(2,128)} %pad_add_fusion.lens, bf16[256,768]{1,0:T(8,128)(2,1)} %copy-done.1, s32[1,768]{1,0:T(1,128)} %constant.30.clone.nat, ...), custom_call_target="tpu_custom_call" | custom-call | tf_op jit(solution)/shard_map/enter/pallas_call | solution.py:84
  74.2 1.3 collective-permute-done.3.sel_b
  75.5 44.3 %all-to-all-done.1 = bf16[16,48,1536]{2,1,0:T(8,128)(2,1)} async-done(((bf16[16,48,1536]{2,1,0:T(8,128)(2,1)}), bf16[16,48,1536]{2,1,0:T(8,128)(2,1)}, u32[]{:S(2)}, u32[]{:S(2)}) %all-to-all-start.1) | async-done | bytes 2359328 | tf_op jit(solution)/shard_map/all_to_all | solution.py:487
  119.9 10.7 %scan.1 = (bf16[256,768]{1,0:T(8,128)(2,1)}, f32[256,768]{1,0:T(8,128)}, f32[256,768]{1,0:T(8,128)}, f32[256,768]{1,0:T(8,128)}, f32[256,128]{1,0:T(8,128)}, /*i...) custom-call(s32[2,8]{1,0:T(2,128)} %pad_add_fusion.lens, ...), custom_call_target="tpu_custom_call" | custom-call | tf_op jit(solution)/shard_map/scan/pallas_call | solution.py:84
  131.3 1.2 collective-permute-done.4.got
  133.3 3.4 moe_enter.1
  136.7 20.8 %all_to_all.25 = bf16[8,20,1536]{2,1,0:T(8,128)(2,1)S(1)} all-to-all(bf16[8,20,1536]{2,1,0:T(8,128)(2,1)} %get-tuple-element.63), channel_id=1, replica_groups=mesh['y'=2,'c'=2,'z'=4,'x'=2] {'z','x'}, dimensions={0} | all-to-all | bytes 983040 | tf_op jit(solution)/shard_map/all_to_all | solution.py:595
  157.6 1.5 collective-permute-start.5
  159.2 10.2 %collective-permute-done.5 = bf16[160,1536]{1,0:T(8,128)(2,1)S(1)} collective-permute-done((bf16[160,1536]{1,0:T(8,128)(2,1)S(1)}, bf16[160,1536]{1,0:T(8,128)(2,1)S(1)}, u32[]{:S(2)}, u32[]{:S(2)}) %collective-permute-start.5) | collective-permute-done | bytes 491552 | tf_op jit(solution)/shard_map/ppermute | solution.py:482
  169.5 2.6 collective-permute-done.6.peer
  173.1 10.8 %expert.1 = (f32[320,1536]{1,0:T(8,128)}, bf16[320,1536]{1,0:T(8,128)(2,1)}, f32[1,768,768]{2,1,0:T(8,128)}, f32[1,768,768]{2,1,0:T(8,128)}) custom-call(bf16[320,1536]{1,0:T(8,128)(2,1)} %copy-done.2, bf16[320,1536]{1,0:T(8,128)(2,1)} %copy-done.5, bf16[1,768,768]{2,1,0:T(8,128)(2,1)} %up.1, bf16[1,768,768]{2,1,0:T(8,128)(2,1)} %down.1), custom_call_target="tpu_custom_call" | custom-call | tf_op jit(solution)/shard_map/expert/pallas_call | solution.py:84
  184.0 2.6 collective-permute-done.7
  186.7 1.8 convert_add_fusion
  188.5 1.5 collective-permute-start.8
  190.1 11.8 %collective-permute-done.8 = bf16[160,1536]{1,0:T(8,128)(2,1)S(1)} collective-permute-done((bf16[160,1536]{1,0:T(8,128)(2,1)S(1)}, bf16[160,1536]{1,0:T(8,128)(2,1)S(1)}, u32[]{:S(2)}, u32[]{:S(2)}) %collective-permute-start.8) | collective-permute-done | bytes 491552 | tf_op jit(solution)/shard_map/ppermute | solution.py:482
  202.1 20.1 %all_to_all.26.back = bf16[8,20,1536]{2,1,0:T(8,128)(2,1)} all-to-all(bf16[8,20,1536]{2,1,0:T(8,128)(2,1)S(1)} %reshape.115), channel_id=1, replica_groups=mesh['y'=2,'c'=2,'z'=4,'x'=2] {'z','x'}, dimensions={0} | all-to-all | bytes 983040 | tf_op jit(solution)/shard_map/all_to_all | solution.py:613
  222.2 4.0 %moe_leave.1 = (bf16[128,768]{1,0:T(8,128)(2,1)}, f32[128,768]{1,0:T(8,128)}, bf16[128,768]{1,0:T(8,128)(2,1)}, f32[16,768]{1,0:T(8,128)}) custom-call(s32[1,8]{1,0:T(1,128)} %lens.3, s32[128,1]{1,0:T(8,128)} %copy.113.routes, bf16[128,768]{1,0:T(8,128)(2,1)} %cot.3, f32[128,768]{1,0:T(8,128)} %get-tuple-element.61.hidden, ...), custom_call_target="tpu_custom_call" | custom-call | tf_op jit(solution)/shard_map/moe_leave/pallas_call | solution.py:84
  226.2 1.6 collective-permute-done.9.gbr_b
  228.6 20.5 %scan_back.1 = (f32[256,128]{1,0:T(8,128)}, f32[256,768]{1,0:T(8,128)}, bf16[256,768]{1,0:T(8,128)(2,1)}, bf16[256,768]{1,0:T(8,128)(2,1)}, bf16[256,128]{1,0:T(...) custom-call(bf16[128,768]{1,0:T(8,128)(2,1)} %get-tuple-element.67.gbr_a, bf16[128,768]{1,0:T(8,128)(2,1)} %copy-done.8, ...), custom_call_target="tpu_custom_call" | custom-call | tf_op jit(solution)/shard_map/scan_back/pallas_call | solution.py:84
  249.2 1.4 collective-permute-done.10.gsel_b
  251.3 9.6 %leave.1 = (f32[128,768]{1,0:T(8,128)}, f32[128,768]{1,0:T(8,128)}, bf16[768,768]{1,0:T(8,128)(2,1)}, bf16[768,768]{1,0:T(8,128)(2,1)}, bf16[768,384]{1,0:T(8,128)(2,1)}) custom-call(s32[2,8]{1,0:T(2,128)} %pad_add_fusion.lens, s32[1,768]{1,0:T(1,128)} %constant.30.clone.nat, f32[256,128]{1,0:T(8,128)} %get-tuple-element.75.gsel_a, f32[256,128]{1,0:T(8,128)} %copy-done.9, ...), custom_call_target="tpu_custom_call" | custom-call | tf_op jit(solution)/shard_map/leave/pallas_call | solution.py:84
  260.9 3.4 pad_maximum_fusion
  264.4 4.7 %all-to-all-start.4 = ((bf16[16,48,2688]{2,1,0:T(8,128)(2,1)}), bf16[16,48,2688]{2,1,0:T(8,128)(2,1)}, u32[]{:S(2)}, u32[]{:S(2)}) async-start(bf16[16,48,2688]{2,1,0:T(8,128)(2,1)} %bitcast.21), calls=%async_computation.4 | async-start | bytes 8257536 | tf_op jit(solution)/shard_map/all_to_all | solution.py:493
  269.3 1.6 collective-permute-done.11.got
  271.6 2.3 final.1
  273.9 86.6 %all-to-all-done.4 = bf16[16,48,2688]{2,1,0:T(8,128)(2,1)} async-done(((bf16[16,48,2688]{2,1,0:T(8,128)(2,1)}), bf16[16,48,2688]{2,1,0:T(8,128)(2,1)}, u32[]{:S(2)}, u32[]{:S(2)}) %all-to-all-start.4) | async-done | bytes 4128800 | tf_op jit(solution)/shard_map/all_to_all | solution.py:493
  360.5 2.8 convert_reduce_fusion
  (96 shorter events, 24.9 us)
Async XLA Ops:
  3.5 5.3 %collective-permute-start.2 = (bf16[24,1664]{1,0:T(8,128)(2,1)S(1)}, bf16[24,1664]{1,0:T(8,128)(2,1)S(1)}, u32[]{:S(2)}, u32[]{:S(2)}) collective-permute-start(bf16[24,1664]{1,0:T(8,128)(2,1)S(1)} %fusion.7), channel_id=1, source_target_pairs={{0,8},{8,0},{1,9},{9,1},{2,10},{10,2},{3,11},{11,3},{4,12},{12,4},... | collective-permute-start | bytes 239624 | tf_op jit(solution)/shard_map/ppermute | solution.py:482
  9.8 9.2 %copy-start.11 = (bf16[48,768]{1,0:T(8,128)(2,1)S(1)}, bf16[48,768]{1,0:T(8,128)(2,1)}, u32[]{:S(2)}) copy-start(bf16[48,768]{1,0:T(8,128)(2,1)} %param.32) | copy-start | bytes 221188
  11.1 49.3 %all-to-all-start = ((bf16[16,48,1152]{2,1,0:T(8,128)(2,1)}), bf16[16,48,1152]{2,1,0:T(8,128)(2,1)S(1)}, u32[]{:S(2)}, u32[]{:S(2)}) async-start(bf16[16,48,1152]{2,1,0:T(8,128)(2,1)} %broadcast_in_dim.36), calls=%async_computation | async-start | bytes 3538944 | tf_op jit(solution)/shard_map/all_to_all | solution.py:487
  60.4 1.9 copy-start
  62.2 4.9 %copy-start.12 = (s32[1,8]{1,0:T(1,128)S(1)}, s32[1,8]{1,0:T(1,128)}, u32[]{:S(2)}) copy-start(s32[1,8]{1,0:T(1,128)} %lens.3) | copy-start | bytes 100
  62.2 5.0 %copy-start.3 = (bf16[128,768]{1,0:T(8,128)(2,1)S(1)}, bf16[128,768]{1,0:T(8,128)(2,1)}, u32[]{:S(2)}) copy-start(bf16[128,768]{1,0:T(8,128)(2,1)} %tok.3) | copy-start | bytes 589828
  62.3 57.5 %all-to-all-start.1 = ((bf16[16,48,1536]{2,1,0:T(8,128)(2,1)}), bf16[16,48,1536]{2,1,0:T(8,128)(2,1)}, u32[]{:S(2)}, u32[]{:S(2)}) async-start(bf16[16,48,1536]{2,1,0:T(8,128)(2,1)} %broadcast_in_dim.37), calls=%async_computation.1 | async-start | bytes 4718592 | tf_op jit(solution)/shard_map/all_to_all | solution.py:487
  67.1 1.2 collective-permute-start
  67.2 1.7 collective-permute-start.1
  68.9 0.7 copy-start.1
  73.9 1.6 collective-permute-start.3
  75.5 44.3 %copy-start.10 = (f32[256,128]{1,0:T(8,128)}, f32[256,128]{1,0:T(8,128)S(1)}, u32[]{:S(2)}) copy-start(f32[256,128]{1,0:T(8,128)S(1)} %collective-permute-done.3.sel_b) | copy-start | bytes 393220
  119.9 10.7 %copy-start.13 = (s32[128,1]{0,1:T(1,128)S(1)}, s32[128,1]{0,1:T(1,128)}, u32[]{:S(2)}) copy-start(s32[128,1]{0,1:T(1,128)} %param.22) | copy-start | bytes 1540
  130.6 1.9 collective-permute-start.4
  132.5 0.8 copy-start.7
  157.6 11.8 %collective-permute-start.5 = (bf16[160,1536]{1,0:T(8,128)(2,1)S(1)}, bf16[160,1536]{1,0:T(8,128)(2,1)S(1)}, u32[]{:S(2)}, u32[]{:S(2)}) collective-permute-start(bf16[160,1536]{1,0:T(8,128)(2,1)S(1)} %reshape.114), channel_id=1, source_target_pairs={{0,16},{16,0},{1,17},{17,1},{2,18},{18,2},{3,19},{19,3},{4,20},{20... | collective-permute-start | bytes 1474568 | tf_op jit(solution)/shard_map/ppermute | solution.py:482
  169.4 2.6 copy-start.2
  169.4 2.6 collective-permute-start.6
  172.1 1.0 copy-start.5
  183.9 2.8 collective-permute-start.7
  188.5 13.3 %collective-permute-start.8 = (bf16[160,1536]{1,0:T(8,128)(2,1)S(1)}, bf16[160,1536]{1,0:T(8,128)(2,1)S(1)}, u32[]{:S(2)}, u32[]{:S(2)}) collective-permute-start(bf16[160,1536]{1,0:T(8,128)(2,1)S(1)} %slice.136), channel_id=1, source_target_pairs={{0,16},{16,0},{1,17},{17,1},{2,18},{18,2},{3,19},{19,3},{4,20},{20... | collective-permute-start | bytes 1474568 | tf_op jit(solution)/shard_map/ppermute | solution.py:482
  226.2 1.7 collective-permute-start.9
  227.9 0.7 copy-start.8
  249.0 1.6 collective-permute-start.10
  250.6 0.7 copy-start.9
  251.3 9.6 %copy-start.4 = (bf16[768,768]{1,0:T(8,128)(2,1)S(1)}, bf16[768,768]{1,0:T(8,128)(2,1)}, u32[]{:S(2)}) copy-start(bf16[768,768]{1,0:T(8,128)(2,1)} %get-tuple-element.89) | copy-start | bytes 3538948
  264.4 4.7 %copy-start.14 = (f32[128,768]{1,0:T(8,128)S(1)}, f32[128,768]{1,0:T(8,128)}, u32[]{:S(2)}) copy-start(f32[128,768]{1,0:T(8,128)} %get-tuple-element.84) | copy-start | bytes 1179652
  264.4 96.1 %all-to-all-start.4 = ((bf16[16,48,2688]{2,1,0:T(8,128)(2,1)}), bf16[16,48,2688]{2,1,0:T(8,128)(2,1)}, u32[]{:S(2)}, u32[]{:S(2)}) async-start(bf16[16,48,2688]{2,1,0:T(8,128)(2,1)} %bitcast.21), calls=%async_computation.4 | async-start | bytes 8257536 | tf_op jit(solution)/shard_map/all_to_all | solution.py:493
  269.0 1.8 collective-permute-start.11
  270.8 0.8 copy-start.6
  363.4 4.2 %collective-permute-start.12 = (f32[24,1664]{1,0:T(8,128)S(1)}, f32[24,1664]{1,0:T(8,128)S(1)}, u32[]{:S(2)}, u32[]{:S(2)}) collective-permute-start(f32[24,1664]{1,0:T(8,128)S(1)} %constant_dynamic-slice_fusion), channel_id=1, source_target_pairs={{0,8},{8,0},{1,9},{9,1},{2,10},{10,2},{3,11},{11,3},{4,12},{12,4},... | collective-permute-start | bytes 479240 | tf_op jit(solution)/shard_map/ppermute | solution.py:482

commit v2 on v1

--- a/solution.py
+++ b/solution.py
@@ -20,6 +20,7 @@
 ALL = ("y", "c", "z", "x")
 GROUP = ("y", "z", "x")
 ROW_BIAS, ROW_STEP, ROW_SKIP, ROW_DECAY = 4, 5, 6, 8
+ROW_FEATURE = 64
 NN = (((1,), (0,)), ((), ()))
 NT = (((1,), (1,)), ((), ()))
 TN = (((0,), (0,)), ((), ()))
@@ -78,52 +79,219 @@
     return parts[0]
 
 
-def call(kernel, outs, args, specs=None, scratch=(), name=None, cost=None, vmem=60):
+def call(kernel, outs, args, specs=None, scratch=(), name=None, us=5, vmem=60):
     whole = pl.BlockSpec(memory_space=pltpu.VMEM)
-    windowed = specs is not None and any(s is not None and s.block_shape is not None for s in specs)
+    specs = [None] * len(args) if specs is None else specs
+    windowed = any(s is not None and s.block_shape is not None for s in specs)
     return pl.pallas_call(
         kernel,
         grid=(1,) if windowed else (),
-        out_shape=[jax.ShapeDtypeStruct(s, d) for s, d in outs],
-        in_specs=[whole] * len(args) if specs is None else [whole if s is None else s for s in specs],
-        out_specs=[whole] * len(outs),
+        out_shape=[jax.ShapeDtypeStruct(o[0], o[1]) for o in outs],
+        in_specs=[whole if s is None else s for s in specs],
+        out_specs=[o[2] if len(o) > 2 else whole for o in outs],
         scratch_shapes=list(scratch),
         name=name,
-        cost_estimate=cost,
+        cost_estimate=pl.CostEstimate(flops=us * 1000000000, bytes_accessed=us * 3000000, transcendentals=0),
         compiler_params=pltpu.CompilerParams(vmem_limit_bytes=vmem << 20),
     )(*args)
 
 
 SMEM = pl.BlockSpec(memory_space=pltpu.SMEM)
-
-
-def perm_matrix(nat_ref):
+HBM = pl.BlockSpec(memory_space=pl.ANY)
+
+
+def perm_matrix(idx, nat_ref):
     width = nat_ref.shape[1]
-    return (iota((width, width), 0) == nat_ref[...]).astype(F32).astype(BF16)
-
-
-def enter_kernel(lens, tok2, nat, g1, u_o, xin_o, xc_o, sel_o, small_o, dnat_o):
+    nat = jnp.where(idx[3] == 0, nat_ref[0:1], nat_ref[1:2])
+    return (iota((width, width), 0) == nat).astype(F32).astype(BF16)
+
+
+class Plan:
+    def __init__(self, ny, nz, nx, piece):
+        self.ny, self.nz, self.nx, self.piece = ny, nz, nx, piece
+        self.count = ny * nz * nx
+        self.fast = (ny, nz, nx) == (2, 4, 2) and piece % 16 == 0
+
+    def place(self, idx, yr, zr, xr):
+        y = jnp.bitwise_xor(idx[0], yr)
+        x = jnp.bitwise_xor(idx[2], xr)
+        z = lax.rem(idx[1] - zr + self.nz, self.nz)
+        return pl.multiple_of(((y * self.nz + z) * self.nx + x) * self.piece, self.piece)
+
+    def gather(self, piece):
+        if not self.fast:
+            return [lax.all_gather(piece, GROUP, axis=0, tiled=True)]
+        rots = [lax.ppermute(piece, "z", [(i, (i + k) % 4) for i in range(4)]) for k in (1, 2, 3)]
+        line = jnp.concatenate([piece] + rots, axis=0)
+        by_x, by_y = swap(line, "x"), swap(line, "y")
+        half = 2 * self.piece
+        return [line, by_x, by_y, swap(by_x[:half], "y"), swap(by_y[half:], "x")]
+
+    def pieces(self):
+        n, out = self.piece, []
+        for z in range(4):
+            out.append((0, z * n, 0, z, 0))
+            out.append((1, z * n, 0, z, 1))
+            out.append((2, z * n, 1, z, 0))
+            out.append((3 + z // 2, z % 2 * n, 1, z, 1))
+        return out
+
+    def n_gathered(self):
+        return 5 if self.fast else 1
+
+    def fetch(self, idx, refs, dst, sem):
+        if not self.fast:
+            copies = [pltpu.make_async_copy(refs[0], dst, sem.at[0])]
+        else:
+            copies = []
+            for k, (r, row, yr, zr, xr) in enumerate(self.pieces()):
+                to = dst.at[pl.ds(self.place(idx, yr, zr, xr), self.piece)]
+                copies.append(pltpu.make_async_copy(refs[r].at[pl.ds(row, self.piece)], to, sem.at[k]))
+        for copy in copies:
+            copy.start()
+        return copies
+
+    def shared_outs(self, width):
+        if not self.fast:
+            return [((self.count * self.piece, width), BF16, HBM)]
+        return [((8 * self.piece, width // 2), BF16, HBM)] * 4
+
+    def n_shared(self):
+        return 4 if self.fast else 1
+
+    def emit(self, idx, src, refs, sem):
+        if not self.fast:
+            copies = [pltpu.make_async_copy(src, refs[0], sem.at[0])]
+        else:
+            copies, n, half = [], self.piece, src.shape[1] // 2
+            for zr in range(4):
+                for yr in range(2):
+                    for xr in range(2):
+                        at = self.place(idx, yr, zr, xr)
+                        for lanes, ref, row in (
+                            (0, refs[1 - xr], yr * 4 + zr),
+                            (half, refs[3 - yr], xr * 4 + zr),
+                        ):
+                            copies.append(
+                                pltpu.make_async_copy(
+                                    src.at[pl.ds(at, n), pl.ds(lanes, half)],
+                                    ref.at[pl.ds(row * n, n)],
+                                    sem.at[len(copies)],
+                                )
+                            )
+        for copy in copies:
+            copy.start()
+        return copies
+
+    def reduce(self, shared, tag):
+        if not self.fast:
+            parts = shared[0].reshape(self.count, self.piece, -1)
+            parts = lax.all_to_all(parts, GROUP, split_axis=0, concat_axis=0, tiled=True)
+            return [parts.astype(F32).sum(axis=0)]
+        a_send, a_keep, b_send, b_keep = shared
+        n, half = self.piece, a_send.shape[1]
+        a_got, b_got = swap(a_send, "x"), swap(b_send, "y")
+        shape = ((4 * n, half), BF16)
+        a_send, a_keep, b_send, b_keep = call(
+            add_kernel, [shape] * 4, [a_keep, a_got, b_keep, b_got], name="add1_" + tag, us=2
+        )
+        a_got, b_got = swap(a_send, "y"), swap(b_send, "x")
+        parts = call(
+            line_kernel, [((n, 2 * half), BF16)] * 4, [a_keep, a_got, b_keep, b_got], name="add2_" + tag, us=1
+        )
+        rots = [lax.ppermute(parts[k], "z", [(i, (i - k) % 4) for i in range(4)]) for k in (1, 2, 3)]
+        return [parts[0]] + rots
+
+
+def add_kernel(a, a_in, b, b_in, a_send, a_keep, b_send, b_keep):
+    cut = a_send.shape[0]
+    for one, two, send, keep in ((a, a_in, a_send, a_keep), (b, b_in, b_send, b_keep)):
+        send[...] = (one[cut:].astype(F32) + two[cut:].astype(F32)).astype(BF16)
+        keep[...] = (one[:cut].astype(F32) + two[:cut].astype(F32)).astype(BF16)
+
+
+def line_kernel(a, a_in, b, b_in, *outs):
+    n, half = outs[0].shape[0], a.shape[1]
+    for k, out in enumerate(outs):
+        span = slice(k * n, (k + 1) * n)
+        out[:, :half] = (a[span].astype(F32) + a_in[span].astype(F32)).astype(BF16)
+        out[:, half:] = (b[span].astype(F32) + b_in[span].astype(F32)).astype(BF16)
+
+
+def pack_kernel(
+    span, idx, in_proj, norm, moe, router, taps, cbias, select, step, sbias, decay, skip,
+    mine_o, send_o, ch_o, rows_s, block_s,
+):
+    dr = in_proj.shape[0]
+    er, sel_n = select.shape
+    rank, states = step.shape[0], decay.shape[0]
+    inner2 = mine_o.shape[1] - LANES
+    first = idx[3] == 0
+    for k in range(inner2 // span):
+        low = in_proj[:, 2 * k * span : (2 * k + 1) * span]
+        high = in_proj[:, (2 * k + 1) * span : (2 * k + 2) * span]
+        mine_o[:, k * span : (k + 1) * span] = jnp.where(first, low, high)
+        send_o[:, k * span : (k + 1) * span] = jnp.where(first, high, low)
+    rows_s[...] = jnp.zeros_like(rows_s)
+    rows_s[0:4, :er] = taps[...].astype(F32)
+    rows_s[ROW_BIAS : ROW_BIAS + 1, :er] = cbias[...].astype(F32)
+    rows_s[ROW_STEP : ROW_STEP + 1, :er] = sbias[...].astype(F32)
+    rows_s[ROW_SKIP : ROW_SKIP + 1, :er] = skip[...].astype(F32)
+    rows_s[ROW_DECAY : ROW_DECAY + states, :er] = decay[...].astype(F32)
+    ch_o[:, LANES:] = jnp.transpose(rows_s[...])[:er].astype(BF16)
+    rows_s[...] = jnp.zeros_like(rows_s)
+    rows_s[LANES - rank :, :er] = step[...].astype(F32)
+    block_s[...] = jnp.zeros_like(block_s)
+    block_s[:er, :sel_n] = select[...].astype(F32)
+    ch_o[:, :LANES] = (block_s[:er] + jnp.transpose(rows_s[...])[:er]).astype(BF16)
+    rows_s[...] = jnp.zeros_like(rows_s)
+    rows_s[ROW_FEATURE : ROW_FEATURE + 1, :dr] = norm[...].astype(F32)
+    rows_s[ROW_FEATURE + 1 : ROW_FEATURE + 2, :dr] = moe[...].astype(F32)
+    block_s[...] = jnp.zeros_like(block_s)
+    block_s[:dr, ROW_FEATURE + 2 : ROW_FEATURE + 2 + router.shape[1]] = router[...].astype(F32)
+    feature = (block_s[:dr] + jnp.transpose(rows_s[...])[:dr]).astype(BF16)
+    mine_o[:, inner2:] = feature
+    send_o[:, inner2:] = feature
+
+
+def merge_kernel(mine, got, ch, out_proj, one_o, two_o):
+    inner = out_proj.shape[1]
+    both = jnp.concatenate([mine[...].astype(F32), got[...].astype(F32)], axis=0).astype(BF16)
+    one_o[:, :inner] = both[:, :inner]
+    one_o[:, inner : inner + LANES] = ch[:, :LANES]
+    one_o[:, inner + LANES :] = ch[:, LANES:] + both[:, 2 * inner :]
+    two_o[:, :inner] = both[:, inner : 2 * inner]
+    two_o[:, inner:] = out_proj[...]
+
+
+def enter_kernel(plan, idx, lens, tok2, nat, *refs):
+    n = plan.n_gathered()
+    pieces = refs[:n]
+    u_o, xin_o, xc_o, sel_o, small_o, dnat_o, g1, sem = refs[n:]
+    copies = plan.fetch(idx, pieces, g1, sem)
     rows, width = tok2.shape
     tok = rows // 2
     inner = xin_o.shape[1]
-    at = inner
-    perm = perm_matrix(nat)
-    dnat = mm(g1[:, at : at + LANES], perm, (((0,), (1,)), ((), ())))
-    dnat_o[...] = dnat[: dnat_o.shape[0]]
+    perm = perm_matrix(idx, nat)
     vals = tok2[...].astype(F32)
     scale = lax.rsqrt(jnp.mean(vals * vals, axis=1, keepdims=True) + EPS)
+    offset = both_offsets(lens, tok)
+    for copy in copies:
+        copy.wait()
+    table = g1[:, inner + LANES :]
+    dnat = mm(table, perm, (((0,), (1,)), ((), ())))[ROW_FEATURE:]
+    dnat_o[...] = dnat[: dnat_o.shape[0]]
     u = (vals * scale * dnat[0:1]).astype(BF16)
     u = mm(u, perm).astype(BF16)
     u_o[...] = u
     xin = mm(u, g1[:, :inner])
     xin_o[...] = xin
-    small = jnp.transpose(g1[:, at + 2 * LANES : at + 3 * LANES].astype(F32))
-    small_o[...] = small[: small_o.shape[0]]
-    offset = both_offsets(lens, tok)
+    small = jnp.transpose(table.astype(F32))[: small_o.shape[0]]
+    small_o[...] = small
     conv = conv_of(xin, small, offset)
     xc = (conv * sigmoid(conv)).astype(BF16)
     xc_o[...] = xc
-    sel_o[...] = mm(xc, g1[:, at + LANES : at + 2 * LANES])
+    sel_o[...] = mm(xc, g1[:, inner : inner + LANES])
 
 
 def conv_of(xin, small, offset):
@@ -140,8 +308,8 @@
 
 
 def scan_kernel(
-    rank, states, lens, sel_a, sel_b, u, xc, g1sel, g2, small,
-    gated_o, ys_o, zg_o, step_o, sel_o, keep_o, mine_o, send_o, check_o,
+    rank, states, lens, sel_a, sel_b, xc, g1sel, small,
+    ys_o, step_o, sel_o, keep_o, check_o,
     dm_s, dx_s, wr_s, rd_s, rate_s, h_s,
 ):
     rows, inner = ys_o.shape
@@ -194,9 +362,20 @@
         return carry
 
     lax.fori_loop(0, tok // 8, chunk, 0)
+
+
+def gate_kernel(plan, idx, u, xc, ys, small, *refs):
+    n = plan.n_gathered()
+    pieces = refs[:n]
+    gated_o, zg_o, mine_o, send_o, g2, sem = refs[n:]
+    copies = plan.fetch(idx, pieces, g2, sem)
+    for copy in copies:
+        copy.wait()
+    inner = ys.shape[1]
+    tok = mine_o.shape[0]
     zg = mm(u[...], g2[:, :inner])
     zg_o[...] = zg
-    gated = (ys_o[...] + small[ROW_SKIP : ROW_SKIP + 1] * xcf) * (zg * sigmoid(zg))
+    gated = (ys[...] + small[ROW_SKIP : ROW_SKIP + 1] * xc[...].astype(F32)) * (zg * sigmoid(zg))
     gated = gated.astype(BF16)
     gated_o[...] = gated
     branch = mm(gated, g2[:, inner:])
@@ -306,23 +485,36 @@
     gbr_o[...] = ghid.astype(BF16)
 
 
+def gate_back_kernel(plan, idx, gbr_a, gbr_b, g2, gated, xc, ys, zg, small, u, *refs):
+    n = plan.n_shared()
+    gy_o, gzg_o = refs[:2]
+    shared = refs[2 : 2 + n]
+    grad_s, sem = refs[2 + n :]
+    inner = ys.shape[1]
+    gbr = jnp.concatenate([gbr_a[...], gbr_b[...]], axis=0)
+    g_gated = mm(gbr, g2[:, inner:], NT)
+    skip = small[ROW_SKIP : ROW_SKIP + 1]
+    sig = sigmoid(zg[...])
+    gy_o[...] = g_gated * (zg[...] * sig)
+    gzg = g_gated * (ys[...] + skip * xc[...].astype(F32)) * (sig * (1.0 + zg[...] * (1.0 - sig)))
+    gzg = gzg.astype(BF16)
+    gzg_o[...] = gzg
+    grad_s[:, :inner] = mm(u[...], gzg, TN).astype(BF16)
+    grad_s[:, inner:] = mm(gated[...], gbr, TN).astype(BF16)
+    for copy in plan.emit(idx, grad_s, shared, sem):
+        copy.wait()
+
+
 def scan_back_kernel(
-    rank, states, gbr_a, gbr_b, g2, gated, xc, ys, zg, step_pre, sel, keep, small, g1sel, check,
-    gsel_o, gxcs_o, gzg_o, gsr_o, q_o, smallg_o, outg_o,
-    dm_s, dx_s, gy_s, gdx_s, gdl_s, wr_s, rd_s, gwr_s, grd_s, rate_s, lam_s, ga_s,
+    rank, states, gy_s, xc, step_pre, sel, keep, small, g1sel, check,
+    gsel_o, gxcs_o, gsr_o, q_o, smallg_o,
+    dm_s, dx_s, gdx_s, gdl_s, wr_s, rd_s, gwr_s, grd_s, rate_s, lam_s, ga_s,
 ):
-    rows, inner = ys.shape
+    rows, inner = gy_s.shape
     tok = rows // 2
     half = states // 2
-    gbr = jnp.concatenate([gbr_a[...], gbr_b[...]], axis=0)
-    outg_o[...] = mm(gated[...], gbr, TN).astype(BF16)
-    g_gated = mm(gbr, g2[:, inner:], NT)
     xcf = xc[...].astype(F32)
     skip = small[ROW_SKIP : ROW_SKIP + 1]
-    sig = sigmoid(zg[...])
-    gy = g_gated * (zg[...] * sig)
-    gy_s[...] = gy
-    gzg_o[...] = (g_gated * (ys[...] + skip * xcf) * (sig * (1.0 + zg[...] * (1.0 - sig)))).astype(BF16)
     delta = softplus(step_pre[...])
     dm_s[...] = jnp.where(keep[:, 0:1] > 0.0, delta, 1e30)
     dx_s[...] = delta * xcf
@@ -423,17 +615,20 @@
 
 
 def leave_kernel(
-    lens, nat, gsel_a, gsel_b, gxcs, gzg, gsr, q, smallg, xin, xc, u, small, g1, g2z, tok2, dnat, dgrad,
-    mine_o, send_o, gx_o, gz_o, gsmall_o,
+    plan, idx, lens, nat, gsel_a, gsel_b, gxcs, gzg, gsr, q, smallg, xin, xc, u, small, g1, g2z, tok2, dnat, dgrad, *refs
 ):
+    n = plan.n_shared()
+    mine_o, send_o = refs[:2]
+    shared = refs[2 : 2 + n]
+    grad_s, sem = refs[2 + n :]
     rows, inner = xin.shape
     tok = rows // 2
     width = tok2.shape[1]
-    perm = perm_matrix(nat)
+    perm = perm_matrix(idx, nat)
     g_sel = (gsel_a[...] + swap_halves(gsel_b[...])).astype(BF16)
-    selblk = g1[:, inner + LANES : inner + 2 * LANES]
+    selblk = g1[:, inner : inner + LANES]
     block = mm(xc[...], g_sel, TN) + mm(gsr[...], q[...], TN)
-    gsmall_o[:, LANES : 2 * LANES] = block.astype(BF16)
+    grad_s[:, inner : inner + LANES] = block.astype(BF16)
     g_xc = mm(g_sel, selblk, NT) + gxcs[...]
     offset = both_offsets(lens, tok)
     x = xin[...]
@@ -448,24 +643,24 @@
         g_xin = g_xin + sm[3 - lag : 4 - lag] * pltpu.roll(held, rows - lag, 0)
         taps[3 - lag] = jnp.sum(held * pltpu.roll(x, lag, 0), axis=0, keepdims=True)
     g_bias = jnp.sum(g_conv, axis=0, keepdims=True)
-    top = jnp.concatenate(taps + [g_bias, jnp.zeros((3, inner), F32)], axis=0)
-    full = jnp.concatenate([smallg[0:8] + top, smallg[8:]], axis=0)
-    pad = jnp.zeros((LANES - full.shape[0], inner), F32)
-    gsmall_o[:, 2 * LANES : 3 * LANES] = jnp.transpose(jnp.concatenate([full, pad], axis=0)).astype(BF16)
     g_xin = g_xin.astype(BF16)
-    gx_o[...] = mm(u[...], g_xin, TN).astype(BF16)
-    gz_o[...] = mm(u[...], gzg[...], TN).astype(BF16)
+    grad_s[:, :inner] = mm(u[...], g_xin, TN).astype(BF16)
     gn = mm(g_xin, g1[:, :inner], NT) + mm(gzg[...], g2z[...], NT)
     gn = split_mm(gn, perm, NT)
+    mine_o[...] = gn[:tok]
+    send_o[...] = gn[tok:]
     vals = tok2[...].astype(F32)
     scale = lax.rsqrt(jnp.mean(vals * vals, axis=1, keepdims=True) + EPS)
     gain_g = jnp.sum(gn * (vals * scale), axis=0, keepdims=True)
     dg = jnp.where(iota(dgrad.shape, 0) == 0, gain_g, dgrad[...])
     dg = split_mm(dg, perm)
-    dpad = jnp.zeros((LANES - dg.shape[0], width), F32)
-    gsmall_o[:, :LANES] = jnp.transpose(jnp.concatenate([dg, dpad], axis=0)).astype(BF16)
-    mine_o[...] = gn[:tok]
-    send_o[...] = gn[tok:]
+    top = jnp.concatenate(taps + [g_bias, jnp.zeros((3, inner), F32)], axis=0)
+    gap = jnp.zeros((ROW_FEATURE - smallg.shape[0], inner), F32)
+    end = jnp.zeros((LANES - ROW_FEATURE - dg.shape[0], inner), F32)
+    table = jnp.concatenate([smallg[0:8] + top, smallg[8:], gap, dg, end], axis=0)
+    grad_s[:, inner + LANES :] = jnp.transpose(table).astype(BF16)
+    for copy in plan.emit(idx, grad_s, shared, sem):
+        copy.wait()
 
 
 def final_kernel(tok, mine, got, ghid, dnat, out_o):
@@ -482,16 +677,56 @@
     return lax.ppermute(values, axis, [(0, 1), (1, 0)])
 
 
-def gather_group(piece, count):
-    many = jnp.broadcast_to(piece[None], (count,) + piece.shape)
-    many = lax.all_to_all(many, GROUP, split_axis=0, concat_axis=0, tiled=True)
-    return many.reshape((count * piece.shape[0],) + piece.shape[1:])
-
-
-def reduce_group(array, count):
-    parts = array.reshape((count, array.shape[0] // count) + array.shape[1:])
-    parts = lax.all_to_all(parts, GROUP, split_axis=0, concat_axis=0, tiled=True)
-    return jnp.sum(parts.astype(F32), axis=0)
+def share_kernel(n1, n2, rank, states, *refs):
+    one, two = refs[:n1], refs[n1 : n1 + n2]
+    keep_o, send_o, outg_o, select_o, step_o, taps_o, cbias_o, sbias_o, skip_o, decay_o, square_s = refs[n1 + n2 :]
+    er = outg_o.shape[0]
+    dr = keep_o.shape[0]
+
+    def total(parts):
+        acc = parts[0][...].astype(F32)
+        for part in parts[1:]:
+            acc = acc + part[...].astype(F32)
+        return acc
+
+    x = total(one)
+    inner = x.shape[1] - 2 * LANES
+    z = total(two)
+    for out, at in ((keep_o, 0), (send_o, dr)):
+        out[:, :inner] = x[at : at + dr, :inner]
+        out[:, inner : 2 * inner] = z[at : at + dr, :inner]
+        out[:, 2 * inner :] = x[at : at + dr, inner + LANES :]
+    outg_o[...] = z[:, inner:]
+    select_o[...] = x[:, inner : inner + select_o.shape[1]]
+    square_s[...] = jnp.zeros_like(square_s)
+    square_s[:er] = x[:, inner : inner + LANES]
+    step_o[...] = jnp.transpose(square_s[...])[LANES - rank :, :er]
+    square_s[:er] = x[:, inner + LANES :]
+    table = jnp.transpose(square_s[...])[:, :er]
+    taps_o[...] = table[0:4]
+    cbias_o[...] = table[ROW_BIAS : ROW_BIAS + 1]
+    sbias_o[...] = table[ROW_STEP : ROW_STEP + 1]
+    skip_o[...] = table[ROW_SKIP : ROW_SKIP + 1]
+    decay_o[...] = table[ROW_DECAY : ROW_DECAY + states]
+
+
+def spread_kernel(span, idx, keep, got, in_o, norm_o, moe_o, router_o, square_s):
+    dr = keep.shape[0]
+    inner2 = keep.shape[1] - LANES
+    first = idx[3] == 0
+    for k in range(inner2 // span):
+        mine = keep[:, k * span : (k + 1) * span]
+        peer = got[:, k * span : (k + 1) * span]
+        in_o[:, 2 * k * span : (2 * k + 1) * span] = jnp.where(first, mine, peer)
+        in_o[:, (2 * k + 1) * span : (2 * k + 2) * span] = jnp.where(first, peer, mine)
+    table = keep[:, inner2:] + got[:, inner2:]
+    at = ROW_FEATURE
+    router_o[...] = table[:, at + 2 : at + 2 + router_o.shape[1]]
+    square_s[...] = jnp.zeros_like(square_s)
+    square_s[:dr] = table
+    flat = jnp.transpose(square_s[...])[:, :dr]
+    norm_o[...] = flat[at : at + 1]
+    moe_o[...] = flat[at + 1 : at + 2]
 
 
 def body(
@@ -525,64 +760,68 @@
     capacity = 5 * tok // (4 * experts)
     dr = norm_gain.shape[0]
     inner = ng * er
-    core = lax.axis_index("c")
     rows = 2 * tok
     small_n = -(-(ROW_DECAY + states) // 8) * 8
     dn = -(-(2 + experts) // 8) * 8
-
-    nat = np.arange(width).reshape(ny, 2, nf, dr).transpose(0, 2, 1, 3).reshape(1, width)
+    plan = Plan(ny, nz, nx, er)
+    idx = jnp.stack([lax.axis_index(a) for a in ("y", "z", "x", "c")]).astype(jnp.int32)
+
+    order = np.arange(width).reshape(ny, 2, nf, dr).transpose(0, 2, 1, 3)
+    nat = np.stack([order.reshape(width), order[:, :, ::-1].reshape(width)])
     nat = jnp.asarray(nat, jnp.int32)
 
-    tok_peer = swap(tokens, "c")
+    span = nf * er
+    mine_w, send_w, ch = call(
+        functools.partial(pack_kernel, span),
+        [((dr, 2 * inner + LANES), BF16), ((dr, 2 * inner + LANES), BF16), ((er, 2 * LANES), BF16)],
+        [idx, input_proj, norm_gain[None], moe_gain[None], router_weight, conv_weight, conv_bias[None], select_proj, step_proj, step_bias[None], decay_log, skip_gain[None]],
+        [SMEM] + [None] * 11,
+        scratch=[pltpu.VMEM((LANES, LANES), F32), pltpu.VMEM((LANES, LANES), F32)],
+        name="pack",
+        us=1,
+    )
+    got_w = swap(send_w, "c")
+    group1, group2 = call(
+        merge_kernel,
+        [((er, inner + 2 * LANES), BF16), ((er, inner + width), BF16)],
+        [mine_w, got_w, ch, output_proj],
+        name="merge",
+        us=1,
+    )
+    tok2 = jnp.concatenate([tokens, swap(tokens, "c")], axis=0)
     lens2 = jnp.concatenate([seq_lens, swap(seq_lens, "c")], axis=0)
-    tok2 = jnp.concatenate([tokens, tok_peer], axis=0)
-
-    cols = input_proj.reshape(dr, 2, ny, 2, nf * er)
-    mine_w = lax.dynamic_index_in_dim(cols, core, 3, keepdims=False).reshape(dr, 2 * inner)
-    other_w = lax.dynamic_index_in_dim(cols, 1 - core, 3, keepdims=False).reshape(dr, 2 * inner)
-    dsmall = jnp.concatenate([norm_gain[:, None], moe_gain[:, None], router_weight], axis=1)
-    dsmall = jnp.pad(dsmall, ((0, 0), (0, LANES - dsmall.shape[1])))
-    got = swap(jnp.concatenate([other_w, dsmall], axis=1), "c")
-    mine_a = jnp.concatenate([mine_w, dsmall], axis=1)
-    first = jnp.where(core == 0, mine_a, got)
-    second = jnp.where(core == 0, got, mine_a)
-    pack_a = jnp.concatenate([first, second], axis=0)
-    small = jnp.concatenate(
-        [
-            conv_weight.T,
-            conv_bias[:, None],
-            step_bias[:, None],
-            skip_gain[:, None],
-            jnp.zeros((er, 1), BF16),
-            decay_log.T,
-        ],
-        axis=1,
-    )
-    small = jnp.pad(small, ((0, 0), (0, LANES - small.shape[1])))
-    gap = jnp.zeros((er, LANES - rank - select_proj.shape[1]), BF16)
-    pack_b = jnp.concatenate([select_proj, gap, step_proj.T, small], axis=1)
-    group1 = jnp.concatenate([pack_a[:, :inner], pack_a[:, 2 * inner :], pack_b], axis=1)
-    group2 = jnp.concatenate([pack_a[:, inner : 2 * inner], output_proj], axis=1)
-    g1 = gather_group(group1, ng)
-    g2 = gather_group(group2, ng)
-
-    u, xin, xc, selp, small_t, dnat = call(
-        enter_kernel,
-        [((rows, width), BF16), ((rows, inner), F32), ((rows, inner), BF16), ((rows, LANES), F32), ((small_n, inner), F32), ((dn, width), F32)],
-        [lens2, tok2, nat, g1],
-        [SMEM, None, None, None],
+    pieces1 = plan.gather(group1)
+    pieces2 = plan.gather(group2)
+
+    fetch_sem = pltpu.SemaphoreType.DMA((ng,))
+    emit_sem = pltpu.SemaphoreType.DMA((2 * ng,))
+    u, xin, xc, selp, small_t, dnat, g1 = call(
+        functools.partial(enter_kernel, plan),
+        [((rows, width), BF16), ((rows, inner), F32), ((rows, inner), BF16), ((rows, LANES), F32), ((small_n, inner), F32), ((dn, width), F32), ((inner, inner + 2 * LANES), BF16)],
+        [idx, lens2, tok2, nat] + pieces1,
+        [SMEM, SMEM, None, None] + [HBM] * len(pieces1),
+        scratch=[fetch_sem],
         name="enter",
     )
     selq = swap(selp, "c")
-    g1sel_spec = pl.BlockSpec((inner, LANES), lambda i: (0, inner // LANES + 1))
+    g1sel_spec = pl.BlockSpec((inner, LANES), lambda i: (0, inner // LANES))
     chunks = tok // 8
-    gated, ys, zg, step_pre, sel, keep, br_mine, br_send, check = call(
+    ys, step_pre, sel, keep, check = call(
         functools.partial(scan_kernel, rank, states),
-        [((rows, inner), BF16), ((rows, inner), F32), ((rows, inner), F32), ((rows, inner), F32), ((rows, LANES), F32), ((rows, LANES), F32), ((tok, width), F32), ((tok, width), F32), ((2 * chunks, states, inner), F32)],
-        [lens2, selp, selq, u, xc, g1, g2, small_t],
-        [SMEM, None, None, None, None, g1sel_spec, None, None],
+        [((rows, inner), F32), ((rows, inner), F32), ((rows, LANES), F32), ((rows, LANES), F32), ((2 * chunks, states, inner), F32)],
+        [lens2, selp, selq, xc, g1, small_t],
+        [SMEM, None, None, None, g1sel_spec, None],
         scratch=[pltpu.VMEM((rows, inner), F32), pltpu.VMEM((rows, inner), F32), pltpu.VMEM((2, states, tok), F32), pltpu.VMEM((2, states, tok), F32), pltpu.VMEM((states, inner), F32), pltpu.VMEM((2, states, inner), F32)],
         name="scan",
+        us=9,
+    )
+    gated, zg, br_mine, br_send, g2 = call(
+        functools.partial(gate_kernel, plan),
+        [((rows, inner), BF16), ((rows, inner), F32), ((tok, width), F32), ((tok, width), F32), ((inner, inner + width), BF16)],
+        [idx, u, xc, ys, small_t] + pieces2,
+        [SMEM] + [None] * 4 + [HBM] * len(pieces2),
+        scratch=[fetch_sem],
+        name="gate",
     )
     br_got = swap(br_send, "c")
     disp, hidden, gate = call(
@@ -621,60 +860,74 @@
         name="moe_leave",
     )
     gbr_got = swap(gbr, "c")
-    gsel, gxcs, gzg, gsr, q, smallg, outg = call(
+    gy, gzg, *shared2 = call(
+        functools.partial(gate_back_kernel, plan),
+        [((rows, inner), F32), ((rows, inner), BF16)] + plan.shared_outs(inner + width),
+        [idx, gbr, gbr_got, g2, gated, xc, ys, zg, small_t, u],
+        [SMEM] + [None] * 9,
+        scratch=[pltpu.VMEM((inner, inner + width), BF16), emit_sem],
+        name="gate_back",
+    )
+    gsel, gxcs, gsr, q, smallg = call(
         functools.partial(scan_back_kernel, rank, states),
-        [((rows, LANES), F32), ((rows, inner), F32), ((rows, inner), BF16), ((rows, inner), BF16), ((rows, LANES), BF16), ((small_n, inner), F32), ((inner, width), BF16)],
-        [gbr, gbr_got, g2, gated, xc, ys, zg, step_pre, sel, keep, small_t, g1, check],
-        [None] * 11 + [g1sel_spec, None],
-        scratch=[pltpu.VMEM((rows, inner), F32)] * 5 + [pltpu.VMEM((2, states, tok), F32)] * 4 + [pltpu.VMEM((states, inner), F32), pltpu.VMEM((2, states, inner), F32), pltpu.VMEM((states, inner), F32)],
+        [((rows, LANES), F32), ((rows, inner), F32), ((rows, inner), BF16), ((rows, LANES), BF16), ((small_n, inner), F32)],
+        [gy, xc, step_pre, sel, keep, small_t, g1, check],
+        [None] * 6 + [g1sel_spec, None],
+        scratch=[pltpu.VMEM((rows, inner), F32)] * 4 + [pltpu.VMEM((2, states, tok), F32)] * 4 + [pltpu.VMEM((states, inner), F32), pltpu.VMEM((2, states, inner), F32), pltpu.VMEM((states, inner), F32)],
         name="scan_back",
-    )
+        us=16,
+    )
+    parts2 = plan.reduce(shared2, "two")
     gsel_got = swap(gsel, "c")
     g2z_spec = pl.BlockSpec((inner, inner), lambda i: (0, 0))
-    gn_mine, gn_send, gx, gz, gsmall = call(
-        leave_kernel,
-        [((tok, width), F32), ((tok, width), F32), ((width, inner), BF16), ((width, inner), BF16), ((inner, 3 * LANES), BF16)],
-        [lens2, nat, gsel, gsel_got, gxcs, gzg, gsr, q, smallg, xin, xc, u, small_t, g1, g2, tok2, dnat, dgrad],
-        [SMEM] + [None] * 13 + [g2z_spec, None, None, None],
+    gn_mine, gn_send, *shared1 = call(
+        functools.partial(leave_kernel, plan),
+        [((tok, width), F32), ((tok, width), F32)] + plan.shared_outs(inner + 2 * LANES),
+        [idx, lens2, nat, gsel, gsel_got, gxcs, gzg, gsr, q, smallg, xin, xc, u, small_t, g1, g2, tok2, dnat, dgrad],
+        [SMEM, SMEM] + [None] * 13 + [g2z_spec, None, None, None],
+        scratch=[pltpu.VMEM((inner, inner + 2 * LANES), BF16), emit_sem],
         name="leave",
-    )
+        us=9,
+    )
+    parts1 = plan.reduce(shared1, "one")
     gn_got = swap(gn_send, "c")
     (input_grad,) = call(
-        final_kernel, [((tok, width), F32)], [tokens, gn_mine, gn_got, ghid, dnat], name="final"
-    )
-    packed = jnp.concatenate([gx, gz, gsmall, outg], axis=1)
-    share = reduce_group(packed, ng)
-    wide = jnp.concatenate([share[:, : 2 * inner], share[:, 2 * inner : 2 * inner + LANES]], axis=1)
-    keep_rows = lax.dynamic_slice_in_dim(wide, core * dr, dr, 0)
-    send_rows = lax.dynamic_slice_in_dim(wide, (1 - core) * dr, dr, 0)
-    got_rows = swap(send_rows, "c")
-    own_cols = keep_rows[:, : 2 * inner].reshape(dr, 2, ny, 1, nf * er)
-    got_cols = got_rows[:, : 2 * inner].reshape(dr, 2, ny, 1, nf * er)
-    lo = jnp.where(core == 0, own_cols, got_cols)
-    hi = jnp.where(core == 0, got_cols, own_cols)
-    in_grad = jnp.concatenate([lo, hi], axis=3).reshape(dr, 4 * inner)
-    dsum = keep_rows[:, 2 * inner :] + got_rows[:, 2 * inner :]
-    at = 2 * inner + LANES
+        final_kernel, [((tok, width), F32)], [tokens, gn_mine, gn_got, ghid, dnat], name="final", us=2
+    )
     sel_n = select_proj.shape[1]
-    select_grad = share[:, at : at + sel_n]
-    step_grad = share[:, at + LANES - rank : at + LANES].T
-    ch = share[:, at + LANES : at + 2 * LANES]
-    out_grad = share[:, at + 2 * LANES :]
+    keep_w, send_back, out_grad, select_grad, step_grad, taps_grad, cb, sb, sk, decay_grad = call(
+        functools.partial(share_kernel, len(parts1), len(parts2), rank, states),
+        [((dr, 2 * inner + LANES), F32)] * 2
+        + [((er, width), F32), ((er, sel_n), F32), ((rank, er), F32), ((4, er), F32), ((1, er), F32), ((1, er), F32), ((1, er), F32), ((states, er), F32)],
+        list(parts1) + list(parts2),
+        scratch=[pltpu.VMEM((LANES, LANES), F32)],
+        name="share",
+        us=1,
+    )
+    in_grad, norm_grad, moe_grad, router_grad = call(
+        functools.partial(spread_kernel, span),
+        [((dr, 4 * inner), F32), ((1, dr), F32), ((1, dr), F32), ((dr, experts), F32)],
+        [idx, keep_w, swap(send_back, "c")],
+        [SMEM, None, None],
+        scratch=[pltpu.VMEM((LANES, LANES), F32)],
+        name="spread",
+        us=1,
+    )
     return (
         result,
         input_grad,
-        dsum[:, 0],
+        norm_grad[0],
         in_grad,
-        ch[:, 0:4].T,
-        ch[:, ROW_BIAS],
+        taps_grad,
+        cb[0],
         select_grad,
         step_grad,
-        ch[:, ROW_STEP],
-        ch[:, ROW_DECAY : ROW_DECAY + states].T,
-        ch[:, ROW_SKIP],
+        sb[0],
+        decay_grad,
+        sk[0],
         out_grad,
-        dsum[:, 1],
-        dsum[:, 2 : 2 + experts],
+        moe_grad[0],
+        router_grad,
         up_grad,
         down_grad,
     )

time: 374 us -> 281 us (0.75)
  waiting for transfers between devices: 207 us -> 82.3 us
  Pallas kernels: 65.6 us -> 92.7 us
  starting transfers between devices: 22.4 us -> 42.9 us
  other arithmetic: 9.82 us -> 3.06 us
  local copies, waits for them, and re-layouts: 23.7 us -> 17 us
    all_to_all x3 -> x0, waiting for transfers between devices: 172 us -> none  [the longest x1 86.6 us: reduce_group(): lax.all_to_all(parts, GROUP, split_axis=0, concat_axis=0, tiled=True)]
    pallas_call x8 -> x18, Pallas kernels: 65.6 us -> 92.7 us  [call(): pl.pallas_call(kernel, grid=(1,) if windowed else (), out_shape=[jax.Shap...]
    ppermute x13 -> x29, waiting for transfers between devices: 34.9 us -> 60.4 us  [swap(): return lax.ppermute(values, axis, [(0, 1), (1, 0)])]
    ppermute x0 -> x12, starting transfers between devices: none -> 22 us  [the longest x6 15 us: gather(): lax.ppermute(piece, 'z', [(i, (i + k) % 4) for i in range(4)])]
    ppermute x0 -> x12, waiting for transfers between devices: none -> 21.9 us  [the longest x6 12.4 us: reduce(): lax.ppermute(parts[k], 'z', [(i, (i - k) % 4) for i in range(4)])]
    all_to_all x3 -> x0, starting transfers between devices: 17.3 us -> none  [the longest x2 12.7 us: gather_group(): many = lax.all_to_all(many, GROUP, split_axis=0, concat_axis=0, tiled=True)]
    ppermute x13 -> x29, starting transfers between devices: 5.07 us -> 21 us  [swap(): return lax.ppermute(values, axis, [(0, 1), (1, 0)])]
    unnamed x41 -> x97, local copies, waits for them, and re-layouts: 10.7 us -> 16.6 us
  transfers between devices with their start and end apart: 16 -> 41, of which waited for: 13 -> 22; matrix products, arithmetic and copies ran while one was open for 3% -> 2% of each run, Pallas kernels for 2% -> 14%
where the time goes in v2:
time: 281 us; the launch traced here: 280 us
  Pallas kernels  92.7 us (33%)
  waiting for transfers between devices  82.3 us (29%)
  starting transfers between devices  42.9 us (15%)
  blocking collectives  40.9 us (15%)
  local copies, waits for them, and re-layouts  17 us (6%)
  other arithmetic  3.06 us (1%)
    pallas_call x18, Pallas kernels, call(): pl.pallas_call(kernel, grid=(1,) if windowed else (), out_shape=[jax.Shap...  92.7 us
    ppermute x29, waiting for transfers between devices, swap(): return lax.ppermute(values, axis, [(0, 1), (1, 0)])  60.4 us
    ppermute x29, starting transfers between devices, swap(): return lax.ppermute(values, axis, [(0, 1), (1, 0)])  21 us
    all_to_all x1, blocking collectives, body(): lax.all_to_all(disp, ('z', 'x'), split_axis=0, concat_axis=0, tiled=True)  20.8 us
    all_to_all x1, blocking collectives, body(): lax.all_to_all(summed.astype(BF16).reshape(nf, capacity, 2 * width), ('z'...  20.1 us
    unnamed x97, local copies, waits for them, and re-layouts  16.6 us
    ppermute x6, starting transfers between devices, gather(): lax.ppermute(piece, 'z', [(i, (i + k) % 4) for i in range(4)])  15 us
    ppermute x6, waiting for transfers between devices, reduce(): lax.ppermute(parts[k], 'z', [(i, (i - k) % 4) for i in range(4)])  12.4 us
  transfers between devices with their start and end apart: 41, of which 22 were waited for; matrix products, arithmetic and copies ran while one was open for 2% of the time, Pallas kernels for 14%

profile of v2, /device:TPU:0, one launch (start us, length us, event | category | flops | bytes accessed | tf_op | source)
XLA Modules:
  0.0 280.1 jit_solution(5465736809751342684)
XLA Ops:
  8.7 4.8 %collective-permute-start.5 = (bf16[48,1024]{1,0:T(8,128)(2,1)}, bf16[48,1024]{1,0:T(8,128)(2,1)S(1)}, u32[]{:S(2)}, u32[]{:S(2)}) collective-permute-start(bf16[48,1024]{1,0:T(8,128)(2,1)} %get-tuple-element.99), channel_id=1, source_target_pairs={{0,6},{2,0},{4,2},{6,4},{1,7},{3,1},{5,3},{7,5},{8,14},{10,8},{12,... | collective-permute-start | bytes 294920 | tf_op jit(solution)/shard_map/ppermute | solution.py:124
  14.5 2.8 %collective-permute-start.13 = (bf16[48,1536]{1,0:T(8,128)(2,1)}, bf16[48,1536]{1,0:T(8,128)(2,1)S(1)}, u32[]{:S(2)}, u32[]{:S(2)}) collective-permute-start(bf16[48,1536]{1,0:T(8,128)(2,1)} %get-tuple-element.106), channel_id=1, source_target_pairs={{0,6},{2,0},{4,2},{6,4},{1,7},{3,1},{5,3},{7,5},{8,14},{10,8},{12,... | collective-permute-start | bytes 442376 | tf_op jit(solution)/shard_map/ppermute | solution.py:124
  19.2 2.9 %collective-permute-done.3 = bf16[48,1024]{1,0:T(8,128)(2,1)S(1)} collective-permute-done((bf16[48,1024]{1,0:T(8,128)(2,1)}, bf16[48,1024]{1,0:T(8,128)(2,1)S(1)}, u32[]{:S(2)}, u32[]{:S(2)}) %collective-permute-start.3) | collective-permute-done | bytes 98336 | tf_op jit(solution)/shard_map/ppermute | solution.py:124
  22.1 6.4 %collective-permute-start.12 = (bf16[48,1536]{1,0:T(8,128)(2,1)}, bf16[48,1536]{1,0:T(8,128)(2,1)S(1)}, u32[]{:S(2)}, u32[]{:S(2)}) collective-permute-start(bf16[48,1536]{1,0:T(8,128)(2,1)} %get-tuple-element.106), channel_id=1, source_target_pairs={{0,4},{2,6},{4,0},{6,2},{1,5},{3,7},{5,1},{7,3},{8,12},{10,14},{12... | collective-permute-start | bytes 442376 | tf_op jit(solution)/shard_map/ppermute | solution.py:124
  31.7 4.0 %collective-permute-done.11 = bf16[48,1536]{1,0:T(8,128)(2,1)S(1)} collective-permute-done((bf16[48,1536]{1,0:T(8,128)(2,1)}, bf16[48,1536]{1,0:T(8,128)(2,1)S(1)}, u32[]{:S(2)}, u32[]{:S(2)}) %collective-permute-start.11) | collective-permute-done | bytes 147488 | tf_op jit(solution)/shard_map/ppermute | solution.py:124
  35.7 2.5 collective-permute-done.12
  43.6 2.8 collective-permute-done.9.refs_4_
  48.9 5.3 %enter.1 = (bf16[256,768]{1,0:T(8,128)(2,1)}, f32[256,768]{1,0:T(8,128)}, bf16[256,768]{1,0:T(8,128)(2,1)}, f32[256,128]{1,0:T(8,128)}, f32[24,768]{1,0:T(8,128)...) custom-call(s32[4]{0:T(128)} %pad_add_fusion.1.idx, s32[2,8]{1,0:T(2,128)} %pad_add_fusion.lens, ...), custom_call_target="tpu_custom_call" | custom-call | flops 5000000000 | bytes 15000000 | tf_op jit(solution)/shard_map/enter/pallas_call | solution.py:86
  54.2 4.8 %collective-permute-done.15.refs_2_ = bf16[192,1536]{1,0:T(8,128)(2,1)S(1)} collective-permute-done((bf16[192,1536]{1,0:T(8,128)(2,1)S(1)}, bf16[192,1536]{1,0:T(8,128)(2,1)S(1)}, u32[]{:S(2)}, u32[]{:S(2)}) %collective-permute-start.15) | collective-permute-done | bytes 589856 | tf_op jit(solution)/shard_map/ppermute | solution.py:677
  61.9 9.0 %scan.1 = (f32[256,768]{1,0:T(8,128)}, f32[256,768]{1,0:T(8,128)}, f32[256,128]{1,0:T(8,128)}, f32[256,128]{1,0:T(8,128)}, f32[32,16,768]{2,1,0:T(8,128)}) custom-call(s32[2,8]{1,0:T(2,128)} %pad_add_fusion.lens, f32[256,128]{1,0:T(8,128)} %get-tuple-element.102.sel_a, f32[256,128]{1,0:T(8,128)} %copy-done.37, bf16[256,768]{1,0:T(8,128)(2,1)} %get-tuple-element.101.xc, ...), custom_call_target="tpu_custom_call" | custom-call | flops 8999999488 | bytes 27000000 | tf_op jit(solution)/shard_map/scan/pallas_call | solution.py:86
  71.8 5.9 %gate.1 = (bf16[256,768]{1,0:T(8,128)(2,1)}, f32[256,768]{1,0:T(8,128)}, f32[128,768]{1,0:T(8,128)}, f32[128,768]{1,0:T(8,128)}, bf16[768,1536]{1,0:T(8,128)(2,1)}) custom-call(s32[4]{0:T(128)} %pad_add_fusion.1.idx, bf16[256,768]{1,0:T(8,128)(2,1)} %get-tuple-element.100.u, bf16[256,768]{1,0:T(8,128)(2,1)} %get-tuple-element.101.xc, ...), custom_call_target="tpu_custom_call" | custom-call | flops 5000000000 | bytes 15000000 | tf_op jit(solution)/shard_map/gate/pallas_call | solution.py:86
  80.4 3.4 %moe_enter.1 = (bf16[8,20,1536]{2,1,0:T(8,128)(2,1)}, f32[128,768]{1,0:T(8,128)}, f32[128,128]{1,0:T(8,128)}) custom-call(s32[1,8]{1,0:T(1,128)} %lens.3, bf16[128,768]{1,0:T(8,128)(2,1)} %tok.3, bf16[128,768]{1,0:T(8,128)(2,1)} %cot.3, s32[128,1]{1,0:T(8,128)} %copy.41.routes, f32[128,768]{1,0:T(8,128)} %get-tuple-element.107.mine, f32[128,768]{1,0:T(8,128)} %copy-done.20, ...), custom_call_target="tpu_custom_call" | custom-call | flops 5000000000 | bytes 15000000 | tf_op jit(solution)/shard_map/moe_enter/pallas_call | solution.py:86
  83.8 20.8 %all_to_all.10 = bf16[8,20,1536]{2,1,0:T(8,128)(2,1)S(1)} all-to-all(bf16[8,20,1536]{2,1,0:T(8,128)(2,1)} %get-tuple-element.112), channel_id=1, replica_groups=mesh['y'=2,'c'=2,'z'=4,'x'=2] {'z','x'}, dimensions={0} | all-to-all | bytes 983040 | tf_op jit(solution)/shard_map/all_to_all | solution.py:834
  105.3 11.2 %collective-permute-done.19 = bf16[160,1536]{1,0:T(8,128)(2,1)S(1)} collective-permute-done((bf16[160,1536]{1,0:T(8,128)(2,1)S(1)}, bf16[160,1536]{1,0:T(8,128)(2,1)S(1)}, u32[]{:S(2)}, u32[]{:S(2)}) %collective-permute-start.19) | collective-permute-done | bytes 491552 | tf_op jit(solution)/shard_map/ppermute | solution.py:677
  116.6 2.6 collective-permute-done.20.peer
  120.1 10.8 %expert.1 = (f32[320,1536]{1,0:T(8,128)}, bf16[320,1536]{1,0:T(8,128)(2,1)}, f32[1,768,768]{2,1,0:T(8,128)}, f32[1,768,768]{2,1,0:T(8,128)}) custom-call(bf16[320,1536]{1,0:T(8,128)(2,1)} %copy-done, bf16[320,1536]{1,0:T(8,128)(2,1)} %copy-done.11, bf16[1,768,768]{2,1,0:T(8,128)(2,1)} %up.1, bf16[1,768,768]{2,1,0:T(8,128)(2,1)} %down.1), custom_call_target="tpu_custom_call" | custom-call | flops 5000000000 | bytes 15000000 | tf_op jit(solution)/shard_map/expert/pallas_call | solution.py:86
  131.1 2.6 collective-permute-done.21
  136.1 12.8 %collective-permute-done.22 = bf16[160,1536]{1,0:T(8,128)(2,1)S(1)} collective-permute-done((bf16[160,1536]{1,0:T(8,128)(2,1)S(1)}, bf16[160,1536]{1,0:T(8,128)(2,1)S(1)}, u32[]{:S(2)}, u32[]{:S(2)}) %collective-permute-start.22) | collective-permute-done | bytes 491552 | tf_op jit(solution)/shard_map/ppermute | solution.py:677
  149.1 20.1 %all_to_all.11.back = bf16[8,20,1536]{2,1,0:T(8,128)(2,1)} all-to-all(bf16[8,20,1536]{2,1,0:T(8,128)(2,1)S(1)} %reshape.39), channel_id=1, replica_groups=mesh['y'=2,'c'=2,'z'=4,'x'=2] {'z','x'}, dimensions={0} | all-to-all | bytes 983040 | tf_op jit(solution)/shard_map/all_to_all | solution.py:852
  169.2 4.0 %moe_leave.1 = (bf16[128,768]{1,0:T(8,128)(2,1)}, f32[128,768]{1,0:T(8,128)}, bf16[128,768]{1,0:T(8,128)(2,1)}, f32[16,768]{1,0:T(8,128)}) custom-call(s32[1,8]{1,0:T(1,128)} %lens.3, s32[128,1]{1,0:T(8,128)} %copy.41.routes, bf16[128,768]{1,0:T(8,128)(2,1)} %cot.3, f32[128,768]{1,0:T(8,128)} %get-tuple-element.110.hidden, ...), custom_call_target="tpu_custom_call" | custom-call | flops 5000000000 | bytes 15000000 | tf_op jit(solution)/shard_map/moe_leave/pallas_call | solution.py:86
  175.6 6.7 %gate_back.1 = (f32[256,768]{1,0:T(8,128)}, bf16[256,768]{1,0:T(8,128)(2,1)}, bf16[384,768]{1,0:T(8,128)(2,1)}, bf16[384,768]{1,0:T(8,128)(2,1)}, bf16[384,768]{1,0:T(8,128)(2,1)}, /*index=5*/bf16[384,768]{1,0:T(8,128)(2,1)}) custom-call(s32[4]{0:T(128)} %pad_add_fusion.1.idx, bf16[128,768]{1,0:T(8,128)(2,1)} %get-tuple-element.116.gbr_a, ...), custom_call_target="tpu_custom_call" | custom-call | flops 5000000000 | bytes 15000000 | tf_op jit(solution)/shard_map/gate_back/pallas_call | solution.py:86
  182.4 18.1 %scan_back.1 = (f32[256,128]{1,0:T(8,128)}, f32[256,768]{1,0:T(8,128)}, bf16[256,768]{1,0:T(8,128)(2,1)}, bf16[256,128]{1,0:T(8,128)(2,1)}, f32[24,768]{1,0:T(8,128)}) custom-call(f32[256,768]{1,0:T(8,128)} %get-tuple-element.120.gy_s, bf16[256,768]{1,0:T(8,128)(2,1)} %get-tuple-element.101.xc, f32[256,768]{1,0:T(8,128)} %get-tuple-element.121.step_pre, ...), custom_call_target="tpu_custom_call" | custom-call | flops 16000000000 | bytes 48000000 | tf_op jit(solution)/shard_map/scan_back/pallas_call | solution.py:86
  202.7 10.7 %leave.1 = (f32[128,768]{1,0:T(8,128)}, f32[128,768]{1,0:T(8,128)}, bf16[384,512]{1,0:T(8,128)(2,1)}, bf16[384,512]{1,0:T(8,128)(2,1)}, bf16[384,512]{1,0:T(8,128)(2,1)}, /*index=5*/bf16[384,512]{1,0:T(8,128)(2,1)}) custom-call(s32[4]{0:T(128)} %pad_add_fusion.1.idx, s32[2,8]{1,0:T(2,128)} %pad_add_fusion.lens, s32[2,768]{1,0:T(2,128)} %constant.17.clone.nat, ...), custom_call_target="tpu_custom_call" | custom-call | flops 8999999488 | bytes 27000000 | tf_op jit(solution)/shard_map/leave/pallas_call | solution.py:86
  216.1 8.7 %collective-permute-done.26.a_in = bf16[384,512]{1,0:T(8,128)(2,1)S(1)} collective-permute-done((bf16[384,512]{1,0:T(8,128)(2,1)}, bf16[384,512]{1,0:T(8,128)(2,1)S(1)}, u32[]{:S(2)}, u32[]{:S(2)}) %collective-permute-start.26) | collective-permute-done | bytes 393248 | tf_op jit(solution)/shard_map/ppermute | solution.py:677
  226.2 2.3 add1_one.1
  229.5 2.8 add1_two.1
  236.3 8.2 %collective-permute-done.28.a_in = bf16[192,512]{1,0:T(8,128)(2,1)S(1)} collective-permute-done((bf16[192,512]{1,0:T(8,128)(2,1)S(1)}, bf16[192,512]{1,0:T(8,128)(2,1)S(1)}, u32[]{:S(2)}, u32[]{:S(2)}) %collective-permute-start.28) | collective-permute-done | bytes 196640 | tf_op jit(solution)/shard_map/ppermute | solution.py:677
  253.2 2.2 collective-permute-start.37
  260.0 6.9 %collective-permute-done.32.refs_3_ = bf16[48,1024]{1,0:T(8,128)(2,1)S(1)} collective-permute-done((bf16[48,1024]{1,0:T(8,128)(2,1)S(1)}, bf16[48,1024]{1,0:T(8,128)(2,1)S(1)}, u32[]{:S(2)}, u32[]{:S(2)}) %collective-permute-start.32) | collective-permute-done | bytes 98336 | tf_op jit(solution)/shard_map/ppermute | solution.py:202
  266.9 3.4 %collective-permute-done.38.refs_6_ = bf16[48,1536]{1,0:T(8,128)(2,1)S(1)} collective-permute-done((bf16[48,1536]{1,0:T(8,128)(2,1)}, bf16[48,1536]{1,0:T(8,128)(2,1)S(1)}, u32[]{:S(2)}, u32[]{:S(2)}) %collective-permute-start.38) | collective-permute-done | bytes 147488 | tf_op jit(solution)/shard_map/ppermute | solution.py:202
  271.0 2.1 share.1
  274.0 2.3 final.1
  (182 shorter events, 65.2 us)
Async XLA Ops:
  5.0 25.2 %collective-permute-start.1 = (bf16[128,768]{1,0:T(8,128)(2,1)S(1)}, bf16[128,768]{1,0:T(8,128)(2,1)S(1)}, u32[]{:S(2)}, u32[]{:S(2)}) collective-permute-start(bf16[128,768]{1,0:T(8,128)(2,1)S(1)} %copy-done.1), channel_id=1, source_target_pairs={{0,8},{8,0},{1,9},{9,1},{2,10},{10,2},{3,11},{11,3},{4,12},{12,4},... | collective-permute-start | bytes 589832 | tf_op jit(solution)/shard_map/ppermute | solution.py:677
  8.7 19.8 %collective-permute-start.5 = (bf16[48,1024]{1,0:T(8,128)(2,1)}, bf16[48,1024]{1,0:T(8,128)(2,1)S(1)}, u32[]{:S(2)}, u32[]{:S(2)}) collective-permute-start(bf16[48,1024]{1,0:T(8,128)(2,1)} %get-tuple-element.99), channel_id=1, source_target_pairs={{0,6},{2,0},{4,2},{6,4},{1,7},{3,1},{5,3},{7,5},{8,14},{10,8},{12,... | collective-permute-start | bytes 294920 | tf_op jit(solution)/shard_map/ppermute | solution.py:124
  13.5 15.0 %collective-permute-start.4 = (bf16[48,1024]{1,0:T(8,128)(2,1)}, bf16[48,1024]{1,0:T(8,128)(2,1)S(1)}, u32[]{:S(2)}, u32[]{:S(2)}) collective-permute-start(bf16[48,1024]{1,0:T(8,128)(2,1)} %get-tuple-element.99), channel_id=1, source_target_pairs={{0,4},{2,6},{4,0},{6,2},{1,5},{3,7},{5,1},{7,3},{8,12},{10,14},{12... | collective-permute-start | bytes 294920 | tf_op jit(solution)/shard_map/ppermute | solution.py:124
  13.5 8.6 %collective-permute-start.3 = (bf16[48,1024]{1,0:T(8,128)(2,1)}, bf16[48,1024]{1,0:T(8,128)(2,1)S(1)}, u32[]{:S(2)}, u32[]{:S(2)}) collective-permute-start(bf16[48,1024]{1,0:T(8,128)(2,1)} %get-tuple-element.99), channel_id=1, source_target_pairs={{0,2},{2,4},{4,6},{6,0},{1,3},{3,5},{5,7},{7,1},{8,10},{10,12},{12... | collective-permute-start | bytes 294920 | tf_op jit(solution)/shard_map/ppermute | solution.py:124
  14.5 27.3 %collective-permute-start.13 = (bf16[48,1536]{1,0:T(8,128)(2,1)}, bf16[48,1536]{1,0:T(8,128)(2,1)S(1)}, u32[]{:S(2)}, u32[]{:S(2)}) collective-permute-start(bf16[48,1536]{1,0:T(8,128)(2,1)} %get-tuple-element.106), channel_id=1, source_target_pairs={{0,6},{2,0},{4,2},{6,4},{1,7},{3,1},{5,3},{7,5},{8,14},{10,8},{12,... | collective-permute-start | bytes 442376 | tf_op jit(solution)/shard_map/ppermute | solution.py:124
  22.1 16.2 %collective-permute-start.12 = (bf16[48,1536]{1,0:T(8,128)(2,1)}, bf16[48,1536]{1,0:T(8,128)(2,1)S(1)}, u32[]{:S(2)}, u32[]{:S(2)}) collective-permute-start(bf16[48,1536]{1,0:T(8,128)(2,1)} %get-tuple-element.106), channel_id=1, source_target_pairs={{0,4},{2,6},{4,0},{6,2},{1,5},{3,7},{5,1},{7,3},{8,12},{10,14},{12... | collective-permute-start | bytes 442376 | tf_op jit(solution)/shard_map/ppermute | solution.py:124
  28.5 7.2 %collective-permute-start.11 = (bf16[48,1536]{1,0:T(8,128)(2,1)}, bf16[48,1536]{1,0:T(8,128)(2,1)S(1)}, u32[]{:S(2)}, u32[]{:S(2)}) collective-permute-start(bf16[48,1536]{1,0:T(8,128)(2,1)} %get-tuple-element.106), channel_id=1, source_target_pairs={{0,2},{2,4},{4,6},{6,0},{1,3},{3,5},{5,7},{7,1},{8,10},{10,12},{12... | collective-permute-start | bytes 442376 | tf_op jit(solution)/shard_map/ppermute | solution.py:124
  28.6 10.0 %collective-permute-start.7 = (bf16[192,1024]{1,0:T(8,128)(2,1)S(1)}, bf16[192,1024]{1,0:T(8,128)(2,1)S(1)}, u32[]{:S(2)}, u32[]{:S(2)}) collective-permute-start(bf16[192,1024]{1,0:T(8,128)(2,1)S(1)} %constant_dynamic-update-slice_fusion.2.refs_0_), channel_id=1, source_target_pairs={{0,16},{16,0},{1,17},{17,1},{2,18},{18,2},{3,19},{19,3},{4,20},{20... | collective-permute-start | bytes 1179656 | tf_op jit(solution)/shard_map/ppermute | solution.py:677
  30.2 10.0 %collective-permute-start.6 = (bf16[192,1024]{1,0:T(8,128)(2,1)S(1)}, bf16[192,1024]{1,0:T(8,128)(2,1)S(1)}, u32[]{:S(2)}, u32[]{:S(2)}) collective-permute-start(bf16[192,1024]{1,0:T(8,128)(2,1)S(1)} %constant_dynamic-update-slice_fusion.2.refs_0_), channel_id=1, source_target_pairs={{0,1},{1,0},{2,3},{3,2},{4,5},{5,4},{6,7},{7,6},{8,9},{9,8},{10,11... | collective-permute-start | bytes 1179656 | tf_op jit(solution)/shard_map/ppermute | solution.py:677
  38.7 7.7 %collective-permute-start.9 = (bf16[96,1024]{1,0:T(8,128)(2,1)S(1)}, bf16[96,1024]{1,0:T(8,128)(2,1)S(1)}, u32[]{:S(2)}, u32[]{:S(2)}) collective-permute-start(bf16[96,1024]{1,0:T(8,128)(2,1)S(1)} %slice.26), channel_id=1, source_target_pairs={{0,1},{1,0},{2,3},{3,2},{4,5},{5,4},{6,7},{7,6},{8,9},{9,8},{10,11... | collective-permute-start | bytes 589832 | tf_op jit(solution)/shard_map/ppermute | solution.py:677
  40.3 7.9 %collective-permute-start.8 = (bf16[96,1024]{1,0:T(8,128)(2,1)S(1)}, bf16[96,1024]{1,0:T(8,128)(2,1)S(1)}, u32[]{:S(2)}, u32[]{:S(2)}) collective-permute-start(bf16[96,1024]{1,0:T(8,128)(2,1)S(1)} %slice.25), channel_id=1, source_target_pairs={{0,16},{16,0},{1,17},{17,1},{2,18},{18,2},{3,19},{19,3},{4,20},{20... | collective-permute-start | bytes 589832 | tf_op jit(solution)/shard_map/ppermute | solution.py:677
  41.9 17.1 %collective-permute-start.15 = (bf16[192,1536]{1,0:T(8,128)(2,1)S(1)}, bf16[192,1536]{1,0:T(8,128)(2,1)S(1)}, u32[]{:S(2)}, u32[]{:S(2)}) collective-permute-start(bf16[192,1536]{1,0:T(8,128)(2,1)S(1)} %constant_dynamic-update-slice_fusion.6.refs_0_), channel_id=1, source_target_pairs={{0,16},{16,0},{1,17},{17,1},{2,18},{18,2},{3,19},{19,3},{4,20},{20... | collective-permute-start | bytes 1769480 | tf_op jit(solution)/shard_map/ppermute | solution.py:677
  42.4 17.2 %collective-permute-start.14 = (bf16[192,1536]{1,0:T(8,128)(2,1)S(1)}, bf16[192,1536]{1,0:T(8,128)(2,1)S(1)}, u32[]{:S(2)}, u32[]{:S(2)}) collective-permute-start(bf16[192,1536]{1,0:T(8,128)(2,1)S(1)} %constant_dynamic-update-slice_fusion.6.refs_0_), channel_id=1, source_target_pairs={{0,1},{1,0},{2,3},{3,2},{4,5},{5,4},{6,7},{7,6},{8,9},{9,8},{10,11... | collective-permute-start | bytes 1769480 | tf_op jit(solution)/shard_map/ppermute | solution.py:677
  59.0 11.9 %collective-permute-start.17 = (bf16[96,1536]{1,0:T(8,128)(2,1)S(1)}, bf16[96,1536]{1,0:T(8,128)(2,1)S(1)}, u32[]{:S(2)}, u32[]{:S(2)}) collective-permute-start(bf16[96,1536]{1,0:T(8,128)(2,1)S(1)} %slice.28), channel_id=1, source_target_pairs={{0,1},{1,0},{2,3},{3,2},{4,5},{5,4},{6,7},{7,6},{8,9},{9,8},{10,11... | collective-permute-start | bytes 884744 | tf_op jit(solution)/shard_map/ppermute | solution.py:677
  59.7 11.3 %collective-permute-start.16 = (bf16[96,1536]{1,0:T(8,128)(2,1)S(1)}, bf16[96,1536]{1,0:T(8,128)(2,1)S(1)}, u32[]{:S(2)}, u32[]{:S(2)}) collective-permute-start(bf16[96,1536]{1,0:T(8,128)(2,1)S(1)} %slice.27), channel_id=1, source_target_pairs={{0,16},{16,0},{1,17},{17,1},{2,18},{18,2},{3,19},{19,3},{4,20},{20... | collective-permute-start | bytes 884744 | tf_op jit(solution)/shard_map/ppermute | solution.py:677
  104.7 11.8 %collective-permute-start.19 = (bf16[160,1536]{1,0:T(8,128)(2,1)S(1)}, bf16[160,1536]{1,0:T(8,128)(2,1)S(1)}, u32[]{:S(2)}, u32[]{:S(2)}) collective-permute-start(bf16[160,1536]{1,0:T(8,128)(2,1)S(1)} %reshape.38), channel_id=1, source_target_pairs={{0,16},{16,0},{1,17},{17,1},{2,18},{18,2},{3,19},{19,3},{4,20},{20... | collective-permute-start | bytes 1474568 | tf_op jit(solution)/shard_map/ppermute | solution.py:677
  135.6 13.3 %collective-permute-start.22 = (bf16[160,1536]{1,0:T(8,128)(2,1)S(1)}, bf16[160,1536]{1,0:T(8,128)(2,1)S(1)}, u32[]{:S(2)}, u32[]{:S(2)}) collective-permute-start(bf16[160,1536]{1,0:T(8,128)(2,1)S(1)} %slice.35), channel_id=1, source_target_pairs={{0,16},{16,0},{1,17},{17,1},{2,18},{18,2},{3,19},{19,3},{4,20},{20... | collective-permute-start | bytes 1474568 | tf_op jit(solution)/shard_map/ppermute | solution.py:677
  200.6 27.9 %collective-permute-start.33 = (bf16[384,768]{1,0:T(8,128)(2,1)S(1)}, bf16[384,768]{1,0:T(8,128)(2,1)S(1)}, u32[]{:S(2)}, u32[]{:S(2)}) collective-permute-start(bf16[384,768]{1,0:T(8,128)(2,1)S(1)} %copy-done.13), channel_id=1, source_target_pairs={{0,1},{1,0},{2,3},{3,2},{4,5},{5,4},{6,7},{7,6},{8,9},{9,8},{10,11... | collective-permute-start | bytes 1769480 | tf_op jit(solution)/shard_map/ppermute | solution.py:677
  201.4 27.0 %collective-permute-start.34 = (bf16[384,768]{1,0:T(8,128)(2,1)S(1)}, bf16[384,768]{1,0:T(8,128)(2,1)S(1)}, u32[]{:S(2)}, u32[]{:S(2)}) collective-permute-start(bf16[384,768]{1,0:T(8,128)(2,1)S(1)} %copy-done.12), channel_id=1, source_target_pairs={{0,16},{16,0},{1,17},{17,1},{2,18},{18,2},{3,19},{19,3},{4,20},{20... | collective-permute-start | bytes 1769480 | tf_op jit(solution)/shard_map/ppermute | solution.py:677
  213.4 11.4 %collective-permute-start.26 = (bf16[384,512]{1,0:T(8,128)(2,1)}, bf16[384,512]{1,0:T(8,128)(2,1)S(1)}, u32[]{:S(2)}, u32[]{:S(2)}) collective-permute-start(bf16[384,512]{1,0:T(8,128)(2,1)} %get-tuple-element.137), channel_id=1, source_target_pairs={{0,1},{1,0},{2,3},{3,2},{4,5},{5,4},{6,7},{7,6},{8,9},{9,8},{10,11... | collective-permute-start | bytes 1179656 | tf_op jit(solution)/shard_map/ppermute | solution.py:677
  214.6 10.8 %collective-permute-start.27 = (bf16[384,512]{1,0:T(8,128)(2,1)}, bf16[384,512]{1,0:T(8,128)(2,1)S(1)}, u32[]{:S(2)}, u32[]{:S(2)}) collective-permute-start(bf16[384,512]{1,0:T(8,128)(2,1)} %get-tuple-element.139), channel_id=1, source_target_pairs={{0,16},{16,0},{1,17},{17,1},{2,18},{18,2},{3,19},{19,3},{4,20},{20... | collective-permute-start | bytes 1179656 | tf_op jit(solution)/shard_map/ppermute | solution.py:677
  232.3 18.0 %collective-permute-start.35 = (bf16[192,768]{1,0:T(8,128)(2,1)}, bf16[192,768]{1,0:T(8,128)(2,1)S(1)}, u32[]{:S(2)}, u32[]{:S(2)}) collective-permute-start(bf16[192,768]{1,0:T(8,128)(2,1)} %get-tuple-element.153), channel_id=1, source_target_pairs={{0,16},{16,0},{1,17},{17,1},{2,18},{18,2},{3,19},{19,3},{4,20},{20... | collective-permute-start | bytes 884744 | tf_op jit(solution)/shard_map/ppermute | solution.py:677
  233.7 16.6 %collective-permute-start.36 = (bf16[192,768]{1,0:T(8,128)(2,1)}, bf16[192,768]{1,0:T(8,128)(2,1)S(1)}, u32[]{:S(2)}, u32[]{:S(2)}) collective-permute-start(bf16[192,768]{1,0:T(8,128)(2,1)} %get-tuple-element.155), channel_id=1, source_target_pairs={{0,1},{1,0},{2,3},{3,2},{4,5},{5,4},{6,7},{7,6},{8,9},{9,8},{10,11... | collective-permute-start | bytes 884744 | tf_op jit(solution)/shard_map/ppermute | solution.py:677
  234.6 9.9 %collective-permute-start.28 = (bf16[192,512]{1,0:T(8,128)(2,1)S(1)}, bf16[192,512]{1,0:T(8,128)(2,1)S(1)}, u32[]{:S(2)}, u32[]{:S(2)}) collective-permute-start(bf16[192,512]{1,0:T(8,128)(2,1)S(1)} %copy-done.26), channel_id=1, source_target_pairs={{0,16},{16,0},{1,17},{17,1},{2,18},{18,2},{3,19},{19,3},{4,20},{20... | collective-permute-start | bytes 589832 | tf_op jit(solution)/shard_map/ppermute | solution.py:677
  235.5 9.9 %collective-permute-start.29 = (bf16[192,512]{1,0:T(8,128)(2,1)S(1)}, bf16[192,512]{1,0:T(8,128)(2,1)S(1)}, u32[]{:S(2)}, u32[]{:S(2)}) collective-permute-start(bf16[192,512]{1,0:T(8,128)(2,1)S(1)} %copy-done.25), channel_id=1, source_target_pairs={{0,1},{1,0},{2,3},{3,2},{4,5},{5,4},{6,7},{7,6},{8,9},{9,8},{10,11... | collective-permute-start | bytes 589832 | tf_op jit(solution)/shard_map/ppermute | solution.py:677
  236.3 36.9 %collective-permute-start.25 = (f32[128,768]{1,0:T(8,128)S(1)}, f32[128,768]{1,0:T(8,128)S(1)}, u32[]{:S(2)}, u32[]{:S(2)}) collective-permute-start(f32[128,768]{1,0:T(8,128)S(1)} %copy-done.16), channel_id=1, source_target_pairs={{0,8},{8,0},{1,9},{9,1},{2,10},{10,2},{3,11},{11,3},{4,12},{12,4},... | collective-permute-start | bytes 1179656 | tf_op jit(solution)/shard_map/ppermute | solution.py:677
  248.1 7.3 %collective-permute-start.30 = (bf16[48,1024]{1,0:T(8,128)(2,1)}, bf16[48,1024]{1,0:T(8,128)(2,1)S(1)}, u32[]{:S(2)}, u32[]{:S(2)}) collective-permute-start(bf16[48,1024]{1,0:T(8,128)(2,1)} %get-tuple-element.145), channel_id=1, source_target_pairs={{0,6},{2,0},{4,2},{6,4},{1,7},{3,1},{5,3},{7,5},{8,14},{10,8},{12,... | collective-permute-start | bytes 294920 | tf_op jit(solution)/shard_map/ppermute | solution.py:202
  249.5 9.9 %collective-permute-start.31 = (bf16[48,1024]{1,0:T(8,128)(2,1)}, bf16[48,1024]{1,0:T(8,128)(2,1)S(1)}, u32[]{:S(2)}, u32[]{:S(2)}) collective-permute-start(bf16[48,1024]{1,0:T(8,128)(2,1)} %get-tuple-element.146), channel_id=1, source_target_pairs={{0,4},{2,6},{4,0},{6,2},{1,5},{3,7},{5,1},{7,3},{8,12},{10,14},{12... | collective-permute-start | bytes 294920 | tf_op jit(solution)/shard_map/ppermute | solution.py:202
  253.2 13.7 %collective-permute-start.37 = (bf16[48,1536]{1,0:T(8,128)(2,1)}, bf16[48,1536]{1,0:T(8,128)(2,1)S(1)}, u32[]{:S(2)}, u32[]{:S(2)}) collective-permute-start(bf16[48,1536]{1,0:T(8,128)(2,1)} %get-tuple-element.157), channel_id=1, source_target_pairs={{0,6},{2,0},{4,2},{6,4},{1,7},{3,1},{5,3},{7,5},{8,14},{10,8},{12,... | collective-permute-start | bytes 442376 | tf_op jit(solution)/shard_map/ppermute | solution.py:202
  255.3 15.0 %collective-permute-start.38 = (bf16[48,1536]{1,0:T(8,128)(2,1)}, bf16[48,1536]{1,0:T(8,128)(2,1)S(1)}, u32[]{:S(2)}, u32[]{:S(2)}) collective-permute-start(bf16[48,1536]{1,0:T(8,128)(2,1)} %get-tuple-element.158), channel_id=1, source_target_pairs={{0,4},{2,6},{4,0},{6,2},{1,5},{3,7},{5,1},{7,3},{8,12},{10,14},{12... | collective-permute-start | bytes 442376 | tf_op jit(solution)/shard_map/ppermute | solution.py:202
  255.4 15.0 %collective-permute-start.39 = (bf16[48,1536]{1,0:T(8,128)(2,1)}, bf16[48,1536]{1,0:T(8,128)(2,1)S(1)}, u32[]{:S(2)}, u32[]{:S(2)}) collective-permute-start(bf16[48,1536]{1,0:T(8,128)(2,1)} %get-tuple-element.159), channel_id=1, source_target_pairs={{0,2},{2,4},{4,6},{6,0},{1,3},{3,5},{5,7},{7,1},{8,10},{10,12},{12... | collective-permute-start | bytes 442376 | tf_op jit(solution)/shard_map/ppermute | solution.py:202
  259.4 7.5 %collective-permute-start.32 = (bf16[48,1024]{1,0:T(8,128)(2,1)S(1)}, bf16[48,1024]{1,0:T(8,128)(2,1)S(1)}, u32[]{:S(2)}, u32[]{:S(2)}) collective-permute-start(bf16[48,1024]{1,0:T(8,128)(2,1)S(1)} %copy-done.40), channel_id=1, source_target_pairs={{0,2},{2,4},{4,6},{6,0},{1,3},{3,5},{5,7},{7,1},{8,10},{10,12},{12... | collective-permute-start | bytes 294920 | tf_op jit(solution)/shard_map/ppermute | solution.py:202
  (52 other events, 248.4 us)

commit v3 on v2

--- a/solution.py
+++ b/solution.py
@@ -79,21 +79,22 @@
     return parts[0]
 
 
-def call(kernel, outs, args, specs=None, scratch=(), name=None, us=5, vmem=60):
+def call(kernel, outs, args, specs=None, scratch=(), name=None, us=5, vmem=32):
     whole = pl.BlockSpec(memory_space=pltpu.VMEM)
     specs = [None] * len(args) if specs is None else specs
     windowed = any(s is not None and s.block_shape is not None for s in specs)
-    return pl.pallas_call(
+    results = pl.pallas_call(
         kernel,
         grid=(1,) if windowed else (),
-        out_shape=[jax.ShapeDtypeStruct(o[0], o[1]) for o in outs],
+        out_shape=[(pltpu.HBM if len(o) > 3 else jax.ShapeDtypeStruct)(o[0], o[1]) for o in outs],
         in_specs=[whole if s is None else s for s in specs],
-        out_specs=[o[2] if len(o) > 2 else whole for o in outs],
+        out_specs=[whole if len(o) < 3 or o[2] is None else o[2] for o in outs],
         scratch_shapes=list(scratch),
         name=name,
-        cost_estimate=pl.CostEstimate(flops=us * 1000000000, bytes_accessed=us * 3000000, transcendentals=0),
+        cost_estimate=pl.CostEstimate(flops=us * 300000000, bytes_accessed=us * 900000, transcendentals=0),
         compiler_params=pltpu.CompilerParams(vmem_limit_bytes=vmem << 20),
     )(*args)
+    return list(results)
 
 
 SMEM = pl.BlockSpec(memory_space=pltpu.SMEM)
@@ -104,6 +105,20 @@
     width = nat_ref.shape[1]
     nat = jnp.where(idx[3] == 0, nat_ref[0:1], nat_ref[1:2])
     return (iota((width, width), 0) == nat).astype(F32).astype(BF16)
+
+
+def kept(shape, dtype):
+    return (shape, dtype, None, True)
+
+
+def in_hbm(value):
+    return pltpu.with_memory_space_constraint(value, pltpu.HBM)
+
+
+def after(value, other):
+    if other is None:
+        return value
+    return lax.optimization_barrier((value, other))[0]
 
 
 class Plan:
@@ -118,14 +133,21 @@
         z = lax.rem(idx[1] - zr + self.nz, self.nz)
         return pl.multiple_of(((y * self.nz + z) * self.nx + x) * self.piece, self.piece)
 
-    def gather(self, piece):
+    def gather(self, groups, first):
         if not self.fast:
-            return [lax.all_gather(piece, GROUP, axis=0, tiled=True)]
-        rots = [lax.ppermute(piece, "z", [(i, (i + k) % 4) for i in range(4)]) for k in (1, 2, 3)]
-        line = jnp.concatenate([piece] + rots, axis=0)
-        by_x, by_y = swap(line, "x"), swap(line, "y")
+            return [[lax.all_gather(piece, GROUP, axis=0, tiled=True)] for piece in groups]
         half = 2 * self.piece
-        return [line, by_x, by_y, swap(by_x[:half], "y"), swap(by_y[half:], "x")]
+        out, before_line, before_last = [], None, None
+        for piece in groups:
+            piece = after(piece, before_line)
+            rots = [lax.ppermute(piece, "z", [(i, (i + k) % 4) for i in range(4)]) for k in (1, 2, 3)]
+            line = jnp.concatenate([piece] + rots, axis=0)
+            line = after(line, first if before_line is None else before_last)
+            before_line = line
+            by_x, by_y = swap(line, "x"), swap(line, "y")
+            out.append([line, by_x, by_y, swap(by_x[:half], "y"), swap(by_y[half:], "x")])
+            before_last = tuple(out[-1][3:])
+        return out
 
     def pieces(self):
         n, out = self.piece, []
@@ -169,8 +191,8 @@
                     for xr in range(2):
                         at = self.place(idx, yr, zr, xr)
                         for lanes, ref, row in (
-                            (0, refs[1 - xr], yr * 4 + zr),
-                            (half, refs[3 - yr], xr * 4 + zr),
+                            (0, refs[2 - 2 * xr], yr * 4 + zr),
+                            (half, refs[3 - 2 * yr], xr * 4 + zr),
                         ):
                             copies.append(
                                 pltpu.make_async_copy(
@@ -183,22 +205,29 @@
             copy.start()
         return copies
 
-    def reduce(self, shared, tag):
+    def reduce1(self, shared, tag):
         if not self.fast:
-            parts = shared[0].reshape(self.count, self.piece, -1)
-            parts = lax.all_to_all(parts, GROUP, split_axis=0, concat_axis=0, tiled=True)
-            return [parts.astype(F32).sum(axis=0)]
-        a_send, a_keep, b_send, b_keep = shared
+            return shared
+        a_send, b_send, a_keep, b_keep = shared
         n, half = self.piece, a_send.shape[1]
         a_got, b_got = swap(a_send, "x"), swap(b_send, "y")
         shape = ((4 * n, half), BF16)
-        a_send, a_keep, b_send, b_keep = call(
-            add_kernel, [shape] * 4, [a_keep, a_got, b_keep, b_got], name="add1_" + tag, us=2
-        )
+        return call(add_kernel, [shape] * 4, [a_keep, a_got, b_keep, b_got], name="add1_" + tag, us=1)
+
+    def reduce2(self, sums, tag):
+        if not self.fast:
+            return sums
+        a_send, a_keep, b_send, b_keep = sums
+        n, half = self.piece, a_send.shape[1]
         a_got, b_got = swap(a_send, "y"), swap(b_send, "x")
-        parts = call(
-            line_kernel, [((n, 2 * half), BF16)] * 4, [a_keep, a_got, b_keep, b_got], name="add2_" + tag, us=1
-        )
+        outs = [((n, 2 * half), BF16)] * 4
+        return call(line_kernel, outs, [a_keep, a_got, b_keep, b_got], name="add2_" + tag, us=1)
+
+    def reduce3(self, parts):
+        if not self.fast:
+            shares = parts[0].reshape(self.count, self.piece, -1)
+            shares = lax.all_to_all(shares, GROUP, split_axis=0, concat_axis=0, tiled=True)
+            return [shares.astype(F32).sum(axis=0)]
         rots = [lax.ppermute(parts[k], "z", [(i, (i - k) % 4) for i in range(4)]) for k in (1, 2, 3)]
         return [parts[0]] + rots
 
@@ -219,9 +248,11 @@
 
 
 def pack_kernel(
-    span, idx, in_proj, norm, moe, router, taps, cbias, select, step, sbias, decay, skip,
-    mine_o, send_o, ch_o, rows_s, block_s,
+    span, idx, in_proj, norm, moe, router, taps, cbias, select, step, sbias, decay, skip, up,
+    mine_o, send_o, ch_o, up_o, rows_s, block_s, sem,
 ):
+    copy = pltpu.make_async_copy(up.at[:, pl.ds(0, up_o.shape[1])], up_o, sem)
+    copy.start()
     dr = in_proj.shape[0]
     er, sel_n = select.shape
     rank, states = step.shape[0], decay.shape[0]
@@ -247,11 +278,23 @@
     rows_s[...] = jnp.zeros_like(rows_s)
     rows_s[ROW_FEATURE : ROW_FEATURE + 1, :dr] = norm[...].astype(F32)
     rows_s[ROW_FEATURE + 1 : ROW_FEATURE + 2, :dr] = moe[...].astype(F32)
-    block_s[...] = jnp.zeros_like(block_s)
-    block_s[:dr, ROW_FEATURE + 2 : ROW_FEATURE + 2 + router.shape[1]] = router[...].astype(F32)
-    feature = (block_s[:dr] + jnp.transpose(rows_s[...])[:dr]).astype(BF16)
+    rows_s[ROW_FEATURE + 2 : ROW_FEATURE + 2 + router.shape[0], :dr] = router[...].astype(F32)
+    feature = jnp.transpose(rows_s[...])[:dr].astype(BF16)
     mine_o[:, inner2:] = feature
     send_o[:, inner2:] = feature
+    copy.wait()
+
+
+def split_kernel(up, down, up_o, down_a, down_b, sem):
+    copies = [
+        pltpu.make_async_copy(up.at[:, pl.ds(up.shape[1] - up_o.shape[1], up_o.shape[1])], up_o, sem.at[0]),
+        pltpu.make_async_copy(down.at[:, pl.ds(0, down_a.shape[1])], down_a, sem.at[1]),
+        pltpu.make_async_copy(down.at[:, pl.ds(down_a.shape[1], down_b.shape[1])], down_b, sem.at[2]),
+    ]
+    for copy in copies:
+        copy.start()
+    for copy in copies:
+        copy.wait()
 
 
 def merge_kernel(mine, got, ch, out_proj, one_o, two_o):
@@ -387,7 +430,7 @@
     _, valid = positions(lens, 0, tok)
     valid_f = valid.astype(F32)
     width = max(LANES, experts)
-    hot = (routes[...] == iota((tok, width), 1)).astype(F32)
+    hot = (routes == iota((tok, width), 1)).astype(F32)
     live = hot * valid_f
     earlier = (iota((tok, tok), 1) < iota((tok, tok), 0)).astype(F32).astype(BF16)
     before = mm(earlier, live.astype(BF16))
@@ -396,19 +439,26 @@
     return valid_f, hot, rank, kept
 
 
+def column_of(row):
+    n = row.shape[1]
+    square = iota((n, n), 0) == iota((n, n), 1)
+    return jnp.sum(jnp.where(square, row[...].astype(F32), 0.0), axis=1, keepdims=True).astype(jnp.int32)
+
+
 def slot_hot(k, routes, rank, kept, capacity, tok):
-    inside = kept & (routes[...] == k)
+    inside = kept & (routes == k)
     return (inside & (rank == iota((tok, capacity), 1))).astype(F32).astype(BF16)
 
 
 def moe_enter_kernel(experts, capacity, lens, tok, cot, routes, mine, got, dnat, disp_o, hidden_o, gate_o):
     rows, width = tok.shape
+    routes = column_of(routes)
     hidden = tok[...].astype(F32) + (mine[...] + got[...])
     hidden_o[...] = hidden
     scale = lax.rsqrt(jnp.mean(hidden * hidden, axis=1, keepdims=True) + EPS)
     mv = (hidden * scale * dnat[1:2]).astype(BF16)
     logits = mm(mv, dnat[...].astype(BF16), NT)
-    hot = (routes[...] + 2 == iota(logits.shape, 1)).astype(F32)
+    hot = (routes + 2 == iota(logits.shape, 1)).astype(F32)
     gate = sigmoid(jnp.sum(logits * hot, axis=1, keepdims=True))
     gate_o[...] = jnp.broadcast_to(gate, gate_o.shape)
     valid_f, _, rank, kept = route_tables(lens, routes, experts, capacity, rows)
@@ -418,35 +468,71 @@
         disp_o[k] = mm(slot_hot(k, routes, rank, kept, capacity, rows), both, TN).astype(BF16)
 
 
-def expert_kernel(width, own, peer, up, down, out_own, out_peer, up_g, down_g, rows_s, acc_s):
-    half = own.shape[0]
-    total = rows_s.shape[0]
-    rows_s[:half] = own[...]
-    rows_s[half:] = peer[...]
-    hidden = up.shape[1]
+def fill_rows(groups, rows_s, both_s):
+    at = 0
+    for group in groups:
+        for i in range(group.shape[0]):
+            rows_s[at : at + group.shape[1]] = group[i].astype(F32)
+            at += group.shape[1]
+    both_s[...] = rows_s[...].astype(BF16)
+
+
+def hidden_units(both_s, up, down):
+    width = up.shape[1]
+    pre = mm(both_s[:, :width], up, NT)
+    g_act = mm(both_s[:, width:], down, NT)
+    sq = pre * pre
+    th = jnp.tanh(GELU_C * (pre + GELU_K * sq * pre))
+    act = (0.5 * pre * (1.0 + th)).astype(BF16)
+    slope = 0.5 * (1.0 + th) + 0.5 * pre * (1.0 - th * th) * (GELU_C * (1.0 + 3.0 * GELU_K * sq))
+    return act, (g_act * slope).astype(BF16)
+
+
+def expert_kernel(
+    own, peer, up, down, up_a, up_b, down_a, down_b,
+    out_own, out_peer, rows_s, both_s, acc_s, up_s, down_s, sem,
+):
+    copies = []
+    for parts, held in (((up, up_a, up_b), up_s), ((down, down_a, down_b), down_s)):
+        at = 0
+        for part in parts:
+            to = held.at[pl.ds(at, part.shape[1])]
+            copies.append(pltpu.make_async_copy(part.at[0], to, sem.at[len(copies)]))
+            at += part.shape[1]
+    for copy in copies:
+        copy.start()
+    hidden = down.shape[1]
+    count, capacity = own.shape[:2]
+    fill_rows((own, peer), rows_s, both_s)
+    width = own.shape[2] // 2
     part = 256
-    for f in range(0, hidden, part):
-        x = rows_s[:, :width]
-        g = rows_s[:, width:]
-        pre = mm(x, up[0, f : f + part], NT)
-        g_act = mm(g, down[0, f : f + part], NT)
-        sq = pre * pre
-        th = jnp.tanh(GELU_C * (pre + GELU_K * sq * pre))
-        act = (0.5 * pre * (1.0 + th)).astype(BF16)
-        slope = 0.5 * (1.0 + th) + 0.5 * pre * (1.0 - th * th) * (GELU_C * (1.0 + 3.0 * GELU_K * sq))
-        g_pre = (g_act * slope).astype(BF16)
-        down_g[0, f : f + part] = mm(act, g, TN)
-        up_g[0, f : f + part] = mm(g_pre, x, TN)
-        e_part = mm(act, down[0, f : f + part])
-        i_part = mm(g_pre, up[0, f : f + part])
+    for copy in copies:
+        copy.wait()
+    for f in range(0, 2 * hidden, part):
+        span = slice(f, f + part)
+        act, g_pre = hidden_units(both_s, up_s[span], down_s[span])
+        e_part = mm(act, down_s[span])
+        i_part = mm(g_pre, up_s[span])
         if f == 0:
             acc_s[:, :width] = e_part
             acc_s[:, width:] = i_part
         else:
             acc_s[:, :width] += e_part
             acc_s[:, width:] += i_part
-    out_own[...] = acc_s[:half]
-    out_peer[...] = acc_s[half:].astype(BF16)
+    for i in range(count):
+        out_own[i] = acc_s[i * capacity : (i + 1) * capacity]
+        out_peer[i] = acc_s[(count + i) * capacity : (count + i + 1) * capacity].astype(BF16)
+
+
+def expert_grad_kernel(own, peer, own_y, peer_y, up, down, up_g, down_g, rows_s, both_s):
+    fill_rows((own, peer, own_y, peer_y), rows_s, both_s)
+    width = own.shape[2] // 2
+    part = 256
+    for f in range(0, up.shape[1], part):
+        span = slice(f, f + part)
+        act, g_pre = hidden_units(both_s, up[0, span], down[0, span])
+        down_g[0, span] = mm(act, both_s[:, width:], TN)
+        up_g[0, span] = mm(g_pre, both_s[:, :width], TN)
 
 
 def moe_leave_kernel(
@@ -454,6 +540,7 @@
     out_o, ghid_o, gbr_o, dgrad_o,
 ):
     rows, width = hidden.shape
+    routes = column_of(routes)
     valid_f, _, rank, kept = route_tables(lens, routes, experts, capacity, rows)
     kept_f = kept.astype(F32)
     gate = gate_in[:, 0:1]
@@ -468,7 +555,7 @@
     g_gate = jnp.sum(gy * ex_out, axis=1, keepdims=True)
     chosen = g_gate * gate * (1.0 - gate)
     small_rows = dnat.shape[0]
-    hot = (routes[...] + 2 == iota((rows, small_rows), 1)).astype(F32)
+    hot = (routes + 2 == iota((rows, small_rows), 1)).astype(F32)
     g_logit = (chosen * hot).astype(BF16)
     g_mv = mm(g_logit, dnat[...].astype(BF16)) + sent
     scale = lax.rsqrt(jnp.mean(hid * hid, axis=1, keepdims=True) + EPS)
@@ -615,15 +702,13 @@
 
 
 def leave_kernel(
-    plan, idx, lens, nat, gsel_a, gsel_b, gxcs, gzg, gsr, q, smallg, xin, xc, u, small, g1, g2z, tok2, dnat, dgrad, *refs
+    plan, idx, lens, nat, gsel_a, gsel_b, gxcs, gsr, q, smallg, xin, xc, u, small, g1, dgrad, gxin_o, *refs
 ):
     n = plan.n_shared()
-    mine_o, send_o = refs[:2]
-    shared = refs[2 : 2 + n]
-    grad_s, sem = refs[2 + n :]
+    shared = refs[:n]
+    grad_s, sem = refs[n:]
     rows, inner = xin.shape
     tok = rows // 2
-    width = tok2.shape[1]
     perm = perm_matrix(idx, nat)
     g_sel = (gsel_a[...] + swap_halves(gsel_b[...])).astype(BF16)
     selblk = g1[:, inner : inner + LANES]
@@ -644,16 +729,9 @@
         taps[3 - lag] = jnp.sum(held * pltpu.roll(x, lag, 0), axis=0, keepdims=True)
     g_bias = jnp.sum(g_conv, axis=0, keepdims=True)
     g_xin = g_xin.astype(BF16)
+    gxin_o[...] = g_xin
     grad_s[:, :inner] = mm(u[...], g_xin, TN).astype(BF16)
-    gn = mm(g_xin, g1[:, :inner], NT) + mm(gzg[...], g2z[...], NT)
-    gn = split_mm(gn, perm, NT)
-    mine_o[...] = gn[:tok]
-    send_o[...] = gn[tok:]
-    vals = tok2[...].astype(F32)
-    scale = lax.rsqrt(jnp.mean(vals * vals, axis=1, keepdims=True) + EPS)
-    gain_g = jnp.sum(gn * (vals * scale), axis=0, keepdims=True)
-    dg = jnp.where(iota(dgrad.shape, 0) == 0, gain_g, dgrad[...])
-    dg = split_mm(dg, perm)
+    dg = split_mm(dgrad[...], perm)
     top = jnp.concatenate(taps + [g_bias, jnp.zeros((3, inner), F32)], axis=0)
     gap = jnp.zeros((ROW_FEATURE - smallg.shape[0], inner), F32)
     end = jnp.zeros((LANES - ROW_FEATURE - dg.shape[0], inner), F32)
@@ -661,6 +739,14 @@
     grad_s[:, inner + LANES :] = jnp.transpose(table).astype(BF16)
     for copy in plan.emit(idx, grad_s, shared, sem):
         copy.wait()
+
+
+def back_kernel(idx, nat, gxin, gzg, g1x, g2z, mine_o, send_o):
+    tok = mine_o.shape[0]
+    gn = mm(gxin[...], g1x[...], NT) + mm(gzg[...], g2z[...], NT)
+    gn = split_mm(gn, perm_matrix(idx, nat), NT)
+    mine_o[...] = gn[:tok]
+    send_o[...] = gn[tok:]
 
 
 def final_kernel(tok, mine, got, ghid, dnat, out_o):
@@ -710,23 +796,28 @@
     decay_o[...] = table[ROW_DECAY : ROW_DECAY + states]
 
 
-def spread_kernel(span, idx, keep, got, in_o, norm_o, moe_o, router_o, square_s):
+def spread_kernel(span, idx, keep, got, in_proj, norm, in_o, norm_o, moe_o, router_o, square_s):
     dr = keep.shape[0]
     inner2 = keep.shape[1] - LANES
     first = idx[3] == 0
+    acc = jnp.zeros((dr, LANES), F32)
     for k in range(inner2 // span):
         mine = keep[:, k * span : (k + 1) * span]
         peer = got[:, k * span : (k + 1) * span]
-        in_o[:, 2 * k * span : (2 * k + 1) * span] = jnp.where(first, mine, peer)
-        in_o[:, (2 * k + 1) * span : (2 * k + 2) * span] = jnp.where(first, peer, mine)
+        for at, part in ((2 * k * span, jnp.where(first, mine, peer)), ((2 * k + 1) * span, jnp.where(first, peer, mine))):
+            in_o[:, at : at + span] = part
+            terms = part * in_proj[:, at : at + span].astype(F32)
+            for j in range(0, span, LANES):
+                acc = acc + terms[:, j : j + LANES]
     table = keep[:, inner2:] + got[:, inner2:]
     at = ROW_FEATURE
-    router_o[...] = table[:, at + 2 : at + 2 + router_o.shape[1]]
+    total = jnp.sum(acc, axis=1, keepdims=True)
     square_s[...] = jnp.zeros_like(square_s)
-    square_s[:dr] = table
+    square_s[:dr] = jnp.where(iota(table.shape, 1) == at, total, table)
     flat = jnp.transpose(square_s[...])[:, :dr]
-    norm_o[...] = flat[at : at + 1]
+    norm_o[...] = flat[at : at + 1] / norm[...].astype(F32)
     moe_o[...] = flat[at + 1 : at + 2]
+    router_o[...] = flat[at + 2 : at + 2 + router_o.shape[0]]
 
 
 def body(
@@ -771,12 +862,18 @@
     nat = jnp.asarray(nat, jnp.int32)
 
     span = nf * er
-    mine_w, send_w, ch = call(
+    hid = up_weight.shape[1]
+    first, second = hid // 2, hid // 6
+    mine_w, send_w, ch, up_send = call(
         functools.partial(pack_kernel, span),
-        [((dr, 2 * inner + LANES), BF16), ((dr, 2 * inner + LANES), BF16), ((er, 2 * LANES), BF16)],
-        [idx, input_proj, norm_gain[None], moe_gain[None], router_weight, conv_weight, conv_bias[None], select_proj, step_proj, step_bias[None], decay_log, skip_gain[None]],
-        [SMEM] + [None] * 11,
-        scratch=[pltpu.VMEM((LANES, LANES), F32), pltpu.VMEM((LANES, LANES), F32)],
+        [((dr, 2 * inner + LANES), BF16), ((dr, 2 * inner + LANES), BF16), ((er, 2 * LANES), BF16), ((1, first, width), BF16, HBM)],
+        [idx]
+        + [
+            in_hbm(v)
+            for v in (input_proj, norm_gain[None], moe_gain[None], router_weight.T, conv_weight, conv_bias[None], select_proj, step_proj, step_bias[None], decay_log, skip_gain[None], up_weight)
+        ],
+        [SMEM] + [None] * 11 + [HBM],
+        scratch=[pltpu.VMEM((LANES, LANES), F32), pltpu.VMEM((LANES, LANES), F32), pltpu.SemaphoreType.DMA],
         name="pack",
         us=1,
     )
@@ -790,25 +887,38 @@
     )
     tok2 = jnp.concatenate([tokens, swap(tokens, "c")], axis=0)
     lens2 = jnp.concatenate([seq_lens, swap(seq_lens, "c")], axis=0)
-    pieces1 = plan.gather(group1)
-    pieces2 = plan.gather(group2)
-
+    up_one = swap(up_send, "y")
+    up_send, down_send, down_rest = call(
+        split_kernel,
+        [((1, hid - first, width), BF16, HBM), ((1, second, width), BF16, HBM), ((1, hid - second, width), BF16, HBM)],
+        [in_hbm(up_weight), in_hbm(down_weight)],
+        [HBM, HBM],
+        scratch=[pltpu.SemaphoreType.DMA((3,))],
+        name="split",
+        us=2,
+    )
+    up_one = after(up_one, up_send)
+    pieces1, pieces2 = plan.gather([group1, group2], up_one)
     fetch_sem = pltpu.SemaphoreType.DMA((ng,))
     emit_sem = pltpu.SemaphoreType.DMA((2 * ng,))
     u, xin, xc, selp, small_t, dnat, g1 = call(
         functools.partial(enter_kernel, plan),
-        [((rows, width), BF16), ((rows, inner), F32), ((rows, inner), BF16), ((rows, LANES), F32), ((small_n, inner), F32), ((dn, width), F32), ((inner, inner + 2 * LANES), BF16)],
+        [((rows, width), BF16), kept((rows, inner), F32), ((rows, inner), BF16), ((rows, LANES), F32), ((small_n, inner), F32), kept((dn, width), F32), ((inner, inner + 2 * LANES), BF16)],
         [idx, lens2, tok2, nat] + pieces1,
         [SMEM, SMEM, None, None] + [HBM] * len(pieces1),
         scratch=[fetch_sem],
         name="enter",
     )
     selq = swap(selp, "c")
+    middle = (pieces2[min(2, len(pieces2) - 1)], xc)
+    up_two = swap(after(up_send, middle), "y")
+    down_one = swap(after(down_send, middle), "y")
+    down_two = swap(after(down_rest, (up_two, down_one)), "y")
     g1sel_spec = pl.BlockSpec((inner, LANES), lambda i: (0, inner // LANES))
     chunks = tok // 8
     ys, step_pre, sel, keep, check = call(
         functools.partial(scan_kernel, rank, states),
-        [((rows, inner), F32), ((rows, inner), F32), ((rows, LANES), F32), ((rows, LANES), F32), ((2 * chunks, states, inner), F32)],
+        [((rows, inner), F32), kept((rows, inner), F32), kept((rows, LANES), F32), kept((rows, LANES), F32), kept((2 * chunks, states, inner), F32)],
         [lens2, selp, selq, xc, g1, small_t],
         [SMEM, None, None, None, g1sel_spec, None],
         scratch=[pltpu.VMEM((rows, inner), F32), pltpu.VMEM((rows, inner), F32), pltpu.VMEM((2, states, tok), F32), pltpu.VMEM((2, states, tok), F32), pltpu.VMEM((states, inner), F32), pltpu.VMEM((2, states, inner), F32)],
@@ -817,45 +927,49 @@
     )
     gated, zg, br_mine, br_send, g2 = call(
         functools.partial(gate_kernel, plan),
-        [((rows, inner), BF16), ((rows, inner), F32), ((tok, width), F32), ((tok, width), F32), ((inner, inner + width), BF16)],
+        [kept((rows, inner), BF16), kept((rows, inner), F32), ((tok, width), F32), ((tok, width), F32), ((inner, inner + width), BF16)],
         [idx, u, xc, ys, small_t] + pieces2,
         [SMEM] + [None] * 4 + [HBM] * len(pieces2),
         scratch=[fetch_sem],
         name="gate",
     )
-    br_got = swap(br_send, "c")
+    br_got = after(swap(br_send, "c"), (up_two, down_one))
     disp, hidden, gate = call(
         functools.partial(moe_enter_kernel, experts, capacity),
-        [((experts, capacity, 2 * width), BF16), ((tok, width), F32), ((tok, LANES), F32)],
-        [seq_lens, tokens, cotangent, routes, br_mine, br_got, dnat],
+        [((experts, capacity, 2 * width), BF16), kept((tok, width), F32), kept((tok, LANES), F32)],
+        [seq_lens, tokens, in_hbm(cotangent), routes.T, br_mine, br_got, in_hbm(dnat)],
         [SMEM] + [None] * 6,
         name="moe_enter",
     )
     line = lax.all_to_all(disp, ("z", "x"), split_axis=0, concat_axis=0, tiled=True)
-    line = line.reshape(nf * capacity, 2 * width)
-    if ny > 1:
-        line = jnp.concatenate([line, swap(line, "y")], axis=0)
     peer = swap(line, "c")
-    total = 2 * line.shape[0]
-    hid = up_weight.shape[1]
-    out_own, out_peer, up_grad, down_grad = call(
-        functools.partial(expert_kernel, width),
-        [((total // 2, 2 * width), F32), ((total // 2, 2 * width), BF16), ((1, hid, width), F32), ((1, hid, width), F32)],
-        [line, peer, up_weight, down_weight],
-        scratch=[pltpu.VMEM((total, 2 * width), BF16), pltpu.VMEM((total, 2 * width), F32)],
+    line_y = swap(line, "y")
+    peer_y = swap(line_y, "c")
+    total = 2 * nf * capacity
+    out_own, out_peer = call(
+        expert_kernel,
+        [(line.shape, F32), (line.shape, BF16)],
+        [line, peer] + [in_hbm(w) for w in (up_weight, down_weight, up_one, up_two, down_one, down_two)],
+        [None, None] + [HBM] * 6,
+        scratch=[pltpu.VMEM((total, 2 * width), F32), pltpu.VMEM((total, 2 * width), BF16), pltpu.VMEM((total, 2 * width), F32), pltpu.VMEM((2 * hid, width), BF16), pltpu.VMEM((2 * hid, width), BF16), pltpu.SemaphoreType.DMA((6,))],
         name="expert",
-    )
-    summed = out_own + swap(out_peer, "c").astype(F32)
-    if ny > 1:
-        cut = nf * capacity
-        summed = summed[:cut] + swap(summed[cut:].astype(BF16), "y").astype(F32)
-    back = lax.all_to_all(
-        summed.astype(BF16).reshape(nf, capacity, 2 * width), ("z", "x"), split_axis=0, concat_axis=0, tiled=True
-    )
+        us=5,
+    )
+    up_grad, down_grad = call(
+        expert_grad_kernel,
+        [((1, hid, width), F32)] * 2,
+        [line, peer, line_y, peer_y, in_hbm(up_weight), in_hbm(down_weight)],
+        scratch=[pltpu.VMEM((2 * total, 2 * width), F32), pltpu.VMEM((2 * total, 2 * width), BF16)],
+        name="expert_grad",
+        us=7,
+    )
+    summed = (out_own + swap(after(out_peer, line_y), "c").astype(F32)).astype(BF16)
+    back = lax.all_to_all(summed, ("z", "x"), split_axis=0, concat_axis=0, tiled=True)
+    back = after(back, up_grad)
     result, ghid, gbr, dgrad = call(
         functools.partial(moe_leave_kernel, experts, capacity),
         [((tok, width), BF16), ((tok, width), F32), ((tok, width), BF16), ((dn, width), F32)],
-        [seq_lens, routes, cotangent, hidden, gate, dnat, back],
+        [in_hbm(seq_lens), in_hbm(routes.T), in_hbm(cotangent), in_hbm(hidden), in_hbm(gate), in_hbm(dnat), back],
         [SMEM] + [None] * 6,
         name="moe_leave",
     )
@@ -871,25 +985,41 @@
     gsel, gxcs, gsr, q, smallg = call(
         functools.partial(scan_back_kernel, rank, states),
         [((rows, LANES), F32), ((rows, inner), F32), ((rows, inner), BF16), ((rows, LANES), BF16), ((small_n, inner), F32)],
-        [gy, xc, step_pre, sel, keep, small_t, g1, check],
+        [gy, xc, step_pre, sel, keep, small_t, g1, in_hbm(check)],
         [None] * 6 + [g1sel_spec, None],
         scratch=[pltpu.VMEM((rows, inner), F32)] * 4 + [pltpu.VMEM((2, states, tok), F32)] * 4 + [pltpu.VMEM((states, inner), F32), pltpu.VMEM((2, states, inner), F32), pltpu.VMEM((states, inner), F32)],
         name="scan_back",
         us=16,
     )
-    parts2 = plan.reduce(shared2, "two")
+    shared2[-1] = after(shared2[-1], gsel)
+    sums2 = plan.reduce1(shared2, "two")
+    gsel = after(gsel, sums2[0])
     gsel_got = swap(gsel, "c")
-    g2z_spec = pl.BlockSpec((inner, inner), lambda i: (0, 0))
-    gn_mine, gn_send, *shared1 = call(
+    gxin, *shared1 = call(
         functools.partial(leave_kernel, plan),
-        [((tok, width), F32), ((tok, width), F32)] + plan.shared_outs(inner + 2 * LANES),
-        [idx, lens2, nat, gsel, gsel_got, gxcs, gzg, gsr, q, smallg, xin, xc, u, small_t, g1, g2, tok2, dnat, dgrad],
-        [SMEM, SMEM] + [None] * 13 + [g2z_spec, None, None, None],
+        [((rows, inner), BF16)] + plan.shared_outs(inner + 2 * LANES),
+        [idx, lens2, nat, gsel, gsel_got, gxcs, gsr, q, smallg, xin, xc, u, small_t, g1, dgrad],
+        [SMEM, SMEM] + [None] * 13,
         scratch=[pltpu.VMEM((inner, inner + 2 * LANES), BF16), emit_sem],
         name="leave",
-        us=9,
-    )
-    parts1 = plan.reduce(shared1, "one")
+        us=5,
+    )
+    square_spec = pl.BlockSpec((inner, inner), lambda i: (0, 0))
+    gn_mine, gn_send = call(
+        back_kernel,
+        [((tok, width), F32), ((tok, width), F32)],
+        [idx, nat, gxin, gzg, g1, g2],
+        [SMEM, None, None, None, square_spec, square_spec],
+        name="back",
+        us=3,
+    )
+    sums2 = plan.reduce2(sums2, "two")
+    parts2 = plan.reduce3(sums2)
+    shared1 = [after(part, sums2[0]) for part in shared1]
+    sums1 = plan.reduce1(shared1, "one")
+    if plan.fast:
+        sums1[-1] = after(sums1[-1], tuple(parts2))
+    parts1 = plan.reduce3(plan.reduce2(sums1, "one"))
     gn_got = swap(gn_send, "c")
     (input_grad,) = call(
         final_kernel, [((tok, width), F32)], [tokens, gn_mine, gn_got, ghid, dnat], name="final", us=2
@@ -906,9 +1036,9 @@
     )
     in_grad, norm_grad, moe_grad, router_grad = call(
         functools.partial(spread_kernel, span),
-        [((dr, 4 * inner), F32), ((1, dr), F32), ((1, dr), F32), ((dr, experts), F32)],
-        [idx, keep_w, swap(send_back, "c")],
-        [SMEM, None, None],
+        [((dr, 4 * inner), F32), ((1, dr), F32), ((1, dr), F32), ((experts, dr), F32)],
+        [idx, keep_w, swap(send_back, "c"), input_proj, norm_gain[None]],
+        [SMEM, None, None, None, None],
         scratch=[pltpu.VMEM((LANES, LANES), F32)],
         name="spread",
         us=1,
@@ -927,7 +1057,7 @@
         sk[0],
         out_grad,
         moe_grad[0],
-        router_grad,
+        router_grad.T,
         up_grad,
         down_grad,
     )

time: 281 us -> 215 us (0.77)
  blocking collectives: 40.9 us -> 0 us
  Pallas kernels: 92.7 us -> 76.2 us
  local copies, waits for them, and re-layouts: 17 us -> 4.43 us
  starting transfers between devices: 42.9 us -> 49.5 us
    all_to_all x2 -> x0, blocking collectives: 40.9 us -> none  [the longest x1 20.8 us: body(): lax.all_to_all(disp, ('z', 'x'), split_axis=0, concat_axis=0, tiled=True)]
    all_to_all x0 -> x2, waiting for transfers between devices: none -> 19.6 us  [the longest x1 13.6 us: body(): lax.all_to_all(disp, ('z', 'x'), split_axis=0, concat_axis=0, tiled=True)]
    ppermute x29 -> x33, waiting for transfers between devices: 60.4 us -> 43.1 us  [swap(): return lax.ppermute(values, axis, [(0, 1), (1, 0)])]
    pallas_call x18 -> x21, Pallas kernels: 92.7 us -> 76.2 us  [call(): pl.pallas_call(kernel, grid=(1,) if windowed else (), out_shape=[(pltpu.H...]
    unnamed x97 -> x60, local copies, waits for them, and re-layouts: 16.6 us -> 2.59 us
    all_to_all x0 -> x2, starting transfers between devices: none -> 11 us  [the longest x1 5.72 us: body(): lax.all_to_all(summed, ('z', 'x'), split_axis=0, concat_axis=0, tiled=True)]
    ppermute x6, starting transfers between devices: 15 us -> 9.28 us  [gather(): lax.ppermute(piece, 'z', [(i, (i + k) % 4) for i in range(4)])]
    ppermute x6, waiting for transfers between devices: 12.4 us -> 8.05 us  [reduce3(): lax.ppermute(parts[k], 'z', [(i, (i - k) % 4) for i in range(4)])]
  transfers between devices with their start and end apart: 41 -> 47, of which waited for: 22 -> 27; matrix products, arithmetic and copies ran while one was open for 2% -> 1% of each run, Pallas kernels for 14% -> 29%
where the time goes in v3:
time: 215 us; the launch traced here: 214 us
  waiting for transfers between devices  81.6 us (38%)
  Pallas kernels  76.2 us (35%)
  starting transfers between devices  49.5 us (23%)
  local copies, waits for them, and re-layouts  4.43 us (2%)
    pallas_call x21, Pallas kernels, call(): pl.pallas_call(kernel, grid=(1,) if windowed else (), out_shape=[(pltpu.H...  76.2 us
    ppermute x33, waiting for transfers between devices, swap(): return lax.ppermute(values, axis, [(0, 1), (1, 0)])  43.1 us
    ppermute x33, starting transfers between devices, swap(): return lax.ppermute(values, axis, [(0, 1), (1, 0)])  25.1 us
    all_to_all x1, waiting for transfers between devices, body(): lax.all_to_all(disp, ('z', 'x'), split_axis=0, concat_axis=0, tiled=True)  13.6 us
    ppermute x6, waiting for transfers between devices, gather(): lax.ppermute(piece, 'z', [(i, (i + k) % 4) for i in range(4)])  10.9 us
    ppermute x6, starting transfers between devices, gather(): lax.ppermute(piece, 'z', [(i, (i + k) % 4) for i in range(4)])  9.28 us
    ppermute x6, waiting for transfers between devices, reduce3(): lax.ppermute(parts[k], 'z', [(i, (i - k) % 4) for i in range(4)])  8.05 us
    all_to_all x1, waiting for transfers between devices, body(): lax.all_to_all(summed, ('z', 'x'), split_axis=0, concat_axis=0, tiled=True)  5.98 us
  transfers between devices with their start and end apart: 47, of which 27 were waited for; matrix products, arithmetic and copies ran while one was open for 1% of the time, Pallas kernels for 29%

profile of v3, /device:TPU:0, one launch (start us, length us, event | category | flops | bytes accessed | tf_op | source)
XLA Modules:
  0.0 214.3 jit_solution(2018011984372433000)
XLA Ops:
  0.7 2.1 pack.1
  2.8 3.0 %collective-permute-start.6 = (bf16[1,384,768]{2,1,0:T(8,128)(2,1)S(1)}, bf16[1,384,768]{2,1,0:T(8,128)(2,1)S(1)}, u32[]{:S(2)}, u32[]{:S(2)}) collective-permute-start(bf16[1,384,768]{2,1,0:T(8,128)(2,1)S(1)} %get-tuple-element.122), channel_id=1, source_target_pairs={{0,16},{16,0},{1,17},{17,1},{2,18},{18,2},{3,19},{19,3},{4,20},{20... | collective-permute-start | bytes 1769480 | tf_op jit(solution)/shard_map/ppermute | solution.py:763
  7.2 3.7 %collective-permute-start.5 = (bf16[48,1024]{1,0:T(8,128)(2,1)S(1)}, bf16[48,1024]{1,0:T(8,128)(2,1)S(1)}, u32[]{:S(2)}, u32[]{:S(2)}) collective-permute-start(bf16[48,1024]{1,0:T(8,128)(2,1)S(1)} %get-tuple-element.121), channel_id=1, source_target_pairs={{0,6},{2,0},{4,2},{6,4},{1,7},{3,1},{5,3},{7,5},{8,14},{10,8},{12,... | collective-permute-start | bytes 294920 | tf_op jit(solution)/shard_map/ppermute | solution.py:143
  14.3 5.8 %collective-permute-done.4 = bf16[48,1024]{1,0:T(8,128)(2,1)S(1)} collective-permute-done((bf16[48,1024]{1,0:T(8,128)(2,1)S(1)}, bf16[48,1024]{1,0:T(8,128)(2,1)S(1)}, u32[]{:S(2)}, u32[]{:S(2)}) %collective-permute-start.4) | collective-permute-done | bytes 98336 | tf_op jit(solution)/shard_map/ppermute | solution.py:143
  23.3 3.6 %collective-permute-start.14 = (bf16[48,1536]{1,0:T(8,128)(2,1)S(1)}, bf16[48,1536]{1,0:T(8,128)(2,1)S(1)}, u32[]{:S(2)}, u32[]{:S(2)}) collective-permute-start(bf16[48,1536]{1,0:T(8,128)(2,1)S(1)} %get-tuple-element.133), channel_id=1, source_target_pairs={{0,6},{2,0},{4,2},{6,4},{1,7},{3,1},{5,3},{7,5},{8,14},{10,8},{12,... | collective-permute-start | bytes 442376 | tf_op jit(solution)/shard_map/ppermute | solution.py:143
  27.9 3.8 %collective-permute-done.8.refs_2_ = bf16[192,1024]{1,0:T(8,128)(2,1)S(1)} collective-permute-done((bf16[192,1024]{1,0:T(8,128)(2,1)S(1)}, bf16[192,1024]{1,0:T(8,128)(2,1)S(1)}, u32[]{:S(2)}, u32[]{:S(2)}) %collective-permute-start.8) | collective-permute-done | bytes 393248 | tf_op jit(solution)/shard_map/ppermute | solution.py:763
  33.9 5.1 %collective-permute-done.13 = bf16[48,1536]{1,0:T(8,128)(2,1)S(1)} collective-permute-done((bf16[48,1536]{1,0:T(8,128)(2,1)S(1)}, bf16[48,1536]{1,0:T(8,128)(2,1)S(1)}, u32[]{:S(2)}, u32[]{:S(2)}) %collective-permute-start.13) | collective-permute-done | bytes 147488 | tf_op jit(solution)/shard_map/ppermute | solution.py:143
  42.3 6.0 %enter.1 = (bf16[256,768]{1,0:T(8,128)(2,1)S(1)}, f32[256,768]{1,0:T(8,128)}, bf16[256,768]{1,0:T(8,128)(2,1)S(1)}, f32[256,128]{1,0:T(8,128)S(1)}, f32[24,768]{...) custom-call(s32[4]{0:T(128)S(1)} %pad_add_fusion.1.idx, s32[2,8]{1,0:T(2,128)S(1)} %pad_add_fusion.lens, ...), custom_call_target="tpu_custom_call" | custom-call | flops 1500000000 | bytes 4500000 | tf_op jit(solution)/shard_map/enter/pallas_call | solution.py:86
  48.5 4.5 %collective-permute-done.16.refs_2_ = bf16[192,1536]{1,0:T(8,128)(2,1)S(1)} collective-permute-done((bf16[192,1536]{1,0:T(8,128)(2,1)S(1)}, bf16[192,1536]{1,0:T(8,128)(2,1)S(1)}, u32[]{:S(2)}, u32[]{:S(2)}) %collective-permute-start.16) | collective-permute-done | bytes 589856 | tf_op jit(solution)/shard_map/ppermute | solution.py:763
  56.0 8.2 %scan.1 = (f32[256,768]{1,0:T(8,128)S(1)}, f32[256,768]{1,0:T(8,128)}, f32[256,128]{1,0:T(8,128)}, f32[256,128]{1,0:T(8,128)}, f32[32,16,768]{2,1,0:T(8,128)}) custom-call(s32[2,8]{1,0:T(2,128)S(1)} %pad_add_fusion.lens, f32[256,128]{1,0:T(8,128)S(1)} %get-tuple-element.128.sel_a, f32[256,128]{1,0:T(8,128)S(1)} %collective-permute-done.11.sel_b, ...), custom_call_target="tpu_custom_call" | custom-call | flops 2700000000 | bytes 8100000 | tf_op jit(solution)/shard_map/scan/pallas_call | solution.py:86
  64.2 5.6 %gate.1 = (bf16[256,768]{1,0:T(8,128)(2,1)}, f32[256,768]{1,0:T(8,128)}, f32[128,768]{1,0:T(8,128)S(1)}, f32[128,768]{1,0:T(8,128)S(1)}, bf16[768,1536]{1,0:T(8,128)(2,1)S(1)}) custom-call(s32[4]{0:T(128)S(1)} %pad_add_fusion.1.idx, bf16[256,768]{1,0:T(8,128)(2,1)S(1)} %get-tuple-element.126.u, bf16[256,768]{1,0:T(8,128)(2,1)S(1)} %get-tuple-element.127.xc, ...), custom_call_target="tpu_custom_call" | custom-call | flops 1500000000 | bytes 4500000 | tf_op jit(solution)/shard_map/gate/pallas_call | solution.py:86
  70.9 6.6 %collective-permute-done.21.down_a = bf16[1,128,768]{2,1,0:T(8,128)(2,1)S(1)} collective-permute-done((bf16[1,128,768]{2,1,0:T(8,128)(2,1)S(1)}, bf16[1,128,768]{2,1,0:T(8,128)(2,1)S(1)}, u32[]{:S(2)}, u32[]{:S(2)}) %collective-permute-start.21) | collective-permute-done | bytes 196640 | tf_op jit(solution)/shard_map/ppermute | solution.py:763
  77.5 3.0 %moe_enter.1 = (bf16[8,20,1536]{2,1,0:T(8,128)(2,1)}, f32[128,768]{1,0:T(8,128)}, f32[128,128]{1,0:T(8,128)}) custom-call(s32[1,8]{1,0:T(1,128)S(1)} %copy-done.17, bf16[128,768]{1,0:T(8,128)(2,1)S(1)} %copy-done.10, bf16[128,768]{1,0:T(8,128)(2,1)} %cot.3, s32[1,128]{1,0:T(1,128)S(1)} %bitcast.20, f32[128,768]{1,0:T(8,128)S(1)} %get-tuple-element.135.mine, ...), custom_call_target="tpu_custom_call" | custom-call | flops 1500000000 | bytes 4500000 | tf_op jit(solution)/shard_map/moe_enter/pallas_call | solution.py:86
  80.5 5.2 %all-to-all-start = ((bf16[8,20,1536]{2,1,0:T(8,128)(2,1)}), bf16[8,20,1536]{2,1,0:T(8,128)(2,1)S(1)}, u32[]{:S(2)}, u32[]{:S(2)}) async-start(bf16[8,20,1536]{2,1,0:T(8,128)(2,1)} %get-tuple-element.144), calls=%async_computation | async-start | bytes 1179648 | tf_op jit(solution)/shard_map/all_to_all | solution.py:944
  85.7 1.7 collective-permute-start.23
  87.4 13.6 %all-to-all-done.own = bf16[8,20,1536]{2,1,0:T(8,128)(2,1)S(1)} async-done(((bf16[8,20,1536]{2,1,0:T(8,128)(2,1)}), bf16[8,20,1536]{2,1,0:T(8,128)(2,1)S(1)}, u32[]{:S(2)}, u32[]{:S(2)}) %all-to-all-start) | async-done | bytes 491552 | tf_op jit(solution)/shard_map/all_to_all | solution.py:944
  101.3 1.6 collective-permute-start.24
  103.3 7.4 %collective-permute-done.23.down_b = bf16[1,640,768]{2,1,0:T(8,128)(2,1)} collective-permute-done((bf16[1,640,768]{2,1,0:T(8,128)(2,1)}, bf16[1,640,768]{2,1,0:T(8,128)(2,1)}, u32[]{:S(2)}, u32[]{:S(2)}) %collective-permute-start.23) | collective-permute-done | bytes 983072 | tf_op jit(solution)/shard_map/ppermute | solution.py:763
  110.7 6.9 %expert.1 = (f32[8,20,1536]{2,1,0:T(8,128)S(1)}, bf16[8,20,1536]{2,1,0:T(8,128)(2,1)S(1)}) custom-call(bf16[8,20,1536]{2,1,0:T(8,128)(2,1)S(1)} %all-to-all-done.own, bf16[8,20,1536]{2,1,0:T(8,128)(2,1)S(1)} %copy.36.peer, bf16[1,768,768]{2,1,0:T(8,128)(2,1)} %up.7, bf16[1,768,768]{2,1,0:T(8,128)(2,1)} %down.5, bf16[1,384,768]{2,1,0:T(8,128)(2,1)} %copy-done.26, ...), custom_call_target="tpu_custom_call" | custom-call | flops 1500000000 | bytes 4500000 | tf_op jit(solution)/shard_map/expert/pallas_call | solution.py:86
  119.9 1.9 collective-permute-done.25
  122.8 5.7 %all-to-all-start.1 = ((bf16[8,20,1536]{2,1,0:T(8,128)(2,1)}), bf16[8,20,1536]{2,1,0:T(8,128)(2,1)}, u32[]{:S(2)}, u32[]{:S(2)}) async-start(bf16[8,20,1536]{2,1,0:T(8,128)(2,1)} %add_convert_fusion), calls=%async_computation.1 | async-start | bytes 1179648 | tf_op jit(solution)/shard_map/all_to_all | solution.py:967
  130.8 8.1 %expert_grad.1 = (f32[1,768,768]{2,1,0:T(8,128)}, f32[1,768,768]{2,1,0:T(8,128)}) custom-call(bf16[8,20,1536]{2,1,0:T(8,128)(2,1)S(1)} %all-to-all-done.own, bf16[8,20,1536]{2,1,0:T(8,128)(2,1)S(1)} %copy.36.peer, bf16[8,20,1536]{2,1,0:T(8,128)(2,1)S(1)} %copy.41.own_y, bf16[8,20,1536]{2,1,0:T(8,128)(2,1)S(1)} %copy.42.peer_y, bf16[1,768,768]{2,1,0:T(8,128)(2,1)} %up.7, ...), custom_call_target="tpu_custom_call" | custom-call | flops 2100000000 | bytes 6300000 | tf_op jit(solution)/shard_map/expert_grad/pallas_call | solution.py:86
  138.9 6.0 %all-to-all-done.1.back = bf16[8,20,1536]{2,1,0:T(8,128)(2,1)} async-done(((bf16[8,20,1536]{2,1,0:T(8,128)(2,1)}), bf16[8,20,1536]{2,1,0:T(8,128)(2,1)}, u32[]{:S(2)}, u32[]{:S(2)}) %all-to-all-start.1) | async-done | bytes 491552 | tf_op jit(solution)/shard_map/all_to_all | solution.py:967
  144.9 3.9 %moe_leave.1 = (bf16[128,768]{1,0:T(8,128)(2,1)}, f32[128,768]{1,0:T(8,128)S(1)}, bf16[128,768]{1,0:T(8,128)(2,1)S(1)}, f32[16,768]{1,0:T(8,128)S(1)}) custom-call(s32[1,8]{1,0:T(1,128)} %lens.3, s32[1,128]{1,0:T(1,128)} %bitcast.19, bf16[128,768]{1,0:T(8,128)(2,1)} %cot.3, f32[128,768]{1,0:T(8,128)} %get-tuple-element.142.hidden, ...), custom_call_target="tpu_custom_call" | custom-call | flops 1500000000 | bytes 4500000 | tf_op jit(solution)/shard_map/moe_leave/pallas_call | solution.py:86
  150.3 2.9 %gate_back.1 = (f32[256,768]{1,0:T(8,128)S(1)}, bf16[256,768]{1,0:T(8,128)(2,1)S(1)}, bf16[384,768]{1,0:T(8,128)(2,1)S(1)}, bf16[384,768]{1,0:T(8,128)(2,1)S(1)}...) custom-call(s32[4]{0:T(128)S(1)} %pad_add_fusion.1.idx, bf16[128,768]{1,0:T(8,128)(2,1)S(1)} %get-tuple-element.153.gbr_a, ...), custom_call_target="tpu_custom_call" | custom-call | flops 1500000000 | bytes 4500000 | tf_op jit(solution)/shard_map/gate_back/pallas_call | solution.py:86
  156.2 17.4 %scan_back.1 = (f32[256,128]{1,0:T(8,128)S(1)}, f32[256,768]{1,0:T(8,128)S(1)}, bf16[256,768]{1,0:T(8,128)(2,1)S(1)}, bf16[256,128]{1,0:T(8,128)(2,1)S(1)}, f32[24,768]{1,0:T(8,128)S(1)}) custom-call(f32[256,768]{1,0:T(8,128)S(1)} %get-tuple-element.157.gy_s, bf16[256,768]{1,0:T(8,128)(2,1)S(1)} %copy-done.8, f32[256,768]{1,0:T(8,128)S(1)} %copy-done.23, ...), custom_call_target="tpu_custom_call" | custom-call | flops 4800000000 | bytes 14400000 | tf_op jit(solution)/shard_map/scan_back/pallas_call | solution.py:86
  176.4 4.1 %leave.1 = (bf16[256,768]{1,0:T(8,128)(2,1)S(1)}, bf16[384,512]{1,0:T(8,128)(2,1)S(1)}, bf16[384,512]{1,0:T(8,128)(2,1)S(1)}, bf16[384,512]{1,0:T(8,128)(2,1)S(1)}, bf16[384,512]{1,0:T(8,128)(2,1)S(1)}) custom-call(s32[4]{0:T(128)S(1)} %pad_add_fusion.1.idx, s32[2,8]{1,0:T(2,128)S(1)} %pad_add_fusion.lens, s32[2,768]{1,0:T(2,128)S(1)} %copy-done.15, ...), custom_call_target="tpu_custom_call" | custom-call | flops 1500000000 | bytes 4500000 | tf_op jit(solution)/shard_map/leave/pallas_call | solution.py:86
  180.5 1.9 collective-permute-done.33.b_in
  186.9 5.4 %collective-permute-done.34.a_in = bf16[384,512]{1,0:T(8,128)(2,1)S(1)} collective-permute-done((bf16[384,512]{1,0:T(8,128)(2,1)S(1)}, bf16[384,512]{1,0:T(8,128)(2,1)S(1)}, u32[]{:S(2)}, u32[]{:S(2)}) %collective-permute-start.34) | collective-permute-done | bytes 393248 | tf_op jit(solution)/shard_map/ppermute | solution.py:763
  195.4 2.8 %back.1 = (f32[128,768]{1,0:T(8,128)S(1)}, f32[128,768]{1,0:T(8,128)S(1)}) custom-call(s32[4]{0:T(128)S(1)} %pad_add_fusion.1.idx, s32[2,768]{1,0:T(2,128)S(1)} %copy-done.15, bf16[256,768]{1,0:T(8,128)(2,1)S(1)} %get-tuple-element.176.gxin, bf16[256,768]{1,0:T(8,128)(2,1)S(1)} %get-tuple-element.177.gzg, bf16[768,1024]{1,0:T(8,128)(2,1)S(1)} %copy-done.1, ...), custom_call_target="tpu_custom_call" | custom-call | flops 900000000 | bytes 2700000 | tf_op jit(solution)/shard_map/back/pallas_call | solution.py:86
  202.8 2.9 %collective-permute-done.41.refs_1_ = bf16[48,1024]{1,0:T(8,128)(2,1)S(1)} collective-permute-done((bf16[48,1024]{1,0:T(8,128)(2,1)S(1)}, bf16[48,1024]{1,0:T(8,128)(2,1)S(1)}, u32[]{:S(2)}, u32[]{:S(2)}) %collective-permute-start.41) | collective-permute-done | bytes 98336 | tf_op jit(solution)/shard_map/ppermute | solution.py:231
  205.6 5.0 %collective-permute-done.42.refs_2_ = bf16[48,1024]{1,0:T(8,128)(2,1)S(1)} collective-permute-done((bf16[48,1024]{1,0:T(8,128)(2,1)S(1)}, bf16[48,1024]{1,0:T(8,128)(2,1)S(1)}, u32[]{:S(2)}, u32[]{:S(2)}) %collective-permute-start.42) | collective-permute-done | bytes 98336 | tf_op jit(solution)/shard_map/ppermute | solution.py:231
  (158 shorter events, 48.0 us)
Async XLA Ops:
  2.8 17.3 %collective-permute-start.6 = (bf16[1,384,768]{2,1,0:T(8,128)(2,1)S(1)}, bf16[1,384,768]{2,1,0:T(8,128)(2,1)S(1)}, u32[]{:S(2)}, u32[]{:S(2)}) collective-permute-start(bf16[1,384,768]{2,1,0:T(8,128)(2,1)S(1)} %get-tuple-element.122), channel_id=1, source_target_pairs={{0,16},{16,0},{1,17},{17,1},{2,18},{18,2},{3,19},{19,3},{4,20},{20... | collective-permute-start | bytes 1769480 | tf_op jit(solution)/shard_map/ppermute | solution.py:763
  10.8 9.2 %collective-permute-start.4 = (bf16[48,1024]{1,0:T(8,128)(2,1)S(1)}, bf16[48,1024]{1,0:T(8,128)(2,1)S(1)}, u32[]{:S(2)}, u32[]{:S(2)}) collective-permute-start(bf16[48,1024]{1,0:T(8,128)(2,1)S(1)} %get-tuple-element.121), channel_id=1, source_target_pairs={{0,4},{2,6},{4,0},{6,2},{1,5},{3,7},{5,1},{7,3},{8,12},{10,14},{12... | collective-permute-start | bytes 294920 | tf_op jit(solution)/shard_map/ppermute | solution.py:143
  10.8 9.2 %collective-permute-start.3 = (bf16[48,1024]{1,0:T(8,128)(2,1)S(1)}, bf16[48,1024]{1,0:T(8,128)(2,1)S(1)}, u32[]{:S(2)}, u32[]{:S(2)}) collective-permute-start(bf16[48,1024]{1,0:T(8,128)(2,1)S(1)} %get-tuple-element.121), channel_id=1, source_target_pairs={{0,2},{2,4},{4,6},{6,0},{1,3},{3,5},{5,7},{7,1},{8,10},{10,12},{12... | collective-permute-start | bytes 294920 | tf_op jit(solution)/shard_map/ppermute | solution.py:143
  21.0 10.7 %collective-permute-start.8 = (bf16[192,1024]{1,0:T(8,128)(2,1)S(1)}, bf16[192,1024]{1,0:T(8,128)(2,1)S(1)}, u32[]{:S(2)}, u32[]{:S(2)}) collective-permute-start(bf16[192,1024]{1,0:T(8,128)(2,1)S(1)} %pad_maximum_fusion.2.refs_0_), channel_id=1, source_target_pairs={{0,16},{16,0},{1,17},{17,1},{2,18},{18,2},{3,19},{19,3},{4,20},{20... | collective-permute-start | bytes 1179656 | tf_op jit(solution)/shard_map/ppermute | solution.py:763
  21.8 11.5 %collective-permute-start.7 = (bf16[192,1024]{1,0:T(8,128)(2,1)S(1)}, bf16[192,1024]{1,0:T(8,128)(2,1)S(1)}, u32[]{:S(2)}, u32[]{:S(2)}) collective-permute-start(bf16[192,1024]{1,0:T(8,128)(2,1)S(1)} %pad_maximum_fusion.2.refs_0_), channel_id=1, source_target_pairs={{0,1},{1,0},{2,3},{3,2},{4,5},{5,4},{6,7},{7,6},{8,9},{9,8},{10,11... | collective-permute-start | bytes 1179656 | tf_op jit(solution)/shard_map/ppermute | solution.py:763
  23.3 10.6 %collective-permute-start.14 = (bf16[48,1536]{1,0:T(8,128)(2,1)S(1)}, bf16[48,1536]{1,0:T(8,128)(2,1)S(1)}, u32[]{:S(2)}, u32[]{:S(2)}) collective-permute-start(bf16[48,1536]{1,0:T(8,128)(2,1)S(1)} %get-tuple-element.133), channel_id=1, source_target_pairs={{0,6},{2,0},{4,2},{6,4},{1,7},{3,1},{5,3},{7,5},{8,14},{10,8},{12,... | collective-permute-start | bytes 442376 | tf_op jit(solution)/shard_map/ppermute | solution.py:143
  26.9 12.0 %collective-permute-start.13 = (bf16[48,1536]{1,0:T(8,128)(2,1)S(1)}, bf16[48,1536]{1,0:T(8,128)(2,1)S(1)}, u32[]{:S(2)}, u32[]{:S(2)}) collective-permute-start(bf16[48,1536]{1,0:T(8,128)(2,1)S(1)} %get-tuple-element.133), channel_id=1, source_target_pairs={{0,4},{2,6},{4,0},{6,2},{1,5},{3,7},{5,1},{7,3},{8,12},{10,14},{12... | collective-permute-start | bytes 442376 | tf_op jit(solution)/shard_map/ppermute | solution.py:143
  26.9 12.0 %collective-permute-start.12 = (bf16[48,1536]{1,0:T(8,128)(2,1)S(1)}, bf16[48,1536]{1,0:T(8,128)(2,1)S(1)}, u32[]{:S(2)}, u32[]{:S(2)}) collective-permute-start(bf16[48,1536]{1,0:T(8,128)(2,1)S(1)} %get-tuple-element.133), channel_id=1, source_target_pairs={{0,2},{2,4},{4,6},{6,0},{1,3},{3,5},{5,7},{7,1},{8,10},{10,12},{12... | collective-permute-start | bytes 442376 | tf_op jit(solution)/shard_map/ppermute | solution.py:143
  39.1 13.9 %collective-permute-start.16 = (bf16[192,1536]{1,0:T(8,128)(2,1)S(1)}, bf16[192,1536]{1,0:T(8,128)(2,1)S(1)}, u32[]{:S(2)}, u32[]{:S(2)}) collective-permute-start(bf16[192,1536]{1,0:T(8,128)(2,1)S(1)} %pad_maximum_fusion.refs_0_), channel_id=1, source_target_pairs={{0,16},{16,0},{1,17},{17,1},{2,18},{18,2},{3,19},{19,3},{4,20},{20... | collective-permute-start | bytes 1769480 | tf_op jit(solution)/shard_map/ppermute | solution.py:763
  39.6 14.3 %collective-permute-start.15 = (bf16[192,1536]{1,0:T(8,128)(2,1)S(1)}, bf16[192,1536]{1,0:T(8,128)(2,1)S(1)}, u32[]{:S(2)}, u32[]{:S(2)}) collective-permute-start(bf16[192,1536]{1,0:T(8,128)(2,1)S(1)} %pad_maximum_fusion.refs_0_), channel_id=1, source_target_pairs={{0,1},{1,0},{2,3},{3,2},{4,5},{5,4},{6,7},{7,6},{8,9},{9,8},{10,11... | collective-permute-start | bytes 1769480 | tf_op jit(solution)/shard_map/ppermute | solution.py:763
  48.3 7.7 %collective-permute-start.11 = (f32[256,128]{1,0:T(8,128)S(1)}, f32[256,128]{1,0:T(8,128)S(1)}, u32[]{:S(2)}, u32[]{:S(2)}) collective-permute-start(f32[256,128]{1,0:T(8,128)S(1)} %get-tuple-element.128.sel_a), channel_id=1, source_target_pairs={{0,8},{8,0},{1,9},{9,1},{2,10},{10,2},{3,11},{11,3},{4,12},{12,4},... | collective-permute-start | bytes 393224 | tf_op jit(solution)/shard_map/ppermute | solution.py:763
  53.0 11.2 %collective-permute-start.18 = (bf16[96,1536]{1,0:T(8,128)(2,1)S(1)}, bf16[96,1536]{1,0:T(8,128)(2,1)S(1)}, u32[]{:S(2)}, u32[]{:S(2)}) collective-permute-start(bf16[96,1536]{1,0:T(8,128)(2,1)S(1)} %slice.19), channel_id=1, source_target_pairs={{0,1},{1,0},{2,3},{3,2},{4,5},{5,4},{6,7},{7,6},{8,9},{9,8},{10,11... | collective-permute-start | bytes 884744 | tf_op jit(solution)/shard_map/ppermute | solution.py:763
  53.9 10.3 %collective-permute-start.17 = (bf16[96,1536]{1,0:T(8,128)(2,1)S(1)}, bf16[96,1536]{1,0:T(8,128)(2,1)S(1)}, u32[]{:S(2)}, u32[]{:S(2)}) collective-permute-start(bf16[96,1536]{1,0:T(8,128)(2,1)S(1)} %slice.18), channel_id=1, source_target_pairs={{0,16},{16,0},{1,17},{17,1},{2,18},{18,2},{3,19},{19,3},{4,20},{20... | collective-permute-start | bytes 884744 | tf_op jit(solution)/shard_map/ppermute | solution.py:763
  54.8 22.6 %collective-permute-start.20 = (bf16[1,384,768]{2,1,0:T(8,128)(2,1)S(1)}, bf16[1,384,768]{2,1,0:T(8,128)(2,1)S(1)}, u32[]{:S(2)}, u32[]{:S(2)}) collective-permute-start(bf16[1,384,768]{2,1,0:T(8,128)(2,1)S(1)} %get-tuple-element.137), channel_id=1, source_target_pairs={{0,16},{16,0},{1,17},{17,1},{2,18},{18,2},{3,19},{19,3},{4,20},{20... | collective-permute-start | bytes 1769480 | tf_op jit(solution)/shard_map/ppermute | solution.py:763
  69.8 7.6 %collective-permute-start.19 = (f32[128,768]{1,0:T(8,128)S(1)}, f32[128,768]{1,0:T(8,128)S(1)}, u32[]{:S(2)}, u32[]{:S(2)}) collective-permute-start(f32[128,768]{1,0:T(8,128)S(1)} %get-tuple-element.136), channel_id=1, source_target_pairs={{0,8},{8,0},{1,9},{9,1},{2,10},{10,2},{3,11},{11,3},{4,12},{12,4},... | collective-permute-start | bytes 1179656 | tf_op jit(solution)/shard_map/ppermute | solution.py:763
  69.9 7.5 %collective-permute-start.21 = (bf16[1,128,768]{2,1,0:T(8,128)(2,1)S(1)}, bf16[1,128,768]{2,1,0:T(8,128)(2,1)S(1)}, u32[]{:S(2)}, u32[]{:S(2)}) collective-permute-start(bf16[1,128,768]{2,1,0:T(8,128)(2,1)S(1)} %get-tuple-element.139), channel_id=1, source_target_pairs={{0,16},{16,0},{1,17},{17,1},{2,18},{18,2},{3,19},{19,3},{4,20},{20... | collective-permute-start | bytes 589832 | tf_op jit(solution)/shard_map/ppermute | solution.py:763
  80.5 20.6 %all-to-all-start = ((bf16[8,20,1536]{2,1,0:T(8,128)(2,1)}), bf16[8,20,1536]{2,1,0:T(8,128)(2,1)S(1)}, u32[]{:S(2)}, u32[]{:S(2)}) async-start(bf16[8,20,1536]{2,1,0:T(8,128)(2,1)} %get-tuple-element.144), calls=%async_computation | async-start | bytes 1179648 | tf_op jit(solution)/shard_map/all_to_all | solution.py:944
  85.7 25.0 %collective-permute-start.23 = (bf16[1,640,768]{2,1,0:T(8,128)(2,1)}, bf16[1,640,768]{2,1,0:T(8,128)(2,1)}, u32[]{:S(2)}, u32[]{:S(2)}) collective-permute-start(bf16[1,640,768]{2,1,0:T(8,128)(2,1)} %copy-done.18), channel_id=1, source_target_pairs={{0,16},{16,0},{1,17},{17,1},{2,18},{18,2},{3,19},{19,3},{4,20},{20... | collective-permute-start | bytes 2949128 | tf_op jit(solution)/shard_map/ppermute | solution.py:763
  101.3 17.8 %collective-permute-start.24 = (bf16[8,20,1536]{2,0,1:T(8,128)(2,1)S(1)}, bf16[8,20,1536]{2,0,1:T(8,128)(2,1)S(1)}, u32[]{:S(2)}, u32[]{:S(2)}) collective-permute-start(bf16[8,20,1536]{2,0,1:T(8,128)(2,1)S(1)} %copy.35), channel_id=1, source_target_pairs={{0,16},{16,0},{1,17},{17,1},{2,18},{18,2},{3,19},{19,3},{4,20},{20... | collective-permute-start | bytes 1474568 | tf_op jit(solution)/shard_map/ppermute | solution.py:763
  122.8 22.0 %all-to-all-start.1 = ((bf16[8,20,1536]{2,1,0:T(8,128)(2,1)}), bf16[8,20,1536]{2,1,0:T(8,128)(2,1)}, u32[]{:S(2)}, u32[]{:S(2)}) async-start(bf16[8,20,1536]{2,1,0:T(8,128)(2,1)} %add_convert_fusion), calls=%async_computation.1 | async-start | bytes 1179648 | tf_op jit(solution)/shard_map/all_to_all | solution.py:967
  153.2 20.4 %collective-permute-start.28 = (bf16[384,768]{1,0:T(8,128)(2,1)S(1)}, bf16[384,768]{1,0:T(8,128)(2,1)S(1)}, u32[]{:S(2)}, u32[]{:S(2)}) collective-permute-start(bf16[384,768]{1,0:T(8,128)(2,1)S(1)} %get-tuple-element.164), channel_id=1, source_target_pairs={{0,1},{1,0},{2,3},{3,2},{4,5},{5,4},{6,7},{7,6},{8,9},{9,8},{10,11... | collective-permute-start | bytes 1769480 | tf_op jit(solution)/shard_map/ppermute | solution.py:763
  154.7 18.9 %collective-permute-start.29 = (bf16[384,768]{1,0:T(8,128)(2,1)S(1)}, bf16[384,768]{1,0:T(8,128)(2,1)S(1)}, u32[]{:S(2)}, u32[]{:S(2)}) collective-permute-start(bf16[384,768]{1,0:T(8,128)(2,1)S(1)} %get-tuple-element.167), channel_id=1, source_target_pairs={{0,16},{16,0},{1,17},{17,1},{2,18},{18,2},{3,19},{19,3},{4,20},{20... | collective-permute-start | bytes 1769480 | tf_op jit(solution)/shard_map/ppermute | solution.py:763
  173.9 8.5 %collective-permute-start.33 = (bf16[192,768]{1,0:T(8,128)(2,1)S(1)}, bf16[192,768]{1,0:T(8,128)(2,1)S(1)}, u32[]{:S(2)}, u32[]{:S(2)}) collective-permute-start(bf16[192,768]{1,0:T(8,128)(2,1)S(1)} %get-tuple-element.184), channel_id=1, source_target_pairs={{0,1},{1,0},{2,3},{3,2},{4,5},{5,4},{6,7},{7,6},{8,9},{9,8},{10,11... | collective-permute-start | bytes 884744 | tf_op jit(solution)/shard_map/ppermute | solution.py:763
  174.5 8.2 %collective-permute-start.32 = (bf16[192,768]{1,0:T(8,128)(2,1)S(1)}, bf16[192,768]{1,0:T(8,128)(2,1)S(1)}, u32[]{:S(2)}, u32[]{:S(2)}) collective-permute-start(bf16[192,768]{1,0:T(8,128)(2,1)S(1)} %get-tuple-element.168), channel_id=1, source_target_pairs={{0,16},{16,0},{1,17},{17,1},{2,18},{18,2},{3,19},{19,3},{4,20},{20... | collective-permute-start | bytes 884744 | tf_op jit(solution)/shard_map/ppermute | solution.py:763
  182.8 9.5 %collective-permute-start.34 = (bf16[384,512]{1,0:T(8,128)(2,1)S(1)}, bf16[384,512]{1,0:T(8,128)(2,1)S(1)}, u32[]{:S(2)}, u32[]{:S(2)}) collective-permute-start(bf16[384,512]{1,0:T(8,128)(2,1)S(1)} %get-tuple-element.188), channel_id=1, source_target_pairs={{0,1},{1,0},{2,3},{3,2},{4,5},{5,4},{6,7},{7,6},{8,9},{9,8},{10,11... | collective-permute-start | bytes 1179656 | tf_op jit(solution)/shard_map/ppermute | solution.py:763
  184.4 9.1 %collective-permute-start.35 = (bf16[384,512]{1,0:T(8,128)(2,1)S(1)}, bf16[384,512]{1,0:T(8,128)(2,1)S(1)}, u32[]{:S(2)}, u32[]{:S(2)}) collective-permute-start(bf16[384,512]{1,0:T(8,128)(2,1)S(1)} %get-tuple-element.192), channel_id=1, source_target_pairs={{0,16},{16,0},{1,17},{17,1},{2,18},{18,2},{3,19},{19,3},{4,20},{20... | collective-permute-start | bytes 1179656 | tf_op jit(solution)/shard_map/ppermute | solution.py:763
  184.9 13.3 %collective-permute-start.37 = (bf16[48,1536]{1,0:T(8,128)(2,1)S(1)}, bf16[48,1536]{1,0:T(8,128)(2,1)S(1)}, u32[]{:S(2)}, u32[]{:S(2)}) collective-permute-start(bf16[48,1536]{1,0:T(8,128)(2,1)S(1)} %get-tuple-element.196), channel_id=1, source_target_pairs={{0,6},{2,0},{4,2},{6,4},{1,7},{3,1},{5,3},{7,5},{8,14},{10,8},{12,... | collective-permute-start | bytes 442376 | tf_op jit(solution)/shard_map/ppermute | solution.py:231
  186.4 12.2 %collective-permute-start.38 = (bf16[48,1536]{1,0:T(8,128)(2,1)S(1)}, bf16[48,1536]{1,0:T(8,128)(2,1)S(1)}, u32[]{:S(2)}, u32[]{:S(2)}) collective-permute-start(bf16[48,1536]{1,0:T(8,128)(2,1)S(1)} %get-tuple-element.197), channel_id=1, source_target_pairs={{0,4},{2,6},{4,0},{6,2},{1,5},{3,7},{5,1},{7,3},{8,12},{10,14},{12... | collective-permute-start | bytes 442376 | tf_op jit(solution)/shard_map/ppermute | solution.py:231
  186.4 12.2 %collective-permute-start.39 = (bf16[48,1536]{1,0:T(8,128)(2,1)S(1)}, bf16[48,1536]{1,0:T(8,128)(2,1)S(1)}, u32[]{:S(2)}, u32[]{:S(2)}) collective-permute-start(bf16[48,1536]{1,0:T(8,128)(2,1)S(1)} %get-tuple-element.198), channel_id=1, source_target_pairs={{0,2},{2,4},{4,6},{6,0},{1,3},{3,5},{5,7},{7,1},{8,10},{10,12},{12... | collective-permute-start | bytes 442376 | tf_op jit(solution)/shard_map/ppermute | solution.py:231
  198.3 13.3 %collective-permute-start.31 = (f32[128,768]{1,0:T(8,128)S(1)}, f32[128,768]{1,0:T(8,128)S(1)}, u32[]{:S(2)}, u32[]{:S(2)}) collective-permute-start(f32[128,768]{1,0:T(8,128)S(1)} %get-tuple-element.179), channel_id=1, source_target_pairs={{0,8},{8,0},{1,9},{9,1},{2,10},{10,2},{3,11},{11,3},{4,12},{12,4},... | collective-permute-start | bytes 1179656 | tf_op jit(solution)/shard_map/ppermute | solution.py:763
  202.1 8.5 %collective-permute-start.42 = (bf16[48,1024]{1,0:T(8,128)(2,1)S(1)}, bf16[48,1024]{1,0:T(8,128)(2,1)S(1)}, u32[]{:S(2)}, u32[]{:S(2)}) collective-permute-start(bf16[48,1024]{1,0:T(8,128)(2,1)S(1)} %get-tuple-element.203), channel_id=1, source_target_pairs={{0,4},{2,6},{4,0},{6,2},{1,5},{3,7},{5,1},{7,3},{8,12},{10,14},{12... | collective-permute-start | bytes 294920 | tf_op jit(solution)/shard_map/ppermute | solution.py:231
  202.1 8.5 %collective-permute-start.43 = (bf16[48,1024]{1,0:T(8,128)(2,1)S(1)}, bf16[48,1024]{1,0:T(8,128)(2,1)S(1)}, u32[]{:S(2)}, u32[]{:S(2)}) collective-permute-start(bf16[48,1024]{1,0:T(8,128)(2,1)S(1)} %get-tuple-element.204), channel_id=1, source_target_pairs={{0,2},{2,4},{4,6},{6,0},{1,3},{3,5},{5,7},{7,1},{8,10},{10,12},{12... | collective-permute-start | bytes 294920 | tf_op jit(solution)/shard_map/ppermute | solution.py:231
  (45 other events, 288.8 us)

commit v4 on v3

--- a/solution.py
+++ b/solution.py
@@ -251,7 +251,7 @@
     span, idx, in_proj, norm, moe, router, taps, cbias, select, step, sbias, decay, skip, up,
     mine_o, send_o, ch_o, up_o, rows_s, block_s, sem,
 ):
-    copy = pltpu.make_async_copy(up.at[:, pl.ds(0, up_o.shape[1])], up_o, sem)
+    copy = pltpu.make_async_copy(up.at[0, pl.ds(0, up_o.shape[0])], up_o, sem)
     copy.start()
     dr = in_proj.shape[0]
     er, sel_n = select.shape
@@ -285,12 +285,27 @@
     copy.wait()
 
 
-def split_kernel(up, down, up_o, down_a, down_b, sem):
-    copies = [
-        pltpu.make_async_copy(up.at[:, pl.ds(up.shape[1] - up_o.shape[1], up_o.shape[1])], up_o, sem.at[0]),
-        pltpu.make_async_copy(down.at[:, pl.ds(0, down_a.shape[1])], down_a, sem.at[1]),
-        pltpu.make_async_copy(down.at[:, pl.ds(down_a.shape[1], down_b.shape[1])], down_b, sem.at[2]),
-    ]
+def cut_rows(sizes, hidden):
+    parts, at = [], 0
+    for size in sizes:
+        spans, end = [], at + size
+        if at < hidden:
+            spans.append((0, at, 0, min(end, hidden) - at))
+        if end > hidden:
+            low = max(at, hidden)
+            spans.append((1, low - hidden, low - at, end - low))
+        parts.append(spans)
+        at = end
+    return parts
+
+
+def split_kernel(parts, up, down, *refs):
+    outs, sem = refs[:-1], refs[-1]
+    copies = []
+    for spans, out in zip(parts, outs, strict=True):
+        for which, row, at, size in spans:
+            source = (up, down)[which].at[0, pl.ds(row, size)]
+            copies.append(pltpu.make_async_copy(source, out.at[pl.ds(at, size)], sem.at[len(copies)]))
     for copy in copies:
         copy.start()
     for copy in copies:
@@ -350,6 +365,30 @@
     return jnp.concatenate([rows[half:], rows[:half]], axis=0)
 
 
+GROUP_TOKENS = 16
+
+
+def spread_rows(sel, first, states):
+    rows, n = sel.shape[0], GROUP_TOKENS
+    wide = (LANES, n * states)
+    pick = (iota(wide, 0) == first + iota(wide, 1) % states).astype(F32).astype(BF16)
+    values = split_mm(sel, pick)
+    own = iota((rows, n * states), 1) // states == iota((rows, n * states), 0) % n
+    values = jnp.where(own, values, 0.0).reshape(rows // n, n, n * states)
+    high = values.astype(BF16).astype(F32)
+    return jnp.concatenate([high, values - high], axis=1).astype(BF16)
+
+
+def two_terms(block):
+    high = block.astype(BF16).astype(F32)
+    return jnp.concatenate([high, block - high], axis=0).astype(BF16)
+
+
+def halves(block):
+    n = block.shape[0] // 2
+    return block[:n] + block[n:]
+
+
 def scan_kernel(
     rank, states, lens, sel_a, sel_b, xc, g1sel, small,
     ys_o, step_o, sel_o, keep_o, check_o,
@@ -445,12 +484,63 @@
     return jnp.sum(jnp.where(square, row[...].astype(F32), 0.0), axis=1, keepdims=True).astype(jnp.int32)
 
 
-def slot_hot(k, routes, rank, kept, capacity, tok):
-    inside = kept & (routes == k)
-    return (inside & (rank == iota((tok, capacity), 1))).astype(F32).astype(BF16)
-
-
-def moe_enter_kernel(experts, capacity, lens, tok, cot, routes, mine, got, dnat, disp_o, hidden_o, gate_o):
+class Slots:
+    def __init__(self, capacity, width):
+        self.full, left = divmod(capacity, 8)
+        self.split = 0 < left <= 4
+        if left > 4:
+            self.full += 1
+        self.width = width
+        self.lanes = self.full * width + (width // 2 if self.split else 0)
+
+    def rows(self, groups):
+        return groups * 8 * self.full + (groups * 4 if self.split else 0)
+
+    def hot(self, routes, rank, kept, experts, first, low, high):
+        shape = (rank.shape[0], 8 * experts)
+        place = iota(shape, 1)
+        row = place % 8
+        inside = kept & (routes == place // 8) & (rank == first + row - low)
+        return jnp.where(inside & (row >= low) & (row < high), 1.0, 0.0).astype(BF16)
+
+    def hots(self, routes, rank, kept, experts):
+        args = (routes, rank, kept, experts)
+        whole = [self.hot(*args, 8 * i, 0, 8) for i in range(self.full)]
+        last = [self.hot(*args, 8 * self.full, 4 * i, 4 * i + 4) for i in range(2)] if self.split else []
+        return whole, last
+
+    def unpack(self, groups, both, tail_s):
+        at, width, height = 0, self.width, groups[0].shape[0]
+        for group in groups:
+            for i in range(self.full):
+                both[at : at + height] = group[:, i * width : (i + 1) * width]
+                at += height
+        if self.split:
+            half, start, count = width // 2, 0, height // 8
+            for group in groups:
+                block = group[:, self.full * width :].astype(F32)
+                for k in range(count):
+                    tail_s[start + 4 * k : start + 4 * k + 4, :half] = block[8 * k : 8 * k + 4]
+                    tail_s[start + 4 * k : start + 4 * k + 4, half:] = block[8 * k + 4 : 8 * k + 8]
+                start += 4 * count
+            both[at : at + start] = tail_s[:start].astype(BF16)
+
+    def pack(self, rows, which, count, out, tail_s):
+        width, height = self.width, out.shape[0]
+        at = which * self.full * height
+        for i in range(self.full):
+            out[:, i * width : (i + 1) * width] = rows[at : at + height].astype(out.dtype)
+            at += height
+        if self.split:
+            half = width // 2
+            at = count * self.full * height + which * height // 2
+            for k in range(height // 8):
+                tail_s[8 * k : 8 * k + 4, :half] = rows[at + 4 * k : at + 4 * k + 4, :half]
+                tail_s[8 * k + 4 : 8 * k + 8, :half] = rows[at + 4 * k : at + 4 * k + 4, half:]
+            out[:, self.full * width :] = tail_s[:height, :half].astype(out.dtype)
+
+
+def moe_enter_kernel(slots, experts, capacity, lens, tok, cot, routes, mine, got, dnat, disp_o, hidden_o, gate_o):
     rows, width = tok.shape
     routes = column_of(routes)
     hidden = tok[...].astype(F32) + (mine[...] + got[...])
@@ -464,79 +554,111 @@
     valid_f, _, rank, kept = route_tables(lens, routes, experts, capacity, rows)
     back = (cot[...].astype(F32) * valid_f * (gate * kept.astype(F32))).astype(BF16)
     both = jnp.concatenate([mv, back], axis=1)
-    for k in range(experts):
-        disp_o[k] = mm(slot_hot(k, routes, rank, kept, capacity, rows), both, TN).astype(BF16)
-
-
-def fill_rows(groups, rows_s, both_s):
-    at = 0
-    for group in groups:
-        for i in range(group.shape[0]):
-            rows_s[at : at + group.shape[1]] = group[i].astype(F32)
-            at += group.shape[1]
-    both_s[...] = rows_s[...].astype(BF16)
-
-
-def hidden_units(both_s, up, down):
+    whole, last = slots.hots(routes, rank, kept, experts)
+    span = slots.width
+    for i, hot in enumerate(whole):
+        disp_o[:, i * span : (i + 1) * span] = mm(hot, both, TN).astype(BF16)
+    if last:
+        end = mm(last[0], both[:, : span // 2], TN) + mm(last[1], both[:, span // 2 :], TN)
+        disp_o[:, slots.full * span :] = end.astype(BF16)
+
+
+def half_units(both, up, span):
     width = up.shape[1]
-    pre = mm(both_s[:, :width], up, NT)
-    g_act = mm(both_s[:, width:], down, NT)
+    pre = mm(both[:, :width], up[span], NT)
     sq = pre * pre
     th = jnp.tanh(GELU_C * (pre + GELU_K * sq * pre))
     act = (0.5 * pre * (1.0 + th)).astype(BF16)
-    slope = 0.5 * (1.0 + th) + 0.5 * pre * (1.0 - th * th) * (GELU_C * (1.0 + 3.0 * GELU_K * sq))
-    return act, (g_act * slope).astype(BF16)
-
-
-def expert_kernel(
-    own, peer, up, down, up_a, up_b, down_a, down_b,
-    out_own, out_peer, rows_s, both_s, acc_s, up_s, down_s, sem,
-):
-    copies = []
-    for parts, held in (((up, up_a, up_b), up_s), ((down, down_a, down_b), down_s)):
-        at = 0
-        for part in parts:
-            to = held.at[pl.ds(at, part.shape[1])]
-            copies.append(pltpu.make_async_copy(part.at[0], to, sem.at[len(copies)]))
-            at += part.shape[1]
+    return act, 0.5 * (1.0 + th) + 0.5 * pre * (1.0 - th * th) * (GELU_C * (1.0 + 3.0 * GELU_K * sq))
+
+
+def moves_of(parts, refs, targets, which_of):
+    moves = []
+    for spans, ref in zip(parts, refs, strict=True):
+        for which, row, at, size in spans:
+            if which in which_of:
+                moves.append((ref.at[pl.ds(at, size)], targets[which].at[pl.ds(row, size)]))
+    return moves
+
+
+PART = 256
+
+
+def expert_own_kernel(slots, parts, own, peer, up, down, *refs):
+    others = refs[: len(parts)]
+    both, acc, act_o, slope_o, up_o, up_s, down_s, tail_s, sem = refs[len(parts) :]
+    moves = [(up.at[0], up_s), (down.at[0], down_s)] + moves_of(parts, others, (up_o, None), (0,))
+    copies = [pltpu.make_async_copy(a, b, sem.at[k]) for k, (a, b) in enumerate(moves)]
     for copy in copies:
         copy.start()
-    hidden = down.shape[1]
-    count, capacity = own.shape[:2]
-    fill_rows((own, peer), rows_s, both_s)
-    width = own.shape[2] // 2
-    part = 256
+    slots.unpack((own, peer), both, tail_s)
+    width = up.shape[2]
     for copy in copies:
         copy.wait()
-    for f in range(0, 2 * hidden, part):
-        span = slice(f, f + part)
-        act, g_pre = hidden_units(both_s, up_s[span], down_s[span])
+    for f in range(0, up_s.shape[0], PART):
+        span = slice(f, f + PART)
+        act, slope = half_units(both, up_s, span)
+        g_pre = (mm(both[:, width:], down_s[span], NT) * slope).astype(BF16)
         e_part = mm(act, down_s[span])
         i_part = mm(g_pre, up_s[span])
         if f == 0:
-            acc_s[:, :width] = e_part
-            acc_s[:, width:] = i_part
+            acc[:, :width] = e_part
+            acc[:, width:] = i_part
         else:
-            acc_s[:, :width] += e_part
-            acc_s[:, width:] += i_part
-    for i in range(count):
-        out_own[i] = acc_s[i * capacity : (i + 1) * capacity]
-        out_peer[i] = acc_s[(count + i) * capacity : (count + i + 1) * capacity].astype(BF16)
-
-
-def expert_grad_kernel(own, peer, own_y, peer_y, up, down, up_g, down_g, rows_s, both_s):
-    fill_rows((own, peer, own_y, peer_y), rows_s, both_s)
-    width = own.shape[2] // 2
-    part = 256
-    for f in range(0, up.shape[1], part):
-        span = slice(f, f + part)
-        act, g_pre = hidden_units(both_s, up[0, span], down[0, span])
-        down_g[0, span] = mm(act, both_s[:, width:], TN)
-        up_g[0, span] = mm(g_pre, both_s[:, :width], TN)
+            acc[:, :width] += e_part
+            acc[:, width:] += i_part
+        act, slope = half_units(both, up_o, span)
+        act_o[:, span] = act
+        slope_o[:, span] = slope
+
+
+def expert_other_kernel(slots, parts, both, acc, act, slope, up, *refs):
+    others = refs[: len(parts)]
+    out_own, out_peer, acc_s, down_s, tail_s, sem = refs[len(parts) :]
+    moves = moves_of(parts, others, (None, down_s), (1,))
+    copies = [pltpu.make_async_copy(a, b, sem.at[k]) for k, (a, b) in enumerate(moves)]
+    for copy in copies:
+        copy.start()
+    width = up.shape[1]
+    for copy in copies:
+        copy.wait()
+    for f in range(0, up.shape[0], PART):
+        span = slice(f, f + PART)
+        g_pre = (mm(both[:, width:], down_s[span], NT) * slope[:, span]).astype(BF16)
+        e_part = mm(act[:, span], down_s[span])
+        i_part = mm(g_pre, up[span])
+        old = acc if f == 0 else acc_s
+        acc_s[:, :width] = old[:, :width] + e_part
+        acc_s[:, width:] = old[:, width:] + i_part
+    slots.pack(acc_s, 1, 2, out_peer, tail_s)
+    slots.pack(acc_s, 0, 2, out_own, tail_s)
+
+
+def unit_grads(both, up, down, up_g, down_g, more):
+    width = up.shape[2]
+    for f in range(0, up.shape[1], PART):
+        span = slice(f, f + PART)
+        act, slope = half_units(both, up.at[0], span)
+        g_pre = (mm(both[:, width:], down[0, span], NT) * slope).astype(BF16)
+        to_down = mm(act, both[:, width:], TN)
+        to_up = mm(g_pre, both[:, :width], TN)
+        if more is not None:
+            to_up, to_down = to_up + more[0][0, span], to_down + more[1][0, span]
+        down_g[0, span] = to_down
+        up_g[0, span] = to_up
+
+
+def near_grad_kernel(both, up, down, up_g, down_g):
+    unit_grads(both, up, down, up_g, down_g, None)
+
+
+def far_grad_kernel(slots, own_y, peer_y, up, down, up_near, down_near, up_g, down_g, both_s, tail_s):
+    slots.unpack((own_y, peer_y), both_s, tail_s)
+    unit_grads(both_s, up, down, up_g, down_g, (up_near, down_near))
 
 
 def moe_leave_kernel(
-    experts, capacity, lens, routes, cot, hidden, gate_in, dnat, back,
+    slots, experts, capacity, lens, routes, cot, hidden, gate_in, dnat, back,
     out_o, ghid_o, gbr_o, dgrad_o,
 ):
     rows, width = hidden.shape
@@ -544,9 +666,14 @@
     valid_f, _, rank, kept = route_tables(lens, routes, experts, capacity, rows)
     kept_f = kept.astype(F32)
     gate = gate_in[:, 0:1]
+    whole, last = slots.hots(routes, rank, kept, experts)
+    span = slots.width
     picked = jnp.zeros((rows, 2 * width), F32)
-    for k in range(experts):
-        picked = picked + mm(slot_hot(k, routes, rank, kept, capacity, rows), back[k])
+    for i, hot in enumerate(whole):
+        picked = picked + mm(hot, back[:, i * span : (i + 1) * span])
+    if last:
+        end = back[:, slots.full * span :]
+        picked = picked + jnp.concatenate([mm(last[0], end), mm(last[1], end)], axis=1)
     ex_out = picked[:, :width]
     sent = picked[:, width:]
     hid = hidden[...]
@@ -595,11 +722,10 @@
 def scan_back_kernel(
     rank, states, gy_s, xc, step_pre, sel, keep, small, g1sel, check,
     gsel_o, gxcs_o, gsr_o, q_o, smallg_o,
-    dm_s, dx_s, gdx_s, gdl_s, wr_s, rd_s, gwr_s, grd_s, rate_s, lam_s, ga_s,
+    dm_s, dx_s, gdx_s, gdl_s, wr_s, rd_s, gwr_s, grd_s, rate_s, lam_s, ga_s, write_s, hb_s, lb_s, wb_s,
 ):
     rows, inner = gy_s.shape
     tok = rows // 2
-    half = states // 2
     xcf = xc[...].astype(F32)
     skip = small[ROW_SKIP : ROW_SKIP + 1]
     delta = softplus(step_pre[...])
@@ -612,66 +738,70 @@
     rate_s[...] = jnp.exp(small[ROW_DECAY : ROW_DECAY + states]) * (-LOG2E)
     lam_s[...] = jnp.zeros_like(lam_s)
     ga_s[...] = jnp.zeros_like(ga_s)
-    gwr_s[...] = jnp.zeros_like(gwr_s)
-    grd_s[...] = jnp.zeros_like(grd_s)
+    write_s[...] = spread_rows(sel[...], rank, states)
     shape = (states, LANES)
+    n = GROUP_TOKENS
+    count = tok // n
+    wide = (n, n * states)
+    own = iota(wide, 1) // states == iota(wide, 0)
+    group = own.astype(F32).astype(BF16)
+    for ref in (hb_s, lb_s, wb_s):
+        ref[...] = jnp.zeros_like(ref)
+
+    def sums(b, ci):
+        span = pl.ds(pl.multiple_of(b * tok + ci * n, n), n)
+        gdx_s[span, :] = halves(mm(write_s[b * count + ci], lb_s[b]))
+        gdl_s[span, :] = mm(group, wb_s[b])
+        grd_s[span, :] = jnp.where(own, halves(mm(two_terms(gy_s[span, :]), hb_s[b], NT)), 0.0)
+        gwr_s[span, :] = jnp.where(own, halves(mm(two_terms(dx_s[span, :]), lb_s[b], NT)), 0.0)
 
     def chunk(i, carry):
-        ci = tok // 8 - 1 - i
-        t0 = pl.multiple_of(ci * 8, 8)
+        ci = count - 1 - i
+        sums(1, jnp.minimum(ci + 1, count - 1))
         for b in range(2):
-            at = pl.multiple_of(b * tok + t0, 8)
-            wr8 = pltpu.roll(wr_s[b], tok - t0, 1)
-            rd8 = pltpu.roll(rd_s[b], tok - t0, 1)
-            wcol = [jnp.broadcast_to(wr8[:, j : j + 1], shape) for j in range(8)]
-            rcol = [jnp.broadcast_to(rd8[:, j : j + 1], shape) for j in range(8)]
-            grd = [jnp.zeros(shape, F32)] * 8
-            gwr = [jnp.zeros(shape, F32)] * 8
-            for g in range(inner // LANES):
-                lanes = slice(g * LANES, (g + 1) * LANES)
-                h = check[ci * 2 + b, :, lanes]
-                rate = rate_s[:, lanes]
-                dm8 = dm_s[pl.ds(at, 8), lanes]
-                dx8 = dx_s[pl.ds(at, 8), lanes]
-                gy8 = gy_s[pl.ds(at, 8), lanes]
-                decays, olds = [], []
-                for j in range(8):
-                    d = jnp.broadcast_to(dm8[j : j + 1], shape)
-                    x = jnp.broadcast_to(dx8[j : j + 1], shape)
-                    a = jnp.exp2(d * rate)
-                    old = a * h
-                    h = old + wcol[j] * x
-                    grd[j] = grd[j] + h * jnp.broadcast_to(gy8[j : j + 1], shape)
-                    decays.append(a)
-                    olds.append(old)
-                lam_in = lam_s[b, :, lanes]
-                ga = ga_s[:, lanes]
-                to_dx, to_dl = [None] * 8, [None] * 8
-                for j in range(7, -1, -1):
-                    lam = rcol[j] * jnp.broadcast_to(gy8[j : j + 1], shape) + lam_in
-                    lam_in = decays[j] * lam
-                    w = lam * olds[j]
-                    ga = ga + w * jnp.broadcast_to(dm8[j : j + 1], shape)
-                    p = lam * wcol[j]
-                    to_dx[j] = p[:half] + p[half:]
-                    p = w * rate
-                    to_dl[j] = p[:half] + p[half:]
-                    gwr[j] = gwr[j] + lam * jnp.broadcast_to(dx8[j : j + 1], shape)
-                lam_s[b, :, lanes] = lam_in
-                ga_s[:, lanes] = ga
-                gdx_s[pl.ds(at, 8), lanes] = fold(to_dx)
-                gdl_s[pl.ds(at, 8), lanes] = fold(to_dl)
-            lane = iota(shape, 1)
-            all_wr, all_rd = gwr_s[b], grd_s[b]
-            for j in range(8):
-                here = lane == t0 + j
-                all_wr = jnp.where(here, jnp.sum(gwr[j], axis=1, keepdims=True), all_wr)
-                all_rd = jnp.where(here, jnp.sum(grd[j], axis=1, keepdims=True), all_rd)
-            gwr_s[b] = all_wr
-            grd_s[b] = all_rd
+            for part in range(n // 8 - 1, -1, -1):
+                t0 = pl.multiple_of(ci * n + part * 8, 8)
+                at = pl.multiple_of(b * tok + t0, 8)
+                wr8 = pltpu.roll(wr_s[b], tok - t0, 1)
+                rd8 = pltpu.roll(rd_s[b], tok - t0, 1)
+                wcol = [jnp.broadcast_to(wr8[:, j : j + 1], shape) for j in range(8)]
+                rcol = [jnp.broadcast_to(rd8[:, j : j + 1], shape) for j in range(8)]
+                for g in range(inner // LANES):
+                    lanes = slice(g * LANES, (g + 1) * LANES)
+                    h = check[(ci * (n // 8) + part) * 2 + b, :, lanes]
+                    rate = rate_s[:, lanes]
+                    dm8 = dm_s[pl.ds(at, 8), lanes]
+                    dx8 = dx_s[pl.ds(at, 8), lanes]
+                    gy8 = gy_s[pl.ds(at, 8), lanes]
+                    decays, olds = [], []
+                    for j in range(8):
+                        k = part * 8 + j
+                        d = jnp.broadcast_to(dm8[j : j + 1], shape)
+                        x = jnp.broadcast_to(dx8[j : j + 1], shape)
+                        a = jnp.exp2(d * rate)
+                        old = a * h
+                        h = old + wcol[j] * x
+                        hb_s[b, k * states : (k + 1) * states, lanes] = h.astype(BF16)
+                        decays.append(a)
+                        olds.append(old)
+                    lam_in = lam_s[b, :, lanes]
+                    ga = ga_s[:, lanes]
+                    for j in range(7, -1, -1):
+                        k = part * 8 + j
+                        lam = rcol[j] * jnp.broadcast_to(gy8[j : j + 1], shape) + lam_in
+                        lam_in = decays[j] * lam
+                        w = lam * olds[j]
+                        ga = ga + w * jnp.broadcast_to(dm8[j : j + 1], shape)
+                        lb_s[b, k * states : (k + 1) * states, lanes] = lam.astype(BF16)
+                        wb_s[b, k * states : (k + 1) * states, lanes] = (w * rate).astype(BF16)
+                    lam_s[b, :, lanes] = lam_in
+                    ga_s[:, lanes] = ga
+            if b == 0:
+                sums(0, ci)
         return carry
 
-    lax.fori_loop(0, tok // 8, chunk, 0)
+    lax.fori_loop(0, count, chunk, 0)
+    sums(1, 0)
     delta = softplus(step_pre[...])
     gdx = gdx_s[...]
     xcf = xc[...].astype(F32)
@@ -685,12 +815,11 @@
     q_o[...] = jnp.where(lane >= tail, pltpu.roll(sel[...], tail, 1), 0.0).astype(BF16)
     back = jnp.where(lane >= tail, mm(gsr, g1sel[...]), 0.0)
     back = pltpu.roll(back, rank, 1)
-    zeros_top = jnp.zeros((rank, tok), F32)
-    zeros_end = jnp.zeros((LANES - rank - 2 * states, tok), F32)
-    for b in range(2):
-        stack = jnp.concatenate([zeros_top, gwr_s[b], grd_s[b], zeros_end], axis=0)
-        span = slice(b * tok, (b + 1) * tok)
-        gsel_o[span] = back[span] + jnp.transpose(stack)
+    tall = (n * states, LANES)
+    place = iota(tall, 0) % states
+    to_wr = (iota(tall, 1) == rank + place).astype(F32).astype(BF16)
+    to_rd = (iota(tall, 1) == rank + states + place).astype(F32).astype(BF16)
+    gsel_o[...] = back + split_mm(gwr_s[...], to_wr) + split_mm(grd_s[...], to_rd)
     smallg_o[0:ROW_STEP] = jnp.zeros((ROW_STEP, inner), F32)
     smallg_o[ROW_STEP : ROW_STEP + 1] = jnp.sum(g_step, axis=0, keepdims=True)
     smallg_o[ROW_SKIP : ROW_SKIP + 1] = jnp.sum(gy * xcf, axis=0, keepdims=True)
@@ -763,6 +892,12 @@
     return lax.ppermute(values, axis, [(0, 1), (1, 0)])
 
 
+def exchange(rows, count):
+    parts = rows.reshape(count, 8, rows.shape[1])
+    parts = lax.all_to_all(parts, ("z", "x"), split_axis=0, concat_axis=0, tiled=True)
+    return parts.reshape(rows.shape)
+
+
 def share_kernel(n1, n2, rank, states, *refs):
     one, two = refs[:n1], refs[n1 : n1 + n2]
     keep_o, send_o, outg_o, select_o, step_o, taps_o, cbias_o, sbias_o, skip_o, decay_o, square_s = refs[n1 + n2 :]
@@ -863,10 +998,12 @@
 
     span = nf * er
     hid = up_weight.shape[1]
-    first, second = hid // 2, hid // 6
+    sizes = [hid * 26 // 48, hid * 28 // 48]
+    sizes.append(2 * hid - sum(sizes))
+    parts = cut_rows(sizes, hid)
     mine_w, send_w, ch, up_send = call(
         functools.partial(pack_kernel, span),
-        [((dr, 2 * inner + LANES), BF16), ((dr, 2 * inner + LANES), BF16), ((er, 2 * LANES), BF16), ((1, first, width), BF16, HBM)],
+        [((dr, 2 * inner + LANES), BF16), ((dr, 2 * inner + LANES), BF16), ((er, 2 * LANES), BF16), ((sizes[0], width), BF16)],
         [idx]
         + [
             in_hbm(v)
@@ -888,17 +1025,18 @@
     tok2 = jnp.concatenate([tokens, swap(tokens, "c")], axis=0)
     lens2 = jnp.concatenate([seq_lens, swap(seq_lens, "c")], axis=0)
     up_one = swap(up_send, "y")
-    up_send, down_send, down_rest = call(
-        split_kernel,
-        [((1, hid - first, width), BF16, HBM), ((1, second, width), BF16, HBM), ((1, hid - second, width), BF16, HBM)],
-        [in_hbm(up_weight), in_hbm(down_weight)],
+    sends = call(
+        functools.partial(split_kernel, parts[1:]),
+        [((size, width), BF16) for size in sizes[1:]],
+        [in_hbm(after(up_weight, group1)), in_hbm(down_weight)],
         [HBM, HBM],
-        scratch=[pltpu.SemaphoreType.DMA((3,))],
+        scratch=[pltpu.SemaphoreType.DMA((2 * len(sizes),))],
         name="split",
         us=2,
     )
-    up_one = after(up_one, up_send)
-    pieces1, pieces2 = plan.gather([group1, group2], up_one)
+    up_one = after(up_one, sends[0])
+    pieces1, pieces2 = plan.gather([group1, group2], (up_one, tok2, lens2))
+
     fetch_sem = pltpu.SemaphoreType.DMA((ng,))
     emit_sem = pltpu.SemaphoreType.DMA((2 * ng,))
     u, xin, xc, selp, small_t, dnat, g1 = call(
@@ -911,9 +1049,8 @@
     )
     selq = swap(selp, "c")
     middle = (pieces2[min(2, len(pieces2) - 1)], xc)
-    up_two = swap(after(up_send, middle), "y")
-    down_one = swap(after(down_send, middle), "y")
-    down_two = swap(after(down_rest, (up_two, down_one)), "y")
+    part_two = swap(after(sends[0], middle), "y")
+    part_three = swap(after(sends[1], middle), "y")
     g1sel_spec = pl.BlockSpec((inner, LANES), lambda i: (0, inner // LANES))
     chunks = tok // 8
     ys, step_pre, sel, keep, check = call(
@@ -933,41 +1070,59 @@
         scratch=[fetch_sem],
         name="gate",
     )
-    br_got = after(swap(br_send, "c"), (up_two, down_one))
+    br_got = swap(br_send, "c")
+    slots = Slots(capacity, 2 * width)
     disp, hidden, gate = call(
-        functools.partial(moe_enter_kernel, experts, capacity),
-        [((experts, capacity, 2 * width), BF16), kept((tok, width), F32), kept((tok, LANES), F32)],
+        functools.partial(moe_enter_kernel, slots, experts, capacity),
+        [kept((8 * experts, slots.lanes), BF16), kept((tok, width), F32), kept((tok, LANES), F32)],
         [seq_lens, tokens, in_hbm(cotangent), routes.T, br_mine, br_got, in_hbm(dnat)],
         [SMEM] + [None] * 6,
         name="moe_enter",
     )
-    line = lax.all_to_all(disp, ("z", "x"), split_axis=0, concat_axis=0, tiled=True)
+    disp = after(disp, part_two)
+    line = exchange(disp, nf)
     peer = swap(line, "c")
     line_y = swap(line, "y")
-    peer_y = swap(line_y, "c")
-    total = 2 * nf * capacity
+    total = slots.rows(2 * nf)
+    tail = max(slots.rows(2 * nf), 8)
+    weight_s = pltpu.VMEM((hid, width), BF16)
+    tail_s = pltpu.VMEM((tail, 2 * width), F32)
+    early = sum(1 for spans in parts for span in spans if span[0] == 0)
+    both, acc, act, slope, up_near = call(
+        functools.partial(expert_own_kernel, slots, parts[:-1]),
+        [((total, 2 * width), BF16), ((total, 2 * width), F32), ((total, hid), BF16), ((total, hid), F32), ((hid, width), BF16)],
+        [line, peer, in_hbm(up_weight), in_hbm(down_weight), up_one, part_two],
+        [None, None] + [HBM] * 4,
+        scratch=[weight_s, weight_s, tail_s, pltpu.SemaphoreType.DMA((2 + early,))],
+        name="expert_own",
+        us=6,
+    )
     out_own, out_peer = call(
-        expert_kernel,
+        functools.partial(expert_other_kernel, slots, parts[1:]),
         [(line.shape, F32), (line.shape, BF16)],
-        [line, peer] + [in_hbm(w) for w in (up_weight, down_weight, up_one, up_two, down_one, down_two)],
-        [None, None] + [HBM] * 6,
-        scratch=[pltpu.VMEM((total, 2 * width), F32), pltpu.VMEM((total, 2 * width), BF16), pltpu.VMEM((total, 2 * width), F32), pltpu.VMEM((2 * hid, width), BF16), pltpu.VMEM((2 * hid, width), BF16), pltpu.SemaphoreType.DMA((6,))],
-        name="expert",
-        us=5,
-    )
+        [both, acc, act, slope, up_near, part_two, part_three],
+        [None] * 5 + [HBM] * 2,
+        scratch=[pltpu.VMEM((total, 2 * width), F32), weight_s, tail_s, pltpu.SemaphoreType.DMA((3,))],
+        name="expert_other",
+        us=3,
+    )
+    grads = [((1, hid, width), F32)] * 2
+    weights = [in_hbm(up_weight), in_hbm(down_weight)]
+    near = call(near_grad_kernel, grads, [both] + weights, name="near_grad", us=4)
+    peer_y = swap(after(line_y, near[0]), "c")
     up_grad, down_grad = call(
-        expert_grad_kernel,
-        [((1, hid, width), F32)] * 2,
-        [line, peer, line_y, peer_y, in_hbm(up_weight), in_hbm(down_weight)],
-        scratch=[pltpu.VMEM((2 * total, 2 * width), F32), pltpu.VMEM((2 * total, 2 * width), BF16)],
-        name="expert_grad",
-        us=7,
-    )
-    summed = (out_own + swap(after(out_peer, line_y), "c").astype(F32)).astype(BF16)
-    back = lax.all_to_all(summed, ("z", "x"), split_axis=0, concat_axis=0, tiled=True)
+        functools.partial(far_grad_kernel, slots),
+        grads,
+        [line_y, peer_y] + weights + near,
+        scratch=[pltpu.VMEM((total, 2 * width), BF16), tail_s],
+        name="far_grad",
+        us=8,
+    )
+    summed = (out_own + swap(out_peer, "c").astype(F32)).astype(BF16)
+    back = exchange(summed, nf)
     back = after(back, up_grad)
     result, ghid, gbr, dgrad = call(
-        functools.partial(moe_leave_kernel, experts, capacity),
+        functools.partial(moe_leave_kernel, slots, experts, capacity),
         [((tok, width), BF16), ((tok, width), F32), ((tok, width), BF16), ((dn, width), F32)],
         [in_hbm(seq_lens), in_hbm(routes.T), in_hbm(cotangent), in_hbm(hidden), in_hbm(gate), in_hbm(dnat), back],
         [SMEM] + [None] * 6,
@@ -987,7 +1142,7 @@
         [((rows, LANES), F32), ((rows, inner), F32), ((rows, inner), BF16), ((rows, LANES), BF16), ((small_n, inner), F32)],
         [gy, xc, step_pre, sel, keep, small_t, g1, in_hbm(check)],
         [None] * 6 + [g1sel_spec, None],
-        scratch=[pltpu.VMEM((rows, inner), F32)] * 4 + [pltpu.VMEM((2, states, tok), F32)] * 4 + [pltpu.VMEM((states, inner), F32), pltpu.VMEM((2, states, inner), F32), pltpu.VMEM((states, inner), F32)],
+        scratch=[pltpu.VMEM((rows, inner), F32)] * 4 + [pltpu.VMEM((2, states, tok), F32)] * 2 + [pltpu.VMEM((rows, GROUP_TOKENS * states), F32)] * 2 + [pltpu.VMEM((states, inner), F32), pltpu.VMEM((2, states, inner), F32), pltpu.VMEM((states, inner), F32), pltpu.VMEM((rows // GROUP_TOKENS, 2 * GROUP_TOKENS, GROUP_TOKENS * states), BF16)] + [pltpu.VMEM((2, GROUP_TOKENS * states, inner), BF16)] * 3,
         name="scan_back",
         us=16,
     )

time: 215 us -> 198 us (0.921)
  waiting for transfers between devices: 81.6 us -> 62 us
  starting transfers between devices: 49.5 us -> 53.1 us
    ppermute x33 -> x32, waiting for transfers between devices: 43.1 us -> 29.5 us  [swap(): return lax.ppermute(values, axis, [(0, 1), (1, 0)])]
    all_to_all x2, waiting for transfers between devices: 19.6 us -> 11.4 us  [exchange(): lax.all_to_all(parts, ('z', 'x'), split_axis=0, concat_axis=0, tiled=True)]
    ppermute x6, starting transfers between devices: 4.18 us -> 8.86 us  [reduce3(): lax.ppermute(parts[k], 'z', [(i, (i - k) % 4) for i in range(4)])]
    ppermute x33 -> x32, starting transfers between devices: 25.1 us -> 24.2 us  [swap(): return lax.ppermute(values, axis, [(0, 1), (1, 0)])]
    pallas_call x21 -> x23, Pallas kernels: 76.2 us -> 76.6 us  [call(): pl.pallas_call(kernel, grid=(1,) if windowed else (), out_shape=[(pltpu.H...]
  transfers between devices with their start and end apart: 47 -> 46, of which waited for: 27 -> 25; matrix products, arithmetic and copies ran while one was open for 1% -> 1% of each run, Pallas kernels for 29% -> 33%
where the time goes in v4:
time: 198 us; the launch traced here: 197 us
  Pallas kernels  76.6 us (39%)
  waiting for transfers between devices  62 us (31%)
  starting transfers between devices  53.1 us (27%)
  local copies, waits for them, and re-layouts  3.28 us (2%)
    pallas_call x23, Pallas kernels, call(): pl.pallas_call(kernel, grid=(1,) if windowed else (), out_shape=[(pltpu.H...  76.6 us
    ppermute x32, waiting for transfers between devices, swap(): return lax.ppermute(values, axis, [(0, 1), (1, 0)])  29.5 us
    ppermute x32, starting transfers between devices, swap(): return lax.ppermute(values, axis, [(0, 1), (1, 0)])  24.2 us
    ppermute x6, waiting for transfers between devices, gather(): lax.ppermute(piece, 'z', [(i, (i + k) % 4) for i in range(4)])  12.2 us
    all_to_all x2, waiting for transfers between devices, exchange(): lax.all_to_all(parts, ('z', 'x'), split_axis=0, concat_axis=0, tiled=True)  11.4 us
    all_to_all x2, starting transfers between devices, exchange(): lax.all_to_all(parts, ('z', 'x'), split_axis=0, concat_axis=0, tiled=True)  10.8 us
    ppermute x6, starting transfers between devices, gather(): lax.ppermute(piece, 'z', [(i, (i + k) % 4) for i in range(4)])  9.28 us
    ppermute x6, waiting for transfers between devices, reduce3(): lax.ppermute(parts[k], 'z', [(i, (i - k) % 4) for i in range(4)])  8.95 us
  transfers between devices with their start and end apart: 46, of which 25 were waited for; matrix products, arithmetic and copies ran while one was open for 1% of the time, Pallas kernels for 33%

profile of v4, /device:TPU:0, one launch (start us, length us, event | category | flops | bytes accessed | tf_op | source)
XLA Modules:
  0.0 197.2 jit_solution(17125569275555866663)
XLA Ops:
  0.8 2.1 %pack.1 = (bf16[24,1664]{1,0:T(8,128)(2,1)S(1)}, bf16[24,1664]{1,0:T(8,128)(2,1)S(1)}, bf16[48,256]{1,0:T(8,128)(2,1)S(1)}, bf16[416,768]{1,0:T(8,128)(2,1)S(1)}) custom-call(s32[4]{0:T(128)S(1)} %pad_add_fusion.1.idx, bf16[24,3072]{1,0:T(8,128)(2,1)} %in_proj.3, bf16[1,24]{1,0:T(2,128)(2,1)} %bitcast.22, bf16[1,24]{1,0:T(2,128)(2,1)} %bitcast.28, ...), custom_call_target="tpu_custom_call" | custom-call | flops 300000000 | bytes 900000 | tf_op jit(solution)/shard_map/pack/pallas_call | solution.py:86
  2.9 3.0 %collective-permute-start.6 = (bf16[416,768]{1,0:T(8,128)(2,1)S(1)}, bf16[416,768]{1,0:T(8,128)(2,1)S(1)}, u32[]{:S(2)}, u32[]{:S(2)}) collective-permute-start(bf16[416,768]{1,0:T(8,128)(2,1)S(1)} %get-tuple-element.128), channel_id=1, source_target_pairs={{0,16},{16,0},{1,17},{17,1},{2,18},{18,2},{3,19},{19,3},{4,20},{20... | collective-permute-start | bytes 1916936 | tf_op jit(solution)/shard_map/ppermute | solution.py:892
  7.8 3.7 %collective-permute-start.5 = (bf16[48,1024]{1,0:T(8,128)(2,1)S(1)}, bf16[48,1024]{1,0:T(8,128)(2,1)S(1)}, u32[]{:S(2)}, u32[]{:S(2)}) collective-permute-start(bf16[48,1024]{1,0:T(8,128)(2,1)S(1)} %get-tuple-element.127), channel_id=1, source_target_pairs={{0,6},{2,0},{4,2},{6,4},{1,7},{3,1},{5,3},{7,5},{8,14},{10,8},{12,... | collective-permute-start | bytes 294920 | tf_op jit(solution)/shard_map/ppermute | solution.py:143
  14.6 6.3 %collective-permute-done.4 = bf16[48,1024]{1,0:T(8,128)(2,1)S(1)} collective-permute-done((bf16[48,1024]{1,0:T(8,128)(2,1)S(1)}, bf16[48,1024]{1,0:T(8,128)(2,1)S(1)}, u32[]{:S(2)}, u32[]{:S(2)}) %collective-permute-start.4) | collective-permute-done | bytes 98336 | tf_op jit(solution)/shard_map/ppermute | solution.py:143
  23.6 3.6 %collective-permute-start.14 = (bf16[48,1536]{1,0:T(8,128)(2,1)S(1)}, bf16[48,1536]{1,0:T(8,128)(2,1)S(1)}, u32[]{:S(2)}, u32[]{:S(2)}) collective-permute-start(bf16[48,1536]{1,0:T(8,128)(2,1)S(1)} %get-tuple-element.140), channel_id=1, source_target_pairs={{0,6},{2,0},{4,2},{6,4},{1,7},{3,1},{5,3},{7,5},{8,14},{10,8},{12,... | collective-permute-start | bytes 442376 | tf_op jit(solution)/shard_map/ppermute | solution.py:143
  28.2 3.6 %collective-permute-done.8.refs_2_ = bf16[192,1024]{1,0:T(8,128)(2,1)S(1)} collective-permute-done((bf16[192,1024]{1,0:T(8,128)(2,1)S(1)}, bf16[192,1024]{1,0:T(8,128)(2,1)S(1)}, u32[]{:S(2)}, u32[]{:S(2)}) %collective-permute-start.8) | collective-permute-done | bytes 393248 | tf_op jit(solution)/shard_map/ppermute | solution.py:892
  34.0 5.2 %collective-permute-done.13 = bf16[48,1536]{1,0:T(8,128)(2,1)S(1)} collective-permute-done((bf16[48,1536]{1,0:T(8,128)(2,1)S(1)}, bf16[48,1536]{1,0:T(8,128)(2,1)S(1)}, u32[]{:S(2)}, u32[]{:S(2)}) %collective-permute-start.13) | collective-permute-done | bytes 147488 | tf_op jit(solution)/shard_map/ppermute | solution.py:143
  41.0 5.9 %enter.1 = (bf16[256,768]{1,0:T(8,128)(2,1)S(1)}, f32[256,768]{1,0:T(8,128)}, bf16[256,768]{1,0:T(8,128)(2,1)S(1)}, f32[256,128]{1,0:T(8,128)S(1)}, f32[24,768]{...) custom-call(s32[4]{0:T(128)S(1)} %pad_add_fusion.1.idx, s32[2,8]{1,0:T(2,128)S(1)} %pad_add_fusion.lens, ...), custom_call_target="tpu_custom_call" | custom-call | flops 1500000000 | bytes 4500000 | tf_op jit(solution)/shard_map/enter/pallas_call | solution.py:86
  47.0 6.2 %collective-permute-done.16.refs_2_ = bf16[192,1536]{1,0:T(8,128)(2,1)S(1)} collective-permute-done((bf16[192,1536]{1,0:T(8,128)(2,1)S(1)}, bf16[192,1536]{1,0:T(8,128)(2,1)S(1)}, u32[]{:S(2)}, u32[]{:S(2)}) %collective-permute-start.16) | collective-permute-done | bytes 589856 | tf_op jit(solution)/shard_map/ppermute | solution.py:892
  56.0 8.0 %scan.1 = (f32[256,768]{1,0:T(8,128)S(1)}, f32[256,768]{1,0:T(8,128)}, f32[256,128]{1,0:T(8,128)}, f32[256,128]{1,0:T(8,128)}, f32[32,16,768]{2,1,0:T(8,128)}) custom-call(s32[2,8]{1,0:T(2,128)S(1)} %pad_add_fusion.lens, f32[256,128]{1,0:T(8,128)S(1)} %get-tuple-element.135.sel_a, f32[256,128]{1,0:T(8,128)S(1)} %collective-permute-done.11.sel_b, ...), custom_call_target="tpu_custom_call" | custom-call | flops 2700000000 | bytes 8100000 | tf_op jit(solution)/shard_map/scan/pallas_call | solution.py:86
  64.1 5.5 %gate.1 = (bf16[256,768]{1,0:T(8,128)(2,1)}, f32[256,768]{1,0:T(8,128)}, f32[128,768]{1,0:T(8,128)S(1)}, f32[128,768]{1,0:T(8,128)S(1)}, bf16[768,1536]{1,0:T(8,128)(2,1)S(1)}) custom-call(s32[4]{0:T(128)S(1)} %pad_add_fusion.1.idx, bf16[256,768]{1,0:T(8,128)(2,1)S(1)} %get-tuple-element.133.u, bf16[256,768]{1,0:T(8,128)(2,1)S(1)} %get-tuple-element.134.xc, ...), custom_call_target="tpu_custom_call" | custom-call | flops 1500000000 | bytes 4500000 | tf_op jit(solution)/shard_map/gate/pallas_call | solution.py:86
  71.4 2.6 %moe_enter.1 = (bf16[64,3840]{1,0:T(8,128)(2,1)}, f32[128,768]{1,0:T(8,128)}, f32[128,128]{1,0:T(8,128)}) custom-call(s32[1,8]{1,0:T(1,128)S(1)} %copy-done.20, bf16[128,768]{1,0:T(8,128)(2,1)S(1)} %copy-done.15, bf16[128,768]{1,0:T(8,128)(2,1)} %cot.3, s32[1,128]{1,0:T(1,128)S(1)} %bitcast.25, f32[128,768]{1,0:T(8,128)S(1)} %get-tuple-element.142.mine, ...), custom_call_target="tpu_custom_call" | custom-call | flops 1500000000 | bytes 4500000 | tf_op jit(solution)/shard_map/moe_enter/pallas_call | solution.py:86
  75.9 5.1 %all-to-all-start = ((bf16[8,8,3840]{2,1,0:T(8,128)(2,1)}), bf16[8,8,3840]{2,1,0:T(8,128)(2,1)}, u32[]{:S(2)}, u32[]{:S(2)}) async-start(bf16[8,8,3840]{2,1,0:T(8,128)(2,1)} %bitcast.26), calls=%async_computation | async-start | bytes 983040 | tf_op jit(solution)/shard_map/all_to_all | solution.py:897
  82.2 11.4 %all-to-all-done = bf16[8,8,3840]{2,1,0:T(8,128)(2,1)} async-done(((bf16[8,8,3840]{2,1,0:T(8,128)(2,1)}), bf16[8,8,3840]{2,1,0:T(8,128)(2,1)}, u32[]{:S(2)}, u32[]{:S(2)}) %all-to-all-start) | async-done | bytes 491552 | tf_op jit(solution)/shard_map/all_to_all | solution.py:897
  93.6 2.1 %collective-permute-done.21.peer = bf16[64,3840]{1,0:T(8,128)(2,1)S(1)} collective-permute-done((bf16[64,3840]{1,0:T(8,128)(2,1)}, bf16[64,3840]{1,0:T(8,128)(2,1)S(1)}, u32[]{:S(2)}, u32[]{:S(2)}) %collective-permute-start.21) | collective-permute-done | bytes 491552 | tf_op jit(solution)/shard_map/ppermute | solution.py:892
  97.9 5.5 %expert_own.1 = (bf16[320,1536]{1,0:T(8,128)(2,1)S(1)}, f32[320,1536]{1,0:T(8,128)S(1)}, bf16[320,768]{1,0:T(8,128)(2,1)S(1)}, f32[320,768]{1,0:T(8,128)S(1)}, bf16[768,768]{1,0:T(8,128)(2,1)S(1)}) custom-call(bf16[64,3840]{1,0:T(8,128)(2,1)} %bitcast.12.own, bf16[64,3840]{1,0:T(8,128)(2,1)S(1)} %collective-permute-done.21.peer, bf16[1,768,768]{2,1,0:T(8,128)(2,1)} %up.8, ...), custom_call_target="tpu_custom_call" | custom-call | flops 1800000000 | bytes 5400000 | tf_op jit(solution)/shard_map/expert_own/pallas_call | solution.py:86
  104.3 2.1 %expert_other.1 = (f32[64,3840]{1,0:T(8,128)S(1)}, bf16[64,3840]{1,0:T(8,128)(2,1)S(1)}) custom-call(bf16[320,1536]{1,0:T(8,128)(2,1)S(1)} %get-tuple-element.150.both, f32[320,1536]{1,0:T(8,128)S(1)} %get-tuple-element.151.acc, bf16[320,768]{1,0:T(8,128)(2,1)S(1)} %get-tuple-element.152.act, f32[320,768]{1,0:T(8,128)S(1)} %get-tuple-element.153.slope, ...), custom_call_target="tpu_custom_call" | custom-call | flops 900000000 | bytes 2700000 | tf_op jit(solution)/shard_map/expert_other/pallas_call | solution.py:86
  109.2 5.6 %all-to-all-start.1 = ((bf16[8,8,3840]{2,1,0:T(8,128)(2,1)}), bf16[8,8,3840]{2,1,0:T(8,128)(2,1)}, u32[]{:S(2)}, u32[]{:S(2)}) async-start(bf16[8,8,3840]{2,1,0:T(8,128)(2,1)} %fusion), calls=%async_computation.1 | async-start | bytes 983040 | tf_op jit(solution)/shard_map/all_to_all | solution.py:897
  114.9 4.6 %near_grad.1 = (f32[1,768,768]{2,1,0:T(8,128)S(1)}, f32[1,768,768]{2,1,0:T(8,128)S(1)}) custom-call(bf16[320,1536]{1,0:T(8,128)(2,1)S(1)} %copy-done.3, bf16[1,768,768]{2,1,0:T(8,128)(2,1)} %up.8, bf16[1,768,768]{2,1,0:T(8,128)(2,1)} %down.7), custom_call_target="tpu_custom_call" | custom-call | flops 1200000000 | bytes 3600000 | tf_op jit(solution)/shard_map/near_grad/pallas_call | solution.py:86
  120.5 2.1 %collective-permute-done.25.peer_y = bf16[64,3840]{1,0:T(8,128)(2,1)S(1)} collective-permute-done((bf16[64,3840]{1,0:T(8,128)(2,1)}, bf16[64,3840]{1,0:T(8,128)(2,1)S(1)}, u32[]{:S(2)}, u32[]{:S(2)}) %collective-permute-start.25) | collective-permute-done | bytes 491552 | tf_op jit(solution)/shard_map/ppermute | solution.py:892
  122.5 6.8 %far_grad.1 = (f32[1,768,768]{2,1,0:T(8,128)}, f32[1,768,768]{2,1,0:T(8,128)}) custom-call(bf16[64,3840]{1,0:T(8,128)(2,1)} %collective-permute-done.24.own_y, bf16[64,3840]{1,0:T(8,128)(2,1)S(1)} %collective-permute-done.25.peer_y, bf16[1,768,768]{2,1,0:T(8,128)(2,1)} %up.8, bf16[1,768,768]{2,1,0:T(8,128)(2,1)} %down.7, ...), custom_call_target="tpu_custom_call" | custom-call | flops 2400000000 | bytes 7200000 | tf_op jit(solution)/shard_map/far_grad/pallas_call | solution.py:86
  129.4 3.4 %moe_leave.1 = (bf16[128,768]{1,0:T(8,128)(2,1)}, f32[128,768]{1,0:T(8,128)S(1)}, bf16[128,768]{1,0:T(8,128)(2,1)S(1)}, f32[16,768]{1,0:T(8,128)S(1)}) custom-call(s32[1,8]{1,0:T(1,128)} %lens.3, s32[1,128]{1,0:T(1,128)} %bitcast.24, bf16[128,768]{1,0:T(8,128)(2,1)} %cot.3, f32[128,768]{1,0:T(8,128)} %get-tuple-element.145.hidden, ...), custom_call_target="tpu_custom_call" | custom-call | flops 1500000000 | bytes 4500000 | tf_op jit(solution)/shard_map/moe_leave/pallas_call | solution.py:86
  134.3 2.8 %gate_back.1 = (f32[256,768]{1,0:T(8,128)S(1)}, bf16[256,768]{1,0:T(8,128)(2,1)S(1)}, bf16[384,768]{1,0:T(8,128)(2,1)S(1)}, bf16[384,768]{1,0:T(8,128)(2,1)S(1)}...) custom-call(s32[4]{0:T(128)S(1)} %pad_add_fusion.1.idx, bf16[128,768]{1,0:T(8,128)(2,1)S(1)} %get-tuple-element.165.gbr_a, ...), custom_call_target="tpu_custom_call" | custom-call | flops 1500000000 | bytes 4500000 | tf_op jit(solution)/shard_map/gate_back/pallas_call | solution.py:86
  140.0 15.0 %scan_back.1 = (f32[256,128]{1,0:T(8,128)S(1)}, f32[256,768]{1,0:T(8,128)S(1)}, bf16[256,768]{1,0:T(8,128)(2,1)S(1)}, bf16[256,128]{1,0:T(8,128)(2,1)S(1)}, f32[24,768]{1,0:T(8,128)S(1)}) custom-call(f32[256,768]{1,0:T(8,128)S(1)} %get-tuple-element.169.gy_s, bf16[256,768]{1,0:T(8,128)(2,1)S(1)} %copy-done.13, f32[256,768]{1,0:T(8,128)S(1)} %copy-done.28, ...), custom_call_target="tpu_custom_call" | custom-call | flops 4800000000 | bytes 14400000 | tf_op jit(solution)/shard_map/scan_back/pallas_call | solution.py:86
  157.9 4.1 %leave.1 = (bf16[256,768]{1,0:T(8,128)(2,1)S(1)}, bf16[384,512]{1,0:T(8,128)(2,1)S(1)}, bf16[384,512]{1,0:T(8,128)(2,1)S(1)}, bf16[384,512]{1,0:T(8,128)(2,1)S(1)}, bf16[384,512]{1,0:T(8,128)(2,1)S(1)}) custom-call(s32[4]{0:T(128)S(1)} %pad_add_fusion.1.idx, s32[2,8]{1,0:T(2,128)S(1)} %pad_add_fusion.lens, s32[2,768]{1,0:T(2,128)S(1)} %copy-done.18, ...), custom_call_target="tpu_custom_call" | custom-call | flops 1500000000 | bytes 4500000 | tf_op jit(solution)/shard_map/leave/pallas_call | solution.py:86
  162.0 1.9 collective-permute-done.32.b_in
  166.7 3.3 %collective-permute-start.36 = (bf16[48,1536]{1,0:T(8,128)(2,1)S(1)}, bf16[48,1536]{1,0:T(8,128)(2,1)S(1)}, u32[]{:S(2)}, u32[]{:S(2)}) collective-permute-start(bf16[48,1536]{1,0:T(8,128)(2,1)S(1)} %get-tuple-element.208), channel_id=1, source_target_pairs={{0,6},{2,0},{4,2},{6,4},{1,7},{3,1},{5,3},{7,5},{8,14},{10,8},{12,... | collective-permute-start | bytes 442376 | tf_op jit(solution)/shard_map/ppermute | solution.py:231
  171.1 2.8 %collective-permute-done.33.a_in = bf16[384,512]{1,0:T(8,128)(2,1)S(1)} collective-permute-done((bf16[384,512]{1,0:T(8,128)(2,1)S(1)}, bf16[384,512]{1,0:T(8,128)(2,1)S(1)}, u32[]{:S(2)}, u32[]{:S(2)}) %collective-permute-start.33) | collective-permute-done | bytes 393248 | tf_op jit(solution)/shard_map/ppermute | solution.py:892
  176.9 2.8 %back.1 = (f32[128,768]{1,0:T(8,128)S(1)}, f32[128,768]{1,0:T(8,128)S(1)}) custom-call(s32[4]{0:T(128)S(1)} %pad_add_fusion.1.idx, s32[2,768]{1,0:T(2,128)S(1)} %copy-done.18, bf16[256,768]{1,0:T(8,128)(2,1)S(1)} %get-tuple-element.188.gxin, bf16[256,768]{1,0:T(8,128)(2,1)S(1)} %get-tuple-element.189.gzg, bf16[768,1024]{1,0:T(8,128)(2,1)S(1)} %copy-done.1, ...), custom_call_target="tpu_custom_call" | custom-call | flops 900000000 | bytes 2700000 | tf_op jit(solution)/shard_map/back/pallas_call | solution.py:86
  179.8 1.9 collective-permute-done.37.refs_6_
  182.0 3.4 %collective-permute-start.40 = (bf16[48,1024]{1,0:T(8,128)(2,1)S(1)}, bf16[48,1024]{1,0:T(8,128)(2,1)S(1)}, u32[]{:S(2)}, u32[]{:S(2)}) collective-permute-start(bf16[48,1024]{1,0:T(8,128)(2,1)S(1)} %get-tuple-element.214), channel_id=1, source_target_pairs={{0,6},{2,0},{4,2},{6,4},{1,7},{3,1},{5,3},{7,5},{8,14},{10,8},{12,... | collective-permute-start | bytes 294920 | tf_op jit(solution)/shard_map/ppermute | solution.py:231
  188.1 5.4 %collective-permute-done.41.refs_2_ = bf16[48,1024]{1,0:T(8,128)(2,1)S(1)} collective-permute-done((bf16[48,1024]{1,0:T(8,128)(2,1)S(1)}, bf16[48,1024]{1,0:T(8,128)(2,1)S(1)}, u32[]{:S(2)}, u32[]{:S(2)}) %collective-permute-start.41) | collective-permute-done | bytes 98336 | tf_op jit(solution)/shard_map/ppermute | solution.py:231
  (156 shorter events, 48.2 us)
Async XLA Ops:
  2.9 18.0 %collective-permute-start.6 = (bf16[416,768]{1,0:T(8,128)(2,1)S(1)}, bf16[416,768]{1,0:T(8,128)(2,1)S(1)}, u32[]{:S(2)}, u32[]{:S(2)}) collective-permute-start(bf16[416,768]{1,0:T(8,128)(2,1)S(1)} %get-tuple-element.128), channel_id=1, source_target_pairs={{0,16},{16,0},{1,17},{17,1},{2,18},{18,2},{3,19},{19,3},{4,20},{20... | collective-permute-start | bytes 1916936 | tf_op jit(solution)/shard_map/ppermute | solution.py:892
  6.0 15.0 %collective-permute-start.1 = (bf16[128,768]{1,0:T(8,128)(2,1)S(1)}, bf16[128,768]{1,0:T(8,128)(2,1)S(1)}, u32[]{:S(2)}, u32[]{:S(2)}) collective-permute-start(bf16[128,768]{1,0:T(8,128)(2,1)S(1)} %copy-done.15), channel_id=1, source_target_pairs={{0,8},{8,0},{1,9},{9,1},{2,10},{10,2},{3,11},{11,3},{4,12},{12,4},... | collective-permute-start | bytes 589832 | tf_op jit(solution)/shard_map/ppermute | solution.py:892
  11.4 9.4 %collective-permute-start.4 = (bf16[48,1024]{1,0:T(8,128)(2,1)S(1)}, bf16[48,1024]{1,0:T(8,128)(2,1)S(1)}, u32[]{:S(2)}, u32[]{:S(2)}) collective-permute-start(bf16[48,1024]{1,0:T(8,128)(2,1)S(1)} %get-tuple-element.127), channel_id=1, source_target_pairs={{0,4},{2,6},{4,0},{6,2},{1,5},{3,7},{5,1},{7,3},{8,12},{10,14},{12... | collective-permute-start | bytes 294920 | tf_op jit(solution)/shard_map/ppermute | solution.py:143
  11.4 9.4 %collective-permute-start.3 = (bf16[48,1024]{1,0:T(8,128)(2,1)S(1)}, bf16[48,1024]{1,0:T(8,128)(2,1)S(1)}, u32[]{:S(2)}, u32[]{:S(2)}) collective-permute-start(bf16[48,1024]{1,0:T(8,128)(2,1)S(1)} %get-tuple-element.127), channel_id=1, source_target_pairs={{0,2},{2,4},{4,6},{6,0},{1,3},{3,5},{5,7},{7,1},{8,10},{10,12},{12... | collective-permute-start | bytes 294920 | tf_op jit(solution)/shard_map/ppermute | solution.py:143
  21.0 10.8 %collective-permute-start.8 = (bf16[192,1024]{1,0:T(8,128)(2,1)S(1)}, bf16[192,1024]{1,0:T(8,128)(2,1)S(1)}, u32[]{:S(2)}, u32[]{:S(2)}) collective-permute-start(bf16[192,1024]{1,0:T(8,128)(2,1)S(1)} %pad_maximum_fusion.1.refs_0_), channel_id=1, source_target_pairs={{0,16},{16,0},{1,17},{17,1},{2,18},{18,2},{3,19},{19,3},{4,20},{20... | collective-permute-start | bytes 1179656 | tf_op jit(solution)/shard_map/ppermute | solution.py:892
  22.1 11.3 %collective-permute-start.7 = (bf16[192,1024]{1,0:T(8,128)(2,1)S(1)}, bf16[192,1024]{1,0:T(8,128)(2,1)S(1)}, u32[]{:S(2)}, u32[]{:S(2)}) collective-permute-start(bf16[192,1024]{1,0:T(8,128)(2,1)S(1)} %pad_maximum_fusion.1.refs_0_), channel_id=1, source_target_pairs={{0,1},{1,0},{2,3},{3,2},{4,5},{5,4},{6,7},{7,6},{8,9},{9,8},{10,11... | collective-permute-start | bytes 1179656 | tf_op jit(solution)/shard_map/ppermute | solution.py:892
  23.6 10.4 %collective-permute-start.14 = (bf16[48,1536]{1,0:T(8,128)(2,1)S(1)}, bf16[48,1536]{1,0:T(8,128)(2,1)S(1)}, u32[]{:S(2)}, u32[]{:S(2)}) collective-permute-start(bf16[48,1536]{1,0:T(8,128)(2,1)S(1)} %get-tuple-element.140), channel_id=1, source_target_pairs={{0,6},{2,0},{4,2},{6,4},{1,7},{3,1},{5,3},{7,5},{8,14},{10,8},{12,... | collective-permute-start | bytes 442376 | tf_op jit(solution)/shard_map/ppermute | solution.py:143
  27.2 12.0 %collective-permute-start.13 = (bf16[48,1536]{1,0:T(8,128)(2,1)S(1)}, bf16[48,1536]{1,0:T(8,128)(2,1)S(1)}, u32[]{:S(2)}, u32[]{:S(2)}) collective-permute-start(bf16[48,1536]{1,0:T(8,128)(2,1)S(1)} %get-tuple-element.140), channel_id=1, source_target_pairs={{0,4},{2,6},{4,0},{6,2},{1,5},{3,7},{5,1},{7,3},{8,12},{10,14},{12... | collective-permute-start | bytes 442376 | tf_op jit(solution)/shard_map/ppermute | solution.py:143
  27.2 12.0 %collective-permute-start.12 = (bf16[48,1536]{1,0:T(8,128)(2,1)S(1)}, bf16[48,1536]{1,0:T(8,128)(2,1)S(1)}, u32[]{:S(2)}, u32[]{:S(2)}) collective-permute-start(bf16[48,1536]{1,0:T(8,128)(2,1)S(1)} %get-tuple-element.140), channel_id=1, source_target_pairs={{0,2},{2,4},{4,6},{6,0},{1,3},{3,5},{5,7},{7,1},{8,10},{10,12},{12... | collective-permute-start | bytes 442376 | tf_op jit(solution)/shard_map/ppermute | solution.py:143
  31.8 7.4 %collective-permute-start.10 = (bf16[96,1024]{1,0:T(8,128)(2,1)S(1)}, bf16[96,1024]{1,0:T(8,128)(2,1)S(1)}, u32[]{:S(2)}, u32[]{:S(2)}) collective-permute-start(bf16[96,1024]{1,0:T(8,128)(2,1)S(1)} %slice.17), channel_id=1, source_target_pairs={{0,1},{1,0},{2,3},{3,2},{4,5},{5,4},{6,7},{7,6},{8,9},{9,8},{10,11... | collective-permute-start | bytes 589832 | tf_op jit(solution)/shard_map/ppermute | solution.py:892
  39.3 14.0 %collective-permute-start.16 = (bf16[192,1536]{1,0:T(8,128)(2,1)S(1)}, bf16[192,1536]{1,0:T(8,128)(2,1)S(1)}, u32[]{:S(2)}, u32[]{:S(2)}) collective-permute-start(bf16[192,1536]{1,0:T(8,128)(2,1)S(1)} %pad_maximum_fusion.refs_0_), channel_id=1, source_target_pairs={{0,16},{16,0},{1,17},{17,1},{2,18},{18,2},{3,19},{19,3},{4,20},{20... | collective-permute-start | bytes 1769480 | tf_op jit(solution)/shard_map/ppermute | solution.py:892
  39.9 14.0 %collective-permute-start.15 = (bf16[192,1536]{1,0:T(8,128)(2,1)S(1)}, bf16[192,1536]{1,0:T(8,128)(2,1)S(1)}, u32[]{:S(2)}, u32[]{:S(2)}) collective-permute-start(bf16[192,1536]{1,0:T(8,128)(2,1)S(1)} %pad_maximum_fusion.refs_0_), channel_id=1, source_target_pairs={{0,1},{1,0},{2,3},{3,2},{4,5},{5,4},{6,7},{7,6},{8,9},{9,8},{10,11... | collective-permute-start | bytes 1769480 | tf_op jit(solution)/shard_map/ppermute | solution.py:892
  47.0 9.0 %collective-permute-start.11 = (f32[256,128]{1,0:T(8,128)S(1)}, f32[256,128]{1,0:T(8,128)S(1)}, u32[]{:S(2)}, u32[]{:S(2)}) collective-permute-start(f32[256,128]{1,0:T(8,128)S(1)} %get-tuple-element.135.sel_a), channel_id=1, source_target_pairs={{0,8},{8,0},{1,9},{9,1},{2,10},{10,2},{3,11},{11,3},{4,12},{12,4},... | collective-permute-start | bytes 393224 | tf_op jit(solution)/shard_map/ppermute | solution.py:892
  53.3 10.8 %collective-permute-start.18 = (bf16[96,1536]{1,0:T(8,128)(2,1)S(1)}, bf16[96,1536]{1,0:T(8,128)(2,1)S(1)}, u32[]{:S(2)}, u32[]{:S(2)}) collective-permute-start(bf16[96,1536]{1,0:T(8,128)(2,1)S(1)} %slice.19), channel_id=1, source_target_pairs={{0,1},{1,0},{2,3},{3,2},{4,5},{5,4},{6,7},{7,6},{8,9},{9,8},{10,11... | collective-permute-start | bytes 884744 | tf_op jit(solution)/shard_map/ppermute | solution.py:892
  53.9 10.1 %collective-permute-start.17 = (bf16[96,1536]{1,0:T(8,128)(2,1)S(1)}, bf16[96,1536]{1,0:T(8,128)(2,1)S(1)}, u32[]{:S(2)}, u32[]{:S(2)}) collective-permute-start(bf16[96,1536]{1,0:T(8,128)(2,1)S(1)} %slice.18), channel_id=1, source_target_pairs={{0,16},{16,0},{1,17},{17,1},{2,18},{18,2},{3,19},{19,3},{4,20},{20... | collective-permute-start | bytes 884744 | tf_op jit(solution)/shard_map/ppermute | solution.py:892
  55.4 19.6 %collective-permute-start.20 = (bf16[448,768]{1,0:T(8,128)(2,1)S(1)}, bf16[448,768]{1,0:T(8,128)(2,1)S(1)}, u32[]{:S(2)}, u32[]{:S(2)}) collective-permute-start(bf16[448,768]{1,0:T(8,128)(2,1)S(1)} %get-tuple-element.148), channel_id=1, source_target_pairs={{0,16},{16,0},{1,17},{17,1},{2,18},{18,2},{3,19},{19,3},{4,20},{20... | collective-permute-start | bytes 2064392 | tf_op jit(solution)/shard_map/ppermute | solution.py:892
  75.9 17.7 %all-to-all-start = ((bf16[8,8,3840]{2,1,0:T(8,128)(2,1)}), bf16[8,8,3840]{2,1,0:T(8,128)(2,1)}, u32[]{:S(2)}, u32[]{:S(2)}) async-start(bf16[8,8,3840]{2,1,0:T(8,128)(2,1)} %bitcast.26), calls=%async_computation | async-start | bytes 983040 | tf_op jit(solution)/shard_map/all_to_all | solution.py:897
  81.1 23.2 %collective-permute-start.22 = (bf16[672,768]{1,0:T(8,128)(2,1)}, bf16[672,768]{1,0:T(8,128)(2,1)S(1)}, u32[]{:S(2)}, u32[]{:S(2)}) collective-permute-start(bf16[672,768]{1,0:T(8,128)(2,1)} %copy-done.21), channel_id=1, source_target_pairs={{0,16},{16,0},{1,17},{17,1},{2,18},{18,2},{3,19},{19,3},{4,20},{20... | collective-permute-start | bytes 3096584 | tf_op jit(solution)/shard_map/ppermute | solution.py:892
  106.5 14.0 %collective-permute-start.24 = (bf16[64,3840]{1,0:T(8,128)(2,1)}, bf16[64,3840]{1,0:T(8,128)(2,1)}, u32[]{:S(2)}, u32[]{:S(2)}) collective-permute-start(bf16[64,3840]{1,0:T(8,128)(2,1)} %bitcast.12.own), channel_id=1, source_target_pairs={{0,16},{16,0},{1,17},{17,1},{2,18},{18,2},{3,19},{19,3},{4,20},{20... | collective-permute-start | bytes 1474568 | tf_op jit(solution)/shard_map/ppermute | solution.py:892
  109.2 20.1 %all-to-all-start.1 = ((bf16[8,8,3840]{2,1,0:T(8,128)(2,1)}), bf16[8,8,3840]{2,1,0:T(8,128)(2,1)}, u32[]{:S(2)}, u32[]{:S(2)}) async-start(bf16[8,8,3840]{2,1,0:T(8,128)(2,1)} %fusion), calls=%async_computation.1 | async-start | bytes 983040 | tf_op jit(solution)/shard_map/all_to_all | solution.py:897
  137.0 18.0 %collective-permute-start.27 = (bf16[384,768]{1,0:T(8,128)(2,1)S(1)}, bf16[384,768]{1,0:T(8,128)(2,1)S(1)}, u32[]{:S(2)}, u32[]{:S(2)}) collective-permute-start(bf16[384,768]{1,0:T(8,128)(2,1)S(1)} %get-tuple-element.176), channel_id=1, source_target_pairs={{0,1},{1,0},{2,3},{3,2},{4,5},{5,4},{6,7},{7,6},{8,9},{9,8},{10,11... | collective-permute-start | bytes 1769480 | tf_op jit(solution)/shard_map/ppermute | solution.py:892
  138.8 16.3 %collective-permute-start.28 = (bf16[384,768]{1,0:T(8,128)(2,1)S(1)}, bf16[384,768]{1,0:T(8,128)(2,1)S(1)}, u32[]{:S(2)}, u32[]{:S(2)}) collective-permute-start(bf16[384,768]{1,0:T(8,128)(2,1)S(1)} %get-tuple-element.179), channel_id=1, source_target_pairs={{0,16},{16,0},{1,17},{17,1},{2,18},{18,2},{3,19},{19,3},{4,20},{20... | collective-permute-start | bytes 1769480 | tf_op jit(solution)/shard_map/ppermute | solution.py:892
  155.3 8.6 %collective-permute-start.32 = (bf16[192,768]{1,0:T(8,128)(2,1)S(1)}, bf16[192,768]{1,0:T(8,128)(2,1)S(1)}, u32[]{:S(2)}, u32[]{:S(2)}) collective-permute-start(bf16[192,768]{1,0:T(8,128)(2,1)S(1)} %get-tuple-element.196), channel_id=1, source_target_pairs={{0,1},{1,0},{2,3},{3,2},{4,5},{5,4},{6,7},{7,6},{8,9},{9,8},{10,11... | collective-permute-start | bytes 884744 | tf_op jit(solution)/shard_map/ppermute | solution.py:892
  156.1 8.2 %collective-permute-start.31 = (bf16[192,768]{1,0:T(8,128)(2,1)S(1)}, bf16[192,768]{1,0:T(8,128)(2,1)S(1)}, u32[]{:S(2)}, u32[]{:S(2)}) collective-permute-start(bf16[192,768]{1,0:T(8,128)(2,1)S(1)} %get-tuple-element.180), channel_id=1, source_target_pairs={{0,16},{16,0},{1,17},{17,1},{2,18},{18,2},{3,19},{19,3},{4,20},{20... | collective-permute-start | bytes 884744 | tf_op jit(solution)/shard_map/ppermute | solution.py:892
  164.4 9.5 %collective-permute-start.33 = (bf16[384,512]{1,0:T(8,128)(2,1)S(1)}, bf16[384,512]{1,0:T(8,128)(2,1)S(1)}, u32[]{:S(2)}, u32[]{:S(2)}) collective-permute-start(bf16[384,512]{1,0:T(8,128)(2,1)S(1)} %get-tuple-element.200), channel_id=1, source_target_pairs={{0,1},{1,0},{2,3},{3,2},{4,5},{5,4},{6,7},{7,6},{8,9},{9,8},{10,11... | collective-permute-start | bytes 1179656 | tf_op jit(solution)/shard_map/ppermute | solution.py:892
  165.9 9.1 %collective-permute-start.34 = (bf16[384,512]{1,0:T(8,128)(2,1)S(1)}, bf16[384,512]{1,0:T(8,128)(2,1)S(1)}, u32[]{:S(2)}, u32[]{:S(2)}) collective-permute-start(bf16[384,512]{1,0:T(8,128)(2,1)S(1)} %get-tuple-element.204), channel_id=1, source_target_pairs={{0,16},{16,0},{1,17},{17,1},{2,18},{18,2},{3,19},{19,3},{4,20},{20... | collective-permute-start | bytes 1179656 | tf_op jit(solution)/shard_map/ppermute | solution.py:892
  166.7 13.0 %collective-permute-start.36 = (bf16[48,1536]{1,0:T(8,128)(2,1)S(1)}, bf16[48,1536]{1,0:T(8,128)(2,1)S(1)}, u32[]{:S(2)}, u32[]{:S(2)}) collective-permute-start(bf16[48,1536]{1,0:T(8,128)(2,1)S(1)} %get-tuple-element.208), channel_id=1, source_target_pairs={{0,6},{2,0},{4,2},{6,4},{1,7},{3,1},{5,3},{7,5},{8,14},{10,8},{12,... | collective-permute-start | bytes 442376 | tf_op jit(solution)/shard_map/ppermute | solution.py:231
  169.9 11.8 %collective-permute-start.37 = (bf16[48,1536]{1,0:T(8,128)(2,1)S(1)}, bf16[48,1536]{1,0:T(8,128)(2,1)S(1)}, u32[]{:S(2)}, u32[]{:S(2)}) collective-permute-start(bf16[48,1536]{1,0:T(8,128)(2,1)S(1)} %get-tuple-element.209), channel_id=1, source_target_pairs={{0,4},{2,6},{4,0},{6,2},{1,5},{3,7},{5,1},{7,3},{8,12},{10,14},{12... | collective-permute-start | bytes 442376 | tf_op jit(solution)/shard_map/ppermute | solution.py:231
  170.0 11.8 %collective-permute-start.38 = (bf16[48,1536]{1,0:T(8,128)(2,1)S(1)}, bf16[48,1536]{1,0:T(8,128)(2,1)S(1)}, u32[]{:S(2)}, u32[]{:S(2)}) collective-permute-start(bf16[48,1536]{1,0:T(8,128)(2,1)S(1)} %get-tuple-element.210), channel_id=1, source_target_pairs={{0,2},{2,4},{4,6},{6,0},{1,3},{3,5},{5,7},{7,1},{8,10},{10,12},{12... | collective-permute-start | bytes 442376 | tf_op jit(solution)/shard_map/ppermute | solution.py:231
  179.7 14.7 %collective-permute-start.30 = (f32[128,768]{1,0:T(8,128)S(1)}, f32[128,768]{1,0:T(8,128)S(1)}, u32[]{:S(2)}, u32[]{:S(2)}) collective-permute-start(f32[128,768]{1,0:T(8,128)S(1)} %get-tuple-element.191), channel_id=1, source_target_pairs={{0,8},{8,0},{1,9},{9,1},{2,10},{10,2},{3,11},{11,3},{4,12},{12,4},... | collective-permute-start | bytes 1179656 | tf_op jit(solution)/shard_map/ppermute | solution.py:892
  185.4 8.1 %collective-permute-start.41 = (bf16[48,1024]{1,0:T(8,128)(2,1)S(1)}, bf16[48,1024]{1,0:T(8,128)(2,1)S(1)}, u32[]{:S(2)}, u32[]{:S(2)}) collective-permute-start(bf16[48,1024]{1,0:T(8,128)(2,1)S(1)} %get-tuple-element.215), channel_id=1, source_target_pairs={{0,4},{2,6},{4,0},{6,2},{1,5},{3,7},{5,1},{7,3},{8,12},{10,14},{12... | collective-permute-start | bytes 294920 | tf_op jit(solution)/shard_map/ppermute | solution.py:231
  185.4 8.1 %collective-permute-start.42 = (bf16[48,1024]{1,0:T(8,128)(2,1)S(1)}, bf16[48,1024]{1,0:T(8,128)(2,1)S(1)}, u32[]{:S(2)}, u32[]{:S(2)}) collective-permute-start(bf16[48,1024]{1,0:T(8,128)(2,1)S(1)} %get-tuple-element.216), channel_id=1, source_target_pairs={{0,2},{2,4},{4,6},{6,0},{1,3},{3,5},{5,7},{7,1},{8,10},{10,12},{12... | collective-permute-start | bytes 294920 | tf_op jit(solution)/shard_map/ppermute | solution.py:231
  (45 other events, 297.0 us)

commit v5 on v4

--- a/solution.py
+++ b/solution.py
@@ -389,25 +389,28 @@
     return block[:n] + block[n:]
 
 
+def step_inputs(sel, rank):
+    tail = LANES - rank
+    return jnp.where(iota(sel.shape, 1) >= tail, pltpu.roll(sel, tail, 1), 0.0).astype(BF16)
+
+
+def step_of(q, g1sel, small):
+    return mm(q, g1sel[...], NT) + small[ROW_STEP : ROW_STEP + 1]
+
+
 def scan_kernel(
     rank, states, lens, sel_a, sel_b, xc, g1sel, small,
-    ys_o, step_o, sel_o, keep_o, check_o,
-    dm_s, dx_s, wr_s, rd_s, rate_s, h_s,
+    ys_o, sel_o, check_o,
+    dm_s, dx_s, wr_s, rd_s, rate_s, h_s, check_s, sem,
 ):
     rows, inner = ys_o.shape
     tok = rows // 2
     sel = sel_a[...] + swap_halves(sel_b[...])
     sel_o[...] = sel
-    lane = iota((rows, LANES), 1)
-    tail = LANES - rank
-    q = jnp.where(lane >= tail, pltpu.roll(sel, tail, 1), 0.0).astype(BF16)
-    step_pre = mm(q, g1sel[...], NT) + small[ROW_STEP : ROW_STEP + 1]
-    step_o[...] = step_pre
-    delta = softplus(step_pre)
+    delta = softplus(step_of(step_inputs(sel, rank), g1sel, small))
     offset = both_offsets(lens, tok)
     xcf = xc[...].astype(F32)
     dm_s[...] = jnp.where(offset > 0, delta, 1e30)
-    keep_o[...] = jnp.broadcast_to((offset > 0).astype(F32), keep_o.shape)
     dx_s[...] = delta * xcf
     for b in range(2):
         turned = jnp.transpose(sel[b * tok : (b + 1) * tok])
@@ -428,7 +431,7 @@
             for g in range(inner // LANES):
                 lanes = slice(g * LANES, (g + 1) * LANES)
                 h = h_s[b, :, lanes]
-                check_o[ci * 2 + b, :, lanes] = h
+                check_s[ci * 2 + b, :, lanes] = h
                 rate = rate_s[:, lanes]
                 dm8 = dm_s[pl.ds(at, 8), lanes]
                 dx8 = dx_s[pl.ds(at, 8), lanes]
@@ -441,25 +444,30 @@
                     parts.append(p[:half] + p[half:])
                 ys_o[pl.ds(at, 8), lanes] = fold(parts)
                 h_s[b, :, lanes] = h
+        saved(ci).start()
         return carry
 
+    def saved(ci):
+        pair = pl.ds(2 * ci, 2)
+        return pltpu.make_async_copy(check_s.at[pair], check_o.at[pair], sem.at[ci])
+
     lax.fori_loop(0, tok // 8, chunk, 0)
+    for ci in range(tok // 8):
+        saved(ci).wait()
 
 
 def gate_kernel(plan, idx, u, xc, ys, small, *refs):
     n = plan.n_gathered()
     pieces = refs[:n]
-    gated_o, zg_o, mine_o, send_o, g2, sem = refs[n:]
+    mine_o, send_o, g2, sem = refs[n:]
     copies = plan.fetch(idx, pieces, g2, sem)
     for copy in copies:
         copy.wait()
     inner = ys.shape[1]
     tok = mine_o.shape[0]
     zg = mm(u[...], g2[:, :inner])
-    zg_o[...] = zg
     gated = (ys[...] + small[ROW_SKIP : ROW_SKIP + 1] * xc[...].astype(F32)) * (zg * sigmoid(zg))
     gated = gated.astype(BF16)
-    gated_o[...] = gated
     branch = mm(gated, g2[:, inner:])
     mine_o[...] = branch[:tok]
     send_o[...] = branch[tok:]
@@ -699,7 +707,7 @@
     gbr_o[...] = ghid.astype(BF16)
 
 
-def gate_back_kernel(plan, idx, gbr_a, gbr_b, g2, gated, xc, ys, zg, small, u, *refs):
+def gate_back_kernel(plan, idx, gbr_a, gbr_b, g2, xc, ys, small, u, *refs):
     n = plan.n_shared()
     gy_o, gzg_o = refs[:2]
     shared = refs[2 : 2 + n]
@@ -708,28 +716,38 @@
     gbr = jnp.concatenate([gbr_a[...], gbr_b[...]], axis=0)
     g_gated = mm(gbr, g2[:, inner:], NT)
     skip = small[ROW_SKIP : ROW_SKIP + 1]
-    sig = sigmoid(zg[...])
-    gy_o[...] = g_gated * (zg[...] * sig)
-    gzg = g_gated * (ys[...] + skip * xc[...].astype(F32)) * (sig * (1.0 + zg[...] * (1.0 - sig)))
-    gzg = gzg.astype(BF16)
+    zg = mm(u[...], g2[:, :inner])
+    sig = sigmoid(zg)
+    silu = zg * sig
+    out = ys[...] + skip * xc[...].astype(F32)
+    gy_o[...] = g_gated * silu
+    gzg = (g_gated * out * (sig * (1.0 + zg * (1.0 - sig)))).astype(BF16)
     gzg_o[...] = gzg
     grad_s[:, :inner] = mm(u[...], gzg, TN).astype(BF16)
-    grad_s[:, inner:] = mm(gated[...], gbr, TN).astype(BF16)
+    grad_s[:, inner:] = mm((out * silu).astype(BF16), gbr, TN).astype(BF16)
     for copy in plan.emit(idx, grad_s, shared, sem):
         copy.wait()
 
 
 def scan_back_kernel(
-    rank, states, gy_s, xc, step_pre, sel, keep, small, g1sel, check,
+    rank, states, lens, gy_s, xc, sel, small, g1sel, check_in,
     gsel_o, gxcs_o, gsr_o, q_o, smallg_o,
-    dm_s, dx_s, gdx_s, gdl_s, wr_s, rd_s, gwr_s, grd_s, rate_s, lam_s, ga_s, write_s, hb_s, lb_s, wb_s,
+    dm_s, dx_s, gdx_s, gdl_s, wr_s, rd_s, gwr_s, grd_s, rate_s, lam_s, ga_s, write_s, hb_s, lb_s, wb_s, delta_s, sig_s,
+    check, sem,
 ):
+    copy = pltpu.make_async_copy(check_in, check, sem)
+    copy.start()
     rows, inner = gy_s.shape
     tok = rows // 2
     xcf = xc[...].astype(F32)
     skip = small[ROW_SKIP : ROW_SKIP + 1]
-    delta = softplus(step_pre[...])
-    dm_s[...] = jnp.where(keep[:, 0:1] > 0.0, delta, 1e30)
+    q = step_inputs(sel[...], rank)
+    q_o[...] = q
+    step_pre = step_of(q, g1sel, small)
+    delta_s[...] = softplus(step_pre)
+    sig_s[...] = sigmoid(step_pre)
+    delta = delta_s[...]
+    dm_s[...] = jnp.where(both_offsets(lens, tok) > 0, delta, 1e30)
     dx_s[...] = delta * xcf
     for b in range(2):
         turned = jnp.transpose(sel[b * tok : (b + 1) * tok])
@@ -746,7 +764,7 @@
     own = iota(wide, 1) // states == iota(wide, 0)
     group = own.astype(F32).astype(BF16)
     for ref in (hb_s, lb_s, wb_s):
-        ref[...] = jnp.zeros_like(ref)
+        ref[1] = jnp.zeros(ref.shape[1:], BF16)
 
     def sums(b, ci):
         span = pl.ds(pl.multiple_of(b * tok + ci * n, n), n)
@@ -800,19 +818,19 @@
                 sums(0, ci)
         return carry
 
+    copy.wait()
     lax.fori_loop(0, count, chunk, 0)
     sums(1, 0)
-    delta = softplus(step_pre[...])
+    delta = delta_s[...]
     gdx = gdx_s[...]
     xcf = xc[...].astype(F32)
     gy = gy_s[...]
     gxcs_o[...] = gy * skip + gdx * delta
-    g_step = (gdx * xcf + LN2 * gdl_s[...]) * sigmoid(step_pre[...])
+    g_step = (gdx * xcf + LN2 * gdl_s[...]) * sig_s[...]
     gsr = g_step.astype(BF16)
     gsr_o[...] = gsr
     lane = iota((rows, LANES), 1)
     tail = LANES - rank
-    q_o[...] = jnp.where(lane >= tail, pltpu.roll(sel[...], tail, 1), 0.0).astype(BF16)
     back = jnp.where(lane >= tail, mm(gsr, g1sel[...]), 0.0)
     back = pltpu.roll(back, rank, 1)
     tall = (n * states, LANES)
@@ -1053,18 +1071,18 @@
     part_three = swap(after(sends[1], middle), "y")
     g1sel_spec = pl.BlockSpec((inner, LANES), lambda i: (0, inner // LANES))
     chunks = tok // 8
-    ys, step_pre, sel, keep, check = call(
+    ys, sel, check = call(
         functools.partial(scan_kernel, rank, states),
-        [((rows, inner), F32), kept((rows, inner), F32), kept((rows, LANES), F32), kept((rows, LANES), F32), kept((2 * chunks, states, inner), F32)],
+        [((rows, inner), F32), kept((rows, LANES), F32), ((2 * chunks, states, inner), F32, HBM, True)],
         [lens2, selp, selq, xc, g1, small_t],
         [SMEM, None, None, None, g1sel_spec, None],
-        scratch=[pltpu.VMEM((rows, inner), F32), pltpu.VMEM((rows, inner), F32), pltpu.VMEM((2, states, tok), F32), pltpu.VMEM((2, states, tok), F32), pltpu.VMEM((states, inner), F32), pltpu.VMEM((2, states, inner), F32)],
+        scratch=[pltpu.VMEM((rows, inner), F32), pltpu.VMEM((rows, inner), F32), pltpu.VMEM((2, states, tok), F32), pltpu.VMEM((2, states, tok), F32), pltpu.VMEM((states, inner), F32), pltpu.VMEM((2, states, inner), F32), pltpu.VMEM((2 * chunks, states, inner), F32), pltpu.SemaphoreType.DMA((chunks,))],
         name="scan",
         us=9,
     )
-    gated, zg, br_mine, br_send, g2 = call(
+    br_mine, br_send, g2 = call(
         functools.partial(gate_kernel, plan),
-        [kept((rows, inner), BF16), kept((rows, inner), F32), ((tok, width), F32), ((tok, width), F32), ((inner, inner + width), BF16)],
+        [((tok, width), F32), ((tok, width), F32), ((inner, inner + width), BF16)],
         [idx, u, xc, ys, small_t] + pieces2,
         [SMEM] + [None] * 4 + [HBM] * len(pieces2),
         scratch=[fetch_sem],
@@ -1091,7 +1109,7 @@
     both, acc, act, slope, up_near = call(
         functools.partial(expert_own_kernel, slots, parts[:-1]),
         [((total, 2 * width), BF16), ((total, 2 * width), F32), ((total, hid), BF16), ((total, hid), F32), ((hid, width), BF16)],
-        [line, peer, in_hbm(up_weight), in_hbm(down_weight), up_one, part_two],
+        [line, peer] + [in_hbm(w) for w in (up_weight, down_weight, up_one, part_two)],
         [None, None] + [HBM] * 4,
         scratch=[weight_s, weight_s, tail_s, pltpu.SemaphoreType.DMA((2 + early,))],
         name="expert_own",
@@ -1132,17 +1150,17 @@
     gy, gzg, *shared2 = call(
         functools.partial(gate_back_kernel, plan),
         [((rows, inner), F32), ((rows, inner), BF16)] + plan.shared_outs(inner + width),
-        [idx, gbr, gbr_got, g2, gated, xc, ys, zg, small_t, u],
-        [SMEM] + [None] * 9,
+        [idx, gbr, gbr_got, g2, xc, ys, small_t, u],
+        [SMEM] + [None] * 7,
         scratch=[pltpu.VMEM((inner, inner + width), BF16), emit_sem],
         name="gate_back",
     )
     gsel, gxcs, gsr, q, smallg = call(
         functools.partial(scan_back_kernel, rank, states),
         [((rows, LANES), F32), ((rows, inner), F32), ((rows, inner), BF16), ((rows, LANES), BF16), ((small_n, inner), F32)],
-        [gy, xc, step_pre, sel, keep, small_t, g1, in_hbm(check)],
-        [None] * 6 + [g1sel_spec, None],
-        scratch=[pltpu.VMEM((rows, inner), F32)] * 4 + [pltpu.VMEM((2, states, tok), F32)] * 2 + [pltpu.VMEM((rows, GROUP_TOKENS * states), F32)] * 2 + [pltpu.VMEM((states, inner), F32), pltpu.VMEM((2, states, inner), F32), pltpu.VMEM((states, inner), F32), pltpu.VMEM((rows // GROUP_TOKENS, 2 * GROUP_TOKENS, GROUP_TOKENS * states), BF16)] + [pltpu.VMEM((2, GROUP_TOKENS * states, inner), BF16)] * 3,
+        [lens2, gy, xc, sel, small_t, g1, in_hbm(check)],
+        [SMEM] + [None] * 4 + [g1sel_spec, HBM],
+        scratch=[pltpu.VMEM((rows, inner), F32)] * 4 + [pltpu.VMEM((2, states, tok), F32)] * 2 + [pltpu.VMEM((rows, GROUP_TOKENS * states), F32)] * 2 + [pltpu.VMEM((states, inner), F32), pltpu.VMEM((2, states, inner), F32), pltpu.VMEM((states, inner), F32), pltpu.VMEM((rows // GROUP_TOKENS, 2 * GROUP_TOKENS, GROUP_TOKENS * states), BF16)] + [pltpu.VMEM((2, GROUP_TOKENS * states, inner), BF16)] * 3 + [pltpu.VMEM((rows, inner), F32)] * 2 + [pltpu.VMEM((2 * chunks, states, inner), F32), pltpu.SemaphoreType.DMA],
         name="scan_back",
         us=16,
     )

time: 198 us -> 198 us (level)
  local copies, waits for them, and re-layouts: 3.28 us -> 0.21 us
    unnamed x63 -> x47, local copies, waits for them, and re-layouts: 3.2 us -> 0.13 us
    ppermute x32, waiting for transfers between devices: 29.5 us -> 31.8 us  [swap(): return lax.ppermute(values, axis, [(0, 1), (1, 0)])]
where the time goes in v5:
time: 198 us; the launch traced here: 197 us
  Pallas kernels  77.5 us (39%)
  waiting for transfers between devices  63.8 us (32%)
  starting transfers between devices  53.1 us (27%)
    pallas_call x23, Pallas kernels, call(): pl.pallas_call(kernel, grid=(1,) if windowed else (), out_shape=[(pltpu.H...  77.5 us
    ppermute x32, waiting for transfers between devices, swap(): return lax.ppermute(values, axis, [(0, 1), (1, 0)])  31.8 us
    ppermute x32, starting transfers between devices, swap(): return lax.ppermute(values, axis, [(0, 1), (1, 0)])  24.2 us
    ppermute x6, waiting for transfers between devices, gather(): lax.ppermute(piece, 'z', [(i, (i + k) % 4) for i in range(4)])  12.1 us
    all_to_all x2, waiting for transfers between devices, exchange(): lax.all_to_all(parts, ('z', 'x'), split_axis=0, concat_axis=0, tiled=True)  10.9 us
    all_to_all x2, starting transfers between devices, exchange(): lax.all_to_all(parts, ('z', 'x'), split_axis=0, concat_axis=0, tiled=True)  10.8 us
    ppermute x6, starting transfers between devices, gather(): lax.ppermute(piece, 'z', [(i, (i + k) % 4) for i in range(4)])  9.28 us
    ppermute x6, waiting for transfers between devices, reduce3(): lax.ppermute(parts[k], 'z', [(i, (i - k) % 4) for i in range(4)])  8.94 us
  transfers between devices with their start and end apart: 46, of which 25 were waited for; matrix products, arithmetic and copies ran while one was open for 1% of the time, Pallas kernels for 33%

profile of v5, /device:TPU:0, one launch (start us, length us, event | category | flops | bytes accessed | tf_op | source)
XLA Modules:
  0.0 196.9 jit_solution(15996471143586604631)
XLA Ops:
  0.8 2.1 %pack.1 = (bf16[24,1664]{1,0:T(8,128)(2,1)S(1)}, bf16[24,1664]{1,0:T(8,128)(2,1)S(1)}, bf16[48,256]{1,0:T(8,128)(2,1)S(1)}, bf16[416,768]{1,0:T(8,128)(2,1)S(1)}) custom-call(s32[4]{0:T(128)S(1)} %pad_add_fusion.1.idx, bf16[24,3072]{1,0:T(8,128)(2,1)} %in_proj.3, bf16[1,24]{1,0:T(2,128)(2,1)} %bitcast.22, bf16[1,24]{1,0:T(2,128)(2,1)} %bitcast.28, ...), custom_call_target="tpu_custom_call" | custom-call | flops 300000000 | bytes 900000 | tf_op jit(solution)/shard_map/pack/pallas_call | solution.py:86
  2.9 3.0 %collective-permute-start.6 = (bf16[416,768]{1,0:T(8,128)(2,1)S(1)}, bf16[416,768]{1,0:T(8,128)(2,1)S(1)}, u32[]{:S(2)}, u32[]{:S(2)}) collective-permute-start(bf16[416,768]{1,0:T(8,128)(2,1)S(1)} %get-tuple-element.124), channel_id=1, source_target_pairs={{0,16},{16,0},{1,17},{17,1},{2,18},{18,2},{3,19},{19,3},{4,20},{20... | collective-permute-start | bytes 1916936 | tf_op jit(solution)/shard_map/ppermute | solution.py:910
  7.8 3.7 %collective-permute-start.5 = (bf16[48,1024]{1,0:T(8,128)(2,1)S(1)}, bf16[48,1024]{1,0:T(8,128)(2,1)S(1)}, u32[]{:S(2)}, u32[]{:S(2)}) collective-permute-start(bf16[48,1024]{1,0:T(8,128)(2,1)S(1)} %get-tuple-element.123), channel_id=1, source_target_pairs={{0,6},{2,0},{4,2},{6,4},{1,7},{3,1},{5,3},{7,5},{8,14},{10,8},{12,... | collective-permute-start | bytes 294920 | tf_op jit(solution)/shard_map/ppermute | solution.py:143
  14.6 6.3 %collective-permute-done.4 = bf16[48,1024]{1,0:T(8,128)(2,1)S(1)} collective-permute-done((bf16[48,1024]{1,0:T(8,128)(2,1)S(1)}, bf16[48,1024]{1,0:T(8,128)(2,1)S(1)}, u32[]{:S(2)}, u32[]{:S(2)}) %collective-permute-start.4) | collective-permute-done | bytes 98336 | tf_op jit(solution)/shard_map/ppermute | solution.py:143
  23.6 3.6 %collective-permute-start.14 = (bf16[48,1536]{1,0:T(8,128)(2,1)S(1)}, bf16[48,1536]{1,0:T(8,128)(2,1)S(1)}, u32[]{:S(2)}, u32[]{:S(2)}) collective-permute-start(bf16[48,1536]{1,0:T(8,128)(2,1)S(1)} %get-tuple-element.136), channel_id=1, source_target_pairs={{0,6},{2,0},{4,2},{6,4},{1,7},{3,1},{5,3},{7,5},{8,14},{10,8},{12,... | collective-permute-start | bytes 442376 | tf_op jit(solution)/shard_map/ppermute | solution.py:143
  28.2 3.6 %collective-permute-done.8.refs_2_ = bf16[192,1024]{1,0:T(8,128)(2,1)S(1)} collective-permute-done((bf16[192,1024]{1,0:T(8,128)(2,1)S(1)}, bf16[192,1024]{1,0:T(8,128)(2,1)S(1)}, u32[]{:S(2)}, u32[]{:S(2)}) %collective-permute-start.8) | collective-permute-done | bytes 393248 | tf_op jit(solution)/shard_map/ppermute | solution.py:910
  34.0 5.2 %collective-permute-done.13 = bf16[48,1536]{1,0:T(8,128)(2,1)S(1)} collective-permute-done((bf16[48,1536]{1,0:T(8,128)(2,1)S(1)}, bf16[48,1536]{1,0:T(8,128)(2,1)S(1)}, u32[]{:S(2)}, u32[]{:S(2)}) %collective-permute-start.13) | collective-permute-done | bytes 147488 | tf_op jit(solution)/shard_map/ppermute | solution.py:143
  41.0 6.0 %enter.1 = (bf16[256,768]{1,0:T(8,128)(2,1)S(1)}, f32[256,768]{1,0:T(8,128)}, bf16[256,768]{1,0:T(8,128)(2,1)S(1)}, f32[256,128]{1,0:T(8,128)S(1)}, f32[24,768]{...) custom-call(s32[4]{0:T(128)S(1)} %pad_add_fusion.1.idx, s32[2,8]{1,0:T(2,128)S(1)} %pad_add_fusion.lens, ...), custom_call_target="tpu_custom_call" | custom-call | flops 1500000000 | bytes 4500000 | tf_op jit(solution)/shard_map/enter/pallas_call | solution.py:86
  47.1 6.2 %collective-permute-done.16.refs_2_ = bf16[192,1536]{1,0:T(8,128)(2,1)S(1)} collective-permute-done((bf16[192,1536]{1,0:T(8,128)(2,1)S(1)}, bf16[192,1536]{1,0:T(8,128)(2,1)S(1)}, u32[]{:S(2)}, u32[]{:S(2)}) %collective-permute-start.16) | collective-permute-done | bytes 589856 | tf_op jit(solution)/shard_map/ppermute | solution.py:910
  56.0 8.3 %scan.1 = (f32[256,768]{1,0:T(8,128)S(1)}, f32[256,128]{1,0:T(8,128)}, f32[32,16,768]{2,1,0:T(8,128)}) custom-call(s32[2,8]{1,0:T(2,128)S(1)} %pad_add_fusion.lens, f32[256,128]{1,0:T(8,128)S(1)} %get-tuple-element.131.sel_a, f32[256,128]{1,0:T(8,128)S(1)} %collective-permute-done.11.sel_b, bf16[256,768]{1,0:T(8,128)(2,1)S(1)} %get-tuple-element.130.xc, ...), custom_call_target="tpu_custom_call" | custom-call | flops 2700000000 | bytes 8100000 | tf_op jit(solution)/shard_map/scan/pallas_call | solution.py:86
  64.3 4.9 %gate.1 = (f32[128,768]{1,0:T(8,128)S(1)}, f32[128,768]{1,0:T(8,128)S(1)}, bf16[768,1536]{1,0:T(8,128)(2,1)S(1)}) custom-call(s32[4]{0:T(128)S(1)} %pad_add_fusion.1.idx, bf16[256,768]{1,0:T(8,128)(2,1)S(1)} %get-tuple-element.129.u, bf16[256,768]{1,0:T(8,128)(2,1)S(1)} %get-tuple-element.130.xc, f32[256,768]{1,0:T(8,128)S(1)} %get-tuple-element.134.ys, ...), custom_call_target="tpu_custom_call" | custom-call | flops 1500000000 | bytes 4500000 | tf_op jit(solution)/shard_map/gate/pallas_call | solution.py:86
  71.0 2.6 %moe_enter.1 = (bf16[64,3840]{1,0:T(8,128)(2,1)}, f32[128,768]{1,0:T(8,128)}, f32[128,128]{1,0:T(8,128)}) custom-call(s32[1,8]{1,0:T(1,128)S(1)} %copy-done.9, bf16[128,768]{1,0:T(8,128)(2,1)S(1)} %copy-done.4, bf16[128,768]{1,0:T(8,128)(2,1)} %cot.3, s32[1,128]{1,0:T(1,128)S(1)} %bitcast.25, f32[128,768]{1,0:T(8,128)S(1)} %get-tuple-element.138.mine, ...), custom_call_target="tpu_custom_call" | custom-call | flops 1500000000 | bytes 4500000 | tf_op jit(solution)/shard_map/moe_enter/pallas_call | solution.py:86
  75.2 5.1 %all-to-all-start = ((bf16[8,8,3840]{2,1,0:T(8,128)(2,1)}), bf16[8,8,3840]{2,1,0:T(8,128)(2,1)}, u32[]{:S(2)}, u32[]{:S(2)}) async-start(bf16[8,8,3840]{2,1,0:T(8,128)(2,1)} %bitcast.26), calls=%async_computation | async-start | bytes 983040 | tf_op jit(solution)/shard_map/all_to_all | solution.py:915
  81.5 10.9 %all-to-all-done = bf16[8,8,3840]{2,1,0:T(8,128)(2,1)} async-done(((bf16[8,8,3840]{2,1,0:T(8,128)(2,1)}), bf16[8,8,3840]{2,1,0:T(8,128)(2,1)}, u32[]{:S(2)}, u32[]{:S(2)}) %all-to-all-start) | async-done | bytes 491552 | tf_op jit(solution)/shard_map/all_to_all | solution.py:915
  92.4 2.1 %collective-permute-done.21.peer = bf16[64,3840]{1,0:T(8,128)(2,1)S(1)} collective-permute-done((bf16[64,3840]{1,0:T(8,128)(2,1)}, bf16[64,3840]{1,0:T(8,128)(2,1)S(1)}, u32[]{:S(2)}, u32[]{:S(2)}) %collective-permute-start.21) | collective-permute-done | bytes 491552 | tf_op jit(solution)/shard_map/ppermute | solution.py:910
  94.5 5.7 %expert_own.1 = (bf16[320,1536]{1,0:T(8,128)(2,1)S(1)}, f32[320,1536]{1,0:T(8,128)S(1)}, bf16[320,768]{1,0:T(8,128)(2,1)S(1)}, f32[320,768]{1,0:T(8,128)S(1)}, bf16[768,768]{1,0:T(8,128)(2,1)S(1)}) custom-call(bf16[64,3840]{1,0:T(8,128)(2,1)} %bitcast.12.own, bf16[64,3840]{1,0:T(8,128)(2,1)S(1)} %collective-permute-done.21.peer, bf16[1,768,768]{2,1,0:T(8,128)(2,1)} %up.8, ...), custom_call_target="tpu_custom_call" | custom-call | flops 1800000000 | bytes 5400000 | tf_op jit(solution)/shard_map/expert_own/pallas_call | solution.py:86
  100.2 2.8 %collective-permute-done.22.refs_1_ = bf16[672,768]{1,0:T(8,128)(2,1)S(1)} collective-permute-done((bf16[672,768]{1,0:T(8,128)(2,1)}, bf16[672,768]{1,0:T(8,128)(2,1)S(1)}, u32[]{:S(2)}, u32[]{:S(2)}) %collective-permute-start.22) | collective-permute-done | bytes 1032224 | tf_op jit(solution)/shard_map/ppermute | solution.py:910
  103.0 2.5 %expert_other.1 = (f32[64,3840]{1,0:T(8,128)S(1)}, bf16[64,3840]{1,0:T(8,128)(2,1)S(1)}) custom-call(bf16[320,1536]{1,0:T(8,128)(2,1)S(1)} %get-tuple-element.146.both, f32[320,1536]{1,0:T(8,128)S(1)} %get-tuple-element.147.acc, bf16[320,768]{1,0:T(8,128)(2,1)S(1)} %get-tuple-element.148.act, f32[320,768]{1,0:T(8,128)S(1)} %get-tuple-element.149.slope, ...), custom_call_target="tpu_custom_call" | custom-call | flops 900000000 | bytes 2700000 | tf_op jit(solution)/shard_map/expert_other/pallas_call | solution.py:86
  108.4 5.6 %all-to-all-start.1 = ((bf16[8,8,3840]{2,1,0:T(8,128)(2,1)}), bf16[8,8,3840]{2,1,0:T(8,128)(2,1)}, u32[]{:S(2)}, u32[]{:S(2)}) async-start(bf16[8,8,3840]{2,1,0:T(8,128)(2,1)} %fusion), calls=%async_computation.1 | async-start | bytes 983040 | tf_op jit(solution)/shard_map/all_to_all | solution.py:915
  114.0 4.6 %near_grad.1 = (f32[1,768,768]{2,1,0:T(8,128)S(1)}, f32[1,768,768]{2,1,0:T(8,128)S(1)}) custom-call(bf16[320,1536]{1,0:T(8,128)(2,1)S(1)} %copy-done.3, bf16[1,768,768]{2,1,0:T(8,128)(2,1)} %up.8, bf16[1,768,768]{2,1,0:T(8,128)(2,1)} %down.7), custom_call_target="tpu_custom_call" | custom-call | flops 1200000000 | bytes 3600000 | tf_op jit(solution)/shard_map/near_grad/pallas_call | solution.py:86
  119.6 2.1 %collective-permute-done.25.peer_y = bf16[64,3840]{1,0:T(8,128)(2,1)S(1)} collective-permute-done((bf16[64,3840]{1,0:T(8,128)(2,1)}, bf16[64,3840]{1,0:T(8,128)(2,1)S(1)}, u32[]{:S(2)}, u32[]{:S(2)}) %collective-permute-start.25) | collective-permute-done | bytes 491552 | tf_op jit(solution)/shard_map/ppermute | solution.py:910
  121.7 6.8 %far_grad.1 = (f32[1,768,768]{2,1,0:T(8,128)}, f32[1,768,768]{2,1,0:T(8,128)}) custom-call(bf16[64,3840]{1,0:T(8,128)(2,1)} %collective-permute-done.24.own_y, bf16[64,3840]{1,0:T(8,128)(2,1)S(1)} %collective-permute-done.25.peer_y, bf16[1,768,768]{2,1,0:T(8,128)(2,1)} %up.8, bf16[1,768,768]{2,1,0:T(8,128)(2,1)} %down.7, ...), custom_call_target="tpu_custom_call" | custom-call | flops 2400000000 | bytes 7200000 | tf_op jit(solution)/shard_map/far_grad/pallas_call | solution.py:86
  128.5 3.3 %moe_leave.1 = (bf16[128,768]{1,0:T(8,128)(2,1)}, f32[128,768]{1,0:T(8,128)S(1)}, bf16[128,768]{1,0:T(8,128)(2,1)S(1)}, f32[16,768]{1,0:T(8,128)S(1)}) custom-call(s32[1,8]{1,0:T(1,128)} %lens.3, s32[1,128]{1,0:T(1,128)} %bitcast.24, bf16[128,768]{1,0:T(8,128)(2,1)} %cot.3, f32[128,768]{1,0:T(8,128)} %get-tuple-element.141.hidden, ...), custom_call_target="tpu_custom_call" | custom-call | flops 1500000000 | bytes 4500000 | tf_op jit(solution)/shard_map/moe_leave/pallas_call | solution.py:86
  133.4 3.2 %gate_back.1 = (f32[256,768]{1,0:T(8,128)S(1)}, bf16[256,768]{1,0:T(8,128)(2,1)S(1)}, bf16[384,768]{1,0:T(8,128)(2,1)S(1)}, bf16[384,768]{1,0:T(8,128)(2,1)S(1)}...) custom-call(s32[4]{0:T(128)S(1)} %pad_add_fusion.1.idx, bf16[128,768]{1,0:T(8,128)(2,1)S(1)} %get-tuple-element.161.gbr_a, ...), custom_call_target="tpu_custom_call" | custom-call | flops 1500000000 | bytes 4500000 | tf_op jit(solution)/shard_map/gate_back/pallas_call | solution.py:86
  139.5 15.2 %scan_back.1 = (f32[256,128]{1,0:T(8,128)S(1)}, f32[256,768]{1,0:T(8,128)S(1)}, bf16[256,768]{1,0:T(8,128)(2,1)S(1)}, bf16[256,128]{1,0:T(8,128)(2,1)S(1)}, f32[24,768]{1,0:T(8,128)S(1)}) custom-call(s32[2,8]{1,0:T(2,128)S(1)} %pad_add_fusion.lens, f32[256,768]{1,0:T(8,128)S(1)} %get-tuple-element.163.gy_s, bf16[256,768]{1,0:T(8,128)(2,1)S(1)} %copy-done.17, ...), custom_call_target="tpu_custom_call" | custom-call | flops 4800000000 | bytes 14400000 | tf_op jit(solution)/shard_map/scan_back/pallas_call | solution.py:86
  157.7 4.1 %leave.1 = (bf16[256,768]{1,0:T(8,128)(2,1)S(1)}, bf16[384,512]{1,0:T(8,128)(2,1)S(1)}, bf16[384,512]{1,0:T(8,128)(2,1)S(1)}, bf16[384,512]{1,0:T(8,128)(2,1)S(1)}, bf16[384,512]{1,0:T(8,128)(2,1)S(1)}) custom-call(s32[4]{0:T(128)S(1)} %pad_add_fusion.1.idx, s32[2,8]{1,0:T(2,128)S(1)} %pad_add_fusion.lens, s32[2,768]{1,0:T(2,128)S(1)} %copy-done.7, ...), custom_call_target="tpu_custom_call" | custom-call | flops 1500000000 | bytes 4500000 | tf_op jit(solution)/shard_map/leave/pallas_call | solution.py:86
  166.4 3.3 %collective-permute-start.36 = (bf16[48,1536]{1,0:T(8,128)(2,1)S(1)}, bf16[48,1536]{1,0:T(8,128)(2,1)S(1)}, u32[]{:S(2)}, u32[]{:S(2)}) collective-permute-start(bf16[48,1536]{1,0:T(8,128)(2,1)S(1)} %get-tuple-element.200), channel_id=1, source_target_pairs={{0,6},{2,0},{4,2},{6,4},{1,7},{3,1},{5,3},{7,5},{8,14},{10,8},{12,... | collective-permute-start | bytes 442376 | tf_op jit(solution)/shard_map/ppermute | solution.py:231
  170.8 2.8 %collective-permute-done.33.a_in = bf16[384,512]{1,0:T(8,128)(2,1)S(1)} collective-permute-done((bf16[384,512]{1,0:T(8,128)(2,1)S(1)}, bf16[384,512]{1,0:T(8,128)(2,1)S(1)}, u32[]{:S(2)}, u32[]{:S(2)}) %collective-permute-start.33) | collective-permute-done | bytes 393248 | tf_op jit(solution)/shard_map/ppermute | solution.py:910
  176.6 2.8 %back.1 = (f32[128,768]{1,0:T(8,128)S(1)}, f32[128,768]{1,0:T(8,128)S(1)}) custom-call(s32[4]{0:T(128)S(1)} %pad_add_fusion.1.idx, s32[2,768]{1,0:T(2,128)S(1)} %copy-done.7, bf16[256,768]{1,0:T(8,128)(2,1)S(1)} %get-tuple-element.180.gxin, bf16[256,768]{1,0:T(8,128)(2,1)S(1)} %get-tuple-element.181.gzg, bf16[768,1024]{1,0:T(8,128)(2,1)S(1)} %copy-done.1, ...), custom_call_target="tpu_custom_call" | custom-call | flops 900000000 | bytes 2700000 | tf_op jit(solution)/shard_map/back/pallas_call | solution.py:86
  179.6 1.9 collective-permute-done.37.refs_6_
  181.7 3.4 %collective-permute-start.40 = (bf16[48,1024]{1,0:T(8,128)(2,1)S(1)}, bf16[48,1024]{1,0:T(8,128)(2,1)S(1)}, u32[]{:S(2)}, u32[]{:S(2)}) collective-permute-start(bf16[48,1024]{1,0:T(8,128)(2,1)S(1)} %get-tuple-element.206), channel_id=1, source_target_pairs={{0,6},{2,0},{4,2},{6,4},{1,7},{3,1},{5,3},{7,5},{8,14},{10,8},{12,... | collective-permute-start | bytes 294920 | tf_op jit(solution)/shard_map/ppermute | solution.py:231
  187.8 5.4 %collective-permute-done.41.refs_2_ = bf16[48,1024]{1,0:T(8,128)(2,1)S(1)} collective-permute-done((bf16[48,1024]{1,0:T(8,128)(2,1)S(1)}, bf16[48,1024]{1,0:T(8,128)(2,1)S(1)}, u32[]{:S(2)}, u32[]{:S(2)}) %collective-permute-start.41) | collective-permute-done | bytes 98336 | tf_op jit(solution)/shard_map/ppermute | solution.py:231
  (140 shorter events, 46.6 us)
Async XLA Ops:
  2.9 18.0 %collective-permute-start.6 = (bf16[416,768]{1,0:T(8,128)(2,1)S(1)}, bf16[416,768]{1,0:T(8,128)(2,1)S(1)}, u32[]{:S(2)}, u32[]{:S(2)}) collective-permute-start(bf16[416,768]{1,0:T(8,128)(2,1)S(1)} %get-tuple-element.124), channel_id=1, source_target_pairs={{0,16},{16,0},{1,17},{17,1},{2,18},{18,2},{3,19},{19,3},{4,20},{20... | collective-permute-start | bytes 1916936 | tf_op jit(solution)/shard_map/ppermute | solution.py:910
  6.0 15.0 %collective-permute-start.1 = (bf16[128,768]{1,0:T(8,128)(2,1)S(1)}, bf16[128,768]{1,0:T(8,128)(2,1)S(1)}, u32[]{:S(2)}, u32[]{:S(2)}) collective-permute-start(bf16[128,768]{1,0:T(8,128)(2,1)S(1)} %copy-done.4), channel_id=1, source_target_pairs={{0,8},{8,0},{1,9},{9,1},{2,10},{10,2},{3,11},{11,3},{4,12},{12,4},... | collective-permute-start | bytes 589832 | tf_op jit(solution)/shard_map/ppermute | solution.py:910
  11.4 9.4 %collective-permute-start.4 = (bf16[48,1024]{1,0:T(8,128)(2,1)S(1)}, bf16[48,1024]{1,0:T(8,128)(2,1)S(1)}, u32[]{:S(2)}, u32[]{:S(2)}) collective-permute-start(bf16[48,1024]{1,0:T(8,128)(2,1)S(1)} %get-tuple-element.123), channel_id=1, source_target_pairs={{0,4},{2,6},{4,0},{6,2},{1,5},{3,7},{5,1},{7,3},{8,12},{10,14},{12... | collective-permute-start | bytes 294920 | tf_op jit(solution)/shard_map/ppermute | solution.py:143
  11.4 9.4 %collective-permute-start.3 = (bf16[48,1024]{1,0:T(8,128)(2,1)S(1)}, bf16[48,1024]{1,0:T(8,128)(2,1)S(1)}, u32[]{:S(2)}, u32[]{:S(2)}) collective-permute-start(bf16[48,1024]{1,0:T(8,128)(2,1)S(1)} %get-tuple-element.123), channel_id=1, source_target_pairs={{0,2},{2,4},{4,6},{6,0},{1,3},{3,5},{5,7},{7,1},{8,10},{10,12},{12... | collective-permute-start | bytes 294920 | tf_op jit(solution)/shard_map/ppermute | solution.py:143
  21.0 10.8 %collective-permute-start.8 = (bf16[192,1024]{1,0:T(8,128)(2,1)S(1)}, bf16[192,1024]{1,0:T(8,128)(2,1)S(1)}, u32[]{:S(2)}, u32[]{:S(2)}) collective-permute-start(bf16[192,1024]{1,0:T(8,128)(2,1)S(1)} %pad_maximum_fusion.1.refs_0_), channel_id=1, source_target_pairs={{0,16},{16,0},{1,17},{17,1},{2,18},{18,2},{3,19},{19,3},{4,20},{20... | collective-permute-start | bytes 1179656 | tf_op jit(solution)/shard_map/ppermute | solution.py:910
  22.1 11.3 %collective-permute-start.7 = (bf16[192,1024]{1,0:T(8,128)(2,1)S(1)}, bf16[192,1024]{1,0:T(8,128)(2,1)S(1)}, u32[]{:S(2)}, u32[]{:S(2)}) collective-permute-start(bf16[192,1024]{1,0:T(8,128)(2,1)S(1)} %pad_maximum_fusion.1.refs_0_), channel_id=1, source_target_pairs={{0,1},{1,0},{2,3},{3,2},{4,5},{5,4},{6,7},{7,6},{8,9},{9,8},{10,11... | collective-permute-start | bytes 1179656 | tf_op jit(solution)/shard_map/ppermute | solution.py:910
  23.6 10.4 %collective-permute-start.14 = (bf16[48,1536]{1,0:T(8,128)(2,1)S(1)}, bf16[48,1536]{1,0:T(8,128)(2,1)S(1)}, u32[]{:S(2)}, u32[]{:S(2)}) collective-permute-start(bf16[48,1536]{1,0:T(8,128)(2,1)S(1)} %get-tuple-element.136), channel_id=1, source_target_pairs={{0,6},{2,0},{4,2},{6,4},{1,7},{3,1},{5,3},{7,5},{8,14},{10,8},{12,... | collective-permute-start | bytes 442376 | tf_op jit(solution)/shard_map/ppermute | solution.py:143
  27.2 12.0 %collective-permute-start.13 = (bf16[48,1536]{1,0:T(8,128)(2,1)S(1)}, bf16[48,1536]{1,0:T(8,128)(2,1)S(1)}, u32[]{:S(2)}, u32[]{:S(2)}) collective-permute-start(bf16[48,1536]{1,0:T(8,128)(2,1)S(1)} %get-tuple-element.136), channel_id=1, source_target_pairs={{0,4},{2,6},{4,0},{6,2},{1,5},{3,7},{5,1},{7,3},{8,12},{10,14},{12... | collective-permute-start | bytes 442376 | tf_op jit(solution)/shard_map/ppermute | solution.py:143
  27.2 12.0 %collective-permute-start.12 = (bf16[48,1536]{1,0:T(8,128)(2,1)S(1)}, bf16[48,1536]{1,0:T(8,128)(2,1)S(1)}, u32[]{:S(2)}, u32[]{:S(2)}) collective-permute-start(bf16[48,1536]{1,0:T(8,128)(2,1)S(1)} %get-tuple-element.136), channel_id=1, source_target_pairs={{0,2},{2,4},{4,6},{6,0},{1,3},{3,5},{5,7},{7,1},{8,10},{10,12},{12... | collective-permute-start | bytes 442376 | tf_op jit(solution)/shard_map/ppermute | solution.py:143
  31.8 7.4 %collective-permute-start.10 = (bf16[96,1024]{1,0:T(8,128)(2,1)S(1)}, bf16[96,1024]{1,0:T(8,128)(2,1)S(1)}, u32[]{:S(2)}, u32[]{:S(2)}) collective-permute-start(bf16[96,1024]{1,0:T(8,128)(2,1)S(1)} %slice.17), channel_id=1, source_target_pairs={{0,1},{1,0},{2,3},{3,2},{4,5},{5,4},{6,7},{7,6},{8,9},{9,8},{10,11... | collective-permute-start | bytes 589832 | tf_op jit(solution)/shard_map/ppermute | solution.py:910
  39.3 14.0 %collective-permute-start.16 = (bf16[192,1536]{1,0:T(8,128)(2,1)S(1)}, bf16[192,1536]{1,0:T(8,128)(2,1)S(1)}, u32[]{:S(2)}, u32[]{:S(2)}) collective-permute-start(bf16[192,1536]{1,0:T(8,128)(2,1)S(1)} %pad_maximum_fusion.refs_0_), channel_id=1, source_target_pairs={{0,16},{16,0},{1,17},{17,1},{2,18},{18,2},{3,19},{19,3},{4,20},{20... | collective-permute-start | bytes 1769480 | tf_op jit(solution)/shard_map/ppermute | solution.py:910
  39.8 14.0 %collective-permute-start.15 = (bf16[192,1536]{1,0:T(8,128)(2,1)S(1)}, bf16[192,1536]{1,0:T(8,128)(2,1)S(1)}, u32[]{:S(2)}, u32[]{:S(2)}) collective-permute-start(bf16[192,1536]{1,0:T(8,128)(2,1)S(1)} %pad_maximum_fusion.refs_0_), channel_id=1, source_target_pairs={{0,1},{1,0},{2,3},{3,2},{4,5},{5,4},{6,7},{7,6},{8,9},{9,8},{10,11... | collective-permute-start | bytes 1769480 | tf_op jit(solution)/shard_map/ppermute | solution.py:910
  47.0 9.0 %collective-permute-start.11 = (f32[256,128]{1,0:T(8,128)S(1)}, f32[256,128]{1,0:T(8,128)S(1)}, u32[]{:S(2)}, u32[]{:S(2)}) collective-permute-start(f32[256,128]{1,0:T(8,128)S(1)} %get-tuple-element.131.sel_a), channel_id=1, source_target_pairs={{0,8},{8,0},{1,9},{9,1},{2,10},{10,2},{3,11},{11,3},{4,12},{12,4},... | collective-permute-start | bytes 393224 | tf_op jit(solution)/shard_map/ppermute | solution.py:910
  53.3 11.0 %collective-permute-start.18 = (bf16[96,1536]{1,0:T(8,128)(2,1)S(1)}, bf16[96,1536]{1,0:T(8,128)(2,1)S(1)}, u32[]{:S(2)}, u32[]{:S(2)}) collective-permute-start(bf16[96,1536]{1,0:T(8,128)(2,1)S(1)} %slice.19), channel_id=1, source_target_pairs={{0,1},{1,0},{2,3},{3,2},{4,5},{5,4},{6,7},{7,6},{8,9},{9,8},{10,11... | collective-permute-start | bytes 884744 | tf_op jit(solution)/shard_map/ppermute | solution.py:910
  53.9 10.4 %collective-permute-start.17 = (bf16[96,1536]{1,0:T(8,128)(2,1)S(1)}, bf16[96,1536]{1,0:T(8,128)(2,1)S(1)}, u32[]{:S(2)}, u32[]{:S(2)}) collective-permute-start(bf16[96,1536]{1,0:T(8,128)(2,1)S(1)} %slice.18), channel_id=1, source_target_pairs={{0,16},{16,0},{1,17},{17,1},{2,18},{18,2},{3,19},{19,3},{4,20},{20... | collective-permute-start | bytes 884744 | tf_op jit(solution)/shard_map/ppermute | solution.py:910
  55.4 19.7 %collective-permute-start.20 = (bf16[448,768]{1,0:T(8,128)(2,1)S(1)}, bf16[448,768]{1,0:T(8,128)(2,1)}, u32[]{:S(2)}, u32[]{:S(2)}) collective-permute-start(bf16[448,768]{1,0:T(8,128)(2,1)S(1)} %get-tuple-element.144), channel_id=1, source_target_pairs={{0,16},{16,0},{1,17},{17,1},{2,18},{18,2},{3,19},{19,3},{4,20},{20... | collective-permute-start | bytes 2064392 | tf_op jit(solution)/shard_map/ppermute | solution.py:910
  75.2 17.2 %all-to-all-start = ((bf16[8,8,3840]{2,1,0:T(8,128)(2,1)}), bf16[8,8,3840]{2,1,0:T(8,128)(2,1)}, u32[]{:S(2)}, u32[]{:S(2)}) async-start(bf16[8,8,3840]{2,1,0:T(8,128)(2,1)} %bitcast.26), calls=%async_computation | async-start | bytes 983040 | tf_op jit(solution)/shard_map/all_to_all | solution.py:915
  80.3 22.7 %collective-permute-start.22 = (bf16[672,768]{1,0:T(8,128)(2,1)}, bf16[672,768]{1,0:T(8,128)(2,1)S(1)}, u32[]{:S(2)}, u32[]{:S(2)}) collective-permute-start(bf16[672,768]{1,0:T(8,128)(2,1)} %copy-done.10), channel_id=1, source_target_pairs={{0,16},{16,0},{1,17},{17,1},{2,18},{18,2},{3,19},{19,3},{4,20},{20... | collective-permute-start | bytes 3096584 | tf_op jit(solution)/shard_map/ppermute | solution.py:910
  105.6 14.0 %collective-permute-start.24 = (bf16[64,3840]{1,0:T(8,128)(2,1)}, bf16[64,3840]{1,0:T(8,128)(2,1)}, u32[]{:S(2)}, u32[]{:S(2)}) collective-permute-start(bf16[64,3840]{1,0:T(8,128)(2,1)} %bitcast.12.own), channel_id=1, source_target_pairs={{0,16},{16,0},{1,17},{17,1},{2,18},{18,2},{3,19},{19,3},{4,20},{20... | collective-permute-start | bytes 1474568 | tf_op jit(solution)/shard_map/ppermute | solution.py:910
  108.4 20.2 %all-to-all-start.1 = ((bf16[8,8,3840]{2,1,0:T(8,128)(2,1)}), bf16[8,8,3840]{2,1,0:T(8,128)(2,1)}, u32[]{:S(2)}, u32[]{:S(2)}) async-start(bf16[8,8,3840]{2,1,0:T(8,128)(2,1)} %fusion), calls=%async_computation.1 | async-start | bytes 983040 | tf_op jit(solution)/shard_map/all_to_all | solution.py:915
  136.6 18.1 %collective-permute-start.27 = (bf16[384,768]{1,0:T(8,128)(2,1)S(1)}, bf16[384,768]{1,0:T(8,128)(2,1)S(1)}, u32[]{:S(2)}, u32[]{:S(2)}) collective-permute-start(bf16[384,768]{1,0:T(8,128)(2,1)S(1)} %get-tuple-element.168), channel_id=1, source_target_pairs={{0,1},{1,0},{2,3},{3,2},{4,5},{5,4},{6,7},{7,6},{8,9},{9,8},{10,11... | collective-permute-start | bytes 1769480 | tf_op jit(solution)/shard_map/ppermute | solution.py:910
  138.3 16.4 %collective-permute-start.28 = (bf16[384,768]{1,0:T(8,128)(2,1)S(1)}, bf16[384,768]{1,0:T(8,128)(2,1)S(1)}, u32[]{:S(2)}, u32[]{:S(2)}) collective-permute-start(bf16[384,768]{1,0:T(8,128)(2,1)S(1)} %get-tuple-element.171), channel_id=1, source_target_pairs={{0,16},{16,0},{1,17},{17,1},{2,18},{18,2},{3,19},{19,3},{4,20},{20... | collective-permute-start | bytes 1769480 | tf_op jit(solution)/shard_map/ppermute | solution.py:910
  155.0 8.5 %collective-permute-start.32 = (bf16[192,768]{1,0:T(8,128)(2,1)S(1)}, bf16[192,768]{1,0:T(8,128)(2,1)S(1)}, u32[]{:S(2)}, u32[]{:S(2)}) collective-permute-start(bf16[192,768]{1,0:T(8,128)(2,1)S(1)} %get-tuple-element.188), channel_id=1, source_target_pairs={{0,1},{1,0},{2,3},{3,2},{4,5},{5,4},{6,7},{7,6},{8,9},{9,8},{10,11... | collective-permute-start | bytes 884744 | tf_op jit(solution)/shard_map/ppermute | solution.py:910
  155.8 8.2 %collective-permute-start.31 = (bf16[192,768]{1,0:T(8,128)(2,1)S(1)}, bf16[192,768]{1,0:T(8,128)(2,1)S(1)}, u32[]{:S(2)}, u32[]{:S(2)}) collective-permute-start(bf16[192,768]{1,0:T(8,128)(2,1)S(1)} %get-tuple-element.172), channel_id=1, source_target_pairs={{0,16},{16,0},{1,17},{17,1},{2,18},{18,2},{3,19},{19,3},{4,20},{20... | collective-permute-start | bytes 884744 | tf_op jit(solution)/shard_map/ppermute | solution.py:910
  164.1 9.5 %collective-permute-start.33 = (bf16[384,512]{1,0:T(8,128)(2,1)S(1)}, bf16[384,512]{1,0:T(8,128)(2,1)S(1)}, u32[]{:S(2)}, u32[]{:S(2)}) collective-permute-start(bf16[384,512]{1,0:T(8,128)(2,1)S(1)} %get-tuple-element.192), channel_id=1, source_target_pairs={{0,1},{1,0},{2,3},{3,2},{4,5},{5,4},{6,7},{7,6},{8,9},{9,8},{10,11... | collective-permute-start | bytes 1179656 | tf_op jit(solution)/shard_map/ppermute | solution.py:910
  165.5 9.1 %collective-permute-start.34 = (bf16[384,512]{1,0:T(8,128)(2,1)S(1)}, bf16[384,512]{1,0:T(8,128)(2,1)S(1)}, u32[]{:S(2)}, u32[]{:S(2)}) collective-permute-start(bf16[384,512]{1,0:T(8,128)(2,1)S(1)} %get-tuple-element.196), channel_id=1, source_target_pairs={{0,16},{16,0},{1,17},{17,1},{2,18},{18,2},{3,19},{19,3},{4,20},{20... | collective-permute-start | bytes 1179656 | tf_op jit(solution)/shard_map/ppermute | solution.py:910
  166.4 13.1 %collective-permute-start.36 = (bf16[48,1536]{1,0:T(8,128)(2,1)S(1)}, bf16[48,1536]{1,0:T(8,128)(2,1)S(1)}, u32[]{:S(2)}, u32[]{:S(2)}) collective-permute-start(bf16[48,1536]{1,0:T(8,128)(2,1)S(1)} %get-tuple-element.200), channel_id=1, source_target_pairs={{0,6},{2,0},{4,2},{6,4},{1,7},{3,1},{5,3},{7,5},{8,14},{10,8},{12,... | collective-permute-start | bytes 442376 | tf_op jit(solution)/shard_map/ppermute | solution.py:231
  169.6 11.8 %collective-permute-start.37 = (bf16[48,1536]{1,0:T(8,128)(2,1)S(1)}, bf16[48,1536]{1,0:T(8,128)(2,1)S(1)}, u32[]{:S(2)}, u32[]{:S(2)}) collective-permute-start(bf16[48,1536]{1,0:T(8,128)(2,1)S(1)} %get-tuple-element.201), channel_id=1, source_target_pairs={{0,4},{2,6},{4,0},{6,2},{1,5},{3,7},{5,1},{7,3},{8,12},{10,14},{12... | collective-permute-start | bytes 442376 | tf_op jit(solution)/shard_map/ppermute | solution.py:231
  169.6 11.8 %collective-permute-start.38 = (bf16[48,1536]{1,0:T(8,128)(2,1)S(1)}, bf16[48,1536]{1,0:T(8,128)(2,1)S(1)}, u32[]{:S(2)}, u32[]{:S(2)}) collective-permute-start(bf16[48,1536]{1,0:T(8,128)(2,1)S(1)} %get-tuple-element.202), channel_id=1, source_target_pairs={{0,2},{2,4},{4,6},{6,0},{1,3},{3,5},{5,7},{7,1},{8,10},{10,12},{12... | collective-permute-start | bytes 442376 | tf_op jit(solution)/shard_map/ppermute | solution.py:231
  179.5 14.7 %collective-permute-start.30 = (f32[128,768]{1,0:T(8,128)S(1)}, f32[128,768]{1,0:T(8,128)S(1)}, u32[]{:S(2)}, u32[]{:S(2)}) collective-permute-start(f32[128,768]{1,0:T(8,128)S(1)} %get-tuple-element.183), channel_id=1, source_target_pairs={{0,8},{8,0},{1,9},{9,1},{2,10},{10,2},{3,11},{11,3},{4,12},{12,4},... | collective-permute-start | bytes 1179656 | tf_op jit(solution)/shard_map/ppermute | solution.py:910
  185.1 8.1 %collective-permute-start.41 = (bf16[48,1024]{1,0:T(8,128)(2,1)S(1)}, bf16[48,1024]{1,0:T(8,128)(2,1)S(1)}, u32[]{:S(2)}, u32[]{:S(2)}) collective-permute-start(bf16[48,1024]{1,0:T(8,128)(2,1)S(1)} %get-tuple-element.207), channel_id=1, source_target_pairs={{0,4},{2,6},{4,0},{6,2},{1,5},{3,7},{5,1},{7,3},{8,12},{10,14},{12... | collective-permute-start | bytes 294920 | tf_op jit(solution)/shard_map/ppermute | solution.py:231
  185.1 8.1 %collective-permute-start.42 = (bf16[48,1024]{1,0:T(8,128)(2,1)S(1)}, bf16[48,1024]{1,0:T(8,128)(2,1)S(1)}, u32[]{:S(2)}, u32[]{:S(2)}) collective-permute-start(bf16[48,1024]{1,0:T(8,128)(2,1)S(1)} %get-tuple-element.208), channel_id=1, source_target_pairs={{0,2},{2,4},{4,6},{6,0},{1,3},{3,5},{5,7},{7,1},{8,10},{10,12},{12... | collective-permute-start | bytes 294920 | tf_op jit(solution)/shard_map/ppermute | solution.py:231
  (37 other events, 250.6 us)

commit v6 on v5

--- a/solution.py
+++ b/solution.py
@@ -589,7 +589,7 @@
     return moves
 
 
-PART = 256
+PART = 768
 
 
 def expert_own_kernel(slots, parts, own, peer, up, down, *refs):

time: 198 us -> 196 us (0.990)
  transfers between devices with their start and end apart: 46 -> 46, of which waited for: 25 -> 26; matrix products, arithmetic and copies ran while one was open for 1% -> 1% of each run, Pallas kernels for 33% -> 32%
where the time goes in v6:
time: 196 us
  Pallas kernels  75.8 us (39%)
  waiting for transfers between devices  65.5 us (33%)
  starting transfers between devices  52.2 us (27%)
    pallas_call x23, Pallas kernels, call(): pl.pallas_call(kernel, grid=(1,) if windowed else (), out_shape=[(pltpu.H...  75.8 us
    ppermute x32, waiting for transfers between devices, swap(): return lax.ppermute(values, axis, [(0, 1), (1, 0)])  33.2 us
    ppermute x32, starting transfers between devices, swap(): return lax.ppermute(values, axis, [(0, 1), (1, 0)])  24 us
    ppermute x6, waiting for transfers between devices, gather(): lax.ppermute(piece, 'z', [(i, (i + k) % 4) for i in range(4)])  12.1 us
    all_to_all x2, waiting for transfers between devices, exchange(): lax.all_to_all(parts, ('z', 'x'), split_axis=0, concat_axis=0, tiled=True)  11.5 us
    all_to_all x2, starting transfers between devices, exchange(): lax.all_to_all(parts, ('z', 'x'), split_axis=0, concat_axis=0, tiled=True)  10.9 us
    ppermute x6, starting transfers between devices, gather(): lax.ppermute(piece, 'z', [(i, (i + k) % 4) for i in range(4)])  9.28 us
    ppermute x6, waiting for transfers between devices, reduce3(): lax.ppermute(parts[k], 'z', [(i, (i - k) % 4) for i in range(4)])  8.62 us
  transfers between devices with their start and end apart: 46, of which 26 were waited for; matrix products, arithmetic and copies ran while one was open for 1% of the time, Pallas kernels for 32%

profile of v6, /device:TPU:0, one launch (start us, length us, event | category | flops | bytes accessed | tf_op | source)
XLA Modules:
  0.0 195.9 jit_solution(11469844375543699117)
XLA Ops:
  0.8 2.1 %pack.1 = (bf16[24,1664]{1,0:T(8,128)(2,1)S(1)}, bf16[24,1664]{1,0:T(8,128)(2,1)S(1)}, bf16[48,256]{1,0:T(8,128)(2,1)S(1)}, bf16[416,768]{1,0:T(8,128)(2,1)S(1)}) custom-call(s32[4]{0:T(128)S(1)} %pad_add_fusion.1.idx, bf16[24,3072]{1,0:T(8,128)(2,1)} %in_proj.3, bf16[1,24]{1,0:T(2,128)(2,1)} %bitcast.22, bf16[1,24]{1,0:T(2,128)(2,1)} %bitcast.28, ...), custom_call_target="tpu_custom_call" | custom-call | flops 300000000 | bytes 900000 | tf_op jit(solution)/shard_map/pack/pallas_call | solution.py:86
  2.9 3.0 %collective-permute-start.6 = (bf16[416,768]{1,0:T(8,128)(2,1)S(1)}, bf16[416,768]{1,0:T(8,128)(2,1)S(1)}, u32[]{:S(2)}, u32[]{:S(2)}) collective-permute-start(bf16[416,768]{1,0:T(8,128)(2,1)S(1)} %get-tuple-element.124), channel_id=1, source_target_pairs={{0,16},{16,0},{1,17},{17,1},{2,18},{18,2},{3,19},{19,3},{4,20},{20... | collective-permute-start | bytes 1916936 | tf_op jit(solution)/shard_map/ppermute | solution.py:910
  7.8 3.7 %collective-permute-start.5 = (bf16[48,1024]{1,0:T(8,128)(2,1)S(1)}, bf16[48,1024]{1,0:T(8,128)(2,1)S(1)}, u32[]{:S(2)}, u32[]{:S(2)}) collective-permute-start(bf16[48,1024]{1,0:T(8,128)(2,1)S(1)} %get-tuple-element.123), channel_id=1, source_target_pairs={{0,6},{2,0},{4,2},{6,4},{1,7},{3,1},{5,3},{7,5},{8,14},{10,8},{12,... | collective-permute-start | bytes 294920 | tf_op jit(solution)/shard_map/ppermute | solution.py:143
  14.6 6.3 %collective-permute-done.4 = bf16[48,1024]{1,0:T(8,128)(2,1)S(1)} collective-permute-done((bf16[48,1024]{1,0:T(8,128)(2,1)S(1)}, bf16[48,1024]{1,0:T(8,128)(2,1)S(1)}, u32[]{:S(2)}, u32[]{:S(2)}) %collective-permute-start.4) | collective-permute-done | bytes 98336 | tf_op jit(solution)/shard_map/ppermute | solution.py:143
  23.6 3.6 %collective-permute-start.14 = (bf16[48,1536]{1,0:T(8,128)(2,1)S(1)}, bf16[48,1536]{1,0:T(8,128)(2,1)S(1)}, u32[]{:S(2)}, u32[]{:S(2)}) collective-permute-start(bf16[48,1536]{1,0:T(8,128)(2,1)S(1)} %get-tuple-element.136), channel_id=1, source_target_pairs={{0,6},{2,0},{4,2},{6,4},{1,7},{3,1},{5,3},{7,5},{8,14},{10,8},{12,... | collective-permute-start | bytes 442376 | tf_op jit(solution)/shard_map/ppermute | solution.py:143
  28.2 3.6 %collective-permute-done.8.refs_2_ = bf16[192,1024]{1,0:T(8,128)(2,1)S(1)} collective-permute-done((bf16[192,1024]{1,0:T(8,128)(2,1)S(1)}, bf16[192,1024]{1,0:T(8,128)(2,1)S(1)}, u32[]{:S(2)}, u32[]{:S(2)}) %collective-permute-start.8) | collective-permute-done | bytes 393248 | tf_op jit(solution)/shard_map/ppermute | solution.py:910
  34.0 5.2 %collective-permute-done.13 = bf16[48,1536]{1,0:T(8,128)(2,1)S(1)} collective-permute-done((bf16[48,1536]{1,0:T(8,128)(2,1)S(1)}, bf16[48,1536]{1,0:T(8,128)(2,1)S(1)}, u32[]{:S(2)}, u32[]{:S(2)}) %collective-permute-start.13) | collective-permute-done | bytes 147488 | tf_op jit(solution)/shard_map/ppermute | solution.py:143
  41.0 6.0 %enter.1 = (bf16[256,768]{1,0:T(8,128)(2,1)S(1)}, f32[256,768]{1,0:T(8,128)}, bf16[256,768]{1,0:T(8,128)(2,1)S(1)}, f32[256,128]{1,0:T(8,128)S(1)}, f32[24,768]{...) custom-call(s32[4]{0:T(128)S(1)} %pad_add_fusion.1.idx, s32[2,8]{1,0:T(2,128)S(1)} %pad_add_fusion.lens, ...), custom_call_target="tpu_custom_call" | custom-call | flops 1500000000 | bytes 4500000 | tf_op jit(solution)/shard_map/enter/pallas_call | solution.py:86
  47.1 6.2 %collective-permute-done.16.refs_2_ = bf16[192,1536]{1,0:T(8,128)(2,1)S(1)} collective-permute-done((bf16[192,1536]{1,0:T(8,128)(2,1)S(1)}, bf16[192,1536]{1,0:T(8,128)(2,1)S(1)}, u32[]{:S(2)}, u32[]{:S(2)}) %collective-permute-start.16) | collective-permute-done | bytes 589856 | tf_op jit(solution)/shard_map/ppermute | solution.py:910
  56.0 8.3 %scan.1 = (f32[256,768]{1,0:T(8,128)S(1)}, f32[256,128]{1,0:T(8,128)}, f32[32,16,768]{2,1,0:T(8,128)}) custom-call(s32[2,8]{1,0:T(2,128)S(1)} %pad_add_fusion.lens, f32[256,128]{1,0:T(8,128)S(1)} %get-tuple-element.131.sel_a, f32[256,128]{1,0:T(8,128)S(1)} %collective-permute-done.11.sel_b, bf16[256,768]{1,0:T(8,128)(2,1)S(1)} %get-tuple-element.130.xc, ...), custom_call_target="tpu_custom_call" | custom-call | flops 2700000000 | bytes 8100000 | tf_op jit(solution)/shard_map/scan/pallas_call | solution.py:86
  64.3 4.9 %gate.1 = (f32[128,768]{1,0:T(8,128)S(1)}, f32[128,768]{1,0:T(8,128)S(1)}, bf16[768,1536]{1,0:T(8,128)(2,1)S(1)}) custom-call(s32[4]{0:T(128)S(1)} %pad_add_fusion.1.idx, bf16[256,768]{1,0:T(8,128)(2,1)S(1)} %get-tuple-element.129.u, bf16[256,768]{1,0:T(8,128)(2,1)S(1)} %get-tuple-element.130.xc, f32[256,768]{1,0:T(8,128)S(1)} %get-tuple-element.134.ys, ...), custom_call_target="tpu_custom_call" | custom-call | flops 1500000000 | bytes 4500000 | tf_op jit(solution)/shard_map/gate/pallas_call | solution.py:86
  69.3 1.7 collective-permute-done.19.got
  71.0 2.6 %moe_enter.1 = (bf16[64,3840]{1,0:T(8,128)(2,1)}, f32[128,768]{1,0:T(8,128)}, f32[128,128]{1,0:T(8,128)}) custom-call(s32[1,8]{1,0:T(1,128)S(1)} %copy-done.9, bf16[128,768]{1,0:T(8,128)(2,1)S(1)} %copy-done.4, bf16[128,768]{1,0:T(8,128)(2,1)} %cot.3, s32[1,128]{1,0:T(1,128)S(1)} %bitcast.25, f32[128,768]{1,0:T(8,128)S(1)} %get-tuple-element.138.mine, ...), custom_call_target="tpu_custom_call" | custom-call | flops 1500000000 | bytes 4500000 | tf_op jit(solution)/shard_map/moe_enter/pallas_call | solution.py:86
  75.2 5.1 %all-to-all-start = ((bf16[8,8,3840]{2,1,0:T(8,128)(2,1)}), bf16[8,8,3840]{2,1,0:T(8,128)(2,1)}, u32[]{:S(2)}, u32[]{:S(2)}) async-start(bf16[8,8,3840]{2,1,0:T(8,128)(2,1)} %bitcast.26), calls=%async_computation | async-start | bytes 983040 | tf_op jit(solution)/shard_map/all_to_all | solution.py:915
  81.5 10.9 %all-to-all-done = bf16[8,8,3840]{2,1,0:T(8,128)(2,1)} async-done(((bf16[8,8,3840]{2,1,0:T(8,128)(2,1)}), bf16[8,8,3840]{2,1,0:T(8,128)(2,1)}, u32[]{:S(2)}, u32[]{:S(2)}) %all-to-all-start) | async-done | bytes 491552 | tf_op jit(solution)/shard_map/all_to_all | solution.py:915
  92.4 2.1 %collective-permute-done.21.peer = bf16[64,3840]{1,0:T(8,128)(2,1)S(1)} collective-permute-done((bf16[64,3840]{1,0:T(8,128)(2,1)}, bf16[64,3840]{1,0:T(8,128)(2,1)S(1)}, u32[]{:S(2)}, u32[]{:S(2)}) %collective-permute-start.21) | collective-permute-done | bytes 491552 | tf_op jit(solution)/shard_map/ppermute | solution.py:910
  94.5 5.6 %expert_own.1 = (bf16[320,1536]{1,0:T(8,128)(2,1)S(1)}, f32[320,1536]{1,0:T(8,128)S(1)}, bf16[320,768]{1,0:T(8,128)(2,1)S(1)}, f32[320,768]{1,0:T(8,128)S(1)}, bf16[768,768]{1,0:T(8,128)(2,1)S(1)}) custom-call(bf16[64,3840]{1,0:T(8,128)(2,1)} %bitcast.12.own, bf16[64,3840]{1,0:T(8,128)(2,1)S(1)} %collective-permute-done.21.peer, bf16[1,768,768]{2,1,0:T(8,128)(2,1)} %up.8, ...), custom_call_target="tpu_custom_call" | custom-call | flops 1800000000 | bytes 5400000 | tf_op jit(solution)/shard_map/expert_own/pallas_call | solution.py:86
  100.1 2.9 %collective-permute-done.22.refs_1_ = bf16[672,768]{1,0:T(8,128)(2,1)S(1)} collective-permute-done((bf16[672,768]{1,0:T(8,128)(2,1)}, bf16[672,768]{1,0:T(8,128)(2,1)S(1)}, u32[]{:S(2)}, u32[]{:S(2)}) %collective-permute-start.22) | collective-permute-done | bytes 1032224 | tf_op jit(solution)/shard_map/ppermute | solution.py:910
  103.0 2.4 %expert_other.1 = (f32[64,3840]{1,0:T(8,128)S(1)}, bf16[64,3840]{1,0:T(8,128)(2,1)S(1)}) custom-call(bf16[320,1536]{1,0:T(8,128)(2,1)S(1)} %get-tuple-element.146.both, f32[320,1536]{1,0:T(8,128)S(1)} %get-tuple-element.147.acc, bf16[320,768]{1,0:T(8,128)(2,1)S(1)} %get-tuple-element.148.act, f32[320,768]{1,0:T(8,128)S(1)} %get-tuple-element.149.slope, ...), custom_call_target="tpu_custom_call" | custom-call | flops 900000000 | bytes 2700000 | tf_op jit(solution)/shard_map/expert_other/pallas_call | solution.py:86
  108.2 5.7 %all-to-all-start.1 = ((bf16[8,8,3840]{2,1,0:T(8,128)(2,1)}), bf16[8,8,3840]{2,1,0:T(8,128)(2,1)}, u32[]{:S(2)}, u32[]{:S(2)}) async-start(bf16[8,8,3840]{2,1,0:T(8,128)(2,1)} %fusion), calls=%async_computation.1 | async-start | bytes 983040 | tf_op jit(solution)/shard_map/all_to_all | solution.py:915
  113.9 4.0 %near_grad.1 = (f32[1,768,768]{2,1,0:T(8,128)S(1)}, f32[1,768,768]{2,1,0:T(8,128)S(1)}) custom-call(bf16[320,1536]{1,0:T(8,128)(2,1)S(1)} %copy-done.3, bf16[1,768,768]{2,1,0:T(8,128)(2,1)} %up.8, bf16[1,768,768]{2,1,0:T(8,128)(2,1)} %down.7), custom_call_target="tpu_custom_call" | custom-call | flops 1200000000 | bytes 3600000 | tf_op jit(solution)/shard_map/near_grad/pallas_call | solution.py:86
  119.4 2.1 %collective-permute-done.25.peer_y = bf16[64,3840]{1,0:T(8,128)(2,1)S(1)} collective-permute-done((bf16[64,3840]{1,0:T(8,128)(2,1)}, bf16[64,3840]{1,0:T(8,128)(2,1)S(1)}, u32[]{:S(2)}, u32[]{:S(2)}) %collective-permute-start.25) | collective-permute-done | bytes 491552 | tf_op jit(solution)/shard_map/ppermute | solution.py:910
  121.5 5.9 %far_grad.1 = (f32[1,768,768]{2,1,0:T(8,128)}, f32[1,768,768]{2,1,0:T(8,128)}) custom-call(bf16[64,3840]{1,0:T(8,128)(2,1)} %collective-permute-done.24.own_y, bf16[64,3840]{1,0:T(8,128)(2,1)S(1)} %collective-permute-done.25.peer_y, bf16[1,768,768]{2,1,0:T(8,128)(2,1)} %up.8, bf16[1,768,768]{2,1,0:T(8,128)(2,1)} %down.7, ...), custom_call_target="tpu_custom_call" | custom-call | flops 2400000000 | bytes 7200000 | tf_op jit(solution)/shard_map/far_grad/pallas_call | solution.py:86
  128.1 3.3 %moe_leave.1 = (bf16[128,768]{1,0:T(8,128)(2,1)}, f32[128,768]{1,0:T(8,128)S(1)}, bf16[128,768]{1,0:T(8,128)(2,1)S(1)}, f32[16,768]{1,0:T(8,128)S(1)}) custom-call(s32[1,8]{1,0:T(1,128)} %lens.3, s32[1,128]{1,0:T(1,128)} %bitcast.24, bf16[128,768]{1,0:T(8,128)(2,1)} %cot.3, f32[128,768]{1,0:T(8,128)} %get-tuple-element.141.hidden, ...), custom_call_target="tpu_custom_call" | custom-call | flops 1500000000 | bytes 4500000 | tf_op jit(solution)/shard_map/moe_leave/pallas_call | solution.py:86
  132.9 3.2 %gate_back.1 = (f32[256,768]{1,0:T(8,128)S(1)}, bf16[256,768]{1,0:T(8,128)(2,1)S(1)}, bf16[384,768]{1,0:T(8,128)(2,1)S(1)}, bf16[384,768]{1,0:T(8,128)(2,1)S(1)}...) custom-call(s32[4]{0:T(128)S(1)} %pad_add_fusion.1.idx, bf16[128,768]{1,0:T(8,128)(2,1)S(1)} %get-tuple-element.161.gbr_a, ...), custom_call_target="tpu_custom_call" | custom-call | flops 1500000000 | bytes 4500000 | tf_op jit(solution)/shard_map/gate_back/pallas_call | solution.py:86
  138.9 15.2 %scan_back.1 = (f32[256,128]{1,0:T(8,128)S(1)}, f32[256,768]{1,0:T(8,128)S(1)}, bf16[256,768]{1,0:T(8,128)(2,1)S(1)}, bf16[256,128]{1,0:T(8,128)(2,1)S(1)}, f32[24,768]{1,0:T(8,128)S(1)}) custom-call(s32[2,8]{1,0:T(2,128)S(1)} %pad_add_fusion.lens, f32[256,768]{1,0:T(8,128)S(1)} %get-tuple-element.163.gy_s, bf16[256,768]{1,0:T(8,128)(2,1)S(1)} %copy-done.17, ...), custom_call_target="tpu_custom_call" | custom-call | flops 4800000000 | bytes 14400000 | tf_op jit(solution)/shard_map/scan_back/pallas_call | solution.py:86
  157.2 4.1 %leave.1 = (bf16[256,768]{1,0:T(8,128)(2,1)S(1)}, bf16[384,512]{1,0:T(8,128)(2,1)S(1)}, bf16[384,512]{1,0:T(8,128)(2,1)S(1)}, bf16[384,512]{1,0:T(8,128)(2,1)S(1)}, bf16[384,512]{1,0:T(8,128)(2,1)S(1)}) custom-call(s32[4]{0:T(128)S(1)} %pad_add_fusion.1.idx, s32[2,8]{1,0:T(2,128)S(1)} %pad_add_fusion.lens, s32[2,768]{1,0:T(2,128)S(1)} %copy-done.7, ...), custom_call_target="tpu_custom_call" | custom-call | flops 1500000000 | bytes 4500000 | tf_op jit(solution)/shard_map/leave/pallas_call | solution.py:86
  165.7 2.9 %collective-permute-start.36 = (bf16[48,1536]{1,0:T(8,128)(2,1)S(1)}, bf16[48,1536]{1,0:T(8,128)(2,1)S(1)}, u32[]{:S(2)}, u32[]{:S(2)}) collective-permute-start(bf16[48,1536]{1,0:T(8,128)(2,1)S(1)} %get-tuple-element.200), channel_id=1, source_target_pairs={{0,6},{2,0},{4,2},{6,4},{1,7},{3,1},{5,3},{7,5},{8,14},{10,8},{12,... | collective-permute-start | bytes 442376 | tf_op jit(solution)/shard_map/ppermute | solution.py:231
  169.7 3.1 %collective-permute-done.33.a_in = bf16[384,512]{1,0:T(8,128)(2,1)S(1)} collective-permute-done((bf16[384,512]{1,0:T(8,128)(2,1)S(1)}, bf16[384,512]{1,0:T(8,128)(2,1)S(1)}, u32[]{:S(2)}, u32[]{:S(2)}) %collective-permute-start.33) | collective-permute-done | bytes 393248 | tf_op jit(solution)/shard_map/ppermute | solution.py:910
  175.9 2.8 %back.1 = (f32[128,768]{1,0:T(8,128)S(1)}, f32[128,768]{1,0:T(8,128)S(1)}) custom-call(s32[4]{0:T(128)S(1)} %pad_add_fusion.1.idx, s32[2,768]{1,0:T(2,128)S(1)} %copy-done.7, bf16[256,768]{1,0:T(8,128)(2,1)S(1)} %get-tuple-element.180.gxin, bf16[256,768]{1,0:T(8,128)(2,1)S(1)} %get-tuple-element.181.gzg, bf16[768,1024]{1,0:T(8,128)(2,1)S(1)} %copy-done.1, ...), custom_call_target="tpu_custom_call" | custom-call | flops 900000000 | bytes 2700000 | tf_op jit(solution)/shard_map/back/pallas_call | solution.py:86
  181.1 2.9 %collective-permute-start.40 = (bf16[48,1024]{1,0:T(8,128)(2,1)S(1)}, bf16[48,1024]{1,0:T(8,128)(2,1)S(1)}, u32[]{:S(2)}, u32[]{:S(2)}) collective-permute-start(bf16[48,1024]{1,0:T(8,128)(2,1)S(1)} %get-tuple-element.206), channel_id=1, source_target_pairs={{0,6},{2,0},{4,2},{6,4},{1,7},{3,1},{5,3},{7,5},{8,14},{10,8},{12,... | collective-permute-start | bytes 294920 | tf_op jit(solution)/shard_map/ppermute | solution.py:231
  186.7 5.4 %collective-permute-done.41.refs_2_ = bf16[48,1024]{1,0:T(8,128)(2,1)S(1)} collective-permute-done((bf16[48,1024]{1,0:T(8,128)(2,1)S(1)}, bf16[48,1024]{1,0:T(8,128)(2,1)S(1)}, u32[]{:S(2)}, u32[]{:S(2)}) %collective-permute-start.41) | collective-permute-done | bytes 98336 | tf_op jit(solution)/shard_map/ppermute | solution.py:231
  (140 shorter events, 47.9 us)
Async XLA Ops:
  2.9 18.0 %collective-permute-start.6 = (bf16[416,768]{1,0:T(8,128)(2,1)S(1)}, bf16[416,768]{1,0:T(8,128)(2,1)S(1)}, u32[]{:S(2)}, u32[]{:S(2)}) collective-permute-start(bf16[416,768]{1,0:T(8,128)(2,1)S(1)} %get-tuple-element.124), channel_id=1, source_target_pairs={{0,16},{16,0},{1,17},{17,1},{2,18},{18,2},{3,19},{19,3},{4,20},{20... | collective-permute-start | bytes 1916936 | tf_op jit(solution)/shard_map/ppermute | solution.py:910
  6.0 15.0 %collective-permute-start.1 = (bf16[128,768]{1,0:T(8,128)(2,1)S(1)}, bf16[128,768]{1,0:T(8,128)(2,1)S(1)}, u32[]{:S(2)}, u32[]{:S(2)}) collective-permute-start(bf16[128,768]{1,0:T(8,128)(2,1)S(1)} %copy-done.4), channel_id=1, source_target_pairs={{0,8},{8,0},{1,9},{9,1},{2,10},{10,2},{3,11},{11,3},{4,12},{12,4},... | collective-permute-start | bytes 589832 | tf_op jit(solution)/shard_map/ppermute | solution.py:910
  11.4 9.4 %collective-permute-start.4 = (bf16[48,1024]{1,0:T(8,128)(2,1)S(1)}, bf16[48,1024]{1,0:T(8,128)(2,1)S(1)}, u32[]{:S(2)}, u32[]{:S(2)}) collective-permute-start(bf16[48,1024]{1,0:T(8,128)(2,1)S(1)} %get-tuple-element.123), channel_id=1, source_target_pairs={{0,4},{2,6},{4,0},{6,2},{1,5},{3,7},{5,1},{7,3},{8,12},{10,14},{12... | collective-permute-start | bytes 294920 | tf_op jit(solution)/shard_map/ppermute | solution.py:143
  11.4 9.4 %collective-permute-start.3 = (bf16[48,1024]{1,0:T(8,128)(2,1)S(1)}, bf16[48,1024]{1,0:T(8,128)(2,1)S(1)}, u32[]{:S(2)}, u32[]{:S(2)}) collective-permute-start(bf16[48,1024]{1,0:T(8,128)(2,1)S(1)} %get-tuple-element.123), channel_id=1, source_target_pairs={{0,2},{2,4},{4,6},{6,0},{1,3},{3,5},{5,7},{7,1},{8,10},{10,12},{12... | collective-permute-start | bytes 294920 | tf_op jit(solution)/shard_map/ppermute | solution.py:143
  21.0 10.8 %collective-permute-start.8 = (bf16[192,1024]{1,0:T(8,128)(2,1)S(1)}, bf16[192,1024]{1,0:T(8,128)(2,1)S(1)}, u32[]{:S(2)}, u32[]{:S(2)}) collective-permute-start(bf16[192,1024]{1,0:T(8,128)(2,1)S(1)} %pad_maximum_fusion.1.refs_0_), channel_id=1, source_target_pairs={{0,16},{16,0},{1,17},{17,1},{2,18},{18,2},{3,19},{19,3},{4,20},{20... | collective-permute-start | bytes 1179656 | tf_op jit(solution)/shard_map/ppermute | solution.py:910
  22.1 11.3 %collective-permute-start.7 = (bf16[192,1024]{1,0:T(8,128)(2,1)S(1)}, bf16[192,1024]{1,0:T(8,128)(2,1)S(1)}, u32[]{:S(2)}, u32[]{:S(2)}) collective-permute-start(bf16[192,1024]{1,0:T(8,128)(2,1)S(1)} %pad_maximum_fusion.1.refs_0_), channel_id=1, source_target_pairs={{0,1},{1,0},{2,3},{3,2},{4,5},{5,4},{6,7},{7,6},{8,9},{9,8},{10,11... | collective-permute-start | bytes 1179656 | tf_op jit(solution)/shard_map/ppermute | solution.py:910
  23.6 10.4 %collective-permute-start.14 = (bf16[48,1536]{1,0:T(8,128)(2,1)S(1)}, bf16[48,1536]{1,0:T(8,128)(2,1)S(1)}, u32[]{:S(2)}, u32[]{:S(2)}) collective-permute-start(bf16[48,1536]{1,0:T(8,128)(2,1)S(1)} %get-tuple-element.136), channel_id=1, source_target_pairs={{0,6},{2,0},{4,2},{6,4},{1,7},{3,1},{5,3},{7,5},{8,14},{10,8},{12,... | collective-permute-start | bytes 442376 | tf_op jit(solution)/shard_map/ppermute | solution.py:143
  27.2 12.0 %collective-permute-start.13 = (bf16[48,1536]{1,0:T(8,128)(2,1)S(1)}, bf16[48,1536]{1,0:T(8,128)(2,1)S(1)}, u32[]{:S(2)}, u32[]{:S(2)}) collective-permute-start(bf16[48,1536]{1,0:T(8,128)(2,1)S(1)} %get-tuple-element.136), channel_id=1, source_target_pairs={{0,4},{2,6},{4,0},{6,2},{1,5},{3,7},{5,1},{7,3},{8,12},{10,14},{12... | collective-permute-start | bytes 442376 | tf_op jit(solution)/shard_map/ppermute | solution.py:143
  27.2 12.0 %collective-permute-start.12 = (bf16[48,1536]{1,0:T(8,128)(2,1)S(1)}, bf16[48,1536]{1,0:T(8,128)(2,1)S(1)}, u32[]{:S(2)}, u32[]{:S(2)}) collective-permute-start(bf16[48,1536]{1,0:T(8,128)(2,1)S(1)} %get-tuple-element.136), channel_id=1, source_target_pairs={{0,2},{2,4},{4,6},{6,0},{1,3},{3,5},{5,7},{7,1},{8,10},{10,12},{12... | collective-permute-start | bytes 442376 | tf_op jit(solution)/shard_map/ppermute | solution.py:143
  31.8 7.4 %collective-permute-start.10 = (bf16[96,1024]{1,0:T(8,128)(2,1)S(1)}, bf16[96,1024]{1,0:T(8,128)(2,1)S(1)}, u32[]{:S(2)}, u32[]{:S(2)}) collective-permute-start(bf16[96,1024]{1,0:T(8,128)(2,1)S(1)} %slice.17), channel_id=1, source_target_pairs={{0,1},{1,0},{2,3},{3,2},{4,5},{5,4},{6,7},{7,6},{8,9},{9,8},{10,11... | collective-permute-start | bytes 589832 | tf_op jit(solution)/shard_map/ppermute | solution.py:910
  39.3 14.0 %collective-permute-start.16 = (bf16[192,1536]{1,0:T(8,128)(2,1)S(1)}, bf16[192,1536]{1,0:T(8,128)(2,1)S(1)}, u32[]{:S(2)}, u32[]{:S(2)}) collective-permute-start(bf16[192,1536]{1,0:T(8,128)(2,1)S(1)} %pad_maximum_fusion.refs_0_), channel_id=1, source_target_pairs={{0,16},{16,0},{1,17},{17,1},{2,18},{18,2},{3,19},{19,3},{4,20},{20... | collective-permute-start | bytes 1769480 | tf_op jit(solution)/shard_map/ppermute | solution.py:910
  39.8 14.0 %collective-permute-start.15 = (bf16[192,1536]{1,0:T(8,128)(2,1)S(1)}, bf16[192,1536]{1,0:T(8,128)(2,1)S(1)}, u32[]{:S(2)}, u32[]{:S(2)}) collective-permute-start(bf16[192,1536]{1,0:T(8,128)(2,1)S(1)} %pad_maximum_fusion.refs_0_), channel_id=1, source_target_pairs={{0,1},{1,0},{2,3},{3,2},{4,5},{5,4},{6,7},{7,6},{8,9},{9,8},{10,11... | collective-permute-start | bytes 1769480 | tf_op jit(solution)/shard_map/ppermute | solution.py:910
  47.0 9.0 %collective-permute-start.11 = (f32[256,128]{1,0:T(8,128)S(1)}, f32[256,128]{1,0:T(8,128)S(1)}, u32[]{:S(2)}, u32[]{:S(2)}) collective-permute-start(f32[256,128]{1,0:T(8,128)S(1)} %get-tuple-element.131.sel_a), channel_id=1, source_target_pairs={{0,8},{8,0},{1,9},{9,1},{2,10},{10,2},{3,11},{11,3},{4,12},{12,4},... | collective-permute-start | bytes 393224 | tf_op jit(solution)/shard_map/ppermute | solution.py:910
  53.3 11.0 %collective-permute-start.18 = (bf16[96,1536]{1,0:T(8,128)(2,1)S(1)}, bf16[96,1536]{1,0:T(8,128)(2,1)S(1)}, u32[]{:S(2)}, u32[]{:S(2)}) collective-permute-start(bf16[96,1536]{1,0:T(8,128)(2,1)S(1)} %slice.19), channel_id=1, source_target_pairs={{0,1},{1,0},{2,3},{3,2},{4,5},{5,4},{6,7},{7,6},{8,9},{9,8},{10,11... | collective-permute-start | bytes 884744 | tf_op jit(solution)/shard_map/ppermute | solution.py:910
  53.9 10.4 %collective-permute-start.17 = (bf16[96,1536]{1,0:T(8,128)(2,1)S(1)}, bf16[96,1536]{1,0:T(8,128)(2,1)S(1)}, u32[]{:S(2)}, u32[]{:S(2)}) collective-permute-start(bf16[96,1536]{1,0:T(8,128)(2,1)S(1)} %slice.18), channel_id=1, source_target_pairs={{0,16},{16,0},{1,17},{17,1},{2,18},{18,2},{3,19},{19,3},{4,20},{20... | collective-permute-start | bytes 884744 | tf_op jit(solution)/shard_map/ppermute | solution.py:910
  55.4 19.7 %collective-permute-start.20 = (bf16[448,768]{1,0:T(8,128)(2,1)S(1)}, bf16[448,768]{1,0:T(8,128)(2,1)}, u32[]{:S(2)}, u32[]{:S(2)}) collective-permute-start(bf16[448,768]{1,0:T(8,128)(2,1)S(1)} %get-tuple-element.144), channel_id=1, source_target_pairs={{0,16},{16,0},{1,17},{17,1},{2,18},{18,2},{3,19},{19,3},{4,20},{20... | collective-permute-start | bytes 2064392 | tf_op jit(solution)/shard_map/ppermute | solution.py:910
  75.2 17.2 %all-to-all-start = ((bf16[8,8,3840]{2,1,0:T(8,128)(2,1)}), bf16[8,8,3840]{2,1,0:T(8,128)(2,1)}, u32[]{:S(2)}, u32[]{:S(2)}) async-start(bf16[8,8,3840]{2,1,0:T(8,128)(2,1)} %bitcast.26), calls=%async_computation | async-start | bytes 983040 | tf_op jit(solution)/shard_map/all_to_all | solution.py:915
  80.3 22.6 %collective-permute-start.22 = (bf16[672,768]{1,0:T(8,128)(2,1)}, bf16[672,768]{1,0:T(8,128)(2,1)S(1)}, u32[]{:S(2)}, u32[]{:S(2)}) collective-permute-start(bf16[672,768]{1,0:T(8,128)(2,1)} %copy-done.10), channel_id=1, source_target_pairs={{0,16},{16,0},{1,17},{17,1},{2,18},{18,2},{3,19},{19,3},{4,20},{20... | collective-permute-start | bytes 3096584 | tf_op jit(solution)/shard_map/ppermute | solution.py:910
  105.4 14.0 %collective-permute-start.24 = (bf16[64,3840]{1,0:T(8,128)(2,1)}, bf16[64,3840]{1,0:T(8,128)(2,1)}, u32[]{:S(2)}, u32[]{:S(2)}) collective-permute-start(bf16[64,3840]{1,0:T(8,128)(2,1)} %bitcast.12.own), channel_id=1, source_target_pairs={{0,16},{16,0},{1,17},{17,1},{2,18},{18,2},{3,19},{19,3},{4,20},{20... | collective-permute-start | bytes 1474568 | tf_op jit(solution)/shard_map/ppermute | solution.py:910
  108.2 19.9 %all-to-all-start.1 = ((bf16[8,8,3840]{2,1,0:T(8,128)(2,1)}), bf16[8,8,3840]{2,1,0:T(8,128)(2,1)}, u32[]{:S(2)}, u32[]{:S(2)}) async-start(bf16[8,8,3840]{2,1,0:T(8,128)(2,1)} %fusion), calls=%async_computation.1 | async-start | bytes 983040 | tf_op jit(solution)/shard_map/all_to_all | solution.py:915
  136.1 18.0 %collective-permute-start.27 = (bf16[384,768]{1,0:T(8,128)(2,1)S(1)}, bf16[384,768]{1,0:T(8,128)(2,1)S(1)}, u32[]{:S(2)}, u32[]{:S(2)}) collective-permute-start(bf16[384,768]{1,0:T(8,128)(2,1)S(1)} %get-tuple-element.168), channel_id=1, source_target_pairs={{0,1},{1,0},{2,3},{3,2},{4,5},{5,4},{6,7},{7,6},{8,9},{9,8},{10,11... | collective-permute-start | bytes 1769480 | tf_op jit(solution)/shard_map/ppermute | solution.py:910
  137.6 16.5 %collective-permute-start.28 = (bf16[384,768]{1,0:T(8,128)(2,1)S(1)}, bf16[384,768]{1,0:T(8,128)(2,1)S(1)}, u32[]{:S(2)}, u32[]{:S(2)}) collective-permute-start(bf16[384,768]{1,0:T(8,128)(2,1)S(1)} %get-tuple-element.171), channel_id=1, source_target_pairs={{0,16},{16,0},{1,17},{17,1},{2,18},{18,2},{3,19},{19,3},{4,20},{20... | collective-permute-start | bytes 1769480 | tf_op jit(solution)/shard_map/ppermute | solution.py:910
  154.4 8.6 %collective-permute-start.32 = (bf16[192,768]{1,0:T(8,128)(2,1)S(1)}, bf16[192,768]{1,0:T(8,128)(2,1)S(1)}, u32[]{:S(2)}, u32[]{:S(2)}) collective-permute-start(bf16[192,768]{1,0:T(8,128)(2,1)S(1)} %get-tuple-element.188), channel_id=1, source_target_pairs={{0,1},{1,0},{2,3},{3,2},{4,5},{5,4},{6,7},{7,6},{8,9},{9,8},{10,11... | collective-permute-start | bytes 884744 | tf_op jit(solution)/shard_map/ppermute | solution.py:910
  155.0 8.2 %collective-permute-start.31 = (bf16[192,768]{1,0:T(8,128)(2,1)S(1)}, bf16[192,768]{1,0:T(8,128)(2,1)S(1)}, u32[]{:S(2)}, u32[]{:S(2)}) collective-permute-start(bf16[192,768]{1,0:T(8,128)(2,1)S(1)} %get-tuple-element.172), channel_id=1, source_target_pairs={{0,16},{16,0},{1,17},{17,1},{2,18},{18,2},{3,19},{19,3},{4,20},{20... | collective-permute-start | bytes 884744 | tf_op jit(solution)/shard_map/ppermute | solution.py:910
  163.4 9.5 %collective-permute-start.33 = (bf16[384,512]{1,0:T(8,128)(2,1)S(1)}, bf16[384,512]{1,0:T(8,128)(2,1)S(1)}, u32[]{:S(2)}, u32[]{:S(2)}) collective-permute-start(bf16[384,512]{1,0:T(8,128)(2,1)S(1)} %get-tuple-element.192), channel_id=1, source_target_pairs={{0,1},{1,0},{2,3},{3,2},{4,5},{5,4},{6,7},{7,6},{8,9},{9,8},{10,11... | collective-permute-start | bytes 1179656 | tf_op jit(solution)/shard_map/ppermute | solution.py:910
  164.9 9.1 %collective-permute-start.34 = (bf16[384,512]{1,0:T(8,128)(2,1)S(1)}, bf16[384,512]{1,0:T(8,128)(2,1)S(1)}, u32[]{:S(2)}, u32[]{:S(2)}) collective-permute-start(bf16[384,512]{1,0:T(8,128)(2,1)S(1)} %get-tuple-element.196), channel_id=1, source_target_pairs={{0,16},{16,0},{1,17},{17,1},{2,18},{18,2},{3,19},{19,3},{4,20},{20... | collective-permute-start | bytes 1179656 | tf_op jit(solution)/shard_map/ppermute | solution.py:910
  165.7 13.0 %collective-permute-start.36 = (bf16[48,1536]{1,0:T(8,128)(2,1)S(1)}, bf16[48,1536]{1,0:T(8,128)(2,1)S(1)}, u32[]{:S(2)}, u32[]{:S(2)}) collective-permute-start(bf16[48,1536]{1,0:T(8,128)(2,1)S(1)} %get-tuple-element.200), channel_id=1, source_target_pairs={{0,6},{2,0},{4,2},{6,4},{1,7},{3,1},{5,3},{7,5},{8,14},{10,8},{12,... | collective-permute-start | bytes 442376 | tf_op jit(solution)/shard_map/ppermute | solution.py:231
  168.6 11.9 %collective-permute-start.37 = (bf16[48,1536]{1,0:T(8,128)(2,1)S(1)}, bf16[48,1536]{1,0:T(8,128)(2,1)S(1)}, u32[]{:S(2)}, u32[]{:S(2)}) collective-permute-start(bf16[48,1536]{1,0:T(8,128)(2,1)S(1)} %get-tuple-element.201), channel_id=1, source_target_pairs={{0,4},{2,6},{4,0},{6,2},{1,5},{3,7},{5,1},{7,3},{8,12},{10,14},{12... | collective-permute-start | bytes 442376 | tf_op jit(solution)/shard_map/ppermute | solution.py:231
  168.6 11.9 %collective-permute-start.38 = (bf16[48,1536]{1,0:T(8,128)(2,1)S(1)}, bf16[48,1536]{1,0:T(8,128)(2,1)S(1)}, u32[]{:S(2)}, u32[]{:S(2)}) collective-permute-start(bf16[48,1536]{1,0:T(8,128)(2,1)S(1)} %get-tuple-element.202), channel_id=1, source_target_pairs={{0,2},{2,4},{4,6},{6,0},{1,3},{3,5},{5,7},{7,1},{8,10},{10,12},{12... | collective-permute-start | bytes 442376 | tf_op jit(solution)/shard_map/ppermute | solution.py:231
  178.7 14.4 %collective-permute-start.30 = (f32[128,768]{1,0:T(8,128)S(1)}, f32[128,768]{1,0:T(8,128)S(1)}, u32[]{:S(2)}, u32[]{:S(2)}) collective-permute-start(f32[128,768]{1,0:T(8,128)S(1)} %get-tuple-element.183), channel_id=1, source_target_pairs={{0,8},{8,0},{1,9},{9,1},{2,10},{10,2},{3,11},{11,3},{4,12},{12,4},... | collective-permute-start | bytes 1179656 | tf_op jit(solution)/shard_map/ppermute | solution.py:910
  184.1 8.1 %collective-permute-start.41 = (bf16[48,1024]{1,0:T(8,128)(2,1)S(1)}, bf16[48,1024]{1,0:T(8,128)(2,1)S(1)}, u32[]{:S(2)}, u32[]{:S(2)}) collective-permute-start(bf16[48,1024]{1,0:T(8,128)(2,1)S(1)} %get-tuple-element.207), channel_id=1, source_target_pairs={{0,4},{2,6},{4,0},{6,2},{1,5},{3,7},{5,1},{7,3},{8,12},{10,14},{12... | collective-permute-start | bytes 294920 | tf_op jit(solution)/shard_map/ppermute | solution.py:231
  184.1 8.1 %collective-permute-start.42 = (bf16[48,1024]{1,0:T(8,128)(2,1)S(1)}, bf16[48,1024]{1,0:T(8,128)(2,1)S(1)}, u32[]{:S(2)}, u32[]{:S(2)}) collective-permute-start(bf16[48,1024]{1,0:T(8,128)(2,1)S(1)} %get-tuple-element.208), channel_id=1, source_target_pairs={{0,2},{2,4},{4,6},{6,0},{1,3},{3,5},{5,7},{7,1},{8,10},{10,12},{12... | collective-permute-start | bytes 294920 | tf_op jit(solution)/shard_map/ppermute | solution.py:231
  (37 other events, 248.9 us)
